TPU v7x, 32 devices: a whole 2x2x4 slice. The times are simulated.
32 devices in a mesh: group: 4 (over z), member: 8 (over y, x, core).
Axes of the slice: x: 2, y: 2, z: 4, core: 2. Of those that a mesh axis runs over, the one named last changes fastest.
Arguments:
- features: bfloat16 [256, 512], P(('group', 'member')), may hold values from -6 to 6
- labels: int32 [256], P('group'), may hold values from 0 to 4095, as said below
- centres: bfloat16 [16384, 512], P(('group', 'member')), may hold values from -6 to 6
- block_ids: int32 [4, 32], P(None, ('group', 'member')), may hold values from 0 to 3
- listed: int32 [4, 32], P(None, ('group', 'member')), may hold values from 0 to 1, as said below
Outputs:
- sample_loss: float32 [256], P(('group', 'member'))
- feature_grad: float32 [256, 512], P(('group', 'member'))
- centre_grad: float32 [16384, 512], P(('group', 'member'))
Inputs may be any that keep to these rules, and one draw needn't show every extreme that they name: `listed`: every data group lists at least one block. `labels`: the label is a slot of an active block of the sample's group.
All inputs are finite; a program needn't handle non-finite values.
Results may differ from a plain program's by a relative error of at most 0.0042.
Values may be sent and summed in bfloat16 or wider, within the bound.
No kernel may reach another device: no remote copies, remote signals or barrier semaphores. Data moves between devices by JAX's collectives and lax.ppermute only.
A program may use at most 64 MiB of HBM per device.

v0:
```python
import jax
import jax.numpy as jnp
from jax import lax
from jax.sharding import PartitionSpec as P

BLK = 128


logit_scale = 32.0
cos_margin = 0.35
norm_epsilon = 1e-06


def on_device(features, labels, centres, block_ids, listed):
    groups = lax.axis_size("group")
    member = lax.axis_index("member")
    width = centres.shape[1]
    tok_dev = features.shape[0]
    vectors = features.astype(jnp.float32)
    inv_norm = lax.rsqrt(jnp.sum(vectors * vectors, axis=1, keepdims=True) + norm_epsilon)
    unit_rows = vectors * inv_norm
    held_blocks = centres.reshape(-1, BLK, width)
    outgoing = held_blocks[block_ids[:, 0]]
    flag_out = listed.astype(jnp.bfloat16)
    arrived, flag_in = (
        lax.all_to_all(outgoing, "group", split_axis=0, concat_axis=0, tiled=True),
        lax.all_to_all(flag_out, "group", split_axis=0, concat_axis=0, tiled=True),
    )
    cand_count = groups * BLK
    cand_float = arrived.reshape(cand_count, width).astype(jnp.float32)
    inv_cand = lax.rsqrt(jnp.sum(cand_float * cand_float, axis=1, keepdims=True) + norm_epsilon)
    unit_cand = cand_float * inv_cand
    cand_half = unit_cand.astype(jnp.bfloat16)
    gathered = lax.all_gather(unit_rows.astype(jnp.bfloat16), "member", axis=0, tiled=True)
    cosine = lax.dot_general(
        gathered, cand_half, (((1,), (1,)), ((), ())), preferred_element_type=jnp.float32
    )
    local_label = labels - member * cand_count
    onehot = (lax.broadcasted_iota(jnp.int32, (1, cand_count), 1) == local_label[:, None]).astype(
        jnp.float32
    )
    active = jnp.repeat(flag_in[:, 0].astype(jnp.float32), BLK)[None, :]
    logits = logit_scale * (cosine - cos_margin * onehot)
    exp_logits = jnp.exp(logits) * active
    totals, label_logit = lax.psum(
        (jnp.sum(exp_logits, axis=1), jnp.sum(logits * onehot, axis=1)), "member"
    )
    loss_all = jnp.log(totals) - label_logit
    sample_loss = lax.dynamic_slice_in_dim(loss_all, member * tok_dev, tok_dev, 0)
    weights = (logit_scale * (exp_logits / totals[:, None] - onehot)).astype(jnp.bfloat16)
    unit_grad = lax.psum_scatter(
        jnp.dot(weights, cand_half, preferred_element_type=jnp.float32),
        "member",
        scatter_dimension=0,
        tiled=True,
    )
    feature_grad = inv_norm * (
        unit_grad - jnp.sum(unit_grad * unit_rows, axis=1, keepdims=True) * unit_rows
    )
    slot_grad = lax.dot_general(
        weights, gathered, (((0,), (0,)), ((), ())), preferred_element_type=jnp.float32
    )
    cand_grad = (
        inv_cand * (slot_grad - jnp.sum(slot_grad * unit_cand, axis=1, keepdims=True) * unit_cand)
    ).astype(jnp.bfloat16)
    returned = lax.all_to_all(
        cand_grad.reshape(groups, BLK, width), "group", split_axis=0, concat_axis=0, tiled=True
    )
    flat_back = returned.reshape(groups, BLK * width)
    summed = (
        jnp.zeros((held_blocks.shape[0], BLK * width), jnp.float32)
        .at[block_ids[:, 0]]
        .add(flat_back.astype(jnp.float32))
    )
    centre_grad = summed.reshape(-1, width)
    return (sample_loss, feature_grad, centre_grad)


def solution(mesh):
    in_specs = (
        P(("group", "member"), None),
        P("group"),
        P(("group", "member"), None),
        P(None, ("group", "member")),
        P(None, ("group", "member")),
    )
    out_specs = (P(("group", "member")), P(("group", "member"), None), P(("group", "member"), None))
    return jax.shard_map(
        on_device, mesh=mesh, in_specs=in_specs, out_specs=out_specs, check_vma=False
    )
```

profile of v0, /device:TPU:0, one launch (start us, length us, event | category | flops | bytes accessed | tf_op | source)
XLA Modules:
  0.0 108.8 jit_solution(3867927740630784996)
XLA Ops:
  7.2 0.0 copy-start
  7.2 0.7 convert_bitcast_fusion.1
  7.9 0.7 copy.9
  8.6 6.3 %all-to-all-start.1 = ((bf16[4,1,1]{2,1,0:T(2,128)(2,1)}), bf16[4,1,1]{2,1,0:T(2,128)(2,1)S(1)}, u32[]{:S(2)}, u32[]{:S(2)}) async-start(bf16[4,1,1]{2,1,0:T(2,128)(2,1)} %copy.9), calls=%async_computation.1 | async-start | bytes 4096 | tf_op jit(solution)/shard_map/all_to_all | solution.py:27
  14.9 0.0 copy-start.1
  14.9 0.0 copy-start.3
  14.9 0.7 copy-done.3
  15.6 0.0 copy-done.1
  15.6 0.1 fusion.9
  15.7 0.0 copy-done
  15.7 1.4 %gather_fusion = bf16[4,128,512]{2,1,0:T(8,128)(2,1)} fusion(bf16[4,128,512]{2,1,0:T(8,128)(2,1)S(1)} %bitcast.25, s32[1024]{0:T(1024)S(1)} %pad_clamp_fusion), kind=kCustom, calls=%fused_computation | custom fusion | bytes 1048592 | tf_op jit(solution)/shard_map/gather | solution.py:23
  17.1 3.3 %all-to-all-done.1 = bf16[4,1,1]{2,1,0:T(2,128)(2,1)S(1)} async-done(((bf16[4,1,1]{2,1,0:T(2,128)(2,1)}), bf16[4,1,1]{2,1,0:T(2,128)(2,1)S(1)}, u32[]{:S(2)}, u32[]{:S(2)}) %all-to-all-start.1) | async-done | bytes 40 | tf_op jit(solution)/shard_map/all_to_all | solution.py:27
  20.4 3.5 %all-to-all-start = ((bf16[4,128,512]{2,1,0:T(8,128)(2,1)}), bf16[4,128,512]{2,1,0:T(8,128)(2,1)S(1)}, u32[]{:S(2)}, u32[]{:S(2)}) async-start(bf16[4,128,512]{2,1,0:T(8,128)(2,1)} %gather_fusion), calls=%async_computation | async-start | bytes 1048576 | tf_op jit(solution)/shard_map/all_to_all | solution.py:26
  23.9 0.1 fusion.5
  23.9 0.0 copy-start.4
  23.9 9.4 %all_gather.3 = bf16[64,512]{1,0:T(8,128)(2,1)S(1)} all-gather(bf16[8,512]{1,0:T(8,128)(2,1)S(1)} %fusion.5), channel_id=1, replica_groups=mesh['group'=4,'member'=8] {'member'}, dimensions={0}, use_global_device_ids=true | all-gather | bytes 73728 | tf_op jit(solution)/shard_map/all_gather | solution.py:34
  33.3 0.0 copy-done.4
  33.3 0.1 convert_reduce_fusion
  33.4 0.1 broadcast_bitcast_fusion
  33.5 3.7 %all-to-all-done = bf16[4,128,512]{2,1,0:T(8,128)(2,1)S(1)} async-done(((bf16[4,128,512]{2,1,0:T(8,128)(2,1)}), bf16[4,128,512]{2,1,0:T(8,128)(2,1)S(1)}, u32[]{:S(2)}, u32[]{:S(2)}) %all-to-all-start) | async-done | bytes 524320 | tf_op jit(solution)/shard_map/all_to_all | solution.py:26
  37.2 0.2 multiply_reduce_fusion.1
  37.3 0.2 fusion.1
  37.5 0.4 fusion.2
  37.9 12.7 %all-reduce = (f32[64]{0:T(128)S(1)}, f32[64]{0:T(128)S(1)}) all-reduce(f32[64]{0:T(128)S(1)} %get-tuple-element.4, f32[64]{0:T(128)S(1)} %get-tuple-element.3), channel_id=1, replica_groups=mesh['group'=4,'member'=8] {'member'}, use_global_device_ids=true, to_apply=%region_5.0 | all-reduce | flops 128 | bytes 1024 | tf_op jit(solution)/shard_map/psum | solution.py:45
  50.7 0.5 multiply_reduce_fusion
  51.2 1.1 multiply_convert_fusion
  52.2 3.5 %all-to-all-start.2 = ((bf16[4,128,512]{2,1,0:T(8,128)(2,1)}), bf16[4,128,512]{2,1,0:T(8,128)(2,1)S(1)}, u32[]{:S(2)}, u32[]{:S(2)}) async-start(bf16[4,128,512]{2,1,0:T(8,128)(2,1)} %bitcast.6), calls=%async_computation.3 | async-start | bytes 1048576 | tf_op jit(solution)/shard_map/all_to_all | solution.py:66
  55.7 0.0 reduce-scatter.2.cloned.1.call-start
  55.8 0.9 fusion.12
  56.7 0.0 reduce-scatter.2.cloned.1.call-update
  56.7 0.6 dynamic_slice.3
  57.3 35.2 %reduce-scatter.2.cloned.1.call-done = f32[8,512]{1,0:T(8,128)} async-done(((f32[64,512]{1,0:T(8,128)}), f32[8,512]{1,0:T(8,128)}) %reduce-scatter.2.cloned.1.call-update) | async-done | bytes 16400 | tf_op jit(solution)/shard_map/reduce_scatter | solution.py:51
  92.5 0.0 copy-start.2
  92.5 1.0 fusion.6
  93.5 0.0 copy-done.2
  93.5 0.7 fusion.8
  94.2 0.0 all-to-all-done.2
  94.2 0.1 convert_bitcast_fusion
  94.3 0.7 copy.10
  95.0 0.1 broadcast_in_dim.5
  95.1 5.1 %scatter_fusion = f32[4,65536]{1,0:T(4,128)S(1)} fusion(f32[4,65536]{1,0:T(4,128)S(1)} %broadcast_in_dim.5, s32[4]{0:T(128)S(1)} %fusion.10, f32[4,65536]{1,0:T(4,128)S(1)} %bitcast.26), kind=kCustom, calls=%fused_computation.1 | custom fusion | flops 262144 | bytes 3145744 | tf_op jit(solution)/shard_map/scatter-add | solution.py:73
  100.3 1.7 %reshape.52 = f32[512,512]{1,0:T(8,128)} reshape(f32[4,65536]{1,0:T(4,128)S(1)} %scatter_fusion) | data formatting | bytes 2097152 | tf_op jit(solution)/shard_map/reshape | solution.py:75
  (6 shorter events, 0.0 us)
Async XLA Ops:
  7.2 8.6 %copy-start = (bf16[512,512]{1,0:T(8,128)(2,1)S(1)}, bf16[512,512]{1,0:T(8,128)(2,1)}, u32[]{:S(2)}) copy-start(bf16[512,512]{1,0:T(8,128)(2,1)} %param.7) | copy-start | bytes 1572868
  8.6 11.8 %all-to-all-start.1 = ((bf16[4,1,1]{2,1,0:T(2,128)(2,1)}), bf16[4,1,1]{2,1,0:T(2,128)(2,1)S(1)}, u32[]{:S(2)}, u32[]{:S(2)}) async-start(bf16[4,1,1]{2,1,0:T(2,128)(2,1)} %copy.9), calls=%async_computation.1 | async-start | bytes 4096 | tf_op jit(solution)/shard_map/all_to_all | solution.py:27
  14.9 0.7 copy-start.1
  14.9 0.7 copy-start.3
  20.4 16.8 %all-to-all-start = ((bf16[4,128,512]{2,1,0:T(8,128)(2,1)}), bf16[4,128,512]{2,1,0:T(8,128)(2,1)S(1)}, u32[]{:S(2)}, u32[]{:S(2)}) async-start(bf16[4,128,512]{2,1,0:T(8,128)(2,1)} %gather_fusion), calls=%async_computation | async-start | bytes 1048576 | tf_op jit(solution)/shard_map/all_to_all | solution.py:26
  23.9 9.4 %copy-start.4 = (s32[64]{0:T(128)S(1)}, s32[64]{0:T(128)}, u32[]{:S(2)}) copy-start(s32[64]{0:T(128)} %param.6) | copy-start | bytes 772
  52.2 42.0 %all-to-all-start.2 = ((bf16[4,128,512]{2,1,0:T(8,128)(2,1)}), bf16[4,128,512]{2,1,0:T(8,128)(2,1)S(1)}, u32[]{:S(2)}, u32[]{:S(2)}) async-start(bf16[4,128,512]{2,1,0:T(8,128)(2,1)} %bitcast.6), calls=%async_computation.3 | async-start | bytes 1048576 | tf_op jit(solution)/shard_map/all_to_all | solution.py:66
  55.7 36.8 %reduce-scatter.2.cloned.1.call-start = ((), (), s32[]{:S(2)}) async-start(), calls=%async_computation.4 | async-start | bytes 147456 | tf_op jit(solution)/shard_map/reduce_scatter | solution.py:51
  92.5 1.0 copy-start.2
Sparse Core Ops, SparseCore 0:
  59.6 32.9 reduce-scatter.1
where the time goes:
time: 109 us
  waiting for transfers between devices  42.2 us (39%)
  blocking collectives  22.1 us (20%)
  between operations  14.1 us (13%)
  starting transfers between devices  13.3 us (12%)
  other arithmetic  9.35 us (9%)
  local copies, waits for them, and re-layouts  5.93 us (5%)
  matrix products  1.8 us (2%)
    reduce_scatter x1, waiting for transfers between devices, on_device(): lax.psum_scatter(jnp.dot(weights, cand_half, preferred_element_type=jnp.f...  35.2 us
    psum x1, blocking collectives, on_device(): lax.psum((jnp.sum(exp_logits, axis=1), jnp.sum(logits * onehot, axis=1)),...  12.7 us
    all_gather x1, blocking collectives, on_device(): lax.all_gather(unit_rows.astype(jnp.bfloat16), 'member', axis=0, tiled=True)  9.36 us
    all_to_all x1, starting transfers between devices, on_device(): lax.all_to_all(flag_out, 'group', split_axis=0, concat_axis=0, tiled=True)  6.32 us
    scatter-add x1, other arithmetic, on_device(): summed = jnp.zeros((held_blocks.shape[0], BLK * width), jnp.float32).at[b...  5.12 us
    all_to_all x1, waiting for transfers between devices, on_device(): lax.all_to_all(outgoing, 'group', split_axis=0, concat_axis=0, tiled=True)  3.68 us
    all_to_all x1, starting transfers between devices, on_device(): lax.all_to_all(outgoing, 'group', split_axis=0, concat_axis=0, tiled=True)  3.47 us
    all_to_all x1, starting transfers between devices, on_device(): lax.all_to_all(cand_grad.reshape(groups, BLK, width), 'group', split_axis...  3.47 us
  transfers between devices with their start and end apart: 4, of which 3 were waited for; matrix products, arithmetic and copies ran while one was open for 5% of the time, Pallas kernels for 0%

commit v1 on v0

v1 whole, which is shorter than its diff:
```python
import jax
import jax.numpy as jnp
from jax import lax
from jax.sharding import PartitionSpec as P

BLK = 128
AXES = ("group", "member")

logit_scale = 32.0
cos_margin = 0.35
norm_epsilon = 1e-06


def sum_over_devices(values, devices):
    if devices * values.size > 1 << 20:
        return lax.psum(values, AXES)
    copies = jnp.broadcast_to(values[None], (devices, values.size))
    return jnp.sum(lax.all_to_all(copies, AXES, 0, 0, tiled=True), axis=0)


def on_device(features, labels, centres, block_ids, listed):
    groups = lax.axis_size("group")
    members = lax.axis_size("member")
    devices = groups * members
    group = lax.axis_index("group")
    member = lax.axis_index("member")
    tok_dev, width = features.shape
    group_tok = members * tok_dev
    held = centres.shape[0] // BLK

    vectors = features.astype(jnp.float32)
    inv_norm = lax.rsqrt(jnp.sum(vectors * vectors, axis=1, keepdims=True) + norm_epsilon)
    unit_rows = vectors * inv_norm
    own_labels = lax.dynamic_slice_in_dim(labels, member * tok_dev, tok_dev, 0)
    digits = jnp.stack([own_labels & 127, (own_labels >> 7) & 127, own_labels >> 14], axis=1)
    digits = jnp.pad(digits, ((0, 0), (0, 125))).astype(jnp.bfloat16)
    packed = jnp.concatenate([unit_rows.astype(jnp.bfloat16), digits], axis=1)
    gathered = lax.all_to_all(
        jnp.broadcast_to(packed[None], (devices, tok_dev, width + 128)), AXES, 0, 0, tiled=True
    )

    picked = centres.reshape(held, BLK, width)[block_ids[:, 0]].astype(jnp.float32)
    inv_cand = lax.rsqrt(jnp.sum(picked * picked, axis=2, keepdims=True) + norm_epsilon)
    unit_cand = picked * inv_cand
    cand_half = unit_cand.astype(jnp.bfloat16)

    gathered = gathered.reshape(groups, group_tok, width + 128)
    units = gathered[:, :, :width]
    digits = gathered[:, :, width : width + 3].astype(jnp.int32)
    all_labels = digits[:, :, 0] + (digits[:, :, 1] << 7) + (digits[:, :, 2] << 14)
    cosine = jnp.einsum("gsd,gcd->gsc", units, cand_half, preferred_element_type=jnp.float32)
    local_label = all_labels - (member * groups + group) * BLK
    onehot = (lax.broadcasted_iota(jnp.int32, (1, 1, BLK), 2) == local_label[:, :, None]).astype(
        jnp.float32
    )
    logits = logit_scale * (cosine - cos_margin * onehot)
    exp_logits = jnp.exp(logits) * listed.astype(jnp.float32)[:, :, None]
    sums = jnp.stack([jnp.sum(exp_logits, axis=2), jnp.sum(logits * onehot, axis=2)])
    both = sum_over_devices(sums.reshape(-1), devices).reshape(sums.shape)
    totals = both[0]
    loss_all = (jnp.log(totals) - both[1]).reshape(devices, tok_dev)
    sample_loss = lax.dynamic_slice_in_dim(loss_all, group * members + member, 1, 0)[0]

    weights = (logit_scale * (exp_logits / totals[:, :, None] - onehot)).astype(jnp.bfloat16)
    partial = jnp.einsum("gsc,gcd->gsd", weights, cand_half, preferred_element_type=jnp.float32)
    home = lax.all_to_all(
        partial.astype(jnp.bfloat16).reshape(devices, tok_dev, width), AXES, 0, 0, tiled=True
    )
    slot_grad = jnp.einsum("gsc,gsd->gcd", weights, units, preferred_element_type=jnp.float32)
    cand_grad = inv_cand * (
        slot_grad - jnp.sum(slot_grad * unit_cand, axis=2, keepdims=True) * unit_cand
    )
    cand_grad = cand_grad.astype(jnp.bfloat16).astype(jnp.float32)
    names = block_ids == jnp.arange(held, dtype=jnp.int32)[None, :]
    centre_grad = jnp.sum(
        jnp.where(names[:, :, None, None], cand_grad[:, None], 0.0), axis=0
    ).reshape(held * BLK, width)

    unit_grad = jnp.sum(home.astype(jnp.float32), axis=0)
    feature_grad = inv_norm * (
        unit_grad - jnp.sum(unit_grad * unit_rows, axis=1, keepdims=True) * unit_rows
    )
    return (sample_loss, feature_grad, centre_grad)


def solution(mesh):
    in_specs = (
        P(AXES, None),
        P("group"),
        P(AXES, None),
        P(None, AXES),
        P(None, AXES),
    )
    out_specs = (P(AXES), P(AXES, None), P(AXES, None))
    return jax.shard_map(
        on_device, mesh=mesh, in_specs=in_specs, out_specs=out_specs, check_vma=False
    )
```

time: 109 us -> 51.1 us (0.47)
  blocking collectives: 22.1 us -> 0 us
  waiting for transfers between devices: 42.2 us -> 25 us
  between operations: 14.1 us -> 0.8 us
  local copies, waits for them, and re-layouts: 5.93 us -> 2.88 us
  other arithmetic: 9.35 us -> 7.45 us
    reduce_scatter x1 -> x0, waiting for transfers between devices: 35.2 us -> none  [on_device(): lax.psum_scatter(jnp.dot(weights, cand_half, preferred_element_type=jnp.f...]
    all_to_all x3, waiting for transfers between devices: 6.93 us -> 25 us  [the longest x1 11.1 us: on_device(): lax.all_to_all(jnp.broadcast_to(packed[None], (devices, tok_dev, width +...]
    psum x1 -> x0, blocking collectives: 12.7 us -> none  [on_device(): lax.psum((jnp.sum(exp_logits, axis=1), jnp.sum(logits * onehot, axis=1)),...]
    all_gather x1 -> x0, blocking collectives: 9.36 us -> none  [on_device(): lax.all_gather(unit_rows.astype(jnp.bfloat16), 'member', axis=0, tiled=True)]
    scatter-add x1 -> x0, other arithmetic: 5.12 us -> none  [on_device(): summed = jnp.zeros((held_blocks.shape[0], BLK * width), jnp.float32).at[b...]
    mul x0 -> x2, other arithmetic: none -> 2.14 us  [the longest x1 2.14 us: on_device(): jnp.sum(slot_grad * unit_cand, axis=2, keepdims=True) * unit_cand]
    reshape x1 -> x0, local copies, waits for them, and re-layouts: 1.69 us -> none  [on_device(): centre_grad = summed.reshape(-1, width)]
    reduce_sum x1 -> x4, other arithmetic: 0.18 us -> 1.64 us  [the longest x1 1.35 us: on_device(): jnp.sum(jnp.where(names[:, :, None, None], cand_grad[:, None], 0.0), axis=0)]
  transfers between devices with their start and end apart: 4 -> 3, of which waited for: 3 -> 3; matrix products, arithmetic and copies ran while one was open for 5% -> 10% of each run, Pallas kernels for 0% -> 0%
where the time goes in v1:
time: 51.1 us; the launch traced here: 50.6 us
  waiting for transfers between devices  25 us (49%)
  starting transfers between devices  12.5 us (24%)
  other arithmetic  7.45 us (15%)
  local copies, waits for them, and re-layouts  2.88 us (6%)
  matrix products  1.99 us (4%)
  between operations  0.8 us (2%)
    all_to_all x1, waiting for transfers between devices, on_device(): lax.all_to_all(jnp.broadcast_to(packed[None], (devices, tok_dev, width +...  11.1 us
    all_to_all x1, waiting for transfers between devices, sum_over_devices(): return jnp.sum(lax.all_to_all(copies, AXES, 0, 0, tiled=True), axis=0)  7.34 us
    all_to_all x1, starting transfers between devices, on_device(): lax.all_to_all(jnp.broadcast_to(packed[None], (devices, tok_dev, width +...  7.3 us
    all_to_all x1, waiting for transfers between devices, on_device(): lax.all_to_all(partial.astype(jnp.bfloat16).reshape(devices, tok_dev, wid...  6.56 us
    all_to_all x1, starting transfers between devices, on_device(): lax.all_to_all(partial.astype(jnp.bfloat16).reshape(devices, tok_dev, wid...  2.6 us
    all_to_all x1, starting transfers between devices, sum_over_devices(): return jnp.sum(lax.all_to_all(copies, AXES, 0, 0, tiled=True), axis=0)  2.57 us
    mul x1, other arithmetic, on_device(): jnp.sum(slot_grad * unit_cand, axis=2, keepdims=True) * unit_cand  2.14 us
    reduce_sum x1, other arithmetic, on_device(): jnp.sum(jnp.where(names[:, :, None, None], cand_grad[:, None], 0.0), axis=0)  1.35 us
  transfers between devices with their start and end apart: 3, of which 3 were waited for; matrix products, arithmetic and copies ran while one was open for 10% of the time, Pallas kernels for 0%

profile of v1, /device:TPU:0, one launch (start us, length us, event | category | flops | bytes accessed | tf_op | source)
XLA Modules:
  0.0 50.6 jit_solution(1797562515356434649)
XLA Ops:
  0.6 0.0 copy-start
  0.6 0.0 copy-start.3
  0.7 0.8 %convert_bitcast_fusion.3 = (bf16[8,1]{0,1:T(2,128)(2,1)S(1)}, bf16[8,1]{0,1:T(2,128)(2,1)S(1)}, bf16[8,1]{0,1:T(2,128)(2,1)S(1)}) fusion(s32[64]{0:T(128)} %param.6, s32[]{:T(128)S(6)} %select_n.14), kind=kLoop, calls=%fused_computation.58 | loop fusion | flops 56 | bytes 84 | tf_op jit(solution)/shard_map/stack | solution.py:35
  1.5 0.1 copy.16
  1.6 0.8 %fusion.34 = f32[8]{0:T(128)S(1)} fusion(bf16[8,512]{1,0:T(8,128)(2,1)} %param.5), kind=kLoop, calls=%fused_computation.44 | loop fusion | flops 12280 | bytes 8224 | tf_op jit(solution)/shard_map/reduce_sum | solution.py:32
  2.4 0.8 %fusion.29 = bf16[8,512]{1,0:T(8,128)(2,1)S(1)} fusion(bf16[8,512]{1,0:T(8,128)(2,1)} %param.5, f32[8]{0:T(128)S(1)} %add_rsqrt_fusion.1), kind=kLoop, calls=%fused_computation.38 | loop fusion | flops 12288 | bytes 16416 | tf_op jit(solution)/shard_map/convert_element_type | solution.py:37
  3.2 0.8 %broadcast_in_dim.19 = bf16[32,8,640]{2,1,0:T(8,128)(2,1)} broadcast(bf16[8,640]{1,0:T(8,128)(2,1)S(1)} %fusion.35), dimensions={1,2} | broadcast | bytes 337920 | tf_op jit(solution)/shard_map/broadcast_in_dim | solution.py:39
  3.9 0.0 copy-start.2
  3.9 7.3 %all-to-all-start = ((bf16[32,8,640]{2,1,0:T(8,128)(2,1)}), bf16[32,8,640]{2,1,0:T(8,128)(2,1)S(1)}, u32[]{:S(2)}, u32[]{:S(2)}) async-start(bf16[32,8,640]{2,1,0:T(8,128)(2,1)} %broadcast_in_dim.19), calls=%async_computation | async-start | bytes 655360 | tf_op jit(solution)/shard_map/all_to_all | solution.py:38
  11.2 0.0 copy-done.3
  11.3 0.0 copy-done
  11.3 0.6 %gather_fusion = bf16[4,128,512]{2,1,0:T(8,128)(2,1)S(1)} fusion(bf16[4,128,512]{2,1,0:T(8,128)(2,1)S(1)} %bitcast.19, s32[1024]{0:T(1024)S(1)} %pad_clamp_fusion), kind=kCustom, calls=%fused_computation | custom fusion | bytes 1048592 | tf_op jit(solution)/shard_map/gather | solution.py:42
  11.9 0.2 fusion.15
  12.1 0.0 copy-done.2
  12.1 11.1 %all-to-all-done = bf16[32,8,640]{2,1,0:T(8,128)(2,1)S(1)} async-done(((bf16[32,8,640]{2,1,0:T(8,128)(2,1)}), bf16[32,8,640]{2,1,0:T(8,128)(2,1)S(1)}, u32[]{:S(2)}, u32[]{:S(2)}) %all-to-all-start) | async-done | bytes 327712 | tf_op jit(solution)/shard_map/all_to_all | solution.py:38
  23.2 0.3 fusion.24
  23.5 0.5 fusion.26
  24.0 0.1 broadcast_in_dim.20
  24.1 0.7 %broadcast_in_dim.21 = f32[32,1,512]{2,1,0:T(1,128)} broadcast(f32[512]{0:T(512)S(1)} %broadcast_in_dim.20), dimensions={2} | broadcast | bytes 67584 | tf_op jit(solution)/shard_map/broadcast_in_dim | solution.py:17
  24.7 2.6 %all-to-all-start.1 = ((f32[32,1,512]{2,1,0:T(1,128)}), f32[32,1,512]{2,1,0:T(1,128)S(1)}, u32[]{:S(2)}, u32[]{:S(2)}) async-start(f32[32,1,512]{2,1,0:T(1,128)} %broadcast_in_dim.21), calls=%async_computation.1 | async-start | bytes 131072 | tf_op jit(solution)/shard_map/all_to_all | solution.py:18
  27.3 0.1 iota_compare_fusion.2
  27.4 7.3 %all-to-all-done.1 = f32[32,1,512]{2,1,0:T(1,128)S(1)} async-done(((f32[32,1,512]{2,1,0:T(1,128)}), f32[32,1,512]{2,1,0:T(1,128)S(1)}, u32[]{:S(2)}, u32[]{:S(2)}) %all-to-all-start.1) | async-done | bytes 65568 | tf_op jit(solution)/shard_map/all_to_all | solution.py:18
  34.7 0.1 reduce_sum.85
  34.8 0.1 div.10
  34.9 1.0 %convolution_convert_fusion = bf16[4,64,512]{2,1,0:T(8,128)(2,1)} fusion(bf16[4,128,512]{2,1,0:T(8,128)(2,1)S(1)} %gather_fusion, f32[4,128]{1,0:T(4,128)S(1)} %add_rsqrt_fusion, f32[4,64,128]{2,1,0:T(8,128)S(1)} %get-tuple-element.10, f32[4,64]{1,0:T(4,128)S(1)} %div.10, f32[4]{0:T(128)S(1)} %convert_bitcast_fusion, s32[4,64]{1,0:T(4,128)S(1)} %fusion.24), kind=kOutput, calls=%fused_computation.13 | convolution fusion | flops 34701312 | bytes 921616 | tf_op jit(solution)/shard_map/gsc,gcd->gsd/dot_general | solution.py:65
  35.9 0.5 fusion.19
  36.4 0.1 sub.30
  36.5 2.6 %all-to-all-start.2 = ((bf16[32,8,512]{2,1,0:T(8,128)(2,1)}), bf16[32,8,512]{2,1,0:T(8,128)(2,1)S(1)}, u32[]{:S(2)}, u32[]{:S(2)}) async-start(bf16[32,8,512]{2,1,0:T(8,128)(2,1)} %bitcast.10), calls=%async_computation.2 | async-start | bytes 524288 | tf_op jit(solution)/shard_map/all_to_all | solution.py:66
  39.1 0.5 %dynamic-slice_bitcast_fusion = f32[8]{0:T(128)} fusion(f32[32,8]{1,0:T(8,128)S(1)} %sub.30, s32[]{:T(128)S(6)} %select_n.16), kind=kLoop, calls=%fused_computation.54 | loop fusion | bytes 68 | tf_op jit(solution)/shard_map/squeeze | solution.py:62
  39.6 2.1 %fusion.11 = f32[4,128,512]{2,1,0:T(8,128)S(1)} fusion(f32[4,128,512]{2,1,0:T(8,128)S(1)} %fusion.19, bf16[4,128,512]{2,1,0:T(8,128)(2,1)S(1)} %gather_fusion, f32[4,128]{1,0:T(4,128)S(1)} %add_rsqrt_fusion), kind=kOutput, calls=%fused_computation.12 | output fusion | flops 2622463 | bytes 2623488 | tf_op jit(solution)/shard_map/mul | solution.py:71
  41.8 0.0 copy-start.1
  41.8 1.4 %select_reduce_fusion = f32[4,128,512]{2,1,0:T(8,128)} fusion(f32[4,128,512]{2,1,0:T(8,128)S(1)} %fusion.11, pred[4,4]{1,0:T(4,128)(4,1)S(1)} %iota_compare_fusion.2), kind=kLoop, calls=%fused_computation.2 | loop fusion | flops 1835008 | bytes 2097168 | tf_op jit(solution)/shard_map/reduce_sum | solution.py:75
  43.1 6.6 %all-to-all-done.2 = bf16[32,8,512]{2,1,0:T(8,128)(2,1)S(1)} async-done(((bf16[32,8,512]{2,1,0:T(8,128)(2,1)}), bf16[32,8,512]{2,1,0:T(8,128)(2,1)S(1)}, u32[]{:S(2)}, u32[]{:S(2)}) %all-to-all-start.2) | async-done | bytes 262176 | tf_op jit(solution)/shard_map/all_to_all | solution.py:66
  49.7 0.0 copy-done.1
  49.8 0.2 fusion.31
  49.9 0.7 %fusion.33 = f32[8,512]{1,0:T(8,128)} fusion(f32[8,512]{1,0:T(8,128)S(1)} %convert_reduce_fusion, bf16[8,512]{1,0:T(8,128)(2,1)S(1)} %copy-done.1, f32[8]{0:T(128)S(1)} %fusion.31, f32[8]{0:T(128)S(1)} %add_rsqrt_fusion.1), kind=kLoop, calls=%fused_computation.43 | loop fusion | flops 20480 | bytes 41024 | tf_op jit(solution)/shard_map/mul | solution.py:80
  (11 shorter events, 0.1 us)
Async XLA Ops:
  0.6 10.6 %copy-start = (bf16[512,512]{1,0:T(8,128)(2,1)S(1)}, bf16[512,512]{1,0:T(8,128)(2,1)}, u32[]{:S(2)}) copy-start(bf16[512,512]{1,0:T(8,128)(2,1)} %param.7) | copy-start | bytes 1572868
  0.6 10.6 %copy-start.3 = (s32[4,1]{0,1:T(1,128)S(1)}, s32[4,1]{0,1:T(1,128)}, u32[]{:S(2)}) copy-start(s32[4,1]{0,1:T(1,128)} %param.8) | copy-start | bytes 52
  3.9 8.1 %copy-start.2 = (s32[4,1]{0,1:T(1,128)S(1)}, s32[4,1]{0,1:T(1,128)}, u32[]{:S(2)}) copy-start(s32[4,1]{0,1:T(1,128)} %param.9) | copy-start | bytes 52
  3.9 19.3 %all-to-all-start = ((bf16[32,8,640]{2,1,0:T(8,128)(2,1)}), bf16[32,8,640]{2,1,0:T(8,128)(2,1)S(1)}, u32[]{:S(2)}, u32[]{:S(2)}) async-start(bf16[32,8,640]{2,1,0:T(8,128)(2,1)} %broadcast_in_dim.19), calls=%async_computation | async-start | bytes 655360 | tf_op jit(solution)/shard_map/all_to_all | solution.py:38
  24.7 10.0 %all-to-all-start.1 = ((f32[32,1,512]{2,1,0:T(1,128)}), f32[32,1,512]{2,1,0:T(1,128)S(1)}, u32[]{:S(2)}, u32[]{:S(2)}) async-start(f32[32,1,512]{2,1,0:T(1,128)} %broadcast_in_dim.21), calls=%async_computation.1 | async-start | bytes 131072 | tf_op jit(solution)/shard_map/all_to_all | solution.py:18
  36.5 13.2 %all-to-all-start.2 = ((bf16[32,8,512]{2,1,0:T(8,128)(2,1)}), bf16[32,8,512]{2,1,0:T(8,128)(2,1)S(1)}, u32[]{:S(2)}, u32[]{:S(2)}) async-start(bf16[32,8,512]{2,1,0:T(8,128)(2,1)} %bitcast.10), calls=%async_computation.2 | async-start | bytes 524288 | tf_op jit(solution)/shard_map/all_to_all | solution.py:66
  41.8 8.0 %copy-start.1 = (bf16[8,512]{1,0:T(8,128)(2,1)S(1)}, bf16[8,512]{1,0:T(8,128)(2,1)}, u32[]{:S(2)}) copy-start(bf16[8,512]{1,0:T(8,128)(2,1)} %param.5) | copy-start | bytes 24580

commit v2 on v1

v2 whole, which is shorter than its diff:
```python
import jax
import jax.numpy as jnp
from jax import lax
from jax.sharding import PartitionSpec as P

BLK = 128
AXES = ("group", "member")

logit_scale = 32.0
cos_margin = 0.35
norm_epsilon = 1e-06


def from_ahead(value, axis, step):
    size = lax.axis_size(axis)
    if step % size == 0:
        return value
    return lax.ppermute(value, axis, [((i + step) % size, i) for i in range(size)])


def on_device(features, labels, centres, block_ids, listed):
    groups = lax.axis_size("group")
    members = lax.axis_size("member")
    group = lax.axis_index("group")
    member = lax.axis_index("member")
    tok_dev, width = features.shape
    group_tok = members * tok_dev
    held = centres.shape[0] // BLK

    vectors = features.astype(jnp.float32)
    inv_norm = lax.rsqrt(jnp.sum(vectors * vectors, axis=1, keepdims=True) + norm_epsilon)
    unit_rows = vectors * inv_norm
    digits = jnp.stack([labels & 127, (labels >> 7) & 127, labels >> 14], axis=0)
    digits = digits.reshape(3 * tok_dev, members)
    digits = jnp.pad(digits, ((0, 0), (0, 128 - members))).astype(jnp.bfloat16)
    digits = digits.reshape(3, tok_dev, 128).transpose(1, 0, 2).reshape(tok_dev, 3 * 128)
    packed = jnp.concatenate([unit_rows.astype(jnp.bfloat16), digits], axis=1)
    over_groups = jnp.stack([from_ahead(packed, "group", j) for j in range(groups)])
    digits = over_groups[:, :, width:].astype(jnp.int32).reshape(groups, tok_dev, 3, 128)
    digits = digits.transpose(0, 2, 1, 3)[..., :members].reshape(groups, 3, group_tok)
    all_labels = digits[:, 0] + (digits[:, 1] << 7) + (digits[:, 2] << 14)
    all_labels = jnp.roll(all_labels, -member * tok_dev, axis=1)
    columns = over_groups[:, :, :width]
    units = jnp.stack([from_ahead(columns, "member", i) for i in range(members)], axis=1)
    units = units.reshape(groups, group_tok, width)

    ids = jnp.roll(block_ids[:, 0], -group)
    flags = jnp.roll(listed[:, 0], -group).astype(jnp.float32)
    picked = centres.reshape(held, BLK, width)[ids].astype(jnp.float32)
    inv_cand = lax.rsqrt(jnp.sum(picked * picked, axis=2, keepdims=True) + norm_epsilon)
    unit_cand = picked * inv_cand
    cand_half = unit_cand.astype(jnp.bfloat16)

    cosine = jnp.einsum("gsd,gcd->gsc", units, cand_half, preferred_element_type=jnp.float32)
    local_label = all_labels - (member * groups + group) * BLK
    onehot = (lax.broadcasted_iota(jnp.int32, (1, 1, BLK), 2) == local_label[:, :, None]).astype(
        jnp.float32
    )
    logits = logit_scale * (cosine - cos_margin * onehot)
    exp_logits = jnp.exp(logits) * flags[:, None, None]
    sums = jnp.stack([jnp.sum(exp_logits, axis=2), jnp.sum(logits * onehot, axis=2)])
    sums = sums.reshape(2, groups, members, tok_dev)
    sums = sum(
        jnp.roll(from_ahead(sums, "member", i), i, axis=2) for i in range(members)
    )
    sums = sum(jnp.roll(from_ahead(sums, "group", j), j, axis=1) for j in range(groups))
    sample_loss = jnp.log(sums[0, 0, 0]) - sums[1, 0, 0]
    totals = sums[0].reshape(groups, group_tok)

    weights = (logit_scale * (exp_logits / totals[:, :, None] - onehot)).astype(jnp.bfloat16)
    partial = jnp.einsum("gsc,gcd->gsd", weights, cand_half, preferred_element_type=jnp.float32)
    partial = partial.astype(jnp.bfloat16).reshape(groups, members, tok_dev, width)
    home = sum(
        from_ahead(partial[:, i], "member", -i).astype(jnp.float32) for i in range(members)
    )
    home = home.astype(jnp.bfloat16)
    unit_grad = sum(
        from_ahead(home[j], "group", -j).astype(jnp.float32) for j in range(groups)
    )
    feature_grad = inv_norm * (
        unit_grad - jnp.sum(unit_grad * unit_rows, axis=1, keepdims=True) * unit_rows
    )

    slot_grad = jnp.einsum("gsc,gsd->gcd", weights, units, preferred_element_type=jnp.float32)
    cand_grad = inv_cand * (
        slot_grad - jnp.sum(slot_grad * unit_cand, axis=2, keepdims=True) * unit_cand
    )
    cand_grad = cand_grad.astype(jnp.bfloat16).astype(jnp.float32)
    names = ids[:, None] == jnp.arange(held, dtype=jnp.int32)[None, :]
    centre_grad = jnp.sum(
        jnp.where(names[:, :, None, None], cand_grad[:, None], 0.0), axis=0
    ).reshape(held * BLK, width)
    return (sample_loss, feature_grad, centre_grad)


def solution(mesh):
    in_specs = (
        P(AXES, None),
        P("group"),
        P(AXES, None),
        P(None, AXES),
        P(None, AXES),
    )
    out_specs = (P(AXES), P(AXES, None), P(AXES, None))
    return jax.shard_map(
        on_device, mesh=mesh, in_specs=in_specs, out_specs=out_specs, check_vma=False
    )
```

time: 51.1 us -> 67.6 us (1.32)
  starting transfers between devices: 12.5 us -> 35.9 us
  waiting for transfers between devices: 25 us -> 18.4 us
  other arithmetic: 7.45 us -> 9.56 us
  local copies, waits for them, and re-layouts: 2.88 us -> 1.15 us
  matrix products: 1.99 us -> 1.29 us
    ppermute x0 -> x30, starting transfers between devices: none -> 35.9 us  [from_ahead(): lax.ppermute(value, axis, [((i + step) % size, i) for i in range(size)])]
    all_to_all x3 -> x0, waiting for transfers between devices: 25 us -> none  [the longest x1 11.1 us: on_device(): lax.all_to_all(jnp.broadcast_to(packed[None], (devices, tok_dev, width +...]
    ppermute x0 -> x30, waiting for transfers between devices: none -> 18.4 us  [from_ahead(): lax.ppermute(value, axis, [((i + step) % size, i) for i in range(size)])]
    all_to_all x3 -> x0, starting transfers between devices: 12.5 us -> none  [the longest x1 7.3 us: on_device(): lax.all_to_all(jnp.broadcast_to(packed[None], (devices, tok_dev, width +...]
    concatenate x1 -> x3, other arithmetic: 0.01 us -> 1.68 us  [the longest x1 0.8 us: on_device(): ids = jnp.roll(block_ids[:, 0], -group)]
    broadcast_in_dim x3 -> x0, local copies, waits for them, and re-layouts: 1.5 us -> none  [the longest x1 0.75 us: on_device(): jnp.broadcast_to(packed[None], (devices, tok_dev, width + 128))]
    dot_general x1, matrix products: 1.04 us -> 0.34 us  [on_device(): jnp.einsum('gsc,gcd->gsd', weights, cand_half, preferred_element_type=jnp...]
  transfers between devices with their start and end apart: 3 -> 30, of which waited for: 3 -> 13; matrix products, arithmetic and copies ran while one was open for 10% -> 10% of each run, Pallas kernels for 0% -> 0%
where the time goes in v2:
time: 67.6 us; the launch traced here: 67.3 us
  starting transfers between devices  35.9 us (53%)
  waiting for transfers between devices  18.4 us (27%)
  other arithmetic  9.56 us (14%)
  matrix products  1.29 us (2%)
  local copies, waits for them, and re-layouts  1.15 us (2%)
  between operations  0.95 us (1%)
    ppermute x30, starting transfers between devices, from_ahead(): lax.ppermute(value, axis, [((i + step) % size, i) for i in range(size)])  35.9 us
    ppermute x30, waiting for transfers between devices, from_ahead(): lax.ppermute(value, axis, [((i + step) % size, i) for i in range(size)])  18.4 us
    mul x1, other arithmetic, on_device(): jnp.sum(slot_grad * unit_cand, axis=2, keepdims=True) * unit_cand  2.14 us
  transfers between devices with their start and end apart: 30, of which 13 were waited for; matrix products, arithmetic and copies ran while one was open for 10% of the time, Pallas kernels for 0%

profile of v2, /device:TPU:0, one launch (start us, length us, event | category | flops | bytes accessed | tf_op | source)
XLA Modules:
  0.0 67.3 jit_solution(1181453063501640076)
XLA Ops:
  0.6 0.9 %fusion.47 = f32[8]{0:T(128)S(1)} fusion(bf16[8,512]{1,0:T(8,128)(2,1)} %param.7), kind=kLoop, calls=%fused_computation.76 | loop fusion | flops 12280 | bytes 8224 | tf_op jit(solution)/shard_map/reduce_sum | solution.py:31
  1.5 0.7 convert_bitcast_fusion.2
  2.3 0.8 %fusion.43 = bf16[8,512]{1,0:T(8,128)(2,1)S(1)} fusion(bf16[8,512]{1,0:T(8,128)(2,1)} %param.7, f32[8]{0:T(128)S(1)} %add_rsqrt_fusion.1), kind=kLoop, calls=%fused_computation.70 | loop fusion | flops 12288 | bytes 16416 | tf_op jit(solution)/shard_map/convert_element_type | solution.py:37
  3.1 4.0 %collective-permute-start.1 = (bf16[8,896]{1,0:T(8,128)(2,1)S(1)}, bf16[8,896]{1,0:T(8,128)(2,1)S(1)}, u32[]{:S(2)}, u32[]{:S(2)}) collective-permute-start(bf16[8,896]{1,0:T(8,128)(2,1)S(1)} %get-tuple-element.23), channel_id=1, source_target_pairs={{16,0},{24,8},{0,16},{8,24},{17,1},{25,9},{1,17},{9,25},{18,2},{26... | collective-permute-start | bytes 43016 | tf_op jit(solution)/shard_map/ppermute | solution.py:18
  7.1 1.3 %collective-permute-start = (bf16[8,896]{1,0:T(8,128)(2,1)S(1)}, bf16[8,896]{1,0:T(8,128)(2,1)S(1)}, u32[]{:S(2)}, u32[]{:S(2)}) collective-permute-start(bf16[8,896]{1,0:T(8,128)(2,1)S(1)} %get-tuple-element.23), channel_id=1, source_target_pairs={{8,0},{16,8},{24,16},{0,24},{9,1},{17,9},{25,17},{1,25},{10,2},{18... | collective-permute-start | bytes 43016 | tf_op jit(solution)/shard_map/ppermute | solution.py:18
  8.5 0.7 %collective-permute-start.2 = (bf16[8,896]{1,0:T(8,128)(2,1)S(1)}, bf16[8,896]{1,0:T(8,128)(2,1)S(1)}, u32[]{:S(2)}, u32[]{:S(2)}) collective-permute-start(bf16[8,896]{1,0:T(8,128)(2,1)S(1)} %get-tuple-element.23), channel_id=1, source_target_pairs={{24,0},{0,8},{8,16},{16,24},{25,1},{1,9},{9,17},{17,25},{26,2},{2,... | collective-permute-start | bytes 43016 | tf_op jit(solution)/shard_map/ppermute | solution.py:18
  9.1 0.8 %pad_add_fusion.1 = s32[8]{0:T(128)S(1)} fusion(s32[4]{0:T(128)} %bitcast.128), kind=kLoop, calls=%fused_computation.97 | loop fusion | flops 8 | bytes 48 | tf_op jit(solution)/shard_map/jit(_roll_dynamic)/concatenate | solution.py:47
  10.0 0.8 %pad_add_fusion.2 = s32[8]{0:T(128)S(1)} fusion(s32[4]{0:T(128)} %bitcast.129), kind=kLoop, calls=%fused_computation.98 | loop fusion | flops 8 | bytes 48 | tf_op jit(solution)/shard_map/jit(_roll_dynamic)/concatenate | solution.py:48
  10.8 0.6 gather_fusion
  11.4 0.2 fusion.16
  11.7 2.3 %collective-permute-done.2 = bf16[8,896]{1,0:T(8,128)(2,1)S(1)} collective-permute-done((bf16[8,896]{1,0:T(8,128)(2,1)S(1)}, bf16[8,896]{1,0:T(8,128)(2,1)S(1)}, u32[]{:S(2)}, u32[]{:S(2)}) %collective-permute-start.2) | collective-permute-done | bytes 14368 | tf_op jit(solution)/shard_map/ppermute | solution.py:18
  14.0 1.5 %collective-permute-start.8 = (bf16[4,8,512]{2,1,0:T(8,128)(2,1)S(1)}, bf16[4,8,512]{2,1,0:T(8,128)(2,1)S(1)}, u32[]{:S(2)}, u32[]{:S(2)}) collective-permute-start(bf16[4,8,512]{2,1,0:T(8,128)(2,1)S(1)} %slice.187), channel_id=1, source_target_pairs={{6,0},{7,1},{0,2},{1,3},{2,4},{3,5},{4,6},{5,7},{14,8},{15,9},{8,1... | collective-permute-start | bytes 98312 | tf_op jit(solution)/shard_map/ppermute | solution.py:18
  15.6 1.6 %collective-permute-start.6 = (bf16[4,8,512]{2,1,0:T(8,128)(2,1)S(1)}, bf16[4,8,512]{2,1,0:T(8,128)(2,1)S(1)}, u32[]{:S(2)}, u32[]{:S(2)}) collective-permute-start(bf16[4,8,512]{2,1,0:T(8,128)(2,1)S(1)} %slice.187), channel_id=1, source_target_pairs={{4,0},{5,1},{6,2},{7,3},{0,4},{1,5},{2,6},{3,7},{12,8},{13,9},{14,... | collective-permute-start | bytes 98312 | tf_op jit(solution)/shard_map/ppermute | solution.py:18
  17.1 1.4 %collective-permute-start.5 = (bf16[4,8,512]{2,1,0:T(8,128)(2,1)S(1)}, bf16[4,8,512]{2,1,0:T(8,128)(2,1)S(1)}, u32[]{:S(2)}, u32[]{:S(2)}) collective-permute-start(bf16[4,8,512]{2,1,0:T(8,128)(2,1)S(1)} %slice.187), channel_id=1, source_target_pairs={{3,0},{4,1},{5,2},{6,3},{7,4},{0,5},{1,6},{2,7},{11,8},{12,9},{13,... | collective-permute-start | bytes 98312 | tf_op jit(solution)/shard_map/ppermute | solution.py:18
  18.5 0.3 collective-permute-start.3
  19.1 1.3 %collective-permute-done.3 = bf16[4,8,512]{2,1,0:T(8,128)(2,1)S(1)} collective-permute-done((bf16[4,8,512]{2,1,0:T(8,128)(2,1)S(1)}, bf16[4,8,512]{2,1,0:T(8,128)(2,1)S(1)}, u32[]{:S(2)}, u32[]{:S(2)}) %collective-permute-start.3) | collective-permute-done | bytes 32800 | tf_op jit(solution)/shard_map/ppermute | solution.py:18
  20.4 1.4 %collective-permute-start.4 = (bf16[4,8,512]{2,1,0:T(8,128)(2,1)S(1)}, bf16[4,8,512]{2,1,0:T(8,128)(2,1)S(1)}, u32[]{:S(2)}, u32[]{:S(2)}) collective-permute-start(bf16[4,8,512]{2,1,0:T(8,128)(2,1)S(1)} %slice.187), channel_id=1, source_target_pairs={{2,0},{3,1},{4,2},{5,3},{6,4},{7,5},{0,6},{1,7},{10,8},{11,9},{12,... | collective-permute-start | bytes 98312 | tf_op jit(solution)/shard_map/ppermute | solution.py:18
  21.8 2.5 %collective-permute-done.4 = bf16[4,8,512]{2,1,0:T(8,128)(2,1)S(1)} collective-permute-done((bf16[4,8,512]{2,1,0:T(8,128)(2,1)S(1)}, bf16[4,8,512]{2,1,0:T(8,128)(2,1)S(1)}, u32[]{:S(2)}, u32[]{:S(2)}) %collective-permute-start.4) | collective-permute-done | bytes 32800 | tf_op jit(solution)/shard_map/ppermute | solution.py:18
  24.3 0.5 collective-permute-start.9
  24.9 3.7 %collective-permute-done.9 = bf16[4,8,512]{2,1,0:T(8,128)(2,1)S(1)} collective-permute-done((bf16[4,8,512]{2,1,0:T(8,128)(2,1)S(1)}, bf16[4,8,512]{2,1,0:T(8,128)(2,1)S(1)}, u32[]{:S(2)}, u32[]{:S(2)}) %collective-permute-start.9) | collective-permute-done | bytes 32800 | tf_op jit(solution)/shard_map/ppermute | solution.py:18
  28.6 0.5 select_reduce_fusion.1
  29.3 1.6 %collective-permute-start.13 = (f32[2,4,8,8]{3,2,1,0:T(8,128)S(1)}, f32[2,4,8,8]{3,2,1,0:T(8,128)S(1)}, u32[]{:S(2)}, u32[]{:S(2)}) collective-permute-start(f32[2,4,8,8]{3,2,1,0:T(8,128)S(1)} %constant_dynamic-update-slice_fusion), channel_id=1, source_target_pairs={{4,0},{5,1},{6,2},{7,3},{0,4},{1,5},{2,6},{3,7},{12,8},{13,9},{14,... | collective-permute-start | bytes 6152 | tf_op jit(solution)/shard_map/ppermute | solution.py:18
  30.8 0.5 collective-permute-start.15
  31.3 2.1 %collective-permute-start.14 = (f32[2,4,8,8]{3,2,1,0:T(8,128)S(1)}, f32[2,4,8,8]{3,2,1,0:T(8,128)S(1)}, u32[]{:S(2)}, u32[]{:S(2)}) collective-permute-start(f32[2,4,8,8]{3,2,1,0:T(8,128)S(1)} %constant_dynamic-update-slice_fusion), channel_id=1, source_target_pairs={{5,0},{6,1},{7,2},{0,3},{1,4},{2,5},{3,6},{4,7},{13,8},{14,9},{15,... | collective-permute-start | bytes 6152 | tf_op jit(solution)/shard_map/ppermute | solution.py:18
  33.6 1.9 %collective-permute-start.11 = (f32[2,4,8,8]{3,2,1,0:T(8,128)S(1)}, f32[2,4,8,8]{3,2,1,0:T(8,128)S(1)}, u32[]{:S(2)}, u32[]{:S(2)}) collective-permute-start(f32[2,4,8,8]{3,2,1,0:T(8,128)S(1)} %constant_dynamic-update-slice_fusion), channel_id=1, source_target_pairs={{2,0},{3,1},{4,2},{5,3},{6,4},{7,5},{0,6},{1,7},{10,8},{11,9},{12,... | collective-permute-start | bytes 6152 | tf_op jit(solution)/shard_map/ppermute | solution.py:18
  35.5 1.7 %collective-permute-start.10 = (f32[2,4,8,8]{3,2,1,0:T(8,128)S(1)}, f32[2,4,8,8]{3,2,1,0:T(8,128)S(1)}, u32[]{:S(2)}, u32[]{:S(2)}) collective-permute-start(f32[2,4,8,8]{3,2,1,0:T(8,128)S(1)} %constant_dynamic-update-slice_fusion), channel_id=1, source_target_pairs={{1,0},{2,1},{3,2},{4,3},{5,4},{6,5},{7,6},{0,7},{9,8},{10,9},{11,1... | collective-permute-start | bytes 6152 | tf_op jit(solution)/shard_map/ppermute | solution.py:18
  37.5 1.3 %collective-permute-done.10 = f32[2,4,8,8]{3,2,1,0:T(8,128)S(1)} collective-permute-done((f32[2,4,8,8]{3,2,1,0:T(8,128)S(1)}, f32[2,4,8,8]{3,2,1,0:T(8,128)S(1)}, u32[]{:S(2)}, u32[]{:S(2)}) %collective-permute-start.10) | collective-permute-done | bytes 2080 | tf_op jit(solution)/shard_map/ppermute | solution.py:18
  39.0 1.4 %collective-permute-start.18 = (f32[2,4,8,8]{3,2,1,0:T(8,128)S(1)}, f32[2,4,8,8]{3,2,1,0:T(8,128)S(1)}, u32[]{:S(2)}, u32[]{:S(2)}) collective-permute-start(f32[2,4,8,8]{3,2,1,0:T(8,128)S(1)} %fusion.38), channel_id=1, source_target_pairs={{16,0},{24,8},{0,16},{8,24},{17,1},{25,9},{1,17},{9,25},{18,2},{26... | collective-permute-start | bytes 6152 | tf_op jit(solution)/shard_map/ppermute | solution.py:18
  40.4 2.4 %collective-permute-start.17 = (f32[2,4,8,8]{3,2,1,0:T(8,128)S(1)}, f32[2,4,8,8]{3,2,1,0:T(8,128)S(1)}, u32[]{:S(2)}, u32[]{:S(2)}) collective-permute-start(f32[2,4,8,8]{3,2,1,0:T(8,128)S(1)} %fusion.38), channel_id=1, source_target_pairs={{8,0},{16,8},{24,16},{0,24},{9,1},{17,9},{25,17},{1,25},{10,2},{18... | collective-permute-start | bytes 6152 | tf_op jit(solution)/shard_map/ppermute | solution.py:18
  42.9 1.8 %collective-permute-done.19 = f32[2,4,8,8]{3,2,1,0:T(8,128)S(1)} collective-permute-done((f32[2,4,8,8]{3,2,1,0:T(8,128)S(1)}, f32[2,4,8,8]{3,2,1,0:T(8,128)S(1)}, u32[]{:S(2)}, u32[]{:S(2)}) %collective-permute-start.19) | collective-permute-done | bytes 2080 | tf_op jit(solution)/shard_map/ppermute | solution.py:18
  44.7 0.5 collective-permute-done.17
  45.4 0.3 fusion.14
  45.8 0.5 fusion.20
  46.3 2.1 %collective-permute-start.25 = (bf16[4,8,512]{2,1,0:T(8,128)(2,1)S(1)}, bf16[4,8,512]{2,1,0:T(8,128)(2,1)S(1)}, u32[]{:S(2)}, u32[]{:S(2)}) collective-permute-start(bf16[4,8,512]{2,1,0:T(8,128)(2,1)S(1)} %get-tuple-element.9), channel_id=1, source_target_pairs={{2,0},{3,1},{4,2},{5,3},{6,4},{7,5},{0,6},{1,7},{10,8},{11,9},{12,... | collective-permute-start | bytes 98312 | tf_op jit(solution)/shard_map/ppermute | solution.py:18
  48.5 0.9 %collective-permute-start.24 = (bf16[4,8,512]{2,1,0:T(8,128)(2,1)S(1)}, bf16[4,8,512]{2,1,0:T(8,128)(2,1)S(1)}, u32[]{:S(2)}, u32[]{:S(2)}) collective-permute-start(bf16[4,8,512]{2,1,0:T(8,128)(2,1)S(1)} %get-tuple-element.10), channel_id=1, source_target_pairs={{3,0},{4,1},{5,2},{6,3},{7,4},{0,5},{1,6},{2,7},{11,8},{12,9},{13,... | collective-permute-start | bytes 98312 | tf_op jit(solution)/shard_map/ppermute | solution.py:18
  49.4 1.3 %collective-permute-start.23 = (bf16[4,8,512]{2,1,0:T(8,128)(2,1)S(1)}, bf16[4,8,512]{2,1,0:T(8,128)(2,1)S(1)}, u32[]{:S(2)}, u32[]{:S(2)}) collective-permute-start(bf16[4,8,512]{2,1,0:T(8,128)(2,1)S(1)} %get-tuple-element.11), channel_id=1, source_target_pairs={{4,0},{5,1},{6,2},{7,3},{0,4},{1,5},{2,6},{3,7},{12,8},{13,9},{14,... | collective-permute-start | bytes 98312 | tf_op jit(solution)/shard_map/ppermute | solution.py:18
  50.8 2.1 %fusion.11 = f32[4,128,512]{2,1,0:T(8,128)S(1)} fusion(f32[4,128,512]{2,1,0:T(8,128)S(1)} %fusion.20, bf16[4,128,512]{2,1,0:T(8,128)(2,1)S(1)} %gather_fusion, f32[4,128]{1,0:T(4,128)S(1)} %add_rsqrt_fusion), kind=kOutput, calls=%fused_computation.12 | output fusion | flops 2622463 | bytes 2623488 | tf_op jit(solution)/shard_map/mul | solution.py:86
  53.0 1.1 %collective-permute-start.21 = (bf16[4,8,512]{2,1,0:T(8,128)(2,1)S(1)}, bf16[4,8,512]{2,1,0:T(8,128)(2,1)S(1)}, u32[]{:S(2)}, u32[]{:S(2)}) collective-permute-start(bf16[4,8,512]{2,1,0:T(8,128)(2,1)S(1)} %get-tuple-element.13), channel_id=1, source_target_pairs={{6,0},{7,1},{0,2},{1,3},{2,4},{3,5},{4,6},{5,7},{14,8},{15,9},{8,1... | collective-permute-start | bytes 98312 | tf_op jit(solution)/shard_map/ppermute | solution.py:18
  54.1 1.9 %collective-permute-start.26 = (bf16[4,8,512]{2,1,0:T(8,128)(2,1)S(1)}, bf16[4,8,512]{2,1,0:T(8,128)(2,1)S(1)}, u32[]{:S(2)}, u32[]{:S(2)}) collective-permute-start(bf16[4,8,512]{2,1,0:T(8,128)(2,1)S(1)} %get-tuple-element.14), channel_id=1, source_target_pairs={{1,0},{2,1},{3,2},{4,3},{5,4},{6,5},{7,6},{0,7},{9,8},{10,9},{11,1... | collective-permute-start | bytes 98312 | tf_op jit(solution)/shard_map/ppermute | solution.py:18
  56.0 0.5 fusion.50
  56.5 1.4 %collective-permute-done.21 = bf16[4,8,512]{2,1,0:T(8,128)(2,1)S(1)} collective-permute-done((bf16[4,8,512]{2,1,0:T(8,128)(2,1)S(1)}, bf16[4,8,512]{2,1,0:T(8,128)(2,1)S(1)}, u32[]{:S(2)}, u32[]{:S(2)}) %collective-permute-start.21) | collective-permute-done | bytes 32800 | tf_op jit(solution)/shard_map/ppermute | solution.py:18
  58.0 1.9 %collective-permute-start.27 = (bf16[8,512]{1,0:T(8,128)(2,1)S(1)}, bf16[8,512]{1,0:T(8,128)(2,1)S(1)}, u32[]{:S(2)}, u32[]{:S(2)}) collective-permute-start(bf16[8,512]{1,0:T(8,128)(2,1)S(1)} %get-tuple-element.15), channel_id=1, source_target_pairs={{24,0},{0,8},{8,16},{16,24},{25,1},{1,9},{9,17},{17,25},{26,2},{2,... | collective-permute-start | bytes 24584 | tf_op jit(solution)/shard_map/ppermute | solution.py:18
  59.9 2.0 %collective-permute-start.29 = (bf16[8,512]{1,0:T(8,128)(2,1)S(1)}, bf16[8,512]{1,0:T(8,128)(2,1)S(1)}, u32[]{:S(2)}, u32[]{:S(2)}) collective-permute-start(bf16[8,512]{1,0:T(8,128)(2,1)S(1)} %get-tuple-element.16), channel_id=1, source_target_pairs={{8,0},{16,8},{24,16},{0,24},{9,1},{17,9},{25,17},{1,25},{10,2},{18... | collective-permute-start | bytes 24584 | tf_op jit(solution)/shard_map/ppermute | solution.py:18
  61.9 1.4 %select_reduce_fusion = f32[4,128,512]{2,1,0:T(8,128)} fusion(f32[4,128,512]{2,1,0:T(8,128)S(1)} %fusion.11, pred[4,4]{1,0:T(4,128)(4,1)S(1)} %iota_compare_fusion.1), kind=kLoop, calls=%fused_computation.2 | loop fusion | flops 1835008 | bytes 2097168 | tf_op jit(solution)/shard_map/reduce_sum | solution.py:90
  63.2 0.3 collective-permute-done.27
  63.6 2.8 %collective-permute-done.28 = bf16[8,512]{1,0:T(8,128)(2,1)S(1)} collective-permute-done((bf16[8,512]{1,0:T(8,128)(2,1)S(1)}, bf16[8,512]{1,0:T(8,128)(2,1)S(1)}, u32[]{:S(2)}, u32[]{:S(2)}) %collective-permute-start.28) | collective-permute-done | bytes 8224 | tf_op jit(solution)/shard_map/ppermute | solution.py:18
  66.4 0.2 fusion.44
  66.6 0.7 %fusion.46 = f32[8,512]{1,0:T(8,128)} fusion(bf16[8,512]{1,0:T(8,128)(2,1)S(1)} %copy-done.1, f32[8]{0:T(128)S(1)} %fusion.44, f32[8]{0:T(128)S(1)} %add_rsqrt_fusion.1, bf16[8,512]{1,0:T(8,128)(2,1)S(1)} %collective-permute-done.29, bf16[8,512]{1,0:T(8,128)(2,1)S(1)} %collective-permute-done.28, bf16[8,512]{1,0:T(8,128)(2,1)S(1)} %collective-permute-done.27, ...), kind=kLoop, calls=%fused_computation.75 | loop fusion | flops 49152 | bytes 57408 | tf_op jit(solution)/shard_map/mul | solution.py:80
  (84 shorter events, 1.9 us)
Async XLA Ops:
  0.6 10.2 %copy-start = (bf16[512,512]{1,0:T(8,128)(2,1)S(1)}, bf16[512,512]{1,0:T(8,128)(2,1)}, u32[]{:S(2)}) copy-start(bf16[512,512]{1,0:T(8,128)(2,1)} %param.9) | copy-start | bytes 1572868
  3.1 8.6 %collective-permute-start.1 = (bf16[8,896]{1,0:T(8,128)(2,1)S(1)}, bf16[8,896]{1,0:T(8,128)(2,1)S(1)}, u32[]{:S(2)}, u32[]{:S(2)}) collective-permute-start(bf16[8,896]{1,0:T(8,128)(2,1)S(1)} %get-tuple-element.23), channel_id=1, source_target_pairs={{16,0},{24,8},{0,16},{8,24},{17,1},{25,9},{1,17},{9,25},{18,2},{26... | collective-permute-start | bytes 43016 | tf_op jit(solution)/shard_map/ppermute | solution.py:18
  7.1 4.6 %collective-permute-start = (bf16[8,896]{1,0:T(8,128)(2,1)S(1)}, bf16[8,896]{1,0:T(8,128)(2,1)S(1)}, u32[]{:S(2)}, u32[]{:S(2)}) collective-permute-start(bf16[8,896]{1,0:T(8,128)(2,1)S(1)} %get-tuple-element.23), channel_id=1, source_target_pairs={{8,0},{16,8},{24,16},{0,24},{9,1},{17,9},{25,17},{1,25},{10,2},{18... | collective-permute-start | bytes 43016 | tf_op jit(solution)/shard_map/ppermute | solution.py:18
  8.5 5.5 %collective-permute-start.2 = (bf16[8,896]{1,0:T(8,128)(2,1)S(1)}, bf16[8,896]{1,0:T(8,128)(2,1)S(1)}, u32[]{:S(2)}, u32[]{:S(2)}) collective-permute-start(bf16[8,896]{1,0:T(8,128)(2,1)S(1)} %get-tuple-element.23), channel_id=1, source_target_pairs={{24,0},{0,8},{8,16},{16,24},{25,1},{1,9},{9,17},{17,25},{26,2},{2,... | collective-permute-start | bytes 43016 | tf_op jit(solution)/shard_map/ppermute | solution.py:18
  14.0 10.8 %collective-permute-start.8 = (bf16[4,8,512]{2,1,0:T(8,128)(2,1)S(1)}, bf16[4,8,512]{2,1,0:T(8,128)(2,1)S(1)}, u32[]{:S(2)}, u32[]{:S(2)}) collective-permute-start(bf16[4,8,512]{2,1,0:T(8,128)(2,1)S(1)} %slice.187), channel_id=1, source_target_pairs={{6,0},{7,1},{0,2},{1,3},{2,4},{3,5},{4,6},{5,7},{14,8},{15,9},{8,1... | collective-permute-start | bytes 98312 | tf_op jit(solution)/shard_map/ppermute | solution.py:18
  15.6 9.2 %collective-permute-start.7 = (bf16[4,8,512]{2,1,0:T(8,128)(2,1)S(1)}, bf16[4,8,512]{2,1,0:T(8,128)(2,1)S(1)}, u32[]{:S(2)}, u32[]{:S(2)}) collective-permute-start(bf16[4,8,512]{2,1,0:T(8,128)(2,1)S(1)} %slice.187), channel_id=1, source_target_pairs={{5,0},{6,1},{7,2},{0,3},{1,4},{2,5},{3,6},{4,7},{13,8},{14,9},{15,... | collective-permute-start | bytes 98312 | tf_op jit(solution)/shard_map/ppermute | solution.py:18
  15.6 9.2 %collective-permute-start.6 = (bf16[4,8,512]{2,1,0:T(8,128)(2,1)S(1)}, bf16[4,8,512]{2,1,0:T(8,128)(2,1)S(1)}, u32[]{:S(2)}, u32[]{:S(2)}) collective-permute-start(bf16[4,8,512]{2,1,0:T(8,128)(2,1)S(1)} %slice.187), channel_id=1, source_target_pairs={{4,0},{5,1},{6,2},{7,3},{0,4},{1,5},{2,6},{3,7},{12,8},{13,9},{14,... | collective-permute-start | bytes 98312 | tf_op jit(solution)/shard_map/ppermute | solution.py:18
  17.1 7.7 %collective-permute-start.5 = (bf16[4,8,512]{2,1,0:T(8,128)(2,1)S(1)}, bf16[4,8,512]{2,1,0:T(8,128)(2,1)S(1)}, u32[]{:S(2)}, u32[]{:S(2)}) collective-permute-start(bf16[4,8,512]{2,1,0:T(8,128)(2,1)S(1)} %slice.187), channel_id=1, source_target_pairs={{3,0},{4,1},{5,2},{6,3},{7,4},{0,5},{1,6},{2,7},{11,8},{12,9},{13,... | collective-permute-start | bytes 98312 | tf_op jit(solution)/shard_map/ppermute | solution.py:18
  18.5 1.9 %collective-permute-start.3 = (bf16[4,8,512]{2,1,0:T(8,128)(2,1)S(1)}, bf16[4,8,512]{2,1,0:T(8,128)(2,1)S(1)}, u32[]{:S(2)}, u32[]{:S(2)}) collective-permute-start(bf16[4,8,512]{2,1,0:T(8,128)(2,1)S(1)} %slice.187), channel_id=1, source_target_pairs={{1,0},{2,1},{3,2},{4,3},{5,4},{6,5},{7,6},{0,7},{9,8},{10,9},{11,1... | collective-permute-start | bytes 98312 | tf_op jit(solution)/shard_map/ppermute | solution.py:18
  20.4 3.9 %collective-permute-start.4 = (bf16[4,8,512]{2,1,0:T(8,128)(2,1)S(1)}, bf16[4,8,512]{2,1,0:T(8,128)(2,1)S(1)}, u32[]{:S(2)}, u32[]{:S(2)}) collective-permute-start(bf16[4,8,512]{2,1,0:T(8,128)(2,1)S(1)} %slice.187), channel_id=1, source_target_pairs={{2,0},{3,1},{4,2},{5,3},{6,4},{7,5},{0,6},{1,7},{10,8},{11,9},{12,... | collective-permute-start | bytes 98312 | tf_op jit(solution)/shard_map/ppermute | solution.py:18
  24.3 4.2 %collective-permute-start.9 = (bf16[4,8,512]{2,1,0:T(8,128)(2,1)S(1)}, bf16[4,8,512]{2,1,0:T(8,128)(2,1)S(1)}, u32[]{:S(2)}, u32[]{:S(2)}) collective-permute-start(bf16[4,8,512]{2,1,0:T(8,128)(2,1)S(1)} %slice.187), channel_id=1, source_target_pairs={{7,0},{0,1},{1,2},{2,3},{3,4},{4,5},{5,6},{6,7},{15,8},{8,9},{9,10... | collective-permute-start | bytes 98312 | tf_op jit(solution)/shard_map/ppermute | solution.py:18
  29.2 4.4 %collective-permute-start.16 = (f32[2,4,8,8]{3,2,1,0:T(8,128)S(1)}, f32[2,4,8,8]{3,2,1,0:T(8,128)S(1)}, u32[]{:S(2)}, u32[]{:S(2)}) collective-permute-start(f32[2,4,8,8]{3,2,1,0:T(8,128)S(1)} %constant_dynamic-update-slice_fusion), channel_id=1, source_target_pairs={{7,0},{0,1},{1,2},{2,3},{3,4},{4,5},{5,6},{6,7},{15,8},{8,9},{9,10... | collective-permute-start | bytes 6152 | tf_op jit(solution)/shard_map/ppermute | solution.py:18
  29.3 6.3 %collective-permute-start.13 = (f32[2,4,8,8]{3,2,1,0:T(8,128)S(1)}, f32[2,4,8,8]{3,2,1,0:T(8,128)S(1)}, u32[]{:S(2)}, u32[]{:S(2)}) collective-permute-start(f32[2,4,8,8]{3,2,1,0:T(8,128)S(1)} %constant_dynamic-update-slice_fusion), channel_id=1, source_target_pairs={{4,0},{5,1},{6,2},{7,3},{0,4},{1,5},{2,6},{3,7},{12,8},{13,9},{14,... | collective-permute-start | bytes 6152 | tf_op jit(solution)/shard_map/ppermute | solution.py:18
  30.8 6.4 %collective-permute-start.15 = (f32[2,4,8,8]{3,2,1,0:T(8,128)S(1)}, f32[2,4,8,8]{3,2,1,0:T(8,128)S(1)}, u32[]{:S(2)}, u32[]{:S(2)}) collective-permute-start(f32[2,4,8,8]{3,2,1,0:T(8,128)S(1)} %constant_dynamic-update-slice_fusion), channel_id=1, source_target_pairs={{6,0},{7,1},{0,2},{1,3},{2,4},{3,5},{4,6},{5,7},{14,8},{15,9},{8,1... | collective-permute-start | bytes 6152 | tf_op jit(solution)/shard_map/ppermute | solution.py:18
  31.3 6.0 %collective-permute-start.14 = (f32[2,4,8,8]{3,2,1,0:T(8,128)S(1)}, f32[2,4,8,8]{3,2,1,0:T(8,128)S(1)}, u32[]{:S(2)}, u32[]{:S(2)}) collective-permute-start(f32[2,4,8,8]{3,2,1,0:T(8,128)S(1)} %constant_dynamic-update-slice_fusion), channel_id=1, source_target_pairs={{5,0},{6,1},{7,2},{0,3},{1,4},{2,5},{3,6},{4,7},{13,8},{14,9},{15,... | collective-permute-start | bytes 6152 | tf_op jit(solution)/shard_map/ppermute | solution.py:18
  33.4 4.0 %collective-permute-start.12 = (f32[2,4,8,8]{3,2,1,0:T(8,128)S(1)}, f32[2,4,8,8]{3,2,1,0:T(8,128)S(1)}, u32[]{:S(2)}, u32[]{:S(2)}) collective-permute-start(f32[2,4,8,8]{3,2,1,0:T(8,128)S(1)} %constant_dynamic-update-slice_fusion), channel_id=1, source_target_pairs={{3,0},{4,1},{5,2},{6,3},{7,4},{0,5},{1,6},{2,7},{11,8},{12,9},{13,... | collective-permute-start | bytes 6152 | tf_op jit(solution)/shard_map/ppermute | solution.py:18
  33.6 3.9 %collective-permute-start.11 = (f32[2,4,8,8]{3,2,1,0:T(8,128)S(1)}, f32[2,4,8,8]{3,2,1,0:T(8,128)S(1)}, u32[]{:S(2)}, u32[]{:S(2)}) collective-permute-start(f32[2,4,8,8]{3,2,1,0:T(8,128)S(1)} %constant_dynamic-update-slice_fusion), channel_id=1, source_target_pairs={{2,0},{3,1},{4,2},{5,3},{6,4},{7,5},{0,6},{1,7},{10,8},{11,9},{12,... | collective-permute-start | bytes 6152 | tf_op jit(solution)/shard_map/ppermute | solution.py:18
  35.5 3.3 %collective-permute-start.10 = (f32[2,4,8,8]{3,2,1,0:T(8,128)S(1)}, f32[2,4,8,8]{3,2,1,0:T(8,128)S(1)}, u32[]{:S(2)}, u32[]{:S(2)}) collective-permute-start(f32[2,4,8,8]{3,2,1,0:T(8,128)S(1)} %constant_dynamic-update-slice_fusion), channel_id=1, source_target_pairs={{1,0},{2,1},{3,2},{4,3},{5,4},{6,5},{7,6},{0,7},{9,8},{10,9},{11,1... | collective-permute-start | bytes 6152 | tf_op jit(solution)/shard_map/ppermute | solution.py:18
  38.9 5.8 %collective-permute-start.19 = (f32[2,4,8,8]{3,2,1,0:T(8,128)S(1)}, f32[2,4,8,8]{3,2,1,0:T(8,128)S(1)}, u32[]{:S(2)}, u32[]{:S(2)}) collective-permute-start(f32[2,4,8,8]{3,2,1,0:T(8,128)S(1)} %fusion.38), channel_id=1, source_target_pairs={{24,0},{0,8},{8,16},{16,24},{25,1},{1,9},{9,17},{17,25},{26,2},{2,... | collective-permute-start | bytes 6152 | tf_op jit(solution)/shard_map/ppermute | solution.py:18
  39.0 6.3 %collective-permute-start.18 = (f32[2,4,8,8]{3,2,1,0:T(8,128)S(1)}, f32[2,4,8,8]{3,2,1,0:T(8,128)S(1)}, u32[]{:S(2)}, u32[]{:S(2)}) collective-permute-start(f32[2,4,8,8]{3,2,1,0:T(8,128)S(1)} %fusion.38), channel_id=1, source_target_pairs={{16,0},{24,8},{0,16},{8,24},{17,1},{25,9},{1,17},{9,25},{18,2},{26... | collective-permute-start | bytes 6152 | tf_op jit(solution)/shard_map/ppermute | solution.py:18
  40.4 4.8 %collective-permute-start.17 = (f32[2,4,8,8]{3,2,1,0:T(8,128)S(1)}, f32[2,4,8,8]{3,2,1,0:T(8,128)S(1)}, u32[]{:S(2)}, u32[]{:S(2)}) collective-permute-start(f32[2,4,8,8]{3,2,1,0:T(8,128)S(1)} %fusion.38), channel_id=1, source_target_pairs={{8,0},{16,8},{24,16},{0,24},{9,1},{17,9},{25,17},{1,25},{10,2},{18... | collective-permute-start | bytes 6152 | tf_op jit(solution)/shard_map/ppermute | solution.py:18
  46.3 6.7 %collective-permute-start.20 = (bf16[4,8,512]{2,1,0:T(8,128)(2,1)S(1)}, bf16[4,8,512]{2,1,0:T(8,128)(2,1)S(1)}, u32[]{:S(2)}, u32[]{:S(2)}) collective-permute-start(bf16[4,8,512]{2,1,0:T(8,128)(2,1)S(1)} %get-tuple-element.8), channel_id=1, source_target_pairs={{7,0},{0,1},{1,2},{2,3},{3,4},{4,5},{5,6},{6,7},{15,8},{8,9},{9,10... | collective-permute-start | bytes 98312 | tf_op jit(solution)/shard_map/ppermute | solution.py:18
  46.3 7.8 %collective-permute-start.25 = (bf16[4,8,512]{2,1,0:T(8,128)(2,1)S(1)}, bf16[4,8,512]{2,1,0:T(8,128)(2,1)S(1)}, u32[]{:S(2)}, u32[]{:S(2)}) collective-permute-start(bf16[4,8,512]{2,1,0:T(8,128)(2,1)S(1)} %get-tuple-element.9), channel_id=1, source_target_pairs={{2,0},{3,1},{4,2},{5,3},{6,4},{7,5},{0,6},{1,7},{10,8},{11,9},{12,... | collective-permute-start | bytes 98312 | tf_op jit(solution)/shard_map/ppermute | solution.py:18
  48.5 8.1 %collective-permute-start.24 = (bf16[4,8,512]{2,1,0:T(8,128)(2,1)S(1)}, bf16[4,8,512]{2,1,0:T(8,128)(2,1)S(1)}, u32[]{:S(2)}, u32[]{:S(2)}) collective-permute-start(bf16[4,8,512]{2,1,0:T(8,128)(2,1)S(1)} %get-tuple-element.10), channel_id=1, source_target_pairs={{3,0},{4,1},{5,2},{6,3},{7,4},{0,5},{1,6},{2,7},{11,8},{12,9},{13,... | collective-permute-start | bytes 98312 | tf_op jit(solution)/shard_map/ppermute | solution.py:18
  49.4 7.1 %collective-permute-start.23 = (bf16[4,8,512]{2,1,0:T(8,128)(2,1)S(1)}, bf16[4,8,512]{2,1,0:T(8,128)(2,1)S(1)}, u32[]{:S(2)}, u32[]{:S(2)}) collective-permute-start(bf16[4,8,512]{2,1,0:T(8,128)(2,1)S(1)} %get-tuple-element.11), channel_id=1, source_target_pairs={{4,0},{5,1},{6,2},{7,3},{0,4},{1,5},{2,6},{3,7},{12,8},{13,9},{14,... | collective-permute-start | bytes 98312 | tf_op jit(solution)/shard_map/ppermute | solution.py:18
  50.7 5.8 %collective-permute-start.22 = (bf16[4,8,512]{2,1,0:T(8,128)(2,1)S(1)}, bf16[4,8,512]{2,1,0:T(8,128)(2,1)S(1)}, u32[]{:S(2)}, u32[]{:S(2)}) collective-permute-start(bf16[4,8,512]{2,1,0:T(8,128)(2,1)S(1)} %get-tuple-element.12), channel_id=1, source_target_pairs={{5,0},{6,1},{7,2},{0,3},{1,4},{2,5},{3,6},{4,7},{13,8},{14,9},{15,... | collective-permute-start | bytes 98312 | tf_op jit(solution)/shard_map/ppermute | solution.py:18
  53.0 5.0 %collective-permute-start.21 = (bf16[4,8,512]{2,1,0:T(8,128)(2,1)S(1)}, bf16[4,8,512]{2,1,0:T(8,128)(2,1)S(1)}, u32[]{:S(2)}, u32[]{:S(2)}) collective-permute-start(bf16[4,8,512]{2,1,0:T(8,128)(2,1)S(1)} %get-tuple-element.13), channel_id=1, source_target_pairs={{6,0},{7,1},{0,2},{1,3},{2,4},{3,5},{4,6},{5,7},{14,8},{15,9},{8,1... | collective-permute-start | bytes 98312 | tf_op jit(solution)/shard_map/ppermute | solution.py:18
  54.1 3.8 %collective-permute-start.26 = (bf16[4,8,512]{2,1,0:T(8,128)(2,1)S(1)}, bf16[4,8,512]{2,1,0:T(8,128)(2,1)S(1)}, u32[]{:S(2)}, u32[]{:S(2)}) collective-permute-start(bf16[4,8,512]{2,1,0:T(8,128)(2,1)S(1)} %get-tuple-element.14), channel_id=1, source_target_pairs={{1,0},{2,1},{3,2},{4,3},{5,4},{6,5},{7,6},{0,7},{9,8},{10,9},{11,1... | collective-permute-start | bytes 98312 | tf_op jit(solution)/shard_map/ppermute | solution.py:18
  58.0 5.5 %collective-permute-start.27 = (bf16[8,512]{1,0:T(8,128)(2,1)S(1)}, bf16[8,512]{1,0:T(8,128)(2,1)S(1)}, u32[]{:S(2)}, u32[]{:S(2)}) collective-permute-start(bf16[8,512]{1,0:T(8,128)(2,1)S(1)} %get-tuple-element.15), channel_id=1, source_target_pairs={{24,0},{0,8},{8,16},{16,24},{25,1},{1,9},{9,17},{17,25},{26,2},{2,... | collective-permute-start | bytes 24584 | tf_op jit(solution)/shard_map/ppermute | solution.py:18
  59.9 3.7 %collective-permute-start.29 = (bf16[8,512]{1,0:T(8,128)(2,1)S(1)}, bf16[8,512]{1,0:T(8,128)(2,1)S(1)}, u32[]{:S(2)}, u32[]{:S(2)}) collective-permute-start(bf16[8,512]{1,0:T(8,128)(2,1)S(1)} %get-tuple-element.16), channel_id=1, source_target_pairs={{8,0},{16,8},{24,16},{0,24},{9,1},{17,9},{25,17},{1,25},{10,2},{18... | collective-permute-start | bytes 24584 | tf_op jit(solution)/shard_map/ppermute | solution.py:18
  61.9 4.6 %copy-start.1 = (bf16[8,512]{1,0:T(8,128)(2,1)S(1)}, bf16[8,512]{1,0:T(8,128)(2,1)}, u32[]{:S(2)}) copy-start(bf16[8,512]{1,0:T(8,128)(2,1)} %param.7) | copy-start | bytes 24580
  61.9 4.5 %collective-permute-start.28 = (bf16[8,512]{1,0:T(8,128)(2,1)S(1)}, bf16[8,512]{1,0:T(8,128)(2,1)S(1)}, u32[]{:S(2)}, u32[]{:S(2)}) collective-permute-start(bf16[8,512]{1,0:T(8,128)(2,1)S(1)} %get-tuple-element.17), channel_id=1, source_target_pairs={{16,0},{24,8},{0,16},{8,24},{17,1},{25,9},{1,17},{9,25},{18,2},{26... | collective-permute-start | bytes 24584 | tf_op jit(solution)/shard_map/ppermute | solution.py:18

commit v3 on v1

v3 whole, which is shorter than its diff:
```python
import jax
import jax.numpy as jnp
from jax import lax
from jax.experimental import pallas as pl
from jax.experimental.pallas import tpu as pltpu
from jax.sharding import PartitionSpec as P

BLK = 128
AXES = ("group", "member")

logit_scale = 32.0
cos_margin = 0.35
norm_epsilon = 1e-06

VMEM = pl.BlockSpec(memory_space=pltpu.VMEM)
SMEM = pl.BlockSpec(memory_space=pltpu.SMEM)


def inverse_norm(rows):
    return lax.rsqrt(jnp.sum(rows * rows, axis=-1, keepdims=True) + norm_epsilon)


def contract(left, right, left_dim, right_dim):
    dims = (((left_dim,), (right_dim,)), ((), ()))
    return lax.dot_general(left, right, dims, preferred_element_type=jnp.float32)


def run(kernel, out_shape, in_specs, *operands):
    shapes = jax.tree.leaves(out_shape)
    return pl.pallas_call(
        kernel,
        out_shape=out_shape,
        in_specs=in_specs,
        out_specs=jax.tree.map(lambda _: VMEM, out_shape),
        compiler_params=pltpu.CompilerParams(vmem_limit_bytes=48 * 1024 * 1024),
        cost_estimate=pl.CostEstimate(
            flops=0,
            transcendentals=0,
            bytes_accessed=sum(a.size * a.dtype.itemsize for a in (*shapes, *operands)),
        ),
    )(*operands)


def pack_units(features, copies_out):
    rows = features[...].astype(jnp.float32)
    unit = (rows * inverse_norm(rows)).astype(jnp.bfloat16)
    copies_out[...] = jnp.broadcast_to(unit[None], copies_out.shape)


def own_slots(labels_row, group_tok, member, groups, group):
    first = (member * groups + group) * BLK
    return lax.broadcasted_iota(jnp.int32, (BLK, group_tok), 0) == labels_row - first


def prepare(ids, centres, labels, cand_out, label_rows_out):
    group, member = lax.axis_index("group"), lax.axis_index("member")
    groups, group_tok = labels.shape
    for g in range(groups):
        rows = centres[ids[g, 0]].astype(jnp.float32)
        cand = (rows * inverse_norm(rows)).astype(jnp.bfloat16)
        cand_out[g] = cand
        onehot = own_slots(labels[g : g + 1, :], group_tok, member, groups, group)
        label_rows_out[g] = contract(onehot.astype(jnp.bfloat16), cand, 0, 0).astype(jnp.bfloat16)


def forward(listed, units, cands, labels, expo_out, sums_out, shares_out):
    group, member = lax.axis_index("group"), lax.axis_index("member")
    groups, group_tok = labels.shape
    sums = []
    for g in range(groups):
        cand = cands[g]
        onehot = own_slots(labels[g : g + 1, :], group_tok, member, groups, group)
        cosine = contract(cand, units[g], 1, 1)
        logits = logit_scale * (cosine - jnp.where(onehot, cos_margin, 0.0))
        expo = jnp.exp(logits) * listed[g, 0].astype(jnp.float32)
        expo_out[g] = expo
        totals = jnp.sum(expo, axis=0, keepdims=True)
        label_logit = jnp.sum(jnp.where(onehot, logits, 0.0), axis=0, keepdims=True)
        sums.append(jnp.concatenate([totals, label_logit], axis=1))
        others = jnp.where(onehot, 0.0, expo).astype(jnp.bfloat16)
        shares_out[g] = contract(others, cand, 0, 0).astype(jnp.bfloat16)
    sums = jnp.concatenate(sums, axis=0)
    sums_out[...] = jnp.broadcast_to(sums[None], sums_out.shape)


def backward(
    ids, sums, expo, units, centres, labels, label_rows, grad_out, loss_out, scale_out, pull_out
):
    group, member = lax.axis_index("group"), lax.axis_index("member")
    groups, group_tok = labels.shape
    both = jnp.sum(sums[...], axis=0)
    grad_out[...] = jnp.zeros_like(grad_out)
    for g in range(groups):
        rows = centres[ids[g, 0]].astype(jnp.float32)
        inv_cand = inverse_norm(rows)
        unit_cand = rows * inv_cand
        onehot = own_slots(labels[g : g + 1, :], group_tok, member, groups, group)
        share = expo[g] / both[g : g + 1, :group_tok]
        weights = (logit_scale * (share - jnp.where(onehot, 1.0, 0.0))).astype(jnp.bfloat16)
        slot_grad = contract(weights, units[g], 1, 0)
        along = jnp.sum(slot_grad * unit_cand, axis=1, keepdims=True)
        cand_grad = (inv_cand * (slot_grad - along * unit_cand)).astype(jnp.bfloat16)
        grad_out[ids[g, 0]] += cand_grad.astype(jnp.float32)

    tok_dev = pull_out.shape[0]
    row = lax.broadcasted_iota(jnp.int32, (groups, 2 * group_tok), 0)
    mine = jnp.sum(jnp.where(row == group, both, 0.0), axis=0, keepdims=True)
    lane = lax.broadcasted_iota(jnp.int32, (tok_dev, 2 * group_tok), 1)
    sample = lax.broadcasted_iota(jnp.int32, (tok_dev, 2 * group_tok), 0) + member * tok_dev
    total = jnp.sum(jnp.where(lane == sample, mine, 0.0), axis=1, keepdims=True)
    label_logit = jnp.sum(
        jnp.where(lane == sample + group_tok, mine, 0.0), axis=1, keepdims=True
    )
    loss = jnp.log(total) - label_logit
    square = (tok_dev, tok_dev)
    diagonal = lax.broadcasted_iota(jnp.int32, square, 0) == lax.broadcasted_iota(
        jnp.int32, square, 1
    )
    loss_out[...] = jnp.sum(jnp.where(diagonal, loss, 0.0), axis=0, keepdims=True)
    scale = logit_scale / total
    scale_out[...] = jnp.broadcast_to(scale, scale_out.shape)
    label_row = jnp.sum(label_rows[...].astype(jnp.float32), axis=0)
    pull_out[...] = scale * (total - jnp.exp(label_logit)) * label_row


def finish(features, shares, scale, pull, grad_out):
    rows = features[...].astype(jnp.float32)
    inv_norm = inverse_norm(rows)
    unit = rows * inv_norm
    unit_grad = scale[:, :1] * jnp.sum(shares[...].astype(jnp.float32), axis=0) - pull[...]
    along = jnp.sum(unit_grad * unit, axis=1, keepdims=True)
    grad_out[...] = inv_norm * (unit_grad - along * unit)


def exchange(pieces, axes):
    return lax.all_to_all(pieces, axes, split_axis=0, concat_axis=0, tiled=True)


def on_device(features, labels, centres, block_ids, listed):
    groups = lax.axis_size("group")
    members = lax.axis_size("member")
    devices = groups * members
    tok_dev, width = features.shape
    group_tok = members * tok_dev
    held = centres.shape[0] // BLK
    blocks = centres.reshape(held, BLK, width)
    per_device = (devices, tok_dev, width)
    per_group = (groups, group_tok, width)
    bf16, f32 = jnp.bfloat16, jnp.float32
    shape = jax.ShapeDtypeStruct

    copies = run(pack_units, shape(per_device, bf16), [VMEM], features)
    units = exchange(copies, AXES).reshape(per_group)
    all_labels = exchange(jnp.broadcast_to(labels[None], (groups, group_tok)), "group")

    cands, label_rows = run(
        prepare,
        (shape((groups, BLK, width), bf16), shape(per_group, bf16)),
        [SMEM, VMEM, VMEM],
        block_ids,
        blocks,
        all_labels,
    )
    label_rows = exchange(label_rows.reshape(per_device), AXES)

    expo, sums, shares = run(
        forward,
        (
            shape((groups, BLK, group_tok), f32),
            shape((devices, groups, 2 * group_tok), f32),
            shape(per_group, bf16),
        ),
        [SMEM, VMEM, VMEM, VMEM],
        listed,
        units,
        cands,
        all_labels,
    )
    sums = exchange(sums, AXES)
    shares = exchange(shares.reshape(per_device), AXES)

    centre_grad, loss, scale, pull = run(
        backward,
        (
            shape((held, BLK, width), f32),
            shape((1, tok_dev), f32),
            shape((tok_dev, 128), f32),
            shape((tok_dev, width), f32),
        ),
        [SMEM] + [VMEM] * 6,
        block_ids,
        sums,
        expo,
        units,
        blocks,
        all_labels,
        label_rows,
    )
    feature_grad = run(
        finish, shape((tok_dev, width), f32), [VMEM] * 4, features, shares, scale, pull
    )
    return (loss.reshape(tok_dev), feature_grad, centre_grad.reshape(held * BLK, width))


def on_device_of_many(features, labels, centres, block_ids, listed):
    groups = lax.axis_size("group")
    members = lax.axis_size("member")
    devices = groups * members
    group = lax.axis_index("group")
    member = lax.axis_index("member")
    tok_dev, width = features.shape
    group_tok = members * tok_dev
    held = centres.shape[0] // BLK

    vectors = features.astype(jnp.float32)
    inv_norm = inverse_norm(vectors)
    unit_rows = vectors * inv_norm
    copies = jnp.broadcast_to(unit_rows.astype(jnp.bfloat16), (devices, tok_dev, width))
    units = exchange(copies, AXES).reshape(groups, group_tok, width)
    all_labels = exchange(jnp.broadcast_to(labels[None], (groups, group_tok)), "group")

    picked = centres.reshape(held, BLK, width)[block_ids[:, 0]].astype(jnp.float32)
    inv_cand = inverse_norm(picked)
    unit_cand = picked * inv_cand
    cand_half = unit_cand.astype(jnp.bfloat16)
    cosine = jnp.einsum("gsd,gcd->gsc", units, cand_half, preferred_element_type=jnp.float32)
    local_label = all_labels - (member * groups + group) * BLK
    onehot = (lax.broadcasted_iota(jnp.int32, (1, 1, BLK), 2) == local_label[:, :, None]).astype(
        jnp.float32
    )
    logits = logit_scale * (cosine - cos_margin * onehot)
    exp_logits = jnp.exp(logits) * listed.astype(jnp.float32)[:, :, None]
    totals, label_logit = lax.psum(
        (jnp.sum(exp_logits, axis=2), jnp.sum(logits * onehot, axis=2)), AXES
    )
    loss_all = (jnp.log(totals) - label_logit).reshape(devices, tok_dev)
    sample_loss = lax.dynamic_slice_in_dim(loss_all, group * members + member, 1, 0)[0]

    weights = (logit_scale * (exp_logits / totals[:, :, None] - onehot)).astype(jnp.bfloat16)
    partial = jnp.einsum("gsc,gcd->gsd", weights, cand_half, preferred_element_type=jnp.float32)
    home = exchange(partial.astype(jnp.bfloat16).reshape(devices, tok_dev, width), AXES)
    unit_grad = jnp.sum(home.astype(jnp.float32), axis=0)
    feature_grad = inv_norm * (
        unit_grad - jnp.sum(unit_grad * unit_rows, axis=1, keepdims=True) * unit_rows
    )
    slot_grad = jnp.einsum("gsc,gsd->gcd", weights, units, preferred_element_type=jnp.float32)
    cand_grad = inv_cand * (
        slot_grad - jnp.sum(slot_grad * unit_cand, axis=2, keepdims=True) * unit_cand
    )
    cand_grad = cand_grad.astype(jnp.bfloat16).astype(jnp.float32)
    names = block_ids == jnp.arange(held, dtype=jnp.int32)[None, :]
    centre_grad = jnp.sum(
        jnp.where(names[:, :, None, None], cand_grad[:, None], 0.0), axis=0
    ).reshape(held * BLK, width)
    return (sample_loss, feature_grad, centre_grad)


def solution(mesh):
    in_specs = (
        P(AXES, None),
        P("group"),
        P(AXES, None),
        P(None, AXES),
        P(None, AXES),
    )
    out_specs = (P(AXES), P(AXES, None), P(AXES, None))
    body = on_device if mesh.size <= 64 else on_device_of_many
    return jax.shard_map(
        body, mesh=mesh, in_specs=in_specs, out_specs=out_specs, check_vma=False
    )
```

time: 51.1 us -> 64.4 us (1.26)
  blocking collectives: 0 us -> 9.51 us
  Pallas kernels: 0 us -> 7.88 us
  other arithmetic: 7.45 us -> 0 us
  waiting for transfers between devices: 25 us -> 29.3 us
  matrix products: 1.99 us -> 0 us
  starting transfers between devices: 12.5 us -> 14.4 us
  local copies, waits for them, and re-layouts: 2.88 us -> 2.19 us
    all_to_all x0 -> x1, blocking collectives: none -> 9.51 us  [exchange(): return lax.all_to_all(pieces, axes, split_axis=0, concat_axis=0, tiled=True)]
    pallas_call x0 -> x5, Pallas kernels: none -> 7.88 us  [run(): pl.pallas_call(kernel, out_shape=out_shape, in_specs=in_specs, out_specs=...]
    all_to_all x3 -> x4, waiting for transfers between devices: 25 us -> 29.3 us  [exchange(): return lax.all_to_all(pieces, axes, split_axis=0, concat_axis=0, tiled=True)]
    mul x3 -> x0, other arithmetic: 2.83 us -> none  [the longest x1 2.14 us: on_device(): jnp.sum(slot_grad * unit_cand, axis=2, keepdims=True) * unit_cand]
    reduce_sum x6 -> x0, other arithmetic: 2.64 us -> none  [the longest x1 1.35 us: on_device(): jnp.sum(jnp.where(names[:, :, None, None], cand_grad[:, None], 0.0), axis=0)]
    dot_general x3 -> x0, matrix products: 1.99 us -> none  [the longest x1 1.04 us: on_device(): jnp.einsum('gsc,gcd->gsd', weights, cand_half, preferred_element_type=jnp...]
    all_to_all x3 -> x4, starting transfers between devices: 12.5 us -> 14.4 us  [exchange(): return lax.all_to_all(pieces, axes, split_axis=0, concat_axis=0, tiled=True)]
    another operation x3 -> x0, other arithmetic: 0.81 us -> none  [the longest x2 0.8 us: on_device(): jnp.stack([own_labels & 127, own_labels >> 7 & 127, own_labels >> 14], ax...]
  transfers between devices with their start and end apart: 3 -> 4, of which waited for: 3 -> 4; matrix products, arithmetic and copies ran while one was open for 10% -> 0% of each run, Pallas kernels for 0% -> 11%
where the time goes in v3:
time: 64.4 us; the launch traced here: 64 us
  waiting for transfers between devices  29.3 us (45%)
  starting transfers between devices  14.4 us (22%)
  blocking collectives  9.51 us (15%)
  Pallas kernels  7.88 us (12%)
  local copies, waits for them, and re-layouts  2.19 us (3%)
  between operations  0.7 us (1%)
    all_to_all x4, waiting for transfers between devices, exchange(): return lax.all_to_all(pieces, axes, split_axis=0, concat_axis=0, tiled=True)  29.3 us
    all_to_all x4, starting transfers between devices, exchange(): return lax.all_to_all(pieces, axes, split_axis=0, concat_axis=0, tiled=True)  14.4 us
    all_to_all x1, blocking collectives, exchange(): return lax.all_to_all(pieces, axes, split_axis=0, concat_axis=0, tiled=True)  9.51 us
    pallas_call x5, Pallas kernels, run(): pl.pallas_call(kernel, out_shape=out_shape, in_specs=in_specs, out_specs=...  7.88 us
    broadcast_in_dim x1, local copies, waits for them, and re-layouts, on_device(): jnp.broadcast_to(labels[None], (groups, group_tok))  1.29 us
  transfers between devices with their start and end apart: 4, of which 4 were waited for; matrix products, arithmetic and copies ran while one was open for 0% of the time, Pallas kernels for 11%

profile of v3, /device:TPU:0, one launch (start us, length us, event | category | flops | bytes accessed | tf_op | source)
XLA Modules:
  0.0 64.0 jit_solution(408094228748773311)
XLA Ops:
  0.6 0.0 copy-start
  0.6 1.3 %broadcast_in_dim.2 = s32[4,1,64]{2,1,0:T(1,128)} broadcast(s32[64]{0:T(128)} %param.6), dimensions={2} | broadcast | bytes 1280 | tf_op jit(solution)/shard_map/broadcast_in_dim | solution.py:154
  1.9 6.3 %all-to-all-start.1 = ((s32[4,1,64]{2,1,0:T(1,128)}), s32[4,1,64]{2,1,0:T(1,128)S(1)}, u32[]{:S(2)}, u32[]{:S(2)}) async-start(s32[4,1,64]{2,1,0:T(1,128)} %broadcast_in_dim.2), calls=%async_computation.1 | async-start | bytes 4096 | tf_op jit(solution)/shard_map/all_to_all | solution.py:136
  8.3 0.0 copy-start.1
  8.3 0.7 %copy-done.1 = bf16[8,512]{1,0:T(8,128)(2,1)S(1)} copy-done((bf16[8,512]{1,0:T(8,128)(2,1)S(1)}, bf16[8,512]{1,0:T(8,128)(2,1)}, u32[]{:S(2)}) %copy-start.1) | copy-done | bytes 8216
  8.9 0.8 %shard_map.76 = bf16[32,8,512]{2,1,0:T(8,128)(2,1)} custom-call(bf16[8,512]{1,0:T(8,128)(2,1)S(1)} %copy-done.1), custom_call_target="tpu_custom_call" | custom-call | bytes 270336 | tf_op jit(solution)/shard_map/pallas_call | solution.py:30
  9.8 0.0 copy-start.3
  9.8 4.0 %all-to-all-done.1 = s32[4,1,64]{2,1,0:T(1,128)S(1)} async-done(((s32[4,1,64]{2,1,0:T(1,128)}), s32[4,1,64]{2,1,0:T(1,128)S(1)}, u32[]{:S(2)}, u32[]{:S(2)}) %all-to-all-start.1) | async-done | bytes 1056 | tf_op jit(solution)/shard_map/all_to_all | solution.py:136
  13.7 2.8 %all-to-all-start = ((bf16[32,8,512]{2,1,0:T(8,128)(2,1)}), bf16[32,8,512]{2,1,0:T(8,128)(2,1)S(1)}, u32[]{:S(2)}, u32[]{:S(2)}) async-start(bf16[32,8,512]{2,1,0:T(8,128)(2,1)} %shard_map.76), calls=%async_computation | async-start | bytes 524288 | tf_op jit(solution)/shard_map/all_to_all | solution.py:136
  16.6 0.0 copy-done.3
  16.6 0.1 copy.13.ids
  16.7 0.0 copy-done
  16.7 1.6 %shard_map.77 = (bf16[4,128,512]{2,1,0:T(8,128)(2,1)S(1)}, bf16[4,64,512]{2,1,0:T(8,128)(2,1)}) custom-call(s32[4,1]{1,0:T(4,128)S(1)} %copy.13.ids, bf16[4,128,512]{2,1,0:T(8,128)(2,1)S(1)} %bitcast.9, s32[4,64]{1,0:T(4,128)S(1)} %bitcast.11), custom_call_target="tpu_custom_call" | custom-call | bytes 1311760 | tf_op jit(solution)/shard_map/pallas_call | solution.py:30
  18.3 8.8 %all-to-all-done = bf16[32,8,512]{2,1,0:T(8,128)(2,1)S(1)} async-done(((bf16[32,8,512]{2,1,0:T(8,128)(2,1)}), bf16[32,8,512]{2,1,0:T(8,128)(2,1)S(1)}, u32[]{:S(2)}, u32[]{:S(2)}) %all-to-all-start) | async-done | bytes 262176 | tf_op jit(solution)/shard_map/all_to_all | solution.py:136
  27.1 0.0 copy-start.4
  27.2 2.7 %all-to-all-start.3 = ((bf16[32,8,512]{2,1,0:T(8,128)(2,1)}), bf16[32,8,512]{2,1,0:T(8,128)(2,1)S(1)}, u32[]{:S(2)}, u32[]{:S(2)}) async-start(bf16[32,8,512]{2,1,0:T(8,128)(2,1)} %bitcast.3), calls=%async_computation.3 | async-start | bytes 524288 | tf_op jit(solution)/shard_map/all_to_all | solution.py:136
  29.9 0.0 copy-done.4
  29.9 0.1 copy.12.listed
  30.0 2.5 %shard_map.78 = (f32[4,128,64]{2,1,0:T(8,128)S(1)}, f32[32,4,128]{2,1,0:T(4,128)S(1)}, bf16[4,64,512]{2,1,0:T(8,128)(2,1)}) custom-call(s32[4,1]{1,0:T(4,128)S(1)} %copy.12.listed, bf16[4,64,512]{2,1,0:T(8,128)(2,1)S(1)} %bitcast.7, bf16[4,128,512]{2,1,0:T(8,128)(2,1)S(1)} %get-tuple-element.12.cands, s32[4,64]{1,0:T(4,128)S(1)} %bitcast.12), custom_call_target="tpu_custom_call" | custom-call | bytes 1246224 | tf_op jit(solution)/shard_map/pallas_call | solution.py:30
  32.4 8.0 %all-to-all-done.3.label_rows = bf16[32,8,512]{2,1,0:T(8,128)(2,1)S(1)} async-done(((bf16[32,8,512]{2,1,0:T(8,128)(2,1)}), bf16[32,8,512]{2,1,0:T(8,128)(2,1)S(1)}, u32[]{:S(2)}, u32[]{:S(2)}) %all-to-all-start.3) | async-done | bytes 262176 | tf_op jit(solution)/shard_map/all_to_all | solution.py:136
  40.5 9.5 %all_to_all.28.sums = f32[32,4,128]{2,1,0:T(4,128)S(1)} all-to-all(f32[32,4,128]{2,1,0:T(4,128)S(1)} %get-tuple-element.13), channel_id=1, replica_groups=mesh['group'=4,'member'=8] {'group','member'}, dimensions={0} | all-to-all | bytes 131072 | tf_op jit(solution)/shard_map/all_to_all | solution.py:136
  50.0 2.6 %all-to-all-start.4 = ((bf16[32,8,512]{2,1,0:T(8,128)(2,1)}), bf16[32,8,512]{2,1,0:T(8,128)(2,1)S(1)}, u32[]{:S(2)}, u32[]{:S(2)}) async-start(bf16[32,8,512]{2,1,0:T(8,128)(2,1)} %bitcast.5), calls=%async_computation.4 | async-start | bytes 524288 | tf_op jit(solution)/shard_map/all_to_all | solution.py:136
  52.6 0.0 copy-start.2
  52.6 2.2 %shard_map.79 = (f32[4,128,512]{2,1,0:T(8,128)}, f32[1,8]{1,0:T(1,128)}, f32[8,128]{1,0:T(8,128)S(1)}, f32[8,512]{1,0:T(8,128)S(1)}) custom-call(s32[4,1]{1,0:T(4,128)S(1)} %copy.13.ids, f32[32,4,128]{2,1,0:T(4,128)S(1)} %all_to_all.28.sums, f32[4,128,64]{2,1,0:T(8,128)S(1)} %get-tuple-element.14.expo, bf16[4,64,512]{2,1,0:T(8,128)(2,1)S(1)} %bitcast.8, ...), custom_call_target="tpu_custom_call" | custom-call | bytes 2315312 | tf_op jit(solution)/shard_map/pallas_call | solution.py:30
  54.8 8.4 %all-to-all-done.4.shares = bf16[32,8,512]{2,1,0:T(8,128)(2,1)S(1)} async-done(((bf16[32,8,512]{2,1,0:T(8,128)(2,1)}), bf16[32,8,512]{2,1,0:T(8,128)(2,1)S(1)}, u32[]{:S(2)}, u32[]{:S(2)}) %all-to-all-start.4) | async-done | bytes 262176 | tf_op jit(solution)/shard_map/all_to_all | solution.py:136
  63.2 0.0 copy-done.2
  63.2 0.8 %shard_map.80 = f32[8,512]{1,0:T(8,128)} custom-call(bf16[8,512]{1,0:T(8,128)(2,1)S(1)} %copy-done.2, bf16[32,8,512]{2,1,0:T(8,128)(2,1)S(1)} %all-to-all-done.4.shares, f32[8,128]{1,0:T(8,128)S(1)} %get-tuple-element.18.scale, f32[8,512]{1,0:T(8,128)S(1)} %get-tuple-element.19.pull), custom_call_target="tpu_custom_call" | custom-call | bytes 307200 | tf_op jit(solution)/shard_map/pallas_call | solution.py:30
Async XLA Ops:
  0.6 16.0 %copy-start = (bf16[512,512]{1,0:T(8,128)(2,1)S(1)}, bf16[512,512]{1,0:T(8,128)(2,1)}, u32[]{:S(2)}) copy-start(bf16[512,512]{1,0:T(8,128)(2,1)} %param.7) | copy-start | bytes 1572868
  1.9 11.8 %all-to-all-start.1 = ((s32[4,1,64]{2,1,0:T(1,128)}), s32[4,1,64]{2,1,0:T(1,128)S(1)}, u32[]{:S(2)}, u32[]{:S(2)}) async-start(s32[4,1,64]{2,1,0:T(1,128)} %broadcast_in_dim.2), calls=%async_computation.1 | async-start | bytes 4096 | tf_op jit(solution)/shard_map/all_to_all | solution.py:136
  8.3 0.7 %copy-start.1 = (bf16[8,512]{1,0:T(8,128)(2,1)S(1)}, bf16[8,512]{1,0:T(8,128)(2,1)}, u32[]{:S(2)}) copy-start(bf16[8,512]{1,0:T(8,128)(2,1)} %features.3) | copy-start | bytes 24580
  9.8 6.8 %copy-start.3 = (s32[4,1]{0,1:T(1,128)S(1)}, s32[4,1]{0,1:T(1,128)}, u32[]{:S(2)}) copy-start(s32[4,1]{0,1:T(1,128)} %param.8) | copy-start | bytes 52
  13.7 13.4 %all-to-all-start = ((bf16[32,8,512]{2,1,0:T(8,128)(2,1)}), bf16[32,8,512]{2,1,0:T(8,128)(2,1)S(1)}, u32[]{:S(2)}, u32[]{:S(2)}) async-start(bf16[32,8,512]{2,1,0:T(8,128)(2,1)} %shard_map.76), calls=%async_computation | async-start | bytes 524288 | tf_op jit(solution)/shard_map/all_to_all | solution.py:136
  27.1 2.7 %copy-start.4 = (s32[4,1]{0,1:T(1,128)S(1)}, s32[4,1]{0,1:T(1,128)}, u32[]{:S(2)}) copy-start(s32[4,1]{0,1:T(1,128)} %param.9) | copy-start | bytes 52
  27.2 13.3 %all-to-all-start.3 = ((bf16[32,8,512]{2,1,0:T(8,128)(2,1)}), bf16[32,8,512]{2,1,0:T(8,128)(2,1)S(1)}, u32[]{:S(2)}, u32[]{:S(2)}) async-start(bf16[32,8,512]{2,1,0:T(8,128)(2,1)} %bitcast.3), calls=%async_computation.3 | async-start | bytes 524288 | tf_op jit(solution)/shard_map/all_to_all | solution.py:136
  50.0 13.2 %all-to-all-start.4 = ((bf16[32,8,512]{2,1,0:T(8,128)(2,1)}), bf16[32,8,512]{2,1,0:T(8,128)(2,1)S(1)}, u32[]{:S(2)}, u32[]{:S(2)}) async-start(bf16[32,8,512]{2,1,0:T(8,128)(2,1)} %bitcast.5), calls=%async_computation.4 | async-start | bytes 524288 | tf_op jit(solution)/shard_map/all_to_all | solution.py:136
  52.6 10.6 %copy-start.2 = (bf16[8,512]{1,0:T(8,128)(2,1)S(1)}, bf16[8,512]{1,0:T(8,128)(2,1)}, u32[]{:S(2)}) copy-start(bf16[8,512]{1,0:T(8,128)(2,1)} %features.3) | copy-start | bytes 24580

commit v4 on v3

--- a/solution.py
+++ b/solution.py
@@ -41,10 +41,11 @@
     )(*operands)
 
 
-def pack_units(features, copies_out):
+def pack_units(features, labels, copies_out, labels_out):
     rows = features[...].astype(jnp.float32)
     unit = (rows * inverse_norm(rows)).astype(jnp.bfloat16)
     copies_out[...] = jnp.broadcast_to(unit[None], copies_out.shape)
+    labels_out[...] = labels[...]
 
 
 def own_slots(labels_row, group_tok, member, groups, group):
@@ -52,21 +53,16 @@
     return lax.broadcasted_iota(jnp.int32, (BLK, group_tok), 0) == labels_row - first
 
 
-def prepare(ids, centres, labels, cand_out, label_rows_out):
-    group, member = lax.axis_index("group"), lax.axis_index("member")
-    groups, group_tok = labels.shape
-    for g in range(groups):
+def prepare(ids, centres, cand_out):
+    for g in range(cand_out.shape[0]):
         rows = centres[ids[g, 0]].astype(jnp.float32)
-        cand = (rows * inverse_norm(rows)).astype(jnp.bfloat16)
-        cand_out[g] = cand
-        onehot = own_slots(labels[g : g + 1, :], group_tok, member, groups, group)
-        label_rows_out[g] = contract(onehot.astype(jnp.bfloat16), cand, 0, 0).astype(jnp.bfloat16)
+        cand_out[g] = (rows * inverse_norm(rows)).astype(jnp.bfloat16)
 
 
 def forward(listed, units, cands, labels, expo_out, sums_out, shares_out):
     group, member = lax.axis_index("group"), lax.axis_index("member")
     groups, group_tok = labels.shape
-    sums = []
+    width = units.shape[2]
     for g in range(groups):
         cand = cands[g]
         onehot = own_slots(labels[g : g + 1, :], group_tok, member, groups, group)
@@ -76,19 +72,19 @@
         expo_out[g] = expo
         totals = jnp.sum(expo, axis=0, keepdims=True)
         label_logit = jnp.sum(jnp.where(onehot, logits, 0.0), axis=0, keepdims=True)
-        sums.append(jnp.concatenate([totals, label_logit], axis=1))
+        sums_out[g : g + 1, :] = jnp.concatenate([totals, label_logit], axis=1)
         others = jnp.where(onehot, 0.0, expo).astype(jnp.bfloat16)
-        shares_out[g] = contract(others, cand, 0, 0).astype(jnp.bfloat16)
-    sums = jnp.concatenate(sums, axis=0)
-    sums_out[...] = jnp.broadcast_to(sums[None], sums_out.shape)
+        shares_out[g, :, :width] = contract(others, cand, 0, 0).astype(jnp.bfloat16)
+        label_rows = contract(onehot.astype(jnp.bfloat16), cand, 0, 0)
+        shares_out[g, :, width:] = label_rows.astype(jnp.bfloat16)
 
 
 def backward(
-    ids, sums, expo, units, centres, labels, label_rows, grad_out, loss_out, scale_out, pull_out
+    ids, sums, expo, units, centres, labels, grad_out, loss_out, scale_out, pull_out
 ):
     group, member = lax.axis_index("group"), lax.axis_index("member")
     groups, group_tok = labels.shape
-    both = jnp.sum(sums[...], axis=0)
+    both = sums[...]
     grad_out[...] = jnp.zeros_like(grad_out)
     for g in range(groups):
         rows = centres[ids[g, 0]].astype(jnp.float32)
@@ -119,21 +115,32 @@
     loss_out[...] = jnp.sum(jnp.where(diagonal, loss, 0.0), axis=0, keepdims=True)
     scale = logit_scale / total
     scale_out[...] = jnp.broadcast_to(scale, scale_out.shape)
-    label_row = jnp.sum(label_rows[...].astype(jnp.float32), axis=0)
-    pull_out[...] = scale * (total - jnp.exp(label_logit)) * label_row
+    pull_out[...] = jnp.broadcast_to(scale * (total - jnp.exp(label_logit)), pull_out.shape)
 
 
 def finish(features, shares, scale, pull, grad_out):
     rows = features[...].astype(jnp.float32)
     inv_norm = inverse_norm(rows)
     unit = rows * inv_norm
-    unit_grad = scale[:, :1] * jnp.sum(shares[...].astype(jnp.float32), axis=0) - pull[...]
+    width = rows.shape[1]
+    both = jnp.sum(shares[...].astype(jnp.float32), axis=0)
+    unit_grad = scale[:, :1] * both[:, :width] - pull[:, :1] * both[:, width:]
     along = jnp.sum(unit_grad * unit, axis=1, keepdims=True)
     grad_out[...] = inv_norm * (unit_grad - along * unit)
 
 
 def exchange(pieces, axes):
     return lax.all_to_all(pieces, axes, split_axis=0, concat_axis=0, tiled=True)
+
+
+def gather_groups(row):
+    groups = lax.axis_size("group")
+    rows = [row] + [
+        lax.ppermute(row, "group", [((i + step) % groups, i) for i in range(groups)])
+        for step in range(1, groups)
+    ]
+    ahead = jnp.concatenate(rows, axis=0)
+    return jnp.roll(ahead, lax.axis_index("group"), axis=0)
 
 
 def on_device(features, labels, centres, block_ids, listed):
@@ -149,26 +156,23 @@
     bf16, f32 = jnp.bfloat16, jnp.float32
     shape = jax.ShapeDtypeStruct
 
-    copies = run(pack_units, shape(per_device, bf16), [VMEM], features)
+    copies, own_labels = run(
+        pack_units,
+        (shape(per_device, bf16), shape((1, group_tok), labels.dtype)),
+        [VMEM, VMEM],
+        features,
+        labels.reshape(1, group_tok),
+    )
     units = exchange(copies, AXES).reshape(per_group)
-    all_labels = exchange(jnp.broadcast_to(labels[None], (groups, group_tok)), "group")
-
-    cands, label_rows = run(
-        prepare,
-        (shape((groups, BLK, width), bf16), shape(per_group, bf16)),
-        [SMEM, VMEM, VMEM],
-        block_ids,
-        blocks,
-        all_labels,
-    )
-    label_rows = exchange(label_rows.reshape(per_device), AXES)
+    all_labels = gather_groups(own_labels)
+    cands = run(prepare, shape((groups, BLK, width), bf16), [SMEM, VMEM], block_ids, blocks)
 
     expo, sums, shares = run(
         forward,
         (
             shape((groups, BLK, group_tok), f32),
-            shape((devices, groups, 2 * group_tok), f32),
-            shape(per_group, bf16),
+            shape((groups, 2 * group_tok), f32),
+            shape((groups, group_tok, 2 * width), bf16),
         ),
         [SMEM, VMEM, VMEM, VMEM],
         listed,
@@ -176,8 +180,8 @@
         cands,
         all_labels,
     )
-    sums = exchange(sums, AXES)
-    shares = exchange(shares.reshape(per_device), AXES)
+    shares = exchange(shares.reshape(devices, tok_dev, 2 * width), AXES)
+    sums = lax.psum(sums, AXES)
 
     centre_grad, loss, scale, pull = run(
         backward,
@@ -185,16 +189,15 @@
             shape((held, BLK, width), f32),
             shape((1, tok_dev), f32),
             shape((tok_dev, 128), f32),
-            shape((tok_dev, width), f32),
+            shape((tok_dev, 128), f32),
         ),
-        [SMEM] + [VMEM] * 6,
+        [SMEM] + [VMEM] * 5,
         block_ids,
         sums,
         expo,
         units,
         blocks,
         all_labels,
-        label_rows,
     )
     feature_grad = run(
         finish, shape((tok_dev, width), f32), [VMEM] * 4, features, shares, scale, pull

time: 64.4 us -> 69.8 us (1.084)
  blocking collectives: 9.51 us -> 40.9 us
  waiting for transfers between devices: 29.3 us -> 2.76 us
  Pallas kernels: 7.88 us -> 6.48 us
  starting transfers between devices: 14.4 us -> 15.6 us
    psum x0 -> x1, blocking collectives: none -> 40.9 us  [on_device(): sums = lax.psum(sums, AXES)]
    all_to_all x4 -> x2, waiting for transfers between devices: 29.3 us -> 1.1 us  [exchange(): return lax.all_to_all(pieces, axes, split_axis=0, concat_axis=0, tiled=True)]
    all_to_all x1 -> x0, blocking collectives: 9.51 us -> none  [exchange(): return lax.all_to_all(pieces, axes, split_axis=0, concat_axis=0, tiled=True)]
    ppermute x0 -> x3, starting transfers between devices: none -> 5.65 us  [gather_groups(): lax.ppermute(row, 'group', [((i + step) % groups, i) for i in range(group...]
    all_to_all x4 -> x2, starting transfers between devices: 14.4 us -> 9.92 us  [exchange(): return lax.all_to_all(pieces, axes, split_axis=0, concat_axis=0, tiled=True)]
    unnamed x12 -> x14, local copies, waits for them, and re-layouts: 0.9 us -> 2.81 us
    ppermute x0 -> x3, waiting for transfers between devices: none -> 1.66 us  [gather_groups(): lax.ppermute(row, 'group', [((i + step) % groups, i) for i in range(group...]
    pallas_call x5, Pallas kernels: 7.88 us -> 6.48 us  [run(): pl.pallas_call(kernel, out_shape=out_shape, in_specs=in_specs, out_specs=...]
  transfers between devices with their start and end apart: 4 -> 5, of which waited for: 4 -> 3; matrix products, arithmetic and copies ran while one was open for 0% -> 0% of each run, Pallas kernels for 11% -> 4%
where the time goes in v4:
time: 69.8 us; the launch traced here: 69.2 us
  blocking collectives  40.9 us (59%)
  starting transfers between devices  15.6 us (22%)
  Pallas kernels  6.48 us (9%)
  local copies, waits for them, and re-layouts  2.85 us (4%)
  waiting for transfers between devices  2.76 us (4%)
    psum x1, blocking collectives, on_device(): sums = lax.psum(sums, AXES)  40.9 us
    all_to_all x2, starting transfers between devices, exchange(): return lax.all_to_all(pieces, axes, split_axis=0, concat_axis=0, tiled=True)  9.92 us
    pallas_call x5, Pallas kernels, run(): pl.pallas_call(kernel, out_shape=out_shape, in_specs=in_specs, out_specs=...  6.48 us
    ppermute x3, starting transfers between devices, gather_groups(): lax.ppermute(row, 'group', [((i + step) % groups, i) for i in range(group...  5.65 us
    unnamed x14, local copies, waits for them, and re-layouts  2.81 us
    ppermute x3, waiting for transfers between devices, gather_groups(): lax.ppermute(row, 'group', [((i + step) % groups, i) for i in range(group...  1.66 us
  transfers between devices with their start and end apart: 5, of which 3 were waited for; matrix products, arithmetic and copies ran while one was open for 0% of the time, Pallas kernels for 4%

profile of v4, /device:TPU:0, one launch (start us, length us, event | category | flops | bytes accessed | tf_op | source)
XLA Modules:
  0.0 69.2 jit_solution(11233087723074478296)
XLA Ops:
  0.6 0.0 copy-start
  0.6 0.0 copy-start.1
  0.7 0.7 %copy-done.1 = bf16[8,512]{1,0:T(8,128)(2,1)S(1)} copy-done((bf16[8,512]{1,0:T(8,128)(2,1)S(1)}, bf16[8,512]{1,0:T(8,128)(2,1)}, u32[]{:S(2)}) %copy-start.1) | copy-done | bytes 8216
  1.4 0.0 copy-start.3
  1.4 0.7 copy-done.3
  2.1 0.8 %shard_map.76 = (bf16[32,8,512]{2,1,0:T(8,128)(2,1)}, s32[1,64]{1,0:T(1,128)S(1)}) custom-call(bf16[8,512]{1,0:T(8,128)(2,1)S(1)} %copy-done.1, s32[1,64]{1,0:T(1,128)S(1)} %bitcast.10), custom_call_target="tpu_custom_call" | custom-call | bytes 270848 | tf_op jit(solution)/shard_map/pallas_call | solution.py:30
  2.9 7.3 %all-to-all-start = ((bf16[32,8,512]{2,1,0:T(8,128)(2,1)}), bf16[32,8,512]{2,1,0:T(8,128)(2,1)S(1)}, u32[]{:S(2)}, u32[]{:S(2)}) async-start(bf16[32,8,512]{2,1,0:T(8,128)(2,1)} %get-tuple-element.12), calls=%async_computation | async-start | bytes 524288 | tf_op jit(solution)/shard_map/all_to_all | solution.py:133
  10.2 1.8 %collective-permute-start.2 = (s32[1,64]{1,0:T(1,128)S(1)}, s32[1,64]{1,0:T(1,128)S(1)}, u32[]{:S(2)}, u32[]{:S(2)}) collective-permute-start(s32[1,64]{1,0:T(1,128)S(1)} %get-tuple-element.13), channel_id=1, source_target_pairs={{24,0},{0,8},{8,16},{16,24},{25,1},{1,9},{9,17},{17,25},{26,2},{2,... | collective-permute-start | bytes 776 | tf_op jit(solution)/shard_map/ppermute | solution.py:139
  12.0 2.4 %collective-permute-start.1 = (s32[1,64]{1,0:T(1,128)S(1)}, s32[1,64]{1,0:T(1,128)S(1)}, u32[]{:S(2)}, u32[]{:S(2)}) collective-permute-start(s32[1,64]{1,0:T(1,128)S(1)} %get-tuple-element.13), channel_id=1, source_target_pairs={{16,0},{24,8},{0,16},{8,24},{17,1},{25,9},{1,17},{9,25},{18,2},{26... | collective-permute-start | bytes 776 | tf_op jit(solution)/shard_map/ppermute | solution.py:139
  14.4 1.4 %collective-permute-start = (s32[1,64]{1,0:T(1,128)S(1)}, s32[1,64]{1,0:T(1,128)S(1)}, u32[]{:S(2)}, u32[]{:S(2)}) collective-permute-start(s32[1,64]{1,0:T(1,128)S(1)} %get-tuple-element.13), channel_id=1, source_target_pairs={{8,0},{16,8},{24,16},{0,24},{9,1},{17,9},{25,17},{1,25},{10,2},{18... | collective-permute-start | bytes 776 | tf_op jit(solution)/shard_map/ppermute | solution.py:139
  15.8 0.0 copy-start.4
  15.8 0.7 copy-done.4
  16.5 0.0 copy-start.5
  16.5 0.1 copy.10.ids
  16.6 0.6 copy-done.5
  17.1 0.1 copy.9.listed
  17.2 0.0 copy-done
  17.2 0.8 %shard_map.77.cands = bf16[4,128,512]{2,1,0:T(8,128)(2,1)S(1)} custom-call(s32[4,1]{1,0:T(4,128)S(1)} %copy.10.ids, bf16[4,128,512]{2,1,0:T(8,128)(2,1)S(1)} %bitcast.8), custom_call_target="tpu_custom_call" | custom-call | bytes 1048592 | tf_op jit(solution)/shard_map/pallas_call | solution.py:30
  18.0 1.1 %collective-permute-done.2 = s32[1,64]{1,0:T(1,128)S(1)} collective-permute-done((s32[1,64]{1,0:T(1,128)S(1)}, s32[1,64]{1,0:T(1,128)S(1)}, u32[]{:S(2)}, u32[]{:S(2)}) %collective-permute-start.2) | collective-permute-done | bytes 288 | tf_op jit(solution)/shard_map/ppermute | solution.py:139
  19.1 0.6 collective-permute-done.1
  19.6 0.0 collective-permute-done
  19.7 1.1 %all-to-all-done = bf16[32,8,512]{2,1,0:T(8,128)(2,1)S(1)} async-done(((bf16[32,8,512]{2,1,0:T(8,128)(2,1)}), bf16[32,8,512]{2,1,0:T(8,128)(2,1)S(1)}, u32[]{:S(2)}, u32[]{:S(2)}) %all-to-all-start) | async-done | bytes 262176 | tf_op jit(solution)/shard_map/all_to_all | solution.py:133
  20.8 2.0 %shard_map.78 = (f32[4,128,64]{2,1,0:T(8,128)S(1)}, f32[4,128]{1,0:T(4,128)S(1)}, bf16[4,64,1024]{2,1,0:T(8,128)(2,1)}) custom-call(s32[4,1]{1,0:T(4,128)S(1)} %copy.9.listed, bf16[4,64,512]{2,1,0:T(8,128)(2,1)S(1)} %bitcast.6, bf16[4,128,512]{2,1,0:T(8,128)(2,1)S(1)} %shard_map.77.cands, s32[4,64]{1,0:T(4,128)S(1)} %constant_dynamic-slice_fusion.labels), custom_call_target="tpu_custom_call" | custom-call | bytes 1444880 | tf_op jit(solution)/shard_map/pallas_call | solution.py:30
  22.8 2.6 %all-to-all-start.1 = ((bf16[32,8,1024]{2,1,0:T(8,128)(2,1)}), bf16[32,8,1024]{2,1,0:T(8,128)(2,1)S(1)}, u32[]{:S(2)}, u32[]{:S(2)}) async-start(bf16[32,8,1024]{2,1,0:T(8,128)(2,1)} %bitcast.4), calls=%async_computation.1 | async-start | bytes 1048576 | tf_op jit(solution)/shard_map/all_to_all | solution.py:133
  25.4 40.9 %psum.7.sums = f32[4,128]{1,0:T(4,128)S(1)} all-reduce(f32[4,128]{1,0:T(4,128)S(1)} %get-tuple-element.14), channel_id=1, replica_groups=mesh['group'=4,'member'=8] {'group','member'}, use_global_device_ids=true, to_apply=%region_0.1 | all-reduce | flops 512 | bytes 4096 | tf_op jit(solution)/shard_map/psum | solution.py:184
  66.3 0.0 copy-start.2
  66.3 2.1 %shard_map.79 = (f32[4,128,512]{2,1,0:T(8,128)}, f32[1,8]{1,0:T(1,128)}, f32[8,128]{1,0:T(8,128)S(1)}, f32[8,128]{1,0:T(8,128)S(1)}) custom-call(s32[4,1]{1,0:T(4,128)S(1)} %copy.10.ids, f32[4,128]{1,0:T(4,128)S(1)} %psum.7.sums, f32[4,128,64]{2,1,0:T(8,128)S(1)} %get-tuple-element.15.expo, bf16[4,64,512]{2,1,0:T(8,128)(2,1)S(1)} %bitcast.7, ...), custom_call_target="tpu_custom_call" | custom-call | bytes 1977392 | tf_op jit(solution)/shard_map/pallas_call | solution.py:30
  68.4 0.0 all-to-all-done.1.shares
  68.4 0.0 copy-done.2
  68.4 0.8 %shard_map.80 = f32[8,512]{1,0:T(8,128)} custom-call(bf16[8,512]{1,0:T(8,128)(2,1)S(1)} %copy-done.2, bf16[32,8,1024]{2,1,0:T(8,128)(2,1)S(1)} %all-to-all-done.1.shares, f32[8,128]{1,0:T(8,128)S(1)} %get-tuple-element.18.scale, f32[8,128]{1,0:T(8,128)S(1)} %get-tuple-element.19.pull), custom_call_target="tpu_custom_call" | custom-call | bytes 557056 | tf_op jit(solution)/shard_map/pallas_call | solution.py:30
  (2 shorter events, 0.0 us)
Async XLA Ops:
  0.6 16.6 %copy-start = (bf16[512,512]{1,0:T(8,128)(2,1)S(1)}, bf16[512,512]{1,0:T(8,128)(2,1)}, u32[]{:S(2)}) copy-start(bf16[512,512]{1,0:T(8,128)(2,1)} %param.7) | copy-start | bytes 1572868
  0.6 0.8 %copy-start.1 = (bf16[8,512]{1,0:T(8,128)(2,1)S(1)}, bf16[8,512]{1,0:T(8,128)(2,1)}, u32[]{:S(2)}) copy-start(bf16[8,512]{1,0:T(8,128)(2,1)} %features.3) | copy-start | bytes 24580
  1.4 0.7 copy-start.3
  2.9 17.9 %all-to-all-start = ((bf16[32,8,512]{2,1,0:T(8,128)(2,1)}), bf16[32,8,512]{2,1,0:T(8,128)(2,1)S(1)}, u32[]{:S(2)}, u32[]{:S(2)}) async-start(bf16[32,8,512]{2,1,0:T(8,128)(2,1)} %get-tuple-element.12), calls=%async_computation | async-start | bytes 524288 | tf_op jit(solution)/shard_map/all_to_all | solution.py:133
  10.2 8.9 %collective-permute-start.2 = (s32[1,64]{1,0:T(1,128)S(1)}, s32[1,64]{1,0:T(1,128)S(1)}, u32[]{:S(2)}, u32[]{:S(2)}) collective-permute-start(s32[1,64]{1,0:T(1,128)S(1)} %get-tuple-element.13), channel_id=1, source_target_pairs={{24,0},{0,8},{8,16},{16,24},{25,1},{1,9},{9,17},{17,25},{26,2},{2,... | collective-permute-start | bytes 776 | tf_op jit(solution)/shard_map/ppermute | solution.py:139
  12.0 7.7 %collective-permute-start.1 = (s32[1,64]{1,0:T(1,128)S(1)}, s32[1,64]{1,0:T(1,128)S(1)}, u32[]{:S(2)}, u32[]{:S(2)}) collective-permute-start(s32[1,64]{1,0:T(1,128)S(1)} %get-tuple-element.13), channel_id=1, source_target_pairs={{16,0},{24,8},{0,16},{8,24},{17,1},{25,9},{1,17},{9,25},{18,2},{26... | collective-permute-start | bytes 776 | tf_op jit(solution)/shard_map/ppermute | solution.py:139
  14.4 5.2 %collective-permute-start = (s32[1,64]{1,0:T(1,128)S(1)}, s32[1,64]{1,0:T(1,128)S(1)}, u32[]{:S(2)}, u32[]{:S(2)}) collective-permute-start(s32[1,64]{1,0:T(1,128)S(1)} %get-tuple-element.13), channel_id=1, source_target_pairs={{8,0},{16,8},{24,16},{0,24},{9,1},{17,9},{25,17},{1,25},{10,2},{18... | collective-permute-start | bytes 776 | tf_op jit(solution)/shard_map/ppermute | solution.py:139
  15.8 0.7 copy-start.4
  16.5 0.7 copy-start.5
  22.8 45.6 %all-to-all-start.1 = ((bf16[32,8,1024]{2,1,0:T(8,128)(2,1)}), bf16[32,8,1024]{2,1,0:T(8,128)(2,1)S(1)}, u32[]{:S(2)}, u32[]{:S(2)}) async-start(bf16[32,8,1024]{2,1,0:T(8,128)(2,1)} %bitcast.4), calls=%async_computation.1 | async-start | bytes 1048576 | tf_op jit(solution)/shard_map/all_to_all | solution.py:133
  66.3 2.1 %copy-start.2 = (bf16[8,512]{1,0:T(8,128)(2,1)S(1)}, bf16[8,512]{1,0:T(8,128)(2,1)}, u32[]{:S(2)}) copy-start(bf16[8,512]{1,0:T(8,128)(2,1)} %features.3) | copy-start | bytes 24580

commit v5 on v4

--- a/solution.py
+++ b/solution.py
@@ -13,6 +13,7 @@
 norm_epsilon = 1e-06
 
 VMEM = pl.BlockSpec(memory_space=pltpu.VMEM)
+HBM = pl.BlockSpec(memory_space=pl.ANY)
 SMEM = pl.BlockSpec(memory_space=pltpu.SMEM)
 
 
@@ -25,13 +26,14 @@
     return lax.dot_general(left, right, dims, preferred_element_type=jnp.float32)
 
 
-def run(kernel, out_shape, in_specs, *operands):
+def run(kernel, out_shape, in_specs, *operands, scratch=()):
     shapes = jax.tree.leaves(out_shape)
     return pl.pallas_call(
         kernel,
         out_shape=out_shape,
         in_specs=in_specs,
         out_specs=jax.tree.map(lambda _: VMEM, out_shape),
+        scratch_shapes=scratch,
         compiler_params=pltpu.CompilerParams(vmem_limit_bytes=48 * 1024 * 1024),
         cost_estimate=pl.CostEstimate(
             flops=0,
@@ -41,11 +43,16 @@
     )(*operands)
 
 
-def pack_units(features, labels, copies_out, labels_out):
-    rows = features[...].astype(jnp.float32)
+def pack_units(features, labels, copies_out, labels_out, held, arrived):
+    rows_copy = pltpu.make_async_copy(features, held, arrived.at[0])
+    labels_copy = pltpu.make_async_copy(labels, labels_out, arrived.at[1])
+    rows_copy.start()
+    labels_copy.start()
+    rows_copy.wait()
+    rows = held[...].astype(jnp.float32)
     unit = (rows * inverse_norm(rows)).astype(jnp.bfloat16)
     copies_out[...] = jnp.broadcast_to(unit[None], copies_out.shape)
-    labels_out[...] = labels[...]
+    labels_copy.wait()
 
 
 def own_slots(labels_row, group_tok, member, groups, group):
@@ -73,10 +80,12 @@
         totals = jnp.sum(expo, axis=0, keepdims=True)
         label_logit = jnp.sum(jnp.where(onehot, logits, 0.0), axis=0, keepdims=True)
         sums_out[g : g + 1, :] = jnp.concatenate([totals, label_logit], axis=1)
-        others = jnp.where(onehot, 0.0, expo).astype(jnp.bfloat16)
-        shares_out[g, :, :width] = contract(others, cand, 0, 0).astype(jnp.bfloat16)
-        label_rows = contract(onehot.astype(jnp.bfloat16), cand, 0, 0)
-        shares_out[g, :, width:] = label_rows.astype(jnp.bfloat16)
+        others = jnp.where(onehot, 0.0, expo)
+        label = jnp.where(onehot, 1.0, 0.0)
+        both = jnp.concatenate([others, label], axis=1).astype(jnp.bfloat16)
+        both = contract(both, cand, 0, 0).astype(jnp.bfloat16)
+        shares_out[g, :, :width] = both[:group_tok]
+        shares_out[g, :, width:] = both[group_tok:]
 
 
 def backward(
@@ -143,6 +152,17 @@
     return jnp.roll(ahead, lax.axis_index("group"), axis=0)
 
 
+def sum_over(value, axis):
+    size = lax.axis_size(axis)
+    if size & (size - 1):
+        return lax.psum(value, axis)
+    bit = 1
+    while bit < size:
+        value = value + lax.ppermute(value, axis, [(i, i ^ bit) for i in range(size)])
+        bit *= 2
+    return value
+
+
 def on_device(features, labels, centres, block_ids, listed):
     groups = lax.axis_size("group")
     members = lax.axis_size("member")
@@ -159,9 +179,10 @@
     copies, own_labels = run(
         pack_units,
         (shape(per_device, bf16), shape((1, group_tok), labels.dtype)),
-        [VMEM, VMEM],
+        [HBM, HBM],
         features,
         labels.reshape(1, group_tok),
+        scratch=[pltpu.VMEM(features.shape, features.dtype), pltpu.SemaphoreType.DMA((2,))],
     )
     units = exchange(copies, AXES).reshape(per_group)
     all_labels = gather_groups(own_labels)
@@ -181,7 +202,7 @@
         all_labels,
     )
     shares = exchange(shares.reshape(devices, tok_dev, 2 * width), AXES)
-    sums = lax.psum(sums, AXES)
+    sums = sum_over(sum_over(sums, "member"), "group")
 
     centre_grad, loss, scale, pull = run(
         backward,

time: 69.8 us -> 45.5 us (0.65)
  blocking collectives: 40.9 us -> 0 us
  starting transfers between devices: 15.6 us -> 24.3 us
  waiting for transfers between devices: 2.76 us -> 10.7 us
    psum x1 -> x0, blocking collectives: 40.9 us -> none  [on_device(): sums = lax.psum(sums, AXES)]
    ppermute x0 -> x5, starting transfers between devices: none -> 8.71 us  [sum_over(): lax.ppermute(value, axis, [(i, i ^ bit) for i in range(size)])]
    ppermute x0 -> x5, waiting for transfers between devices: none -> 7.97 us  [sum_over(): lax.ppermute(value, axis, [(i, i ^ bit) for i in range(size)])]
  transfers between devices with their start and end apart: 5 -> 10, of which waited for: 3 -> 8; matrix products, arithmetic and copies ran while one was open for 0% -> 1% of each run, Pallas kernels for 4% -> 6%
where the time goes in v5:
time: 45.5 us; the launch traced here: 45.1 us
  starting transfers between devices  24.3 us (53%)
  waiting for transfers between devices  10.7 us (24%)
  Pallas kernels  6.5 us (14%)
  local copies, waits for them, and re-layouts  2.85 us (6%)
  between operations  0.7 us (2%)
    all_to_all x2, starting transfers between devices, exchange(): return lax.all_to_all(pieces, axes, split_axis=0, concat_axis=0, tiled=True)  9.92 us
    ppermute x5, starting transfers between devices, sum_over(): lax.ppermute(value, axis, [(i, i ^ bit) for i in range(size)])  8.71 us
    ppermute x5, waiting for transfers between devices, sum_over(): lax.ppermute(value, axis, [(i, i ^ bit) for i in range(size)])  7.97 us
    pallas_call x5, Pallas kernels, run(): pl.pallas_call(kernel, out_shape=out_shape, in_specs=in_specs, out_specs=...  6.5 us
    ppermute x3, starting transfers between devices, gather_groups(): lax.ppermute(row, 'group', [((i + step) % groups, i) for i in range(group...  5.65 us
    unnamed x14, local copies, waits for them, and re-layouts  2.81 us
    ppermute x3, waiting for transfers between devices, gather_groups(): lax.ppermute(row, 'group', [((i + step) % groups, i) for i in range(group...  1.66 us
    all_to_all x2, waiting for transfers between devices, exchange(): return lax.all_to_all(pieces, axes, split_axis=0, concat_axis=0, tiled=True)  1.1 us
  transfers between devices with their start and end apart: 10, of which 8 were waited for; matrix products, arithmetic and copies ran while one was open for 1% of the time, Pallas kernels for 6%

profile of v5, /device:TPU:0, one launch (start us, length us, event | category | flops | bytes accessed | tf_op | source)
XLA Modules:
  0.0 45.1 jit_solution(11388859339066590971)
XLA Ops:
  0.6 0.0 copy-start
  0.6 0.0 copy-start.1
  0.7 0.7 %copy-done.1 = bf16[8,512]{1,0:T(8,128)(2,1)S(1)} copy-done((bf16[8,512]{1,0:T(8,128)(2,1)S(1)}, bf16[8,512]{1,0:T(8,128)(2,1)}, u32[]{:S(2)}) %copy-start.1) | copy-done | bytes 8216
  1.4 0.0 copy-start.3
  1.4 0.7 %copy-done.3 = s32[64]{0:T(128)S(1)} copy-done((s32[64]{0:T(128)S(1)}, s32[64]{0:T(128)}, u32[]{:S(2)}) %copy-start.3) | copy-done | bytes 280
  2.1 0.8 %shard_map.76 = (bf16[32,8,512]{2,1,0:T(8,128)(2,1)}, s32[1,64]{1,0:T(1,128)S(1)}) custom-call(bf16[8,512]{1,0:T(8,128)(2,1)S(1)} %copy-done.1, s32[1,64]{1,0:T(1,128)S(1)} %bitcast.10), custom_call_target="tpu_custom_call" | custom-call | bytes 270848 | tf_op jit(solution)/shard_map/pallas_call | solution.py:31
  2.9 7.3 %all-to-all-start = ((bf16[32,8,512]{2,1,0:T(8,128)(2,1)}), bf16[32,8,512]{2,1,0:T(8,128)(2,1)S(1)}, u32[]{:S(2)}, u32[]{:S(2)}) async-start(bf16[32,8,512]{2,1,0:T(8,128)(2,1)} %get-tuple-element.12), calls=%async_computation | async-start | bytes 524288 | tf_op jit(solution)/shard_map/all_to_all | solution.py:142
  10.2 1.8 %collective-permute-start.2 = (s32[1,64]{1,0:T(1,128)S(1)}, s32[1,64]{1,0:T(1,128)S(1)}, u32[]{:S(2)}, u32[]{:S(2)}) collective-permute-start(s32[1,64]{1,0:T(1,128)S(1)} %get-tuple-element.13), channel_id=1, source_target_pairs={{24,0},{0,8},{8,16},{16,24},{25,1},{1,9},{9,17},{17,25},{26,2},{2,... | collective-permute-start | bytes 776 | tf_op jit(solution)/shard_map/ppermute | solution.py:148
  12.0 2.4 %collective-permute-start.1 = (s32[1,64]{1,0:T(1,128)S(1)}, s32[1,64]{1,0:T(1,128)S(1)}, u32[]{:S(2)}, u32[]{:S(2)}) collective-permute-start(s32[1,64]{1,0:T(1,128)S(1)} %get-tuple-element.13), channel_id=1, source_target_pairs={{16,0},{24,8},{0,16},{8,24},{17,1},{25,9},{1,17},{9,25},{18,2},{26... | collective-permute-start | bytes 776 | tf_op jit(solution)/shard_map/ppermute | solution.py:148
  14.4 1.4 %collective-permute-start = (s32[1,64]{1,0:T(1,128)S(1)}, s32[1,64]{1,0:T(1,128)S(1)}, u32[]{:S(2)}, u32[]{:S(2)}) collective-permute-start(s32[1,64]{1,0:T(1,128)S(1)} %get-tuple-element.13), channel_id=1, source_target_pairs={{8,0},{16,8},{24,16},{0,24},{9,1},{17,9},{25,17},{1,25},{10,2},{18... | collective-permute-start | bytes 776 | tf_op jit(solution)/shard_map/ppermute | solution.py:148
  15.9 0.0 copy-start.4
  15.9 0.7 %copy-done.4 = s32[4,1]{0,1:T(1,128)S(1)} copy-done((s32[4,1]{0,1:T(1,128)S(1)}, s32[4,1]{0,1:T(1,128)}, u32[]{:S(2)}) %copy-start.4) | copy-done | bytes 40
  16.5 0.0 copy-start.5
  16.5 0.1 copy.10.ids
  16.6 0.6 %copy-done.5 = s32[4,1]{0,1:T(1,128)S(1)} copy-done((s32[4,1]{0,1:T(1,128)S(1)}, s32[4,1]{0,1:T(1,128)}, u32[]{:S(2)}) %copy-start.5) | copy-done | bytes 40
  17.2 0.1 copy.9.listed
  17.3 0.0 copy-done
  17.3 0.8 %shard_map.77.cands = bf16[4,128,512]{2,1,0:T(8,128)(2,1)S(1)} custom-call(s32[4,1]{1,0:T(4,128)S(1)} %copy.10.ids, bf16[4,128,512]{2,1,0:T(8,128)(2,1)S(1)} %bitcast.8), custom_call_target="tpu_custom_call" | custom-call | bytes 1048592 | tf_op jit(solution)/shard_map/pallas_call | solution.py:31
  18.0 1.1 %collective-permute-done.2 = s32[1,64]{1,0:T(1,128)S(1)} collective-permute-done((s32[1,64]{1,0:T(1,128)S(1)}, s32[1,64]{1,0:T(1,128)S(1)}, u32[]{:S(2)}, u32[]{:S(2)}) %collective-permute-start.2) | collective-permute-done | bytes 288 | tf_op jit(solution)/shard_map/ppermute | solution.py:148
  19.1 0.6 %collective-permute-done.1 = s32[1,64]{1,0:T(1,128)S(1)} collective-permute-done((s32[1,64]{1,0:T(1,128)S(1)}, s32[1,64]{1,0:T(1,128)S(1)}, u32[]{:S(2)}, u32[]{:S(2)}) %collective-permute-start.1) | collective-permute-done | bytes 288 | tf_op jit(solution)/shard_map/ppermute | solution.py:148
  19.7 0.0 collective-permute-done
  19.7 1.1 %all-to-all-done = bf16[32,8,512]{2,1,0:T(8,128)(2,1)S(1)} async-done(((bf16[32,8,512]{2,1,0:T(8,128)(2,1)}), bf16[32,8,512]{2,1,0:T(8,128)(2,1)S(1)}, u32[]{:S(2)}, u32[]{:S(2)}) %all-to-all-start) | async-done | bytes 262176 | tf_op jit(solution)/shard_map/all_to_all | solution.py:142
  20.8 2.0 %shard_map.78 = (f32[4,128,64]{2,1,0:T(8,128)S(1)}, f32[4,128]{1,0:T(4,128)S(1)}, bf16[4,64,1024]{2,1,0:T(8,128)(2,1)}) custom-call(s32[4,1]{1,0:T(4,128)S(1)} %copy.9.listed, bf16[4,64,512]{2,1,0:T(8,128)(2,1)S(1)} %bitcast.6, bf16[4,128,512]{2,1,0:T(8,128)(2,1)S(1)} %shard_map.77.cands, s32[4,64]{1,0:T(4,128)S(1)} %constant_dynamic-slice_fusion.labels), custom_call_target="tpu_custom_call" | custom-call | bytes 1444880 | tf_op jit(solution)/shard_map/pallas_call | solution.py:31
  22.8 2.6 %all-to-all-start.1 = ((bf16[32,8,1024]{2,1,0:T(8,128)(2,1)}), bf16[32,8,1024]{2,1,0:T(8,128)(2,1)S(1)}, u32[]{:S(2)}, u32[]{:S(2)}) async-start(bf16[32,8,1024]{2,1,0:T(8,128)(2,1)} %bitcast.4), calls=%async_computation.1 | async-start | bytes 1048576 | tf_op jit(solution)/shard_map/all_to_all | solution.py:142
  25.4 0.3 collective-permute-start.3
  25.8 0.9 %collective-permute-done.3 = f32[4,128]{1,0:T(4,128)S(1)} collective-permute-done((f32[4,128]{1,0:T(4,128)S(1)}, f32[4,128]{1,0:T(4,128)S(1)}, u32[]{:S(2)}, u32[]{:S(2)}) %collective-permute-start.3) | collective-permute-done | bytes 2080 | tf_op jit(solution)/shard_map/ppermute | solution.py:161
  26.7 1.8 %collective-permute-start.4 = (f32[4,128]{1,0:T(4,128)S(1)}, f32[4,128]{1,0:T(4,128)S(1)}, u32[]{:S(2)}, u32[]{:S(2)}) collective-permute-start(f32[4,128]{1,0:T(4,128)S(1)} %add.27), channel_id=1, source_target_pairs={{0,2},{1,3},{2,0},{3,1},{4,6},{5,7},{6,4},{7,5},{8,10},{9,11},{10,... | collective-permute-start | bytes 6152 | tf_op jit(solution)/shard_map/ppermute | solution.py:161
  28.4 1.8 %collective-permute-done.4 = f32[4,128]{1,0:T(4,128)S(1)} collective-permute-done((f32[4,128]{1,0:T(4,128)S(1)}, f32[4,128]{1,0:T(4,128)S(1)}, u32[]{:S(2)}, u32[]{:S(2)}) %collective-permute-start.4) | collective-permute-done | bytes 2080 | tf_op jit(solution)/shard_map/ppermute | solution.py:161
  30.3 1.8 %collective-permute-start.5 = (f32[4,128]{1,0:T(4,128)S(1)}, f32[4,128]{1,0:T(4,128)S(1)}, u32[]{:S(2)}, u32[]{:S(2)}) collective-permute-start(f32[4,128]{1,0:T(4,128)S(1)} %add.28), channel_id=1, source_target_pairs={{0,4},{1,5},{2,6},{3,7},{4,0},{5,1},{6,2},{7,3},{8,12},{9,13},{10,... | collective-permute-start | bytes 6152 | tf_op jit(solution)/shard_map/ppermute | solution.py:161
  32.0 1.8 %collective-permute-done.5 = f32[4,128]{1,0:T(4,128)S(1)} collective-permute-done((f32[4,128]{1,0:T(4,128)S(1)}, f32[4,128]{1,0:T(4,128)S(1)}, u32[]{:S(2)}, u32[]{:S(2)}) %collective-permute-start.5) | collective-permute-done | bytes 2080 | tf_op jit(solution)/shard_map/ppermute | solution.py:161
  33.9 1.8 %collective-permute-start.6 = (f32[4,128]{1,0:T(4,128)S(1)}, f32[4,128]{1,0:T(4,128)S(1)}, u32[]{:S(2)}, u32[]{:S(2)}) collective-permute-start(f32[4,128]{1,0:T(4,128)S(1)} %add.29), channel_id=1, source_target_pairs={{0,8},{8,0},{16,24},{24,16},{1,9},{9,1},{17,25},{25,17},{2,10},{10... | collective-permute-start | bytes 6152 | tf_op jit(solution)/shard_map/ppermute | solution.py:161
  35.6 1.9 %collective-permute-done.6 = f32[4,128]{1,0:T(4,128)S(1)} collective-permute-done((f32[4,128]{1,0:T(4,128)S(1)}, f32[4,128]{1,0:T(4,128)S(1)}, u32[]{:S(2)}, u32[]{:S(2)}) %collective-permute-start.6) | collective-permute-done | bytes 2080 | tf_op jit(solution)/shard_map/ppermute | solution.py:161
  37.5 3.1 %collective-permute-start.7 = (f32[4,128]{1,0:T(4,128)S(1)}, f32[4,128]{1,0:T(4,128)S(1)}, u32[]{:S(2)}, u32[]{:S(2)}) collective-permute-start(f32[4,128]{1,0:T(4,128)S(1)} %add.30), channel_id=1, source_target_pairs={{0,16},{8,24},{16,0},{24,8},{1,17},{9,25},{17,1},{25,9},{2,18},{10... | collective-permute-start | bytes 6152 | tf_op jit(solution)/shard_map/ppermute | solution.py:161
  40.6 1.6 %collective-permute-done.7 = f32[4,128]{1,0:T(4,128)S(1)} collective-permute-done((f32[4,128]{1,0:T(4,128)S(1)}, f32[4,128]{1,0:T(4,128)S(1)}, u32[]{:S(2)}, u32[]{:S(2)}) %collective-permute-start.7) | collective-permute-done | bytes 2080 | tf_op jit(solution)/shard_map/ppermute | solution.py:161
  42.2 0.0 copy-start.2
  42.2 2.1 %shard_map.79 = (f32[4,128,512]{2,1,0:T(8,128)}, f32[1,8]{1,0:T(1,128)}, f32[8,128]{1,0:T(8,128)S(1)}, f32[8,128]{1,0:T(8,128)S(1)}) custom-call(s32[4,1]{1,0:T(4,128)S(1)} %copy.10.ids, f32[4,128]{1,0:T(4,128)S(1)} %add.31.sums, f32[4,128,64]{2,1,0:T(8,128)S(1)} %get-tuple-element.15.expo, bf16[4,64,512]{2,1,0:T(8,128)(2,1)S(1)} %bitcast.7, ...), custom_call_target="tpu_custom_call" | custom-call | bytes 1977392 | tf_op jit(solution)/shard_map/pallas_call | solution.py:31
  44.3 0.0 all-to-all-done.1.shares
  44.3 0.0 copy-done.2
  44.3 0.8 %shard_map.80 = f32[8,512]{1,0:T(8,128)} custom-call(bf16[8,512]{1,0:T(8,128)(2,1)S(1)} %copy-done.2, bf16[32,8,1024]{2,1,0:T(8,128)(2,1)S(1)} %all-to-all-done.1.shares, f32[8,128]{1,0:T(8,128)S(1)} %get-tuple-element.18.scale, f32[8,128]{1,0:T(8,128)S(1)} %get-tuple-element.19.pull), custom_call_target="tpu_custom_call" | custom-call | bytes 557056 | tf_op jit(solution)/shard_map/pallas_call | solution.py:31
  (7 shorter events, 0.0 us)
Async XLA Ops:
  0.6 16.6 %copy-start = (bf16[512,512]{1,0:T(8,128)(2,1)S(1)}, bf16[512,512]{1,0:T(8,128)(2,1)}, u32[]{:S(2)}) copy-start(bf16[512,512]{1,0:T(8,128)(2,1)} %param.7) | copy-start | bytes 1572868
  0.6 0.8 %copy-start.1 = (bf16[8,512]{1,0:T(8,128)(2,1)S(1)}, bf16[8,512]{1,0:T(8,128)(2,1)}, u32[]{:S(2)}) copy-start(bf16[8,512]{1,0:T(8,128)(2,1)} %features.3) | copy-start | bytes 24580
  1.4 0.7 %copy-start.3 = (s32[64]{0:T(128)S(1)}, s32[64]{0:T(128)}, u32[]{:S(2)}) copy-start(s32[64]{0:T(128)} %param.6) | copy-start | bytes 772
  2.9 17.9 %all-to-all-start = ((bf16[32,8,512]{2,1,0:T(8,128)(2,1)}), bf16[32,8,512]{2,1,0:T(8,128)(2,1)S(1)}, u32[]{:S(2)}, u32[]{:S(2)}) async-start(bf16[32,8,512]{2,1,0:T(8,128)(2,1)} %get-tuple-element.12), calls=%async_computation | async-start | bytes 524288 | tf_op jit(solution)/shard_map/all_to_all | solution.py:142
  10.2 8.9 %collective-permute-start.2 = (s32[1,64]{1,0:T(1,128)S(1)}, s32[1,64]{1,0:T(1,128)S(1)}, u32[]{:S(2)}, u32[]{:S(2)}) collective-permute-start(s32[1,64]{1,0:T(1,128)S(1)} %get-tuple-element.13), channel_id=1, source_target_pairs={{24,0},{0,8},{8,16},{16,24},{25,1},{1,9},{9,17},{17,25},{26,2},{2,... | collective-permute-start | bytes 776 | tf_op jit(solution)/shard_map/ppermute | solution.py:148
  12.0 7.7 %collective-permute-start.1 = (s32[1,64]{1,0:T(1,128)S(1)}, s32[1,64]{1,0:T(1,128)S(1)}, u32[]{:S(2)}, u32[]{:S(2)}) collective-permute-start(s32[1,64]{1,0:T(1,128)S(1)} %get-tuple-element.13), channel_id=1, source_target_pairs={{16,0},{24,8},{0,16},{8,24},{17,1},{25,9},{1,17},{9,25},{18,2},{26... | collective-permute-start | bytes 776 | tf_op jit(solution)/shard_map/ppermute | solution.py:148
  14.4 5.2 %collective-permute-start = (s32[1,64]{1,0:T(1,128)S(1)}, s32[1,64]{1,0:T(1,128)S(1)}, u32[]{:S(2)}, u32[]{:S(2)}) collective-permute-start(s32[1,64]{1,0:T(1,128)S(1)} %get-tuple-element.13), channel_id=1, source_target_pairs={{8,0},{16,8},{24,16},{0,24},{9,1},{17,9},{25,17},{1,25},{10,2},{18... | collective-permute-start | bytes 776 | tf_op jit(solution)/shard_map/ppermute | solution.py:148
  15.9 0.7 %copy-start.4 = (s32[4,1]{0,1:T(1,128)S(1)}, s32[4,1]{0,1:T(1,128)}, u32[]{:S(2)}) copy-start(s32[4,1]{0,1:T(1,128)} %param.8) | copy-start | bytes 52
  16.5 0.7 %copy-start.5 = (s32[4,1]{0,1:T(1,128)S(1)}, s32[4,1]{0,1:T(1,128)}, u32[]{:S(2)}) copy-start(s32[4,1]{0,1:T(1,128)} %param.9) | copy-start | bytes 52
  22.8 21.5 %all-to-all-start.1 = ((bf16[32,8,1024]{2,1,0:T(8,128)(2,1)}), bf16[32,8,1024]{2,1,0:T(8,128)(2,1)S(1)}, u32[]{:S(2)}, u32[]{:S(2)}) async-start(bf16[32,8,1024]{2,1,0:T(8,128)(2,1)} %bitcast.4), calls=%async_computation.1 | async-start | bytes 1048576 | tf_op jit(solution)/shard_map/all_to_all | solution.py:142
  25.4 1.2 %collective-permute-start.3 = (f32[4,128]{1,0:T(4,128)S(1)}, f32[4,128]{1,0:T(4,128)S(1)}, u32[]{:S(2)}, u32[]{:S(2)}) collective-permute-start(f32[4,128]{1,0:T(4,128)S(1)} %get-tuple-element.14), channel_id=1, source_target_pairs={{0,1},{1,0},{2,3},{3,2},{4,5},{5,4},{6,7},{7,6},{8,9},{9,8},{10,11... | collective-permute-start | bytes 6152 | tf_op jit(solution)/shard_map/ppermute | solution.py:161
  26.7 3.6 %collective-permute-start.4 = (f32[4,128]{1,0:T(4,128)S(1)}, f32[4,128]{1,0:T(4,128)S(1)}, u32[]{:S(2)}, u32[]{:S(2)}) collective-permute-start(f32[4,128]{1,0:T(4,128)S(1)} %add.27), channel_id=1, source_target_pairs={{0,2},{1,3},{2,0},{3,1},{4,6},{5,7},{6,4},{7,5},{8,10},{9,11},{10,... | collective-permute-start | bytes 6152 | tf_op jit(solution)/shard_map/ppermute | solution.py:161
  30.3 3.6 %collective-permute-start.5 = (f32[4,128]{1,0:T(4,128)S(1)}, f32[4,128]{1,0:T(4,128)S(1)}, u32[]{:S(2)}, u32[]{:S(2)}) collective-permute-start(f32[4,128]{1,0:T(4,128)S(1)} %add.28), channel_id=1, source_target_pairs={{0,4},{1,5},{2,6},{3,7},{4,0},{5,1},{6,2},{7,3},{8,12},{9,13},{10,... | collective-permute-start | bytes 6152 | tf_op jit(solution)/shard_map/ppermute | solution.py:161
  33.9 3.6 %collective-permute-start.6 = (f32[4,128]{1,0:T(4,128)S(1)}, f32[4,128]{1,0:T(4,128)S(1)}, u32[]{:S(2)}, u32[]{:S(2)}) collective-permute-start(f32[4,128]{1,0:T(4,128)S(1)} %add.29), channel_id=1, source_target_pairs={{0,8},{8,0},{16,24},{24,16},{1,9},{9,1},{17,25},{25,17},{2,10},{10... | collective-permute-start | bytes 6152 | tf_op jit(solution)/shard_map/ppermute | solution.py:161
  37.5 4.7 %collective-permute-start.7 = (f32[4,128]{1,0:T(4,128)S(1)}, f32[4,128]{1,0:T(4,128)S(1)}, u32[]{:S(2)}, u32[]{:S(2)}) collective-permute-start(f32[4,128]{1,0:T(4,128)S(1)} %add.30), channel_id=1, source_target_pairs={{0,16},{8,24},{16,0},{24,8},{1,17},{9,25},{17,1},{25,9},{2,18},{10... | collective-permute-start | bytes 6152 | tf_op jit(solution)/shard_map/ppermute | solution.py:161
  42.2 2.1 %copy-start.2 = (bf16[8,512]{1,0:T(8,128)(2,1)S(1)}, bf16[8,512]{1,0:T(8,128)(2,1)}, u32[]{:S(2)}) copy-start(bf16[8,512]{1,0:T(8,128)(2,1)} %features.3) | copy-start | bytes 24580

commit v6 on v1

v6 whole, which is shorter than its diff:
```python
import jax
import jax.numpy as jnp
from jax import lax
from jax.experimental import pallas as pl
from jax.experimental.pallas import tpu as pltpu
from jax.sharding import PartitionSpec as P

BLK = 128
AXES = ("group", "member")

logit_scale = 32.0
cos_margin = 0.35
norm_epsilon = 1e-06

VMEM = pl.BlockSpec(memory_space=pltpu.VMEM)
SMEM = pl.BlockSpec(memory_space=pltpu.SMEM)


def inverse_norm(rows):
    return lax.rsqrt(jnp.sum(rows * rows, axis=-1, keepdims=True) + norm_epsilon)


def contract(left, right, left_dim, right_dim):
    dims = (((left_dim,), (right_dim,)), ((), ()))
    return lax.dot_general(left, right, dims, preferred_element_type=jnp.float32)


def lanes(rows):
    return lax.broadcasted_iota(jnp.int32, (rows, 128), 1)


def run(kernel, out_shape, in_specs, *operands):
    shapes = jax.tree.leaves(out_shape)
    return pl.pallas_call(
        kernel,
        out_shape=out_shape,
        in_specs=in_specs,
        out_specs=jax.tree.map(lambda _: VMEM, out_shape),
        compiler_params=pltpu.CompilerParams(vmem_limit_bytes=48 * 1024 * 1024),
        cost_estimate=pl.CostEstimate(
            flops=0,
            transcendentals=0,
            bytes_accessed=sum(a.size * a.dtype.itemsize for a in (*shapes, *operands)),
        ),
    )(*operands)


def pack_units(features, labels, copies_out):
    group, member = lax.axis_index("group"), lax.axis_index("member")
    copies, tok_dev, _ = copies_out.shape
    width = features.shape[1]
    rows = features[...].astype(jnp.float32)
    unit = (rows * inverse_norm(rows)).astype(jnp.bfloat16)
    copies_out[:, :, :width] = jnp.broadcast_to(unit[None], (copies, tok_dev, width))

    pairs = lax.axis_size("member") // 2
    place = (group * pairs + member // 2) * tok_dev
    row = jnp.concatenate([labels[...], jnp.zeros((1, 128 - labels.shape[1]), jnp.int32)], axis=1)
    row = jnp.broadcast_to(row, (tok_dev, 128))
    row = pltpu.roll(row, lax.rem(place - member * tok_dev + 128, 128), 1)
    digit = lax.broadcasted_iota(jnp.int32, (tok_dev, 128), 0)
    digits = (row >> (7 * jnp.minimum(digit, 3))) & 127
    lane = lanes(tok_dev)
    digits = jnp.where((lane >= place) & (lane < place + tok_dev), digits, 0)
    copies_out[:, :, width:] = jnp.broadcast_to(
        digits.astype(jnp.float32).astype(jnp.bfloat16)[None], (copies, tok_dev, 128)
    )


def prepare(ids, centres, cand_out, unit_out, inverse_out):
    for g in range(ids.shape[0]):
        here = pl.ds(g * BLK, BLK)
        rows = centres[ids[g, 0]].astype(jnp.float32)
        inverse = inverse_norm(rows)
        unit = rows * inverse
        cand_out[here, :] = unit.astype(jnp.bfloat16)
        unit_out[here, :] = unit
        inverse_out[here, :] = jnp.broadcast_to(inverse, (BLK, 128))


def forward(listed, packed, cands, expo_out, sums_out, shares_out):
    group, member = lax.axis_index("group"), lax.axis_index("member")
    groups = listed.shape[0]
    width = cands.shape[1]
    tok_dev = packed.shape[0] * groups // 128
    per_group = 128 // groups
    units = packed[:, :width]
    digits = jnp.sum(
        packed[:, width:].astype(jnp.float32).reshape(128 // 8, 8, 128), axis=0
    ).astype(jnp.int32)
    labels = digits[0:1] + (digits[1:2] << 7) + (digits[2:3] << 14)
    first = (member * groups + group) * BLK
    onehot = lax.broadcasted_iota(jnp.int32, (BLK, 128), 0) == labels - first

    all_cosines = contract(cands[...], units, 1, 1)
    owner = lanes(1) // per_group
    cosine = jnp.zeros((BLK, 128), jnp.float32)
    active = jnp.zeros((1, 128), jnp.float32)
    for g in range(groups):
        cosine = jnp.where(owner == g, all_cosines[g * BLK : (g + 1) * BLK], cosine)
        active = jnp.where(owner == g, listed[g, 0].astype(jnp.float32), active)
    expo = jnp.exp(logit_scale * (cosine - jnp.where(onehot, cos_margin, 0.0))) * active
    others = jnp.where(onehot, 0.0, expo)
    expo_out[...] = jnp.where(onehot, -1.0, expo)
    sums_out[0:1, :] = jnp.sum(others, axis=0, keepdims=True)
    sums_out[1:2, :] = jnp.sum(jnp.where(onehot, expo, 0.0), axis=0, keepdims=True)

    others = others.T.astype(jnp.bfloat16)
    label = jnp.where(onehot, 1.0, 0.0).T.astype(jnp.bfloat16)
    for g in range(groups):
        here = slice(g * per_group, (g + 1) * per_group)
        cand = cands[g * BLK : (g + 1) * BLK, :]
        both = contract(jnp.concatenate([others[here], label[here]], axis=0), cand, 1, 0)
        both = both.astype(jnp.bfloat16)
        shares_out[here, :width] = both[:per_group]
        shares_out[here, width:] = both[per_group:]


def forward_other(own_sums, *refs):
    *ins, expo_out, sums_out, shares_out = refs
    forward(*ins, expo_out, sums_out.at[2:4], shares_out)
    sums_out[0:2, :] = own_sums[...]


def merge(shares, sums, partner_shares, partner_sums, sent_out):
    wide = shares.shape[1]
    both = shares[...].astype(jnp.float32) + partner_shares[...].astype(jnp.float32)
    sent_out[:, :wide] = both.astype(jnp.bfloat16)
    total = sums[...] + jnp.concatenate([partner_sums[2:4, :], partner_sums[0:2, :]], axis=0)
    high = total.astype(jnp.bfloat16)
    low = (total - high.astype(jnp.float32)).astype(jnp.bfloat16)
    tile = jnp.concatenate([high.astype(jnp.float32), low.astype(jnp.float32)], axis=0)
    tile = jnp.broadcast_to(tile[None], (shares.shape[0] // 8, 8, 128))
    sent_out[:, wide:] = tile.reshape(shares.shape[0], 128).astype(jnp.bfloat16)


def backward(
    ids,
    received,
    own_expo,
    other_expo,
    own_packed,
    other_packed,
    features,
    cand_unit,
    cand_inverse,
    grad_out,
    feature_out,
    loss_out,
):
    group, member = lax.axis_index("group"), lax.axis_index("member")
    groups = ids.shape[0]
    per_group = 128 // groups
    tok_dev, width = features.shape
    sums = received[0].astype(jnp.float32)
    for i in range(1, received.shape[0]):
        sums = sums + received[i].astype(jnp.float32)
    tile = sums[:, 2 * width :]
    tile = tile[:4] + tile[4:]
    own_rest, own_label = tile[0:1], tile[1:2]
    other_rest, other_label = tile[2:3], tile[3:4]

    units = jnp.concatenate([own_packed[:, :width], other_packed[:, :width]], axis=0)
    own_scale = logit_scale / (own_rest + own_label)
    other_scale = logit_scale / (other_rest + other_label)
    own = own_expo[...]
    other = other_expo[...]
    own = jnp.where(own < 0.0, -own_rest, own) * own_scale
    other = jnp.where(other < 0.0, -other_rest, other) * other_scale
    weights = jnp.concatenate([own, other], axis=1)
    owner = jnp.concatenate([lanes(1), lanes(1)], axis=1) // per_group
    grad_out[...] = jnp.zeros_like(grad_out)
    for g in range(groups):
        here = slice(g * BLK, (g + 1) * BLK)
        mine = jnp.where(owner == g, weights, 0.0).astype(jnp.bfloat16)
        slot_grad = contract(mine, units, 1, 0)
        unit = cand_unit[here, :]
        along = jnp.sum(slot_grad * unit, axis=1, keepdims=True)
        cand_grad = cand_inverse[here, :1] * (slot_grad - along * unit)
        grad_out[ids[g, 0]] += cand_grad.astype(jnp.bfloat16).astype(jnp.float32)

    place = (group * (lax.axis_size("member") // 2) + member // 2) * tok_dev
    sample = lax.broadcasted_iota(jnp.int32, (tok_dev, 128), 0) + place
    mine = lanes(tok_dev) == sample
    rest = jnp.sum(jnp.where(mine, own_rest, 0.0), axis=1, keepdims=True)
    label = jnp.sum(jnp.where(mine, own_label, 0.0), axis=1, keepdims=True)
    total = rest + label
    loss = jnp.log(total) - jnp.log(label)
    square = (tok_dev, tok_dev)
    diagonal = lax.broadcasted_iota(jnp.int32, square, 0) == lax.broadcasted_iota(
        jnp.int32, square, 1
    )
    loss_out[...] = jnp.sum(jnp.where(diagonal, loss, 0.0), axis=0, keepdims=True)
    rows = features[...].astype(jnp.float32)
    inv_norm = inverse_norm(rows)
    unit = rows * inv_norm
    unit_grad = logit_scale / total * (sums[:, :width] - rest * sums[:, width : 2 * width])
    along = jnp.sum(unit_grad * unit, axis=1, keepdims=True)
    feature_out[...] = inv_norm * (unit_grad - along * unit)


def exchange(pieces, axes, cores=1):
    groups = None
    if cores > 1:
        size = lax.axis_size(axes)
        groups = [list(range(core, size, cores)) for core in range(cores)]
    return lax.all_to_all(
        pieces, axes, split_axis=0, concat_axis=0, axis_index_groups=groups, tiled=True
    )


def with_partner(value):
    return lax.ppermute(value, "member", [(i, i ^ 1) for i in range(lax.axis_size("member"))])


def on_device(features, labels, centres, block_ids, listed):
    groups = lax.axis_size("group")
    chips = groups * lax.axis_size("member") // 2
    tok_dev, width = features.shape
    held = centres.shape[0] // BLK
    half = chips * tok_dev
    bf16, f32 = jnp.bfloat16, jnp.float32
    shape = jax.ShapeDtypeStruct

    copies = run(
        pack_units,
        shape((chips, tok_dev, width + 128), bf16),
        [VMEM, VMEM],
        features,
        labels.reshape(1, -1),
    )
    own_packed = exchange(copies, AXES, 2).reshape(half, width + 128)
    other_packed = with_partner(own_packed)
    cands, cand_unit, cand_inverse = run(
        prepare,
        (
            shape((groups * BLK, width), bf16),
            shape((groups * BLK, width), f32),
            shape((groups * BLK, 128), f32),
        ),
        [SMEM, VMEM],
        block_ids,
        centres.reshape(held, BLK, width),
    )
    own_expo, own_sums, shares = run(
        forward,
        (shape((BLK, half), f32), shape((2, half), f32), shape((half, 2 * width), bf16)),
        [SMEM, VMEM, VMEM],
        listed,
        own_packed,
        cands,
    )
    other_expo, sums, other_shares = run(
        forward_other,
        (shape((BLK, half), f32), shape((4, half), f32), shape((half, 2 * width), bf16)),
        [VMEM, SMEM, VMEM, VMEM],
        own_sums,
        listed,
        other_packed,
        cands,
    )
    sent = run(
        merge,
        shape((half, 2 * width + 128), bf16),
        [VMEM] * 4,
        shares,
        sums,
        with_partner(other_shares),
        with_partner(sums),
    )
    received = exchange(sent.reshape(chips, tok_dev, 2 * width + 128), AXES, 2)
    centre_grad, feature_grad, loss = run(
        backward,
        (shape((held, BLK, width), f32), shape((tok_dev, width), f32), shape((1, tok_dev), f32)),
        [SMEM] + [VMEM] * 8,
        block_ids,
        received,
        own_expo,
        other_expo,
        own_packed,
        other_packed,
        features,
        cand_unit,
        cand_inverse,
    )
    return (loss.reshape(tok_dev), feature_grad, centre_grad.reshape(held * BLK, width))


def on_device_of_many(features, labels, centres, block_ids, listed):
    groups = lax.axis_size("group")
    members = lax.axis_size("member")
    devices = groups * members
    group = lax.axis_index("group")
    member = lax.axis_index("member")
    tok_dev, width = features.shape
    group_tok = members * tok_dev
    held = centres.shape[0] // BLK

    vectors = features.astype(jnp.float32)
    inv_norm = inverse_norm(vectors)
    unit_rows = vectors * inv_norm
    copies = jnp.broadcast_to(unit_rows.astype(jnp.bfloat16), (devices, tok_dev, width))
    units = exchange(copies, AXES).reshape(groups, group_tok, width)
    all_labels = exchange(jnp.broadcast_to(labels[None], (groups, group_tok)), "group")

    picked = centres.reshape(held, BLK, width)[block_ids[:, 0]].astype(jnp.float32)
    inv_cand = inverse_norm(picked)
    unit_cand = picked * inv_cand
    cand_half = unit_cand.astype(jnp.bfloat16)
    cosine = jnp.einsum("gsd,gcd->gsc", units, cand_half, preferred_element_type=jnp.float32)
    local_label = all_labels - (member * groups + group) * BLK
    onehot = (lax.broadcasted_iota(jnp.int32, (1, 1, BLK), 2) == local_label[:, :, None]).astype(
        jnp.float32
    )
    logits = logit_scale * (cosine - cos_margin * onehot)
    exp_logits = jnp.exp(logits) * listed.astype(jnp.float32)[:, :, None]
    totals, label_logit = lax.psum(
        (jnp.sum(exp_logits, axis=2), jnp.sum(logits * onehot, axis=2)), AXES
    )
    loss_all = (jnp.log(totals) - label_logit).reshape(devices, tok_dev)
    sample_loss = lax.dynamic_slice_in_dim(loss_all, group * members + member, 1, 0)[0]

    weights = (logit_scale * (exp_logits / totals[:, :, None] - onehot)).astype(jnp.bfloat16)
    partial = jnp.einsum("gsc,gcd->gsd", weights, cand_half, preferred_element_type=jnp.float32)
    home = exchange(partial.astype(jnp.bfloat16).reshape(devices, tok_dev, width), AXES)
    unit_grad = jnp.sum(home.astype(jnp.float32), axis=0)
    feature_grad = inv_norm * (
        unit_grad - jnp.sum(unit_grad * unit_rows, axis=1, keepdims=True) * unit_rows
    )
    slot_grad = jnp.einsum("gsc,gsd->gcd", weights, units, preferred_element_type=jnp.float32)
    cand_grad = inv_cand * (
        slot_grad - jnp.sum(slot_grad * unit_cand, axis=2, keepdims=True) * unit_cand
    )
    cand_grad = cand_grad.astype(jnp.bfloat16).astype(jnp.float32)
    names = block_ids == jnp.arange(held, dtype=jnp.int32)[None, :]
    centre_grad = jnp.sum(
        jnp.where(names[:, :, None, None], cand_grad[:, None], 0.0), axis=0
    ).reshape(held * BLK, width)
    return (sample_loss, feature_grad, centre_grad)


def solution(mesh):
    in_specs = (
        P(AXES, None),
        P("group"),
        P(AXES, None),
        P(None, AXES),
        P(None, AXES),
    )
    out_specs = (P(AXES), P(AXES, None), P(AXES, None))

    def body(features, *others):
        half = mesh.size // 2 * features.shape[0]
        fits = half == 128 and 2 * mesh.shape["group"] == features.shape[0] == 8
        return (on_device if fits else on_device_of_many)(features, *others)

    return jax.shard_map(
        body, mesh=mesh, in_specs=in_specs, out_specs=out_specs, check_vma=False
    )
```

time: 51.1 us -> 41.6 us (0.81)
  blocking collectives: 0 us -> 30.2 us
  waiting for transfers between devices: 25 us -> 1.03 us
  starting transfers between devices: 12.5 us -> 0.57 us
  other arithmetic: 7.45 us -> 0 us
  Pallas kernels: 0 us -> 5.56 us
  matrix products: 1.99 us -> 0 us
    all_to_all x0 -> x2, blocking collectives: none -> 30.2 us  [exchange(): lax.all_to_all(pieces, axes, split_axis=0, concat_axis=0, axis_index_grou...]
    all_to_all x3 -> x0, waiting for transfers between devices: 25 us -> none  [the longest x1 11.1 us: on_device(): lax.all_to_all(jnp.broadcast_to(packed[None], (devices, tok_dev, width +...]
    all_to_all x3 -> x0, starting transfers between devices: 12.5 us -> none  [the longest x1 7.3 us: on_device(): lax.all_to_all(jnp.broadcast_to(packed[None], (devices, tok_dev, width +...]
    pallas_call x0 -> x6, Pallas kernels: none -> 5.56 us  [run(): pl.pallas_call(kernel, out_shape=out_shape, in_specs=in_specs, out_specs=...]
    unnamed x9 -> x14, local copies, waits for them, and re-layouts: 0.12 us -> 3.23 us
    mul x3 -> x0, other arithmetic: 2.83 us -> none  [the longest x1 2.14 us: on_device(): jnp.sum(slot_grad * unit_cand, axis=2, keepdims=True) * unit_cand]
    reduce_sum x6 -> x0, other arithmetic: 2.64 us -> none  [the longest x1 1.35 us: on_device(): jnp.sum(jnp.where(names[:, :, None, None], cand_grad[:, None], 0.0), axis=0)]
    dot_general x3 -> x0, matrix products: 1.99 us -> none  [the longest x1 1.04 us: on_device(): jnp.einsum('gsc,gcd->gsd', weights, cand_half, preferred_element_type=jnp...]
  transfers between devices with their start and end apart: 3 -> 3, of which waited for: 3 -> 1; matrix products, arithmetic and copies ran while one was open for 10% -> 0% of each run, Pallas kernels for 0% -> 5%
where the time goes in v6:
time: 41.6 us; the launch traced here: 41.3 us
  blocking collectives  30.2 us (73%)
  Pallas kernels  5.56 us (13%)
  local copies, waits for them, and re-layouts  3.23 us (8%)
  waiting for transfers between devices  1.03 us (2%)
  between operations  0.7 us (2%)
  starting transfers between devices  0.57 us (1%)
    all_to_all x2, blocking collectives, exchange(): lax.all_to_all(pieces, axes, split_axis=0, concat_axis=0, axis_index_grou...  30.2 us
    pallas_call x6, Pallas kernels, run(): pl.pallas_call(kernel, out_shape=out_shape, in_specs=in_specs, out_specs=...  5.56 us
    unnamed x14, local copies, waits for them, and re-layouts  3.23 us
    ppermute x3, waiting for transfers between devices, with_partner(): lax.ppermute(value, 'member', [(i, i ^ 1) for i in range(lax.axis_size('m...  1.03 us
  transfers between devices with their start and end apart: 3, of which 1 were waited for; matrix products, arithmetic and copies ran while one was open for 0% of the time, Pallas kernels for 5%

profile of v6, /device:TPU:0, one launch (start us, length us, event | category | flops | bytes accessed | tf_op | source)
XLA Modules:
  0.0 41.3 jit_solution(15888738878065464882)
XLA Ops:
  0.6 0.0 copy-start.3
  0.6 0.6 %copy-done.3 = s32[64]{0:T(128)S(1)} copy-done((s32[64]{0:T(128)S(1)}, s32[64]{0:T(128)}, u32[]{:S(2)}) %copy-start.3) | copy-done | bytes 280
  1.3 0.0 copy-start.1
  1.3 0.7 %copy-done.1 = bf16[8,512]{1,0:T(8,128)(2,1)S(1)} copy-done((bf16[8,512]{1,0:T(8,128)(2,1)S(1)}, bf16[8,512]{1,0:T(8,128)(2,1)}, u32[]{:S(2)}) %copy-start.1) | copy-done | bytes 8216
  2.0 0.1 shard_map.76
  2.1 16.0 %all_to_all.10 = bf16[16,8,640]{2,1,0:T(8,128)(2,1)S(1)} all-to-all(bf16[16,8,640]{2,1,0:T(8,128)(2,1)S(1)} %shard_map.76), channel_id=1, replica_groups={{0,2,4,6,8,10,12,14,16,18,20,22,24,26,28,30},{1,3,5,7,9,11,13,15,17,19,..., dimensions={0} | all-to-all | bytes 327680 | tf_op jit(solution)/shard_map/all_to_all | solution.py:207
  18.1 0.0 copy-start.4
  18.1 0.0 copy-start.5
  18.1 0.0 collective-permute-start
  18.1 0.6 %copy-done.4 = s32[4,1]{0,1:T(1,128)S(1)} copy-done((s32[4,1]{0,1:T(1,128)S(1)}, s32[4,1]{0,1:T(1,128)}, u32[]{:S(2)}) %copy-start.4) | copy-done | bytes 40
  18.8 0.1 copy.11.ids
  18.9 0.0 copy-done.5
  18.9 0.1 copy.9.listed.refs_0_
  19.0 0.0 copy-start
  19.0 1.0 %copy-done = bf16[512,512]{1,0:T(8,128)(2,1)S(1)} copy-done((bf16[512,512]{1,0:T(8,128)(2,1)S(1)}, bf16[512,512]{1,0:T(8,128)(2,1)}, u32[]{:S(2)}) %copy-start) | copy-done | bytes 524312
  20.0 0.8 %shard_map.77 = (bf16[512,512]{1,0:T(8,128)(2,1)S(1)}, f32[512,512]{1,0:T(8,128)S(1)}, f32[512,128]{1,0:T(8,128)S(1)}) custom-call(s32[4,1]{1,0:T(4,128)S(1)} %copy.11.ids, bf16[4,128,512]{2,1,0:T(8,128)(2,1)S(1)} %bitcast.10), custom_call_target="tpu_custom_call" | custom-call | bytes 2359312 | tf_op jit(solution)/shard_map/pallas_call | solution.py:34
  20.8 1.2 %shard_map.78 = (f32[128,128]{1,0:T(8,128)S(1)}, f32[2,128]{1,0:T(2,128)S(1)}, bf16[128,1024]{1,0:T(8,128)(2,1)S(1)}) custom-call(s32[4,1]{1,0:T(4,128)S(1)} %copy.9.listed.refs_0_, bf16[128,640]{1,0:T(8,128)(2,1)S(1)} %bitcast.7, bf16[512,512]{1,0:T(8,128)(2,1)S(1)} %get-tuple-element.15.cands.refs_2_), custom_call_target="tpu_custom_call" | custom-call | bytes 1016848 | tf_op jit(solution)/shard_map/pallas_call | solution.py:34
  22.1 0.0 collective-permute-done.refs_1_.other_packed
  22.1 1.2 %shard_map.79 = (f32[128,128]{1,0:T(8,128)S(1)}, f32[4,128]{1,0:T(4,128)S(1)}, bf16[128,1024]{1,0:T(8,128)(2,1)S(1)}) custom-call(f32[2,128]{1,0:T(2,128)S(1)} %get-tuple-element.17.own_sums, s32[4,1]{1,0:T(4,128)S(1)} %copy.9.listed.refs_0_, bf16[128,640]{1,0:T(8,128)(2,1)S(1)} %collective-permute-done.refs_1_.other_packed, ...), custom_call_target="tpu_custom_call" | custom-call | bytes 1018896 | tf_op jit(solution)/shard_map/pallas_call | solution.py:34
  23.3 0.1 collective-permute-start.1
  23.4 0.5 %collective-permute-start.2 = (f32[4,128]{1,0:T(4,128)S(1)}, f32[4,128]{1,0:T(4,128)S(1)}, u32[]{:S(2)}, u32[]{:S(2)}) collective-permute-start(f32[4,128]{1,0:T(4,128)S(1)} %get-tuple-element.18.sums), channel_id=1, source_target_pairs={{0,1},{1,0},{2,3},{3,2},{4,5},{5,4},{6,7},{7,6},{8,9},{9,8},{10,11... | collective-permute-start | bytes 6152 | tf_op jit(solution)/shard_map/ppermute | solution.py:213
  23.9 1.0 %collective-permute-done.2.partner_sums = f32[4,128]{1,0:T(4,128)S(1)} collective-permute-done((f32[4,128]{1,0:T(4,128)S(1)}, f32[4,128]{1,0:T(4,128)S(1)}, u32[]{:S(2)}, u32[]{:S(2)}) %collective-permute-start.2) | collective-permute-done | bytes 2080 | tf_op jit(solution)/shard_map/ppermute | solution.py:213
  24.9 0.0 collective-permute-done.1.partner_shares
  24.9 0.1 shard_map.80
  25.0 0.0 copy-start.2
  25.0 14.2 %all_to_all.11.received = bf16[16,8,1152]{2,1,0:T(8,128)(2,1)S(1)} all-to-all(bf16[16,8,1152]{2,1,0:T(8,128)(2,1)S(1)} %bitcast.9), channel_id=1, replica_groups={{0,2,4,6,8,10,12,14,16,18,20,22,24,26,28,30},{1,3,5,7,9,11,13,15,17,19,..., dimensions={0} | all-to-all | bytes 589824 | tf_op jit(solution)/shard_map/all_to_all | solution.py:207
  39.1 0.0 copy-done.2
  39.2 2.1 %shard_map.81 = (f32[4,128,512]{2,1,0:T(8,128)}, f32[8,512]{1,0:T(8,128)}, f32[1,8]{1,0:T(1,128)}) custom-call(s32[4,1]{1,0:T(4,128)S(1)} %copy.11.ids, bf16[16,8,1152]{2,1,0:T(8,128)(2,1)S(1)} %all_to_all.11.received, f32[128,128]{1,0:T(8,128)S(1)} %get-tuple-element.20.own_expo, f32[128,128]{1,0:T(8,128)S(1)} %get-tuple-element.21.other_expo, ...), custom_call_target="tpu_custom_call" | custom-call | bytes 3137584 | tf_op jit(solution)/shard_map/pallas_call | solution.py:34
Async XLA Ops:
  0.6 0.7 %copy-start.3 = (s32[64]{0:T(128)S(1)}, s32[64]{0:T(128)}, u32[]{:S(2)}) copy-start(s32[64]{0:T(128)} %param.6) | copy-start | bytes 772
  1.3 0.7 %copy-start.1 = (bf16[8,512]{1,0:T(8,128)(2,1)S(1)}, bf16[8,512]{1,0:T(8,128)(2,1)}, u32[]{:S(2)}) copy-start(bf16[8,512]{1,0:T(8,128)(2,1)} %features.3) | copy-start | bytes 24580
  18.1 0.7 %copy-start.4 = (s32[4,1]{0,1:T(1,128)S(1)}, s32[4,1]{0,1:T(1,128)}, u32[]{:S(2)}) copy-start(s32[4,1]{0,1:T(1,128)} %param.8) | copy-start | bytes 52
  18.1 0.7 %copy-start.5 = (s32[4,1]{0,1:T(1,128)S(1)}, s32[4,1]{0,1:T(1,128)}, u32[]{:S(2)}) copy-start(s32[4,1]{0,1:T(1,128)} %param.9) | copy-start | bytes 52
  18.1 3.9 %collective-permute-start = (bf16[128,640]{1,0:T(8,128)(2,1)S(1)}, bf16[128,640]{1,0:T(8,128)(2,1)S(1)}, u32[]{:S(2)}, u32[]{:S(2)}) collective-permute-start(bf16[128,640]{1,0:T(8,128)(2,1)S(1)} %bitcast.6), channel_id=1, source_target_pairs={{0,1},{1,0},{2,3},{3,2},{4,5},{5,4},{6,7},{7,6},{8,9},{9,8},{10,11... | collective-permute-start | bytes 491528 | tf_op jit(solution)/shard_map/ppermute | solution.py:213
  19.0 1.0 %copy-start = (bf16[512,512]{1,0:T(8,128)(2,1)S(1)}, bf16[512,512]{1,0:T(8,128)(2,1)}, u32[]{:S(2)}) copy-start(bf16[512,512]{1,0:T(8,128)(2,1)} %param.7) | copy-start | bytes 1572868
  23.3 1.6 %collective-permute-start.1 = (bf16[128,1024]{1,0:T(8,128)(2,1)S(1)}, bf16[128,1024]{1,0:T(8,128)(2,1)S(1)}, u32[]{:S(2)}, u32[]{:S(2)}) collective-permute-start(bf16[128,1024]{1,0:T(8,128)(2,1)S(1)} %get-tuple-element.19), channel_id=1, source_target_pairs={{0,1},{1,0},{2,3},{3,2},{4,5},{5,4},{6,7},{7,6},{8,9},{9,8},{10,11... | collective-permute-start | bytes 786440 | tf_op jit(solution)/shard_map/ppermute | solution.py:213
  23.4 1.5 %collective-permute-start.2 = (f32[4,128]{1,0:T(4,128)S(1)}, f32[4,128]{1,0:T(4,128)S(1)}, u32[]{:S(2)}, u32[]{:S(2)}) collective-permute-start(f32[4,128]{1,0:T(4,128)S(1)} %get-tuple-element.18.sums), channel_id=1, source_target_pairs={{0,1},{1,0},{2,3},{3,2},{4,5},{5,4},{6,7},{7,6},{8,9},{9,8},{10,11... | collective-permute-start | bytes 6152 | tf_op jit(solution)/shard_map/ppermute | solution.py:213
  25.0 14.2 %copy-start.2 = (bf16[8,512]{1,0:T(8,128)(2,1)S(1)}, bf16[8,512]{1,0:T(8,128)(2,1)}, u32[]{:S(2)}) copy-start(bf16[8,512]{1,0:T(8,128)(2,1)} %features.3) | copy-start | bytes 24580

commit v7 on v6

--- a/solution.py
+++ b/solution.py
@@ -7,6 +7,7 @@
 
 BLK = 128
 AXES = ("group", "member")
+CHIPS = ("group", "chip")
 
 logit_scale = 32.0
 cos_margin = 0.35
@@ -46,15 +47,15 @@
 
 
 def pack_units(features, labels, copies_out):
-    group, member = lax.axis_index("group"), lax.axis_index("member")
+    chip = lax.axis_index("chip")
+    member = 2 * chip + lax.axis_index("core")
     copies, tok_dev, _ = copies_out.shape
     width = features.shape[1]
     rows = features[...].astype(jnp.float32)
     unit = (rows * inverse_norm(rows)).astype(jnp.bfloat16)
     copies_out[:, :, :width] = jnp.broadcast_to(unit[None], (copies, tok_dev, width))
 
-    pairs = lax.axis_size("member") // 2
-    place = (group * pairs + member // 2) * tok_dev
+    place = (lax.axis_index("group") * lax.axis_size("chip") + chip) * tok_dev
     row = jnp.concatenate([labels[...], jnp.zeros((1, 128 - labels.shape[1]), jnp.int32)], axis=1)
     row = jnp.broadcast_to(row, (tok_dev, 128))
     row = pltpu.roll(row, lax.rem(place - member * tok_dev + 128, 128), 1)
@@ -79,7 +80,8 @@
 
 
 def forward(listed, packed, cands, expo_out, sums_out, shares_out):
-    group, member = lax.axis_index("group"), lax.axis_index("member")
+    group = lax.axis_index("group")
+    member = 2 * lax.axis_index("chip") + lax.axis_index("core")
     groups = listed.shape[0]
     width = cands.shape[1]
     tok_dev = packed.shape[0] * groups // 128
@@ -148,7 +150,6 @@
     feature_out,
     loss_out,
 ):
-    group, member = lax.axis_index("group"), lax.axis_index("member")
     groups = ids.shape[0]
     per_group = 128 // groups
     tok_dev, width = features.shape
@@ -179,7 +180,8 @@
         cand_grad = cand_inverse[here, :1] * (slot_grad - along * unit)
         grad_out[ids[g, 0]] += cand_grad.astype(jnp.bfloat16).astype(jnp.float32)
 
-    place = (group * (lax.axis_size("member") // 2) + member // 2) * tok_dev
+    chip = lax.axis_index("group") * lax.axis_size("chip") + lax.axis_index("chip")
+    place = chip * tok_dev
     sample = lax.broadcasted_iota(jnp.int32, (tok_dev, 128), 0) + place
     mine = lanes(tok_dev) == sample
     rest = jnp.sum(jnp.where(mine, own_rest, 0.0), axis=1, keepdims=True)
@@ -199,23 +201,17 @@
     feature_out[...] = inv_norm * (unit_grad - along * unit)
 
 
-def exchange(pieces, axes, cores=1):
-    groups = None
-    if cores > 1:
-        size = lax.axis_size(axes)
-        groups = [list(range(core, size, cores)) for core in range(cores)]
-    return lax.all_to_all(
-        pieces, axes, split_axis=0, concat_axis=0, axis_index_groups=groups, tiled=True
-    )
+def exchange(pieces, axes):
+    return lax.all_to_all(pieces, axes, split_axis=0, concat_axis=0, tiled=True)
 
 
 def with_partner(value):
-    return lax.ppermute(value, "member", [(i, i ^ 1) for i in range(lax.axis_size("member"))])
+    return lax.ppermute(value, "core", [(0, 1), (1, 0)])
 
 
 def on_device(features, labels, centres, block_ids, listed):
     groups = lax.axis_size("group")
-    chips = groups * lax.axis_size("member") // 2
+    chips = groups * lax.axis_size("chip")
     tok_dev, width = features.shape
     held = centres.shape[0] // BLK
     half = chips * tok_dev
@@ -229,7 +225,7 @@
         features,
         labels.reshape(1, -1),
     )
-    own_packed = exchange(copies, AXES, 2).reshape(half, width + 128)
+    own_packed = exchange(copies, CHIPS).reshape(half, width + 128)
     other_packed = with_partner(own_packed)
     cands, cand_unit, cand_inverse = run(
         prepare,
@@ -268,7 +264,7 @@
         with_partner(other_shares),
         with_partner(sums),
     )
-    received = exchange(sent.reshape(chips, tok_dev, 2 * width + 128), AXES, 2)
+    received = exchange(sent.reshape(chips, tok_dev, 2 * width + 128), CHIPS)
     centre_grad, feature_grad, loss = run(
         backward,
         (shape((held, BLK, width), f32), shape((tok_dev, width), f32), shape((1, tok_dev), f32)),
@@ -339,21 +335,27 @@
     return (sample_loss, feature_grad, centre_grad)
 
 
+def on_axes(body, mesh, axes):
+    split = P(axes)
+    return jax.shard_map(
+        body,
+        mesh=mesh,
+        in_specs=(split, P("group"), split, P(None, axes), P(None, axes)),
+        out_specs=(split, split, split),
+        check_vma=False,
+    )
+
+
 def solution(mesh):
-    in_specs = (
-        P(AXES, None),
-        P("group"),
-        P(AXES, None),
-        P(None, AXES),
-        P(None, AXES),
-    )
-    out_specs = (P(AXES), P(AXES, None), P(AXES, None))
-
-    def body(features, *others):
-        half = mesh.size // 2 * features.shape[0]
-        fits = half == 128 and 2 * mesh.shape["group"] == features.shape[0] == 8
-        return (on_device if fits else on_device_of_many)(features, *others)
-
-    return jax.shard_map(
-        body, mesh=mesh, in_specs=in_specs, out_specs=out_specs, check_vma=False
-    )
+    groups, members = mesh.shape["group"], mesh.shape["member"]
+    by_core = jax.sharding.Mesh(
+        mesh.devices.reshape(groups, members // 2, 2), ("group", "chip", "core")
+    )
+
+    def program(features, *others):
+        half = features.shape[0] // 2
+        if half == 128 and 2 * groups == features.shape[0] // mesh.size == 8:
+            return on_axes(on_device, by_core, (*CHIPS, "core"))(features, *others)
+        return on_axes(on_device_of_many, mesh, AXES)(features, *others)
+
+    return program

time: 41.6 us -> 41.6 us (level)
  no operation moved by 1% of the time
where the time goes in v7:
time: 41.6 us; the launch traced here: 41.3 us
  blocking collectives  30.2 us (73%)
  Pallas kernels  5.57 us (13%)
  local copies, waits for them, and re-layouts  3.23 us (8%)
  waiting for transfers between devices  1.03 us (2%)
  between operations  0.7 us (2%)
  starting transfers between devices  0.57 us (1%)
    all_to_all x2, blocking collectives, exchange(): return lax.all_to_all(pieces, axes, split_axis=0, concat_axis=0, tiled=True)  30.2 us
    pallas_call x6, Pallas kernels, run(): pl.pallas_call(kernel, out_shape=out_shape, in_specs=in_specs, out_specs=...  5.57 us
    unnamed x14, local copies, waits for them, and re-layouts  3.23 us
    ppermute x3, waiting for transfers between devices, with_partner(): return lax.ppermute(value, 'core', [(0, 1), (1, 0)])  1.03 us
  transfers between devices with their start and end apart: 3, of which 1 were waited for; matrix products, arithmetic and copies ran while one was open for 0% of the time, Pallas kernels for 5%

profile of v7, /device:TPU:0, one launch (start us, length us, event | category | flops | bytes accessed | tf_op | source)
XLA Modules:
  0.0 41.3 jit_solution(8282937608558681895)
XLA Ops:
  0.6 0.0 copy-start.3
  0.6 0.6 %copy-done.3 = s32[64]{0:T(128)S(1)} copy-done((s32[64]{0:T(128)S(1)}, s32[64]{0:T(128)}, u32[]{:S(2)}) %copy-start.3) | copy-done | bytes 280
  1.3 0.0 copy-start.1
  1.3 0.7 %copy-done.1 = bf16[8,512]{1,0:T(8,128)(2,1)S(1)} copy-done((bf16[8,512]{1,0:T(8,128)(2,1)S(1)}, bf16[8,512]{1,0:T(8,128)(2,1)}, u32[]{:S(2)}) %copy-start.1) | copy-done | bytes 8216
  2.0 0.1 shard_map.76
  2.1 16.0 %all_to_all.10 = bf16[16,8,640]{2,1,0:T(8,128)(2,1)S(1)} all-to-all(bf16[16,8,640]{2,1,0:T(8,128)(2,1)S(1)} %shard_map.76), channel_id=1, replica_groups=mesh['group'=4,'chip'=4,'core'=2] {'group','chip'}, dimensions={0} | all-to-all | bytes 327680 | tf_op jit(solution)/shard_map/all_to_all | solution.py:205
  18.1 0.0 copy-start.4
  18.1 0.0 copy-start.5
  18.1 0.0 collective-permute-start
  18.1 0.6 %copy-done.4 = s32[4,1]{0,1:T(1,128)S(1)} copy-done((s32[4,1]{0,1:T(1,128)S(1)}, s32[4,1]{0,1:T(1,128)}, u32[]{:S(2)}) %copy-start.4) | copy-done | bytes 40
  18.8 0.1 copy.11.ids
  18.9 0.0 copy-done.5
  18.9 0.1 copy.9.listed.refs_0_
  19.0 0.0 copy-start
  19.0 1.0 %copy-done = bf16[512,512]{1,0:T(8,128)(2,1)S(1)} copy-done((bf16[512,512]{1,0:T(8,128)(2,1)S(1)}, bf16[512,512]{1,0:T(8,128)(2,1)}, u32[]{:S(2)}) %copy-start) | copy-done | bytes 524312
  20.0 0.8 %shard_map.77 = (bf16[512,512]{1,0:T(8,128)(2,1)S(1)}, f32[512,512]{1,0:T(8,128)S(1)}, f32[512,128]{1,0:T(8,128)S(1)}) custom-call(s32[4,1]{1,0:T(4,128)S(1)} %copy.11.ids, bf16[4,128,512]{2,1,0:T(8,128)(2,1)S(1)} %bitcast.10), custom_call_target="tpu_custom_call" | custom-call | bytes 2359312 | tf_op jit(solution)/shard_map/pallas_call | solution.py:35
  20.8 1.2 %shard_map.78 = (f32[128,128]{1,0:T(8,128)S(1)}, f32[2,128]{1,0:T(2,128)S(1)}, bf16[128,1024]{1,0:T(8,128)(2,1)S(1)}) custom-call(s32[4,1]{1,0:T(4,128)S(1)} %copy.9.listed.refs_0_, bf16[128,640]{1,0:T(8,128)(2,1)S(1)} %bitcast.7, bf16[512,512]{1,0:T(8,128)(2,1)S(1)} %get-tuple-element.15.cands.refs_2_), custom_call_target="tpu_custom_call" | custom-call | bytes 1016848 | tf_op jit(solution)/shard_map/pallas_call | solution.py:35
  22.1 0.0 collective-permute-done.refs_1_.other_packed
  22.1 1.2 %shard_map.79 = (f32[128,128]{1,0:T(8,128)S(1)}, f32[4,128]{1,0:T(4,128)S(1)}, bf16[128,1024]{1,0:T(8,128)(2,1)S(1)}) custom-call(f32[2,128]{1,0:T(2,128)S(1)} %get-tuple-element.17.own_sums, s32[4,1]{1,0:T(4,128)S(1)} %copy.9.listed.refs_0_, bf16[128,640]{1,0:T(8,128)(2,1)S(1)} %collective-permute-done.refs_1_.other_packed, ...), custom_call_target="tpu_custom_call" | custom-call | bytes 1018896 | tf_op jit(solution)/shard_map/pallas_call | solution.py:35
  23.3 0.1 collective-permute-start.1
  23.4 0.5 %collective-permute-start.2 = (f32[4,128]{1,0:T(4,128)S(1)}, f32[4,128]{1,0:T(4,128)S(1)}, u32[]{:S(2)}, u32[]{:S(2)}) collective-permute-start(f32[4,128]{1,0:T(4,128)S(1)} %get-tuple-element.18.sums), channel_id=1, source_target_pairs={{0,1},{1,0},{2,3},{3,2},{4,5},{5,4},{6,7},{7,6},{8,9},{9,8},{10,11... | collective-permute-start | bytes 6152 | tf_op jit(solution)/shard_map/ppermute | solution.py:209
  23.9 1.0 %collective-permute-done.2.partner_sums = f32[4,128]{1,0:T(4,128)S(1)} collective-permute-done((f32[4,128]{1,0:T(4,128)S(1)}, f32[4,128]{1,0:T(4,128)S(1)}, u32[]{:S(2)}, u32[]{:S(2)}) %collective-permute-start.2) | collective-permute-done | bytes 2080 | tf_op jit(solution)/shard_map/ppermute | solution.py:209
  24.9 0.0 collective-permute-done.1.partner_shares
  24.9 0.1 shard_map.80
  25.0 0.0 copy-start.2
  25.0 14.2 %all_to_all.11.received = bf16[16,8,1152]{2,1,0:T(8,128)(2,1)S(1)} all-to-all(bf16[16,8,1152]{2,1,0:T(8,128)(2,1)S(1)} %bitcast.9), channel_id=1, replica_groups=mesh['group'=4,'chip'=4,'core'=2] {'group','chip'}, dimensions={0} | all-to-all | bytes 589824 | tf_op jit(solution)/shard_map/all_to_all | solution.py:205
  39.1 0.0 copy-done.2
  39.2 2.2 %shard_map.81 = (f32[4,128,512]{2,1,0:T(8,128)}, f32[8,512]{1,0:T(8,128)}, f32[1,8]{1,0:T(1,128)}) custom-call(s32[4,1]{1,0:T(4,128)S(1)} %copy.11.ids, bf16[16,8,1152]{2,1,0:T(8,128)(2,1)S(1)} %all_to_all.11.received, f32[128,128]{1,0:T(8,128)S(1)} %get-tuple-element.20.own_expo, f32[128,128]{1,0:T(8,128)S(1)} %get-tuple-element.21.other_expo, ...), custom_call_target="tpu_custom_call" | custom-call | bytes 3137584 | tf_op jit(solution)/shard_map/pallas_call | solution.py:35
Async XLA Ops:
  0.6 0.7 %copy-start.3 = (s32[64]{0:T(128)S(1)}, s32[64]{0:T(128)}, u32[]{:S(2)}) copy-start(s32[64]{0:T(128)} %param.6) | copy-start | bytes 772
  1.3 0.7 %copy-start.1 = (bf16[8,512]{1,0:T(8,128)(2,1)S(1)}, bf16[8,512]{1,0:T(8,128)(2,1)}, u32[]{:S(2)}) copy-start(bf16[8,512]{1,0:T(8,128)(2,1)} %features.3) | copy-start | bytes 24580
  18.1 0.7 %copy-start.4 = (s32[4,1]{0,1:T(1,128)S(1)}, s32[4,1]{0,1:T(1,128)}, u32[]{:S(2)}) copy-start(s32[4,1]{0,1:T(1,128)} %param.8) | copy-start | bytes 52
  18.1 0.7 %copy-start.5 = (s32[4,1]{0,1:T(1,128)S(1)}, s32[4,1]{0,1:T(1,128)}, u32[]{:S(2)}) copy-start(s32[4,1]{0,1:T(1,128)} %param.9) | copy-start | bytes 52
  18.1 3.9 %collective-permute-start = (bf16[128,640]{1,0:T(8,128)(2,1)S(1)}, bf16[128,640]{1,0:T(8,128)(2,1)S(1)}, u32[]{:S(2)}, u32[]{:S(2)}) collective-permute-start(bf16[128,640]{1,0:T(8,128)(2,1)S(1)} %bitcast.6), channel_id=1, source_target_pairs={{0,1},{1,0},{2,3},{3,2},{4,5},{5,4},{6,7},{7,6},{8,9},{9,8},{10,11... | collective-permute-start | bytes 491528 | tf_op jit(solution)/shard_map/ppermute | solution.py:209
  19.0 1.0 %copy-start = (bf16[512,512]{1,0:T(8,128)(2,1)S(1)}, bf16[512,512]{1,0:T(8,128)(2,1)}, u32[]{:S(2)}) copy-start(bf16[512,512]{1,0:T(8,128)(2,1)} %param.7) | copy-start | bytes 1572868
  23.3 1.6 %collective-permute-start.1 = (bf16[128,1024]{1,0:T(8,128)(2,1)S(1)}, bf16[128,1024]{1,0:T(8,128)(2,1)S(1)}, u32[]{:S(2)}, u32[]{:S(2)}) collective-permute-start(bf16[128,1024]{1,0:T(8,128)(2,1)S(1)} %get-tuple-element.19), channel_id=1, source_target_pairs={{0,1},{1,0},{2,3},{3,2},{4,5},{5,4},{6,7},{7,6},{8,9},{9,8},{10,11... | collective-permute-start | bytes 786440 | tf_op jit(solution)/shard_map/ppermute | solution.py:209
  23.4 1.5 %collective-permute-start.2 = (f32[4,128]{1,0:T(4,128)S(1)}, f32[4,128]{1,0:T(4,128)S(1)}, u32[]{:S(2)}, u32[]{:S(2)}) collective-permute-start(f32[4,128]{1,0:T(4,128)S(1)} %get-tuple-element.18.sums), channel_id=1, source_target_pairs={{0,1},{1,0},{2,3},{3,2},{4,5},{5,4},{6,7},{7,6},{8,9},{9,8},{10,11... | collective-permute-start | bytes 6152 | tf_op jit(solution)/shard_map/ppermute | solution.py:209
  25.0 14.2 %copy-start.2 = (bf16[8,512]{1,0:T(8,128)(2,1)S(1)}, bf16[8,512]{1,0:T(8,128)(2,1)}, u32[]{:S(2)}) copy-start(bf16[8,512]{1,0:T(8,128)(2,1)} %features.3) | copy-start | bytes 24580

commit v8 on v7

--- a/solution.py
+++ b/solution.py
@@ -15,6 +15,7 @@
 
 VMEM = pl.BlockSpec(memory_space=pltpu.VMEM)
 SMEM = pl.BlockSpec(memory_space=pltpu.SMEM)
+HBM = pl.BlockSpec(memory_space=pltpu.HBM)
 
 
 def inverse_norm(rows):
@@ -30,13 +31,14 @@
     return lax.broadcasted_iota(jnp.int32, (rows, 128), 1)
 
 
-def run(kernel, out_shape, in_specs, *operands):
+def run(kernel, out_shape, in_specs, *operands, out_spec=VMEM, scratch=()):
     shapes = jax.tree.leaves(out_shape)
     return pl.pallas_call(
         kernel,
         out_shape=out_shape,
         in_specs=in_specs,
-        out_specs=jax.tree.map(lambda _: VMEM, out_shape),
+        out_specs=jax.tree.map(lambda _: out_spec, out_shape),
+        scratch_shapes=scratch,
         compiler_params=pltpu.CompilerParams(vmem_limit_bytes=48 * 1024 * 1024),
         cost_estimate=pl.CostEstimate(
             flops=0,
@@ -46,17 +48,47 @@
     )(*operands)
 
 
-def pack_units(features, labels, copies_out):
+def load(
+    features,
+    labels,
+    centres,
+    ids,
+    listed,
+    copies_out,
+    centres_out,
+    ids_out,
+    listed_out,
+    held_features,
+    held_labels,
+    arrived,
+):
+    moves = [
+        pltpu.make_async_copy(source, target, arrived.at[i])
+        for i, (source, target) in enumerate(
+            (
+                (features, held_features),
+                (labels, held_labels),
+                (centres, centres_out),
+                (ids, ids_out),
+                (listed, listed_out),
+            )
+        )
+    ]
+    for move in moves:
+        move.start()
+    moves[0].wait()
+    moves[1].wait()
     chip = lax.axis_index("chip")
     member = 2 * chip + lax.axis_index("core")
     copies, tok_dev, _ = copies_out.shape
     width = features.shape[1]
-    rows = features[...].astype(jnp.float32)
+    rows = held_features[...].astype(jnp.float32)
     unit = (rows * inverse_norm(rows)).astype(jnp.bfloat16)
     copies_out[:, :, :width] = jnp.broadcast_to(unit[None], (copies, tok_dev, width))
 
     place = (lax.axis_index("group") * lax.axis_size("chip") + chip) * tok_dev
-    row = jnp.concatenate([labels[...], jnp.zeros((1, 128 - labels.shape[1]), jnp.int32)], axis=1)
+    row = held_labels[...]
+    row = jnp.concatenate([row, jnp.zeros((1, 128 - row.shape[1]), jnp.int32)], axis=1)
     row = jnp.broadcast_to(row, (tok_dev, 128))
     row = pltpu.roll(row, lax.rem(place - member * tok_dev + 128, 128), 1)
     digit = lax.broadcasted_iota(jnp.int32, (tok_dev, 128), 0)
@@ -66,25 +98,23 @@
     copies_out[:, :, width:] = jnp.broadcast_to(
         digits.astype(jnp.float32).astype(jnp.bfloat16)[None], (copies, tok_dev, 128)
     )
-
-
-def prepare(ids, centres, cand_out, unit_out, inverse_out):
-    for g in range(ids.shape[0]):
-        here = pl.ds(g * BLK, BLK)
-        rows = centres[ids[g, 0]].astype(jnp.float32)
-        inverse = inverse_norm(rows)
-        unit = rows * inverse
-        cand_out[here, :] = unit.astype(jnp.bfloat16)
-        unit_out[here, :] = unit
-        inverse_out[here, :] = jnp.broadcast_to(inverse, (BLK, 128))
-
-
-def forward(listed, packed, cands, expo_out, sums_out, shares_out):
+    for move in moves[2:]:
+        move.wait()
+
+
+def select(parts, rows):
+    owner = lanes(1) // (128 // len(parts))
+    out = jnp.broadcast_to(parts[0], (rows, 128))
+    for g in range(1, len(parts)):
+        out = jnp.where(owner == g, parts[g], out)
+    return out
+
+
+def forward(ids, listed, packed, centres, inverse, expo_out, sums_out, shares_out):
     group = lax.axis_index("group")
     member = 2 * lax.axis_index("chip") + lax.axis_index("core")
-    groups = listed.shape[0]
-    width = cands.shape[1]
-    tok_dev = packed.shape[0] * groups // 128
+    groups = ids.shape[1]
+    width = centres.shape[2]
     per_group = 128 // groups
     units = packed[:, :width]
     digits = jnp.sum(
@@ -94,33 +124,36 @@
     first = (member * groups + group) * BLK
     onehot = lax.broadcasted_iota(jnp.int32, (BLK, 128), 0) == labels - first
 
-    all_cosines = contract(cands[...], units, 1, 1)
-    owner = lanes(1) // per_group
-    cosine = jnp.zeros((BLK, 128), jnp.float32)
-    active = jnp.zeros((1, 128), jnp.float32)
-    for g in range(groups):
-        cosine = jnp.where(owner == g, all_cosines[g * BLK : (g + 1) * BLK], cosine)
-        active = jnp.where(owner == g, listed[g, 0].astype(jnp.float32), active)
+    blocks = [centres[ids[0, g]] for g in range(groups)]
+    cosine = select([contract(block, units, 1, 1) for block in blocks], BLK) * inverse
+    active = select([listed[0, g].astype(jnp.float32) for g in range(groups)], 1)
     expo = jnp.exp(logit_scale * (cosine - jnp.where(onehot, cos_margin, 0.0))) * active
     others = jnp.where(onehot, 0.0, expo)
     expo_out[...] = jnp.where(onehot, -1.0, expo)
     sums_out[0:1, :] = jnp.sum(others, axis=0, keepdims=True)
     sums_out[1:2, :] = jnp.sum(jnp.where(onehot, expo, 0.0), axis=0, keepdims=True)
 
-    others = others.T.astype(jnp.bfloat16)
+    others = (others * inverse).T.astype(jnp.bfloat16)
     label = jnp.where(onehot, 1.0, 0.0).T.astype(jnp.bfloat16)
     for g in range(groups):
         here = slice(g * per_group, (g + 1) * per_group)
-        cand = cands[g * BLK : (g + 1) * BLK, :]
-        both = contract(jnp.concatenate([others[here], label[here]], axis=0), cand, 1, 0)
+        both = contract(jnp.concatenate([others[here], label[here]], axis=0), blocks[g], 1, 0)
         both = both.astype(jnp.bfloat16)
         shares_out[here, :width] = both[:per_group]
         shares_out[here, width:] = both[per_group:]
 
 
-def forward_other(own_sums, *refs):
-    *ins, expo_out, sums_out, shares_out = refs
-    forward(*ins, expo_out, sums_out.at[2:4], shares_out)
+def forward_own(ids, listed, packed, centres, inverse_out, *outs):
+    inverse = []
+    for g in range(ids.shape[1]):
+        inverse.append(inverse_norm(centres[ids[0, g]].astype(jnp.float32)))
+    inverse = select(inverse, BLK)
+    inverse_out[...] = inverse
+    forward(ids, listed, packed, centres, inverse, *outs)
+
+
+def forward_other(ids, listed, packed, centres, inverse, own_sums, expo_out, sums_out, shares_out):
+    forward(ids, listed, packed, centres, inverse[...], expo_out, sums_out.at[2:4], shares_out)
     sums_out[0:2, :] = own_sums[...]
 
 
@@ -144,15 +177,31 @@
     own_packed,
     other_packed,
     features,
-    cand_unit,
-    cand_inverse,
+    centres,
+    inverse,
     grad_out,
     feature_out,
     loss_out,
+    grad,
+    feature_grad,
+    loss_row,
+    left,
 ):
-    groups = ids.shape[0]
+    groups = ids.shape[1]
+    held = centres.shape[0]
     per_group = 128 // groups
     tok_dev, width = features.shape
+
+    def leave(block):
+        return pltpu.make_async_copy(grad.at[block], grad_out.at[block], left.at[block])
+
+    grad[...] = jnp.zeros_like(grad)
+    for block in range(held):
+        named = ids[0, 0] == block
+        for g in range(1, groups):
+            named = named | (ids[0, g] == block)
+        pl.when(jnp.logical_not(named))(leave(block).start)
+
     sums = received[0].astype(jnp.float32)
     for i in range(1, received.shape[0]):
         sums = sums + received[i].astype(jnp.float32)
@@ -170,19 +219,22 @@
     other = jnp.where(other < 0.0, -other_rest, other) * other_scale
     weights = jnp.concatenate([own, other], axis=1)
     owner = jnp.concatenate([lanes(1), lanes(1)], axis=1) // per_group
-    grad_out[...] = jnp.zeros_like(grad_out)
     for g in range(groups):
-        here = slice(g * BLK, (g + 1) * BLK)
+        block = ids[0, g]
         mine = jnp.where(owner == g, weights, 0.0).astype(jnp.bfloat16)
         slot_grad = contract(mine, units, 1, 0)
-        unit = cand_unit[here, :]
+        factor = inverse[:, g * per_group : g * per_group + 1]
+        unit = centres[block].astype(jnp.float32) * factor
         along = jnp.sum(slot_grad * unit, axis=1, keepdims=True)
-        cand_grad = cand_inverse[here, :1] * (slot_grad - along * unit)
-        grad_out[ids[g, 0]] += cand_grad.astype(jnp.bfloat16).astype(jnp.float32)
+        cand_grad = factor * (slot_grad - along * unit)
+        grad[block] += cand_grad.astype(jnp.bfloat16).astype(jnp.float32)
+        last = jnp.bool_(True)
+        for later in range(g + 1, groups):
+            last = last & (ids[0, later] != block)
+        pl.when(last)(leave(block).start)
 
     chip = lax.axis_index("group") * lax.axis_size("chip") + lax.axis_index("chip")
-    place = chip * tok_dev
-    sample = lax.broadcasted_iota(jnp.int32, (tok_dev, 128), 0) + place
+    sample = lax.broadcasted_iota(jnp.int32, (tok_dev, 128), 0) + chip * tok_dev
     mine = lanes(tok_dev) == sample
     rest = jnp.sum(jnp.where(mine, own_rest, 0.0), axis=1, keepdims=True)
     label = jnp.sum(jnp.where(mine, own_label, 0.0), axis=1, keepdims=True)
@@ -192,13 +244,25 @@
     diagonal = lax.broadcasted_iota(jnp.int32, square, 0) == lax.broadcasted_iota(
         jnp.int32, square, 1
     )
-    loss_out[...] = jnp.sum(jnp.where(diagonal, loss, 0.0), axis=0, keepdims=True)
+    loss_row[...] = jnp.sum(jnp.where(diagonal, loss, 0.0), axis=0, keepdims=True)
     rows = features[...].astype(jnp.float32)
     inv_norm = inverse_norm(rows)
     unit = rows * inv_norm
-    unit_grad = logit_scale / total * (sums[:, :width] - rest * sums[:, width : 2 * width])
+    cand = sums[:, width : 2 * width]
+    cand = (cand * inverse_norm(cand)).astype(jnp.bfloat16).astype(jnp.float32)
+    unit_grad = logit_scale / total * (sums[:, :width] - rest * cand)
     along = jnp.sum(unit_grad * unit, axis=1, keepdims=True)
-    feature_out[...] = inv_norm * (unit_grad - along * unit)
+    feature_grad[...] = inv_norm * (unit_grad - along * unit)
+    ends = [
+        pltpu.make_async_copy(feature_grad, feature_out, left.at[held]),
+        pltpu.make_async_copy(loss_row, loss_out, left.at[held + 1]),
+    ]
+    for move in ends:
+        move.start()
+    for block in range(held):
+        leave(block).wait()
+    for move in ends:
+        move.wait()
 
 
 def exchange(pieces, axes):
@@ -218,42 +282,57 @@
     bf16, f32 = jnp.bfloat16, jnp.float32
     shape = jax.ShapeDtypeStruct
 
-    copies = run(
-        pack_units,
-        shape((chips, tok_dev, width + 128), bf16),
-        [VMEM, VMEM],
-        features,
-        labels.reshape(1, -1),
+    copies, blocks, ids, flags = run(
+        load,
+        (
+            shape((chips, tok_dev, width + 128), bf16),
+            shape((held, BLK, width), bf16),
+            shape((1, groups), block_ids.dtype),
+            shape((1, groups), listed.dtype),
+        ),
+        [HBM] * 5,
+        *(
+            pltpu.with_memory_space_constraint(array, pltpu.HBM)
+            for array in (
+                features,
+                labels.reshape(1, -1),
+                centres.reshape(held, BLK, width),
+                block_ids.reshape(1, groups),
+                listed.reshape(1, groups),
+            )
+        ),
+        scratch=[
+            pltpu.VMEM(features.shape, features.dtype),
+            pltpu.VMEM((1, labels.shape[0]), labels.dtype),
+            pltpu.SemaphoreType.DMA((5,)),
+        ],
     )
     own_packed = exchange(copies, CHIPS).reshape(half, width + 128)
     other_packed = with_partner(own_packed)
-    cands, cand_unit, cand_inverse = run(
-        prepare,
+    inverse, own_expo, own_sums, shares = run(
+        forward_own,
         (
-            shape((groups * BLK, width), bf16),
-            shape((groups * BLK, width), f32),
-            shape((groups * BLK, 128), f32),
+            shape((BLK, 128), f32),
+            shape((BLK, half), f32),
+            shape((2, half), f32),
+            shape((half, 2 * width), bf16),
         ),
-        [SMEM, VMEM],
-        block_ids,
-        centres.reshape(held, BLK, width),
-    )
-    own_expo, own_sums, shares = run(
-        forward,
-        (shape((BLK, half), f32), shape((2, half), f32), shape((half, 2 * width), bf16)),
-        [SMEM, VMEM, VMEM],
-        listed,
+        [SMEM, SMEM, VMEM, VMEM],
+        ids,
+        flags,
         own_packed,
-        cands,
+        blocks,
     )
     other_expo, sums, other_shares = run(
         forward_other,
         (shape((BLK, half), f32), shape((4, half), f32), shape((half, 2 * width), bf16)),
-        [VMEM, SMEM, VMEM, VMEM],
+        [SMEM, SMEM, VMEM, VMEM, VMEM, VMEM],
+        ids,
+        flags,
+        other_packed,
+        blocks,
+        inverse,
         own_sums,
-        listed,
-        other_packed,
-        cands,
     )
     sent = run(
         merge,
@@ -265,19 +344,25 @@
         with_partner(sums),
     )
     received = exchange(sent.reshape(chips, tok_dev, 2 * width + 128), CHIPS)
+    outs = (shape((held, BLK, width), f32), shape((tok_dev, width), f32), shape((1, tok_dev), f32))
     centre_grad, feature_grad, loss = run(
         backward,
-        (shape((held, BLK, width), f32), shape((tok_dev, width), f32), shape((1, tok_dev), f32)),
+        outs,
         [SMEM] + [VMEM] * 8,
-        block_ids,
+        ids,
         received,
         own_expo,
         other_expo,
         own_packed,
         other_packed,
         features,
-        cand_unit,
-        cand_inverse,
+        blocks,
+        inverse,
+        out_spec=HBM,
+        scratch=[
+            *(pltpu.VMEM(out.shape, out.dtype) for out in outs),
+            pltpu.SemaphoreType.DMA((held + 2,)),
+        ],
     )
     return (loss.reshape(tok_dev), feature_grad, centre_grad.reshape(held * BLK, width))
 

time: 41.6 us -> 38.5 us (0.925)
  local copies, waits for them, and re-layouts: 3.23 us -> 0.01 us
    unnamed x14 -> x2, local copies, waits for them, and re-layouts: 3.23 us -> 0.01 us
    pallas_call x6 -> x5, Pallas kernels: 5.57 us -> 5.39 us  [run(): pl.pallas_call(kernel, out_shape=out_shape, in_specs=in_specs, out_specs=...]
  transfers between devices with their start and end apart: 3 -> 3, of which waited for: 1 -> 2; matrix products, arithmetic and copies ran while one was open for 0% -> 0% of each run, Pallas kernels for 5% -> 3%
where the time goes in v8:
time: 38.5 us; the launch traced here: 38.3 us
  blocking collectives  30.3 us (79%)
  Pallas kernels  5.39 us (14%)
  waiting for transfers between devices  1.3 us (3%)
  between operations  0.67 us (2%)
  starting transfers between devices  0.58 us (2%)
    all_to_all x2, blocking collectives, exchange(): return lax.all_to_all(pieces, axes, split_axis=0, concat_axis=0, tiled=True)  30.3 us
    pallas_call x5, Pallas kernels, run(): pl.pallas_call(kernel, out_shape=out_shape, in_specs=in_specs, out_specs=...  5.39 us
    ppermute x3, waiting for transfers between devices, with_partner(): return lax.ppermute(value, 'core', [(0, 1), (1, 0)])  1.3 us
  transfers between devices with their start and end apart: 3, of which 2 were waited for; matrix products, arithmetic and copies ran while one was open for 0% of the time, Pallas kernels for 3%

profile of v8, /device:TPU:0, one launch (start us, length us, event | category | flops | bytes accessed | tf_op | source)
XLA Modules:
  0.0 38.3 jit_solution(13007598062070507431)
XLA Ops:
  0.6 1.1 %shard_map.76 = (bf16[16,8,640]{2,1,0:T(8,128)(2,1)S(1)}, bf16[4,128,512]{2,1,0:T(8,128)(2,1)S(1)}, s32[1,4]{1,0:T(1,128)S(1)}, s32[1,4]{1,0:T(1,128)S(1)}) custom-call(bf16[8,512]{1,0:T(8,128)(2,1)} %features.3, s32[1,64]{1,0:T(1,128)} %bitcast.13, bf16[4,128,512]{2,1,0:T(8,128)(2,1)} %bitcast.12, s32[1,4]{1,0:T(1,128)} %bitcast.14, s32[1,4]{1,0:T(1,128)} %bitcast.15), custom_call_target="tpu_custom_call" | custom-call | bytes 1220928 | tf_op jit(solution)/shard_map/pallas_call | solution.py:36
  1.8 16.0 %all_to_all.10 = bf16[16,8,640]{2,1,0:T(8,128)(2,1)S(1)} all-to-all(bf16[16,8,640]{2,1,0:T(8,128)(2,1)S(1)} %get-tuple-element.19), channel_id=1, replica_groups=mesh['group'=4,'chip'=4,'core'=2] {'group','chip'}, dimensions={0} | all-to-all | bytes 327680 | tf_op jit(solution)/shard_map/all_to_all | solution.py:269
  17.8 0.0 collective-permute-start
  17.8 1.1 %shard_map.77 = (f32[128,128]{1,0:T(8,128)S(1)}, f32[128,128]{1,0:T(8,128)S(1)}, f32[2,128]{1,0:T(2,128)S(1)}, bf16[128,1024]{1,0:T(8,128)(2,1)S(1)}) custom-call(s32[1,4]{1,0:T(1,128)S(1)} %get-tuple-element.17.ids, s32[1,4]{1,0:T(1,128)S(1)} %get-tuple-element.18.listed, bf16[128,640]{1,0:T(8,128)(2,1)S(1)} %bitcast.9, ...), custom_call_target="tpu_custom_call" | custom-call | bytes 1082400 | tf_op jit(solution)/shard_map/pallas_call | solution.py:36
  18.9 0.3 collective-permute-done.packed.other_packed
  19.2 1.1 %shard_map.78 = (f32[128,128]{1,0:T(8,128)S(1)}, f32[4,128]{1,0:T(4,128)S(1)}, bf16[128,1024]{1,0:T(8,128)(2,1)S(1)}) custom-call(s32[1,4]{1,0:T(1,128)S(1)} %get-tuple-element.17.ids, s32[1,4]{1,0:T(1,128)S(1)} %get-tuple-element.18.listed, bf16[128,640]{1,0:T(8,128)(2,1)S(1)} %collective-permute-done.packed.other_packed, ...), custom_call_target="tpu_custom_call" | custom-call | bytes 1084448 | tf_op jit(solution)/shard_map/pallas_call | solution.py:36
  20.3 0.3 collective-permute-start.1
  20.6 0.3 collective-permute-start.2
  20.9 1.0 %collective-permute-done.2.partner_sums = f32[4,128]{1,0:T(4,128)S(1)} collective-permute-done((f32[4,128]{1,0:T(4,128)S(1)}, f32[4,128]{1,0:T(4,128)S(1)}, u32[]{:S(2)}, u32[]{:S(2)}) %collective-permute-start.2) | collective-permute-done | bytes 2080 | tf_op jit(solution)/shard_map/ppermute | solution.py:273
  21.9 0.0 collective-permute-done.1.partner_shares
  21.9 0.1 shard_map.79
  22.0 0.0 copy-start
  22.0 14.3 %all_to_all.11.received = bf16[16,8,1152]{2,1,0:T(8,128)(2,1)S(1)} all-to-all(bf16[16,8,1152]{2,1,0:T(8,128)(2,1)S(1)} %bitcast.11), channel_id=1, replica_groups=mesh['group'=4,'chip'=4,'core'=2] {'group','chip'}, dimensions={0} | all-to-all | bytes 589824 | tf_op jit(solution)/shard_map/all_to_all | solution.py:269
  36.3 0.0 copy-done
  36.3 2.0 %shard_map.80 = (f32[4,128,512]{2,1,0:T(8,128)}, f32[8,512]{1,0:T(8,128)}, f32[1,8]{1,0:T(1,128)}) custom-call(s32[1,4]{1,0:T(1,128)S(1)} %get-tuple-element.17.ids, bf16[16,8,1152]{2,1,0:T(8,128)(2,1)S(1)} %all_to_all.11.received, f32[128,128]{1,0:T(8,128)S(1)} %get-tuple-element.26.own_expo, f32[128,128]{1,0:T(8,128)S(1)} %get-tuple-element.27.other_expo, ...), custom_call_target="tpu_custom_call" | custom-call | bytes 2416688 | tf_op jit(solution)/shard_map/pallas_call | solution.py:36
Async XLA Ops:
  17.8 1.4 %collective-permute-start = (bf16[128,640]{1,0:T(8,128)(2,1)S(1)}, bf16[128,640]{1,0:T(8,128)(2,1)S(1)}, u32[]{:S(2)}, u32[]{:S(2)}) collective-permute-start(bf16[128,640]{1,0:T(8,128)(2,1)S(1)} %bitcast.8), channel_id=1, source_target_pairs={{0,1},{1,0},{2,3},{3,2},{4,5},{5,4},{6,7},{7,6},{8,9},{9,8},{10,11... | collective-permute-start | bytes 491528 | tf_op jit(solution)/shard_map/ppermute | solution.py:273
  20.3 1.6 %collective-permute-start.1 = (bf16[128,1024]{1,0:T(8,128)(2,1)S(1)}, bf16[128,1024]{1,0:T(8,128)(2,1)S(1)}, u32[]{:S(2)}, u32[]{:S(2)}) collective-permute-start(bf16[128,1024]{1,0:T(8,128)(2,1)S(1)} %get-tuple-element.25), channel_id=1, source_target_pairs={{0,1},{1,0},{2,3},{3,2},{4,5},{5,4},{6,7},{7,6},{8,9},{9,8},{10,11... | collective-permute-start | bytes 786440 | tf_op jit(solution)/shard_map/ppermute | solution.py:273
  20.6 1.3 %collective-permute-start.2 = (f32[4,128]{1,0:T(4,128)S(1)}, f32[4,128]{1,0:T(4,128)S(1)}, u32[]{:S(2)}, u32[]{:S(2)}) collective-permute-start(f32[4,128]{1,0:T(4,128)S(1)} %get-tuple-element.24.sums), channel_id=1, source_target_pairs={{0,1},{1,0},{2,3},{3,2},{4,5},{5,4},{6,7},{7,6},{8,9},{9,8},{10,11... | collective-permute-start | bytes 6152 | tf_op jit(solution)/shard_map/ppermute | solution.py:273
  22.0 14.3 %copy-start = (bf16[8,512]{1,0:T(8,128)(2,1)S(1)}, bf16[8,512]{1,0:T(8,128)(2,1)}, u32[]{:S(2)}) copy-start(bf16[8,512]{1,0:T(8,128)(2,1)} %features.3) | copy-start | bytes 24580

commit v9 on v8

--- a/solution.py
+++ b/solution.py
@@ -12,6 +12,7 @@
 logit_scale = 32.0
 cos_margin = 0.35
 norm_epsilon = 1e-06
+UNLISTED = 1e19
 
 VMEM = pl.BlockSpec(memory_space=pltpu.VMEM)
 SMEM = pl.BlockSpec(memory_space=pltpu.SMEM)
@@ -55,11 +56,13 @@
     ids,
     listed,
     copies_out,
-    centres_out,
+    blocks_out,
     ids_out,
-    listed_out,
     held_features,
     held_labels,
+    held_centres,
+    held_ids,
+    held_listed,
     arrived,
 ):
     moves = [
@@ -68,9 +71,10 @@
             (
                 (features, held_features),
                 (labels, held_labels),
-                (centres, centres_out),
+                (ids, held_ids),
+                (listed, held_listed),
                 (ids, ids_out),
-                (listed, listed_out),
+                (centres, held_centres),
             )
         )
     ]
@@ -100,6 +104,9 @@
     )
     for move in moves[2:]:
         move.wait()
+    for g in range(blocks_out.shape[0]):
+        block = held_centres[held_ids[0, g]]
+        blocks_out[g] = jnp.where(held_listed[0, g] > 0, block, jnp.full_like(block, UNLISTED))
 
 
 def select(parts, rows):
@@ -110,63 +117,61 @@
     return out
 
 
-def forward(ids, listed, packed, centres, inverse, expo_out, sums_out, shares_out):
-    group = lax.axis_index("group")
-    member = 2 * lax.axis_index("chip") + lax.axis_index("core")
-    groups = ids.shape[1]
-    width = centres.shape[2]
-    per_group = 128 // groups
+def exponentials(packed, own_blocks, pair_blocks, expo_out, pair_expo_out, inverse_out, sums_out):
+    group, core = lax.axis_index("group"), lax.axis_index("core")
+    groups, _, width = own_blocks.shape
     units = packed[:, :width]
     digits = jnp.sum(
         packed[:, width:].astype(jnp.float32).reshape(128 // 8, 8, 128), axis=0
     ).astype(jnp.int32)
     labels = digits[0:1] + (digits[1:2] << 7) + (digits[2:3] << 14)
-    first = (member * groups + group) * BLK
-    onehot = lax.broadcasted_iota(jnp.int32, (BLK, 128), 0) == labels - first
-
-    blocks = [centres[ids[0, g]] for g in range(groups)]
-    cosine = select([contract(block, units, 1, 1) for block in blocks], BLK) * inverse
-    active = select([listed[0, g].astype(jnp.float32) for g in range(groups)], 1)
-    expo = jnp.exp(logit_scale * (cosine - jnp.where(onehot, cos_margin, 0.0))) * active
-    others = jnp.where(onehot, 0.0, expo)
-    expo_out[...] = jnp.where(onehot, -1.0, expo)
-    sums_out[0:1, :] = jnp.sum(others, axis=0, keepdims=True)
-    sums_out[1:2, :] = jnp.sum(jnp.where(onehot, expo, 0.0), axis=0, keepdims=True)
-
-    others = (others * inverse).T.astype(jnp.bfloat16)
-    label = jnp.where(onehot, 1.0, 0.0).T.astype(jnp.bfloat16)
+    rest = jnp.zeros((1, 128), jnp.float32)
+    at_label = jnp.zeros((1, 128), jnp.float32)
+    for k, (blocks, out) in enumerate(((own_blocks, expo_out), (pair_blocks, pair_expo_out))):
+        member = 2 * lax.axis_index("chip") + (core if k == 0 else 1 - core)
+        first = (member * groups + group) * BLK
+        onehot = lax.broadcasted_iota(jnp.int32, (BLK, 128), 0) == labels - first
+        inverse = select(
+            [inverse_norm(blocks[g].astype(jnp.float32)) for g in range(groups)], BLK
+        )
+        inverse_out[k] = inverse
+        cosine = inverse * select([contract(blocks[g], units, 1, 1) for g in range(groups)], BLK)
+        expo = jnp.exp(logit_scale * (cosine - jnp.where(onehot, cos_margin, 0.0)))
+        expo = jnp.where(inverse > 0.0, expo, 0.0)
+        out[...] = jnp.where(onehot, -1.0, expo)
+        rest += jnp.sum(jnp.where(onehot, 0.0, expo), axis=0, keepdims=True)
+        at_label += jnp.sum(jnp.where(onehot, expo, 0.0), axis=0, keepdims=True)
+    sums_out[0:1, :] = rest
+    sums_out[1:2, :] = at_label
+
+
+def shares(own_expo, pair_expo, inverse, own_blocks, pair_blocks, shares_out):
+    groups, _, width = own_blocks.shape
+    per_group = 128 // groups
+    others, label = [], []
+    for k, expo in enumerate((own_expo[...], pair_expo[...])):
+        others.append((jnp.maximum(expo, 0.0) * inverse[k]).T.astype(jnp.bfloat16))
+        label.append(jnp.where(expo < 0.0, 1.0, 0.0).T.astype(jnp.bfloat16))
+    others = jnp.concatenate(others, axis=1)
+    label = jnp.concatenate(label, axis=1)
     for g in range(groups):
         here = slice(g * per_group, (g + 1) * per_group)
-        both = contract(jnp.concatenate([others[here], label[here]], axis=0), blocks[g], 1, 0)
+        blocks = jnp.concatenate([own_blocks[g], pair_blocks[g]], axis=0)
+        both = contract(jnp.concatenate([others[here], label[here]], axis=0), blocks, 1, 0)
         both = both.astype(jnp.bfloat16)
         shares_out[here, :width] = both[:per_group]
         shares_out[here, width:] = both[per_group:]
 
 
-def forward_own(ids, listed, packed, centres, inverse_out, *outs):
-    inverse = []
-    for g in range(ids.shape[1]):
-        inverse.append(inverse_norm(centres[ids[0, g]].astype(jnp.float32)))
-    inverse = select(inverse, BLK)
-    inverse_out[...] = inverse
-    forward(ids, listed, packed, centres, inverse, *outs)
-
-
-def forward_other(ids, listed, packed, centres, inverse, own_sums, expo_out, sums_out, shares_out):
-    forward(ids, listed, packed, centres, inverse[...], expo_out, sums_out.at[2:4], shares_out)
-    sums_out[0:2, :] = own_sums[...]
-
-
-def merge(shares, sums, partner_shares, partner_sums, sent_out):
-    wide = shares.shape[1]
-    both = shares[...].astype(jnp.float32) + partner_shares[...].astype(jnp.float32)
-    sent_out[:, :wide] = both.astype(jnp.bfloat16)
-    total = sums[...] + jnp.concatenate([partner_sums[2:4, :], partner_sums[0:2, :]], axis=0)
+def with_sums(shares, own_sums, other_sums, sent_out):
+    rows, wide = shares.shape
+    sent_out[:, :wide] = shares[...]
+    total = jnp.concatenate([own_sums[...], other_sums[...]], axis=0)
     high = total.astype(jnp.bfloat16)
     low = (total - high.astype(jnp.float32)).astype(jnp.bfloat16)
     tile = jnp.concatenate([high.astype(jnp.float32), low.astype(jnp.float32)], axis=0)
-    tile = jnp.broadcast_to(tile[None], (shares.shape[0] // 8, 8, 128))
-    sent_out[:, wide:] = tile.reshape(shares.shape[0], 128).astype(jnp.bfloat16)
+    tile = jnp.broadcast_to(tile[None], (rows // 8, 8, 128))
+    sent_out[:, wide:] = tile.reshape(rows, 128).astype(jnp.bfloat16)
 
 
 def backward(
@@ -177,7 +182,7 @@
     own_packed,
     other_packed,
     features,
-    centres,
+    blocks,
     inverse,
     grad_out,
     feature_out,
@@ -188,7 +193,7 @@
     left,
 ):
     groups = ids.shape[1]
-    held = centres.shape[0]
+    held = grad.shape[0]
     per_group = 128 // groups
     tok_dev, width = features.shape
 
@@ -223,8 +228,8 @@
         block = ids[0, g]
         mine = jnp.where(owner == g, weights, 0.0).astype(jnp.bfloat16)
         slot_grad = contract(mine, units, 1, 0)
-        factor = inverse[:, g * per_group : g * per_group + 1]
-        unit = centres[block].astype(jnp.float32) * factor
+        factor = inverse[0, :, g * per_group : g * per_group + 1]
+        unit = blocks[g].astype(jnp.float32) * factor
         along = jnp.sum(slot_grad * unit, axis=1, keepdims=True)
         cand_grad = factor * (slot_grad - along * unit)
         grad[block] += cand_grad.astype(jnp.bfloat16).astype(jnp.float32)
@@ -282,13 +287,12 @@
     bf16, f32 = jnp.bfloat16, jnp.float32
     shape = jax.ShapeDtypeStruct
 
-    copies, blocks, ids, flags = run(
+    copies, own_blocks, ids = run(
         load,
         (
             shape((chips, tok_dev, width + 128), bf16),
-            shape((held, BLK, width), bf16),
+            shape((groups, BLK, width), bf16),
             shape((1, groups), block_ids.dtype),
-            shape((1, groups), listed.dtype),
         ),
         [HBM] * 5,
         *(
@@ -304,44 +308,42 @@
         scratch=[
             pltpu.VMEM(features.shape, features.dtype),
             pltpu.VMEM((1, labels.shape[0]), labels.dtype),
-            pltpu.SemaphoreType.DMA((5,)),
+            pltpu.VMEM((held, BLK, width), centres.dtype),
+            pltpu.SMEM((1, groups), block_ids.dtype),
+            pltpu.SMEM((1, groups), listed.dtype),
+            pltpu.SemaphoreType.DMA((6,)),
         ],
     )
+    pair_blocks = with_partner(own_blocks)
     own_packed = exchange(copies, CHIPS).reshape(half, width + 128)
     other_packed = with_partner(own_packed)
-    inverse, own_expo, own_sums, shares = run(
-        forward_own,
+    own_expo, pair_expo, inverse, sums = run(
+        exponentials,
         (
-            shape((BLK, 128), f32),
             shape((BLK, half), f32),
+            shape((BLK, half), f32),
+            shape((2, BLK, 128), f32),
             shape((2, half), f32),
-            shape((half, 2 * width), bf16),
         ),
-        [SMEM, SMEM, VMEM, VMEM],
-        ids,
-        flags,
+        [VMEM] * 3,
         own_packed,
-        blocks,
-    )
-    other_expo, sums, other_shares = run(
-        forward_other,
-        (shape((BLK, half), f32), shape((4, half), f32), shape((half, 2 * width), bf16)),
-        [SMEM, SMEM, VMEM, VMEM, VMEM, VMEM],
-        ids,
-        flags,
-        other_packed,
-        blocks,
+        own_blocks,
+        pair_blocks,
+    )
+    other_expo = with_partner(pair_expo)
+    other_sums = with_partner(sums)
+    going = run(
+        shares,
+        shape((half, 2 * width), bf16),
+        [VMEM] * 5,
+        own_expo,
+        pair_expo,
         inverse,
-        own_sums,
+        own_blocks,
+        pair_blocks,
     )
     sent = run(
-        merge,
-        shape((half, 2 * width + 128), bf16),
-        [VMEM] * 4,
-        shares,
-        sums,
-        with_partner(other_shares),
-        with_partner(sums),
+        with_sums, shape((half, 2 * width + 128), bf16), [VMEM] * 3, going, sums, other_sums
     )
     received = exchange(sent.reshape(chips, tok_dev, 2 * width + 128), CHIPS)
     outs = (shape((held, BLK, width), f32), shape((tok_dev, width), f32), shape((1, tok_dev), f32))
@@ -356,7 +358,7 @@
         own_packed,
         other_packed,
         features,
-        blocks,
+        own_blocks,
         inverse,
         out_spec=HBM,
         scratch=[

time: 38.5 us -> 38.2 us (level)
  blocking collectives: 30.3 us -> 16.2 us
  waiting for transfers between devices: 1.3 us -> 11.5 us
  starting transfers between devices: 0.58 us -> 4.83 us
  Pallas kernels: 5.39 us -> 4.71 us
    all_to_all x2 -> x1, blocking collectives: 30.3 us -> 16.2 us  [exchange(): return lax.all_to_all(pieces, axes, split_axis=0, concat_axis=0, tiled=True)]
    all_to_all x0 -> x1, waiting for transfers between devices: none -> 9.71 us  [exchange(): return lax.all_to_all(pieces, axes, split_axis=0, concat_axis=0, tiled=True)]
    all_to_all x0 -> x1, starting transfers between devices: none -> 3.67 us  [exchange(): return lax.all_to_all(pieces, axes, split_axis=0, concat_axis=0, tiled=True)]
    pallas_call x5, Pallas kernels: 5.39 us -> 4.71 us  [run(): pl.pallas_call(kernel, out_shape=out_shape, in_specs=in_specs, out_specs=...]
    ppermute x3 -> x4, starting transfers between devices: 0.58 us -> 1.16 us  [with_partner(): return lax.ppermute(value, 'core', [(0, 1), (1, 0)])]
    ppermute x3 -> x4, waiting for transfers between devices: 1.3 us -> 1.76 us  [with_partner(): return lax.ppermute(value, 'core', [(0, 1), (1, 0)])]
  transfers between devices with their start and end apart: 3 -> 5, of which waited for: 2 -> 4; matrix products, arithmetic and copies ran while one was open for 0% -> 0% of each run, Pallas kernels for 3% -> 1%
where the time goes in v9:
time: 38.2 us; the launch traced here: 37.8 us
  blocking collectives  16.2 us (42%)
  waiting for transfers between devices  11.5 us (30%)
  starting transfers between devices  4.83 us (13%)
  Pallas kernels  4.71 us (12%)
  between operations  0.67 us (2%)
    all_to_all x1, blocking collectives, exchange(): return lax.all_to_all(pieces, axes, split_axis=0, concat_axis=0, tiled=True)  16.2 us
    all_to_all x1, waiting for transfers between devices, exchange(): return lax.all_to_all(pieces, axes, split_axis=0, concat_axis=0, tiled=True)  9.71 us
    pallas_call x5, Pallas kernels, run(): pl.pallas_call(kernel, out_shape=out_shape, in_specs=in_specs, out_specs=...  4.71 us
    all_to_all x1, starting transfers between devices, exchange(): return lax.all_to_all(pieces, axes, split_axis=0, concat_axis=0, tiled=True)  3.67 us
    ppermute x4, waiting for transfers between devices, with_partner(): return lax.ppermute(value, 'core', [(0, 1), (1, 0)])  1.76 us
    ppermute x4, starting transfers between devices, with_partner(): return lax.ppermute(value, 'core', [(0, 1), (1, 0)])  1.16 us
  transfers between devices with their start and end apart: 5, of which 4 were waited for; matrix products, arithmetic and copies ran while one was open for 0% of the time, Pallas kernels for 1%

profile of v9, /device:TPU:0, one launch (start us, length us, event | category | flops | bytes accessed | tf_op | source)
XLA Modules:
  0.0 37.8 jit_solution(8959612891151490280)
XLA Ops:
  0.6 1.2 %shard_map.76 = (bf16[16,8,640]{2,1,0:T(8,128)(2,1)S(1)}, bf16[4,128,512]{2,1,0:T(8,128)(2,1)S(1)}, s32[1,4]{1,0:T(1,128)S(1)}) custom-call(bf16[8,512]{1,0:T(8,128)(2,1)} %features.3, s32[1,64]{1,0:T(1,128)} %bitcast.12, bf16[4,128,512]{2,1,0:T(8,128)(2,1)} %bitcast.11, s32[1,4]{1,0:T(1,128)} %bitcast.13, s32[1,4]{1,0:T(1,128)} %bitcast.14), custom_call_target="tpu_custom_call" | custom-call | bytes 1220912 | tf_op jit(solution)/shard_map/pallas_call | solution.py:37
  1.8 0.5 %collective-permute-start = (bf16[4,128,512]{2,1,0:T(8,128)(2,1)S(1)}, bf16[4,128,512]{2,1,0:T(8,128)(2,1)S(1)}, u32[]{:S(2)}, u32[]{:S(2)}) collective-permute-start(bf16[4,128,512]{2,1,0:T(8,128)(2,1)S(1)} %get-tuple-element.15.own_blocks.blocks), channel_id=1, source_target_pairs={{0,1},{1,0},{2,3},{3,2},{4,5},{5,4},{6,7},{7,6},{8,9},{9,8},{10,11... | collective-permute-start | bytes 1572872 | tf_op jit(solution)/shard_map/ppermute | solution.py:278
  2.4 16.2 %all_to_all.10 = bf16[16,8,640]{2,1,0:T(8,128)(2,1)S(1)} all-to-all(bf16[16,8,640]{2,1,0:T(8,128)(2,1)S(1)} %get-tuple-element.14), channel_id=1, replica_groups=mesh['group'=4,'chip'=4,'core'=2] {'group','chip'}, dimensions={0} | all-to-all | bytes 327680 | tf_op jit(solution)/shard_map/all_to_all | solution.py:274
  18.5 0.0 collective-permute-done.pair_blocks
  18.5 0.5 %shard_map.77 = (f32[128,128]{1,0:T(8,128)S(1)}, f32[128,128]{1,0:T(8,128)S(1)}, f32[2,128,128]{2,1,0:T(8,128)S(1)}, f32[2,128]{1,0:T(2,128)S(1)}) custom-call(bf16[128,640]{1,0:T(8,128)(2,1)S(1)} %bitcast.8, bf16[4,128,512]{2,1,0:T(8,128)(2,1)S(1)} %get-tuple-element.15.own_blocks.blocks, bf16[4,128,512]{2,1,0:T(8,128)(2,1)S(1)} %collective-permute-done.pair_blocks), custom_call_target="tpu_custom_call" | custom-call | bytes 1475584 | tf_op jit(solution)/shard_map/pallas_call | solution.py:37
  19.0 0.1 collective-permute-start.1
  19.1 0.3 shard_map.78.shares
  19.4 0.8 %collective-permute-done.1.other_sums = f32[2,128]{1,0:T(2,128)S(1)} collective-permute-done((f32[2,128]{1,0:T(2,128)S(1)}, f32[2,128]{1,0:T(2,128)S(1)}, u32[]{:S(2)}, u32[]{:S(2)}) %collective-permute-start.1) | collective-permute-done | bytes 1056 | tf_op jit(solution)/shard_map/ppermute | solution.py:278
  20.2 0.7 %shard_map.79 = bf16[128,1152]{1,0:T(8,128)(2,1)} custom-call(bf16[128,1024]{1,0:T(8,128)(2,1)S(1)} %shard_map.78.shares, f32[2,128]{1,0:T(2,128)S(1)} %get-tuple-element.19.own_sums, f32[2,128]{1,0:T(2,128)S(1)} %collective-permute-done.1.other_sums), custom_call_target="tpu_custom_call" | custom-call | bytes 559104 | tf_op jit(solution)/shard_map/pallas_call | solution.py:37
  21.0 0.0 copy-start
  21.0 3.7 %all-to-all-start.1 = ((bf16[16,8,1152]{2,1,0:T(8,128)(2,1)}), bf16[16,8,1152]{2,1,0:T(8,128)(2,1)S(1)}, u32[]{:S(2)}, u32[]{:S(2)}) async-start(bf16[16,8,1152]{2,1,0:T(8,128)(2,1)} %bitcast.5), calls=%async_computation.1 | async-start | bytes 589824 | tf_op jit(solution)/shard_map/all_to_all | solution.py:274
  24.6 0.3 collective-permute-start.3
  24.9 0.3 collective-permute-start.2
  25.2 0.9 %collective-permute-done.3.other_packed = bf16[128,640]{1,0:T(8,128)(2,1)S(1)} collective-permute-done((bf16[128,640]{1,0:T(8,128)(2,1)S(1)}, bf16[128,640]{1,0:T(8,128)(2,1)S(1)}, u32[]{:S(2)}, u32[]{:S(2)}) %collective-permute-start.3) | collective-permute-done | bytes 163872 | tf_op jit(solution)/shard_map/ppermute | solution.py:278
  26.1 0.1 collective-permute-done.2.other_expo
  26.2 9.7 %all-to-all-done.1.received = bf16[16,8,1152]{2,1,0:T(8,128)(2,1)S(1)} async-done(((bf16[16,8,1152]{2,1,0:T(8,128)(2,1)}), bf16[16,8,1152]{2,1,0:T(8,128)(2,1)S(1)}, u32[]{:S(2)}, u32[]{:S(2)}) %all-to-all-start.1) | async-done | bytes 294944 | tf_op jit(solution)/shard_map/all_to_all | solution.py:274
  35.9 0.0 copy-done
  35.9 1.9 %shard_map.80 = (f32[4,128,512]{2,1,0:T(8,128)}, f32[8,512]{1,0:T(8,128)}, f32[1,8]{1,0:T(1,128)}) custom-call(s32[1,4]{1,0:T(1,128)S(1)} %get-tuple-element.13.ids, bf16[16,8,1152]{2,1,0:T(8,128)(2,1)S(1)} %all-to-all-done.1.received, f32[128,128]{1,0:T(8,128)S(1)} %get-tuple-element.16.own_expo, f32[128,128]{1,0:T(8,128)S(1)} %collective-permute-done.2.other_expo, ...), custom_call_target="tpu_custom_call" | custom-call | bytes 2482224 | tf_op jit(solution)/shard_map/pallas_call | solution.py:37
Async XLA Ops:
  1.8 16.7 %collective-permute-start = (bf16[4,128,512]{2,1,0:T(8,128)(2,1)S(1)}, bf16[4,128,512]{2,1,0:T(8,128)(2,1)S(1)}, u32[]{:S(2)}, u32[]{:S(2)}) collective-permute-start(bf16[4,128,512]{2,1,0:T(8,128)(2,1)S(1)} %get-tuple-element.15.own_blocks.blocks), channel_id=1, source_target_pairs={{0,1},{1,0},{2,3},{3,2},{4,5},{5,4},{6,7},{7,6},{8,9},{9,8},{10,11... | collective-permute-start | bytes 1572872 | tf_op jit(solution)/shard_map/ppermute | solution.py:278
  19.0 1.2 %collective-permute-start.1 = (f32[2,128]{1,0:T(2,128)S(1)}, f32[2,128]{1,0:T(2,128)S(1)}, u32[]{:S(2)}, u32[]{:S(2)}) collective-permute-start(f32[2,128]{1,0:T(2,128)S(1)} %get-tuple-element.19.own_sums), channel_id=1, source_target_pairs={{0,1},{1,0},{2,3},{3,2},{4,5},{5,4},{6,7},{7,6},{8,9},{9,8},{10,11... | collective-permute-start | bytes 3080 | tf_op jit(solution)/shard_map/ppermute | solution.py:278
  21.0 14.9 %copy-start = (bf16[8,512]{1,0:T(8,128)(2,1)S(1)}, bf16[8,512]{1,0:T(8,128)(2,1)}, u32[]{:S(2)}) copy-start(bf16[8,512]{1,0:T(8,128)(2,1)} %features.3) | copy-start | bytes 24580
  21.0 14.9 %all-to-all-start.1 = ((bf16[16,8,1152]{2,1,0:T(8,128)(2,1)}), bf16[16,8,1152]{2,1,0:T(8,128)(2,1)S(1)}, u32[]{:S(2)}, u32[]{:S(2)}) async-start(bf16[16,8,1152]{2,1,0:T(8,128)(2,1)} %bitcast.5), calls=%async_computation.1 | async-start | bytes 589824 | tf_op jit(solution)/shard_map/all_to_all | solution.py:274
  24.6 1.5 %collective-permute-start.3 = (bf16[128,640]{1,0:T(8,128)(2,1)S(1)}, bf16[128,640]{1,0:T(8,128)(2,1)S(1)}, u32[]{:S(2)}, u32[]{:S(2)}) collective-permute-start(bf16[128,640]{1,0:T(8,128)(2,1)S(1)} %bitcast.9), channel_id=1, source_target_pairs={{0,1},{1,0},{2,3},{3,2},{4,5},{5,4},{6,7},{7,6},{8,9},{9,8},{10,11... | collective-permute-start | bytes 491528 | tf_op jit(solution)/shard_map/ppermute | solution.py:278
  24.9 1.3 %collective-permute-start.2 = (f32[128,128]{1,0:T(8,128)S(1)}, f32[128,128]{1,0:T(8,128)S(1)}, u32[]{:S(2)}, u32[]{:S(2)}) collective-permute-start(f32[128,128]{1,0:T(8,128)S(1)} %get-tuple-element.17.pair_expo), channel_id=1, source_target_pairs={{0,1},{1,0},{2,3},{3,2},{4,5},{5,4},{6,7},{7,6},{8,9},{9,8},{10,11... | collective-permute-start | bytes 196616 | tf_op jit(solution)/shard_map/ppermute | solution.py:278

commit v10 on v9

--- a/solution.py
+++ b/solution.py
@@ -163,7 +163,8 @@
         shares_out[here, width:] = both[per_group:]
 
 
-def with_sums(shares, own_sums, other_sums, sent_out):
+def with_sums(shares, own_sums, other_sums, other_packed, other_expo, sent_out):
+    del other_packed, other_expo
     rows, wide = shares.shape
     sent_out[:, :wide] = shares[...]
     total = jnp.concatenate([own_sums[...], other_sums[...]], axis=0)
@@ -197,16 +198,7 @@
     per_group = 128 // groups
     tok_dev, width = features.shape
 
-    def leave(block):
-        return pltpu.make_async_copy(grad.at[block], grad_out.at[block], left.at[block])
-
     grad[...] = jnp.zeros_like(grad)
-    for block in range(held):
-        named = ids[0, 0] == block
-        for g in range(1, groups):
-            named = named | (ids[0, g] == block)
-        pl.when(jnp.logical_not(named))(leave(block).start)
-
     sums = received[0].astype(jnp.float32)
     for i in range(1, received.shape[0]):
         sums = sums + received[i].astype(jnp.float32)
@@ -214,6 +206,33 @@
     tile = tile[:4] + tile[4:]
     own_rest, own_label = tile[0:1], tile[1:2]
     other_rest, other_label = tile[2:3], tile[3:4]
+
+    chip = lax.axis_index("group") * lax.axis_size("chip") + lax.axis_index("chip")
+    sample = lax.broadcasted_iota(jnp.int32, (tok_dev, 128), 0) + chip * tok_dev
+    mine = lanes(tok_dev) == sample
+    rest = jnp.sum(jnp.where(mine, own_rest, 0.0), axis=1, keepdims=True)
+    label = jnp.sum(jnp.where(mine, own_label, 0.0), axis=1, keepdims=True)
+    total = rest + label
+    loss = jnp.log(total) - jnp.log(label)
+    square = (tok_dev, tok_dev)
+    diagonal = lax.broadcasted_iota(jnp.int32, square, 0) == lax.broadcasted_iota(
+        jnp.int32, square, 1
+    )
+    loss_row[...] = jnp.sum(jnp.where(diagonal, loss, 0.0), axis=0, keepdims=True)
+    rows = features[...].astype(jnp.float32)
+    inv_norm = inverse_norm(rows)
+    unit = rows * inv_norm
+    cand = sums[:, width : 2 * width]
+    cand = (cand * inverse_norm(cand)).astype(jnp.bfloat16).astype(jnp.float32)
+    unit_grad = logit_scale / total * (sums[:, :width] - rest * cand)
+    along = jnp.sum(unit_grad * unit, axis=1, keepdims=True)
+    feature_grad[...] = inv_norm * (unit_grad - along * unit)
+    moves = [
+        pltpu.make_async_copy(feature_grad, feature_out, left.at[held]),
+        pltpu.make_async_copy(loss_row, loss_out, left.at[held + 1]),
+    ]
+    for move in moves:
+        move.start()
 
     units = jnp.concatenate([own_packed[:, :width], other_packed[:, :width]], axis=0)
     own_scale = logit_scale / (own_rest + own_label)
@@ -225,48 +244,18 @@
     weights = jnp.concatenate([own, other], axis=1)
     owner = jnp.concatenate([lanes(1), lanes(1)], axis=1) // per_group
     for g in range(groups):
-        block = ids[0, g]
         mine = jnp.where(owner == g, weights, 0.0).astype(jnp.bfloat16)
         slot_grad = contract(mine, units, 1, 0)
         factor = inverse[0, :, g * per_group : g * per_group + 1]
         unit = blocks[g].astype(jnp.float32) * factor
         along = jnp.sum(slot_grad * unit, axis=1, keepdims=True)
         cand_grad = factor * (slot_grad - along * unit)
-        grad[block] += cand_grad.astype(jnp.bfloat16).astype(jnp.float32)
-        last = jnp.bool_(True)
-        for later in range(g + 1, groups):
-            last = last & (ids[0, later] != block)
-        pl.when(last)(leave(block).start)
-
-    chip = lax.axis_index("group") * lax.axis_size("chip") + lax.axis_index("chip")
-    sample = lax.broadcasted_iota(jnp.int32, (tok_dev, 128), 0) + chip * tok_dev
-    mine = lanes(tok_dev) == sample
-    rest = jnp.sum(jnp.where(mine, own_rest, 0.0), axis=1, keepdims=True)
-    label = jnp.sum(jnp.where(mine, own_label, 0.0), axis=1, keepdims=True)
-    total = rest + label
-    loss = jnp.log(total) - jnp.log(label)
-    square = (tok_dev, tok_dev)
-    diagonal = lax.broadcasted_iota(jnp.int32, square, 0) == lax.broadcasted_iota(
-        jnp.int32, square, 1
-    )
-    loss_row[...] = jnp.sum(jnp.where(diagonal, loss, 0.0), axis=0, keepdims=True)
-    rows = features[...].astype(jnp.float32)
-    inv_norm = inverse_norm(rows)
-    unit = rows * inv_norm
-    cand = sums[:, width : 2 * width]
-    cand = (cand * inverse_norm(cand)).astype(jnp.bfloat16).astype(jnp.float32)
-    unit_grad = logit_scale / total * (sums[:, :width] - rest * cand)
-    along = jnp.sum(unit_grad * unit, axis=1, keepdims=True)
-    feature_grad[...] = inv_norm * (unit_grad - along * unit)
-    ends = [
-        pltpu.make_async_copy(feature_grad, feature_out, left.at[held]),
-        pltpu.make_async_copy(loss_row, loss_out, left.at[held + 1]),
-    ]
-    for move in ends:
+        grad[ids[0, g]] += cand_grad.astype(jnp.bfloat16).astype(jnp.float32)
+    for block in range(held):
+        move = pltpu.make_async_copy(grad.at[block], grad_out.at[block], left.at[block])
         move.start()
-    for block in range(held):
-        leave(block).wait()
-    for move in ends:
+        moves.append(move)
+    for move in moves:
         move.wait()
 
 
@@ -343,7 +332,14 @@
         pair_blocks,
     )
     sent = run(
-        with_sums, shape((half, 2 * width + 128), bf16), [VMEM] * 3, going, sums, other_sums
+        with_sums,
+        shape((half, 2 * width + 128), bf16),
+        [VMEM] * 3 + [pl.BlockSpec(memory_space=pl.ANY)] * 2,
+        going,
+        sums,
+        other_sums,
+        other_packed,
+        other_expo,
     )
     received = exchange(sent.reshape(chips, tok_dev, 2 * width + 128), CHIPS)
     outs = (shape((held, BLK, width), f32), shape((tok_dev, width), f32), shape((1, tok_dev), f32))

time: 38.2 us -> 37.5 us (0.982)
  blocking collectives: 16.2 us -> 30.5 us
  waiting for transfers between devices: 11.5 us -> 0.71 us
  starting transfers between devices: 4.83 us -> 1.17 us
  Pallas kernels: 4.71 us -> 4.24 us
    all_to_all x1 -> x2, blocking collectives: 16.2 us -> 30.5 us  [exchange(): return lax.all_to_all(pieces, axes, split_axis=0, concat_axis=0, tiled=True)]
    all_to_all x1 -> x0, waiting for transfers between devices: 9.71 us -> none  [exchange(): return lax.all_to_all(pieces, axes, split_axis=0, concat_axis=0, tiled=True)]
    all_to_all x1 -> x0, starting transfers between devices: 3.67 us -> none  [exchange(): return lax.all_to_all(pieces, axes, split_axis=0, concat_axis=0, tiled=True)]
    ppermute x4, waiting for transfers between devices: 1.76 us -> 0.71 us  [with_partner(): return lax.ppermute(value, 'core', [(0, 1), (1, 0)])]
    pallas_call x5, Pallas kernels: 4.71 us -> 4.24 us  [run(): pl.pallas_call(kernel, out_shape=out_shape, in_specs=in_specs, out_specs=...]
  transfers between devices with their start and end apart: 5 -> 4, of which waited for: 4 -> 1; matrix products, arithmetic and copies ran while one was open for 0% -> 0% of each run, Pallas kernels for 1% -> 2%
where the time goes in v10:
time: 37.5 us; the launch traced here: 37.3 us
  blocking collectives  30.5 us (81%)
  Pallas kernels  4.24 us (11%)
  starting transfers between devices  1.17 us (3%)
  waiting for transfers between devices  0.71 us (2%)
  between operations  0.67 us (2%)
    all_to_all x2, blocking collectives, exchange(): return lax.all_to_all(pieces, axes, split_axis=0, concat_axis=0, tiled=True)  30.5 us
    pallas_call x5, Pallas kernels, run(): pl.pallas_call(kernel, out_shape=out_shape, in_specs=in_specs, out_specs=...  4.24 us
    ppermute x4, starting transfers between devices, with_partner(): return lax.ppermute(value, 'core', [(0, 1), (1, 0)])  1.17 us
  transfers between devices with their start and end apart: 4, of which 1 were waited for; matrix products, arithmetic and copies ran while one was open for 0% of the time, Pallas kernels for 2%

profile of v10, /device:TPU:0, one launch (start us, length us, event | category | flops | bytes accessed | tf_op | source)
XLA Modules:
  0.0 37.3 jit_solution(5838449809930994117)
XLA Ops:
  0.6 1.2 %shard_map.76 = (bf16[16,8,640]{2,1,0:T(8,128)(2,1)S(1)}, bf16[4,128,512]{2,1,0:T(8,128)(2,1)S(1)}, s32[1,4]{1,0:T(1,128)S(1)}) custom-call(bf16[8,512]{1,0:T(8,128)(2,1)} %features.3, s32[1,64]{1,0:T(1,128)} %bitcast.13, bf16[4,128,512]{2,1,0:T(8,128)(2,1)} %bitcast.12, s32[1,4]{1,0:T(1,128)} %bitcast.14, s32[1,4]{1,0:T(1,128)} %bitcast.15), custom_call_target="tpu_custom_call" | custom-call | bytes 1220912 | tf_op jit(solution)/shard_map/pallas_call | solution.py:37
  1.8 0.5 %collective-permute-start = (bf16[4,128,512]{2,1,0:T(8,128)(2,1)S(1)}, bf16[4,128,512]{2,1,0:T(8,128)(2,1)S(1)}, u32[]{:S(2)}, u32[]{:S(2)}) collective-permute-start(bf16[4,128,512]{2,1,0:T(8,128)(2,1)S(1)} %get-tuple-element.15.own_blocks.blocks), channel_id=1, source_target_pairs={{0,1},{1,0},{2,3},{3,2},{4,5},{5,4},{6,7},{7,6},{8,9},{9,8},{10,11... | collective-permute-start | bytes 1572872 | tf_op jit(solution)/shard_map/ppermute | solution.py:267
  2.4 16.2 %all_to_all.10 = bf16[16,8,640]{2,1,0:T(8,128)(2,1)S(1)} all-to-all(bf16[16,8,640]{2,1,0:T(8,128)(2,1)S(1)} %get-tuple-element.14), channel_id=1, replica_groups=mesh['group'=4,'chip'=4,'core'=2] {'group','chip'}, dimensions={0} | all-to-all | bytes 327680 | tf_op jit(solution)/shard_map/all_to_all | solution.py:263
  18.5 0.0 collective-permute-start.2
  18.5 0.0 collective-permute-done.pair_blocks
  18.5 0.5 %shard_map.77 = (f32[128,128]{1,0:T(8,128)S(1)}, f32[128,128]{1,0:T(8,128)S(1)}, f32[2,128,128]{2,1,0:T(8,128)S(1)}, f32[2,128]{1,0:T(2,128)S(1)}) custom-call(bf16[128,640]{1,0:T(8,128)(2,1)S(1)} %bitcast.9, bf16[4,128,512]{2,1,0:T(8,128)(2,1)S(1)} %get-tuple-element.15.own_blocks.blocks, bf16[4,128,512]{2,1,0:T(8,128)(2,1)S(1)} %collective-permute-done.pair_blocks), custom_call_target="tpu_custom_call" | custom-call | bytes 1475584 | tf_op jit(solution)/shard_map/pallas_call | solution.py:37
  19.0 0.6 %collective-permute-start.3 = (f32[128,128]{1,0:T(8,128)S(1)}, f32[128,128]{1,0:T(8,128)S(1)}, u32[]{:S(2)}, u32[]{:S(2)}) collective-permute-start(f32[128,128]{1,0:T(8,128)S(1)} %get-tuple-element.17.pair_expo), channel_id=1, source_target_pairs={{0,1},{1,0},{2,3},{3,2},{4,5},{5,4},{6,7},{7,6},{8,9},{9,8},{10,11... | collective-permute-start | bytes 196616 | tf_op jit(solution)/shard_map/ppermute | solution.py:267
  19.6 0.1 collective-permute-start.1
  19.7 0.3 shard_map.78.shares
  20.0 0.0 collective-permute-done.2.other_packed
  20.0 0.7 %collective-permute-done.1.other_sums = f32[2,128]{1,0:T(2,128)S(1)} collective-permute-done((f32[2,128]{1,0:T(2,128)S(1)}, f32[2,128]{1,0:T(2,128)S(1)}, u32[]{:S(2)}, u32[]{:S(2)}) %collective-permute-start.1) | collective-permute-done | bytes 1056 | tf_op jit(solution)/shard_map/ppermute | solution.py:267
  20.7 0.0 collective-permute-done.3.other_expo
  20.8 0.0 copy-start
  20.8 14.3 %all_to_all.11.received = bf16[16,8,1152]{2,1,0:T(8,128)(2,1)S(1)} all-to-all(bf16[16,8,1152]{2,1,0:T(8,128)(2,1)S(1)} %bitcast.11), channel_id=1, replica_groups=mesh['group'=4,'chip'=4,'core'=2] {'group','chip'}, dimensions={0} | all-to-all | bytes 589824 | tf_op jit(solution)/shard_map/all_to_all | solution.py:263
  35.1 0.0 copy-done
  35.1 2.2 %shard_map.80 = (f32[4,128,512]{2,1,0:T(8,128)}, f32[8,512]{1,0:T(8,128)}, f32[1,8]{1,0:T(1,128)}) custom-call(s32[1,4]{1,0:T(1,128)S(1)} %get-tuple-element.13.ids, bf16[16,8,1152]{2,1,0:T(8,128)(2,1)S(1)} %all_to_all.11.received, f32[128,128]{1,0:T(8,128)S(1)} %get-tuple-element.16.own_expo, f32[128,128]{1,0:T(8,128)S(1)} %collective-permute-done.3.other_expo, ...), custom_call_target="tpu_custom_call" | custom-call | bytes 2482224 | tf_op jit(solution)/shard_map/pallas_call | solution.py:37
  (1 shorter events, 0.0 us)
Async XLA Ops:
  1.8 16.7 %collective-permute-start = (bf16[4,128,512]{2,1,0:T(8,128)(2,1)S(1)}, bf16[4,128,512]{2,1,0:T(8,128)(2,1)S(1)}, u32[]{:S(2)}, u32[]{:S(2)}) collective-permute-start(bf16[4,128,512]{2,1,0:T(8,128)(2,1)S(1)} %get-tuple-element.15.own_blocks.blocks), channel_id=1, source_target_pairs={{0,1},{1,0},{2,3},{3,2},{4,5},{5,4},{6,7},{7,6},{8,9},{9,8},{10,11... | collective-permute-start | bytes 1572872 | tf_op jit(solution)/shard_map/ppermute | solution.py:267
  18.5 1.5 %collective-permute-start.2 = (bf16[128,640]{1,0:T(8,128)(2,1)S(1)}, bf16[128,640]{1,0:T(8,128)(2,1)S(1)}, u32[]{:S(2)}, u32[]{:S(2)}) collective-permute-start(bf16[128,640]{1,0:T(8,128)(2,1)S(1)} %bitcast.8), channel_id=1, source_target_pairs={{0,1},{1,0},{2,3},{3,2},{4,5},{5,4},{6,7},{7,6},{8,9},{9,8},{10,11... | collective-permute-start | bytes 491528 | tf_op jit(solution)/shard_map/ppermute | solution.py:267
  19.0 1.7 %collective-permute-start.3 = (f32[128,128]{1,0:T(8,128)S(1)}, f32[128,128]{1,0:T(8,128)S(1)}, u32[]{:S(2)}, u32[]{:S(2)}) collective-permute-start(f32[128,128]{1,0:T(8,128)S(1)} %get-tuple-element.17.pair_expo), channel_id=1, source_target_pairs={{0,1},{1,0},{2,3},{3,2},{4,5},{5,4},{6,7},{7,6},{8,9},{9,8},{10,11... | collective-permute-start | bytes 196616 | tf_op jit(solution)/shard_map/ppermute | solution.py:267
  19.6 1.1 %collective-permute-start.1 = (f32[2,128]{1,0:T(2,128)S(1)}, f32[2,128]{1,0:T(2,128)S(1)}, u32[]{:S(2)}, u32[]{:S(2)}) collective-permute-start(f32[2,128]{1,0:T(2,128)S(1)} %get-tuple-element.19.own_sums), channel_id=1, source_target_pairs={{0,1},{1,0},{2,3},{3,2},{4,5},{5,4},{6,7},{7,6},{8,9},{9,8},{10,11... | collective-permute-start | bytes 3080 | tf_op jit(solution)/shard_map/ppermute | solution.py:267
  20.8 14.3 %copy-start = (bf16[8,512]{1,0:T(8,128)(2,1)S(1)}, bf16[8,512]{1,0:T(8,128)(2,1)}, u32[]{:S(2)}) copy-start(bf16[8,512]{1,0:T(8,128)(2,1)} %features.3) | copy-start | bytes 24580

commit v11 on v10

--- a/solution.py
+++ b/solution.py
@@ -57,10 +57,10 @@
     listed,
     copies_out,
     blocks_out,
+    centres_out,
     ids_out,
     held_features,
     held_labels,
-    held_centres,
     held_ids,
     held_listed,
     arrived,
@@ -74,7 +74,7 @@
                 (ids, held_ids),
                 (listed, held_listed),
                 (ids, ids_out),
-                (centres, held_centres),
+                (centres, centres_out),
             )
         )
     ]
@@ -105,7 +105,7 @@
     for move in moves[2:]:
         move.wait()
     for g in range(blocks_out.shape[0]):
-        block = held_centres[held_ids[0, g]]
+        block = centres_out[held_ids[0, g]]
         blocks_out[g] = jnp.where(held_listed[0, g] > 0, block, jnp.full_like(block, UNLISTED))
 
 
@@ -145,7 +145,7 @@
     sums_out[1:2, :] = at_label
 
 
-def shares(own_expo, pair_expo, inverse, own_blocks, pair_blocks, shares_out):
+def shares(own_expo, pair_expo, inverse, own_blocks, pair_blocks, centres, shares_out, norms_out):
     groups, _, width = own_blocks.shape
     per_group = 128 // groups
     others, label = [], []
@@ -161,6 +161,10 @@
         both = both.astype(jnp.bfloat16)
         shares_out[here, :width] = both[:per_group]
         shares_out[here, width:] = both[per_group:]
+    held = centres.shape[0]
+    norms_out[...] = select(
+        [inverse_norm(centres[b].astype(jnp.float32)) for b in range(held)], BLK
+    )
 
 
 def with_sums(shares, own_sums, other_sums, other_packed, other_expo, sent_out):
@@ -183,8 +187,8 @@
     own_packed,
     other_packed,
     features,
-    blocks,
-    inverse,
+    centres,
+    norms,
     grad_out,
     feature_out,
     loss_out,
@@ -194,11 +198,9 @@
     left,
 ):
     groups = ids.shape[1]
-    held = grad.shape[0]
-    per_group = 128 // groups
+    held = centres.shape[0]
     tok_dev, width = features.shape
 
-    grad[...] = jnp.zeros_like(grad)
     sums = received[0].astype(jnp.float32)
     for i in range(1, received.shape[0]):
         sums = sums + received[i].astype(jnp.float32)
@@ -227,12 +229,6 @@
     unit_grad = logit_scale / total * (sums[:, :width] - rest * cand)
     along = jnp.sum(unit_grad * unit, axis=1, keepdims=True)
     feature_grad[...] = inv_norm * (unit_grad - along * unit)
-    moves = [
-        pltpu.make_async_copy(feature_grad, feature_out, left.at[held]),
-        pltpu.make_async_copy(loss_row, loss_out, left.at[held + 1]),
-    ]
-    for move in moves:
-        move.start()
 
     units = jnp.concatenate([own_packed[:, :width], other_packed[:, :width]], axis=0)
     own_scale = logit_scale / (own_rest + own_label)
@@ -242,17 +238,25 @@
     own = jnp.where(own < 0.0, -own_rest, own) * own_scale
     other = jnp.where(other < 0.0, -other_rest, other) * other_scale
     weights = jnp.concatenate([own, other], axis=1)
-    owner = jnp.concatenate([lanes(1), lanes(1)], axis=1) // per_group
-    for g in range(groups):
-        mine = jnp.where(owner == g, weights, 0.0).astype(jnp.bfloat16)
-        slot_grad = contract(mine, units, 1, 0)
-        factor = inverse[0, :, g * per_group : g * per_group + 1]
-        unit = blocks[g].astype(jnp.float32) * factor
+    named = select([ids[0, g] for g in range(groups)], 1)
+    named = jnp.concatenate([named, named], axis=1)
+    for b in range(held):
+        mine = jnp.where(named == b, weights, 0.0).astype(jnp.bfloat16)
+        grad[b] = contract(mine, units, 1, 0)
+    moves = [
+        pltpu.make_async_copy(feature_grad, feature_out, left.at[held]),
+        pltpu.make_async_copy(loss_row, loss_out, left.at[held + 1]),
+    ]
+    for move in moves:
+        move.start()
+    per_block = 128 // held
+    for b in range(held):
+        slot_grad = grad[b]
+        factor = norms[:, b * per_block : b * per_block + 1]
+        unit = centres[b].astype(jnp.float32) * factor
         along = jnp.sum(slot_grad * unit, axis=1, keepdims=True)
-        cand_grad = factor * (slot_grad - along * unit)
-        grad[ids[0, g]] += cand_grad.astype(jnp.bfloat16).astype(jnp.float32)
-    for block in range(held):
-        move = pltpu.make_async_copy(grad.at[block], grad_out.at[block], left.at[block])
+        grad[b] = factor * (slot_grad - along * unit)
+        move = pltpu.make_async_copy(grad.at[b], grad_out.at[b], left.at[b])
         move.start()
         moves.append(move)
     for move in moves:
@@ -276,11 +280,12 @@
     bf16, f32 = jnp.bfloat16, jnp.float32
     shape = jax.ShapeDtypeStruct
 
-    copies, own_blocks, ids = run(
+    copies, own_blocks, blocks, ids = run(
         load,
         (
             shape((chips, tok_dev, width + 128), bf16),
             shape((groups, BLK, width), bf16),
+            shape((held, BLK, width), bf16),
             shape((1, groups), block_ids.dtype),
         ),
         [HBM] * 5,
@@ -297,7 +302,6 @@
         scratch=[
             pltpu.VMEM(features.shape, features.dtype),
             pltpu.VMEM((1, labels.shape[0]), labels.dtype),
-            pltpu.VMEM((held, BLK, width), centres.dtype),
             pltpu.SMEM((1, groups), block_ids.dtype),
             pltpu.SMEM((1, groups), listed.dtype),
             pltpu.SemaphoreType.DMA((6,)),
@@ -321,15 +325,16 @@
     )
     other_expo = with_partner(pair_expo)
     other_sums = with_partner(sums)
-    going = run(
+    going, norms = run(
         shares,
-        shape((half, 2 * width), bf16),
-        [VMEM] * 5,
+        (shape((half, 2 * width), bf16), shape((BLK, 128), f32)),
+        [VMEM] * 6,
         own_expo,
         pair_expo,
         inverse,
         own_blocks,
         pair_blocks,
+        blocks,
     )
     sent = run(
         with_sums,
@@ -354,8 +359,8 @@
         own_packed,
         other_packed,
         features,
-        own_blocks,
-        inverse,
+        blocks,
+        norms,
         out_spec=HBM,
         scratch=[
             *(pltpu.VMEM(out.shape, out.dtype) for out in outs),

time: 37.5 us -> 37.3 us (level)
  no operation moved by 1% of the time
where the time goes in v11:
time: 37.3 us; the launch traced here: 37 us
  blocking collectives  30.5 us (82%)
  Pallas kernels  4.02 us (11%)
  starting transfers between devices  1.17 us (3%)
  waiting for transfers between devices  0.71 us (2%)
  between operations  0.67 us (2%)
    all_to_all x2, blocking collectives, exchange(): return lax.all_to_all(pieces, axes, split_axis=0, concat_axis=0, tiled=True)  30.5 us
    pallas_call x5, Pallas kernels, run(): pl.pallas_call(kernel, out_shape=out_shape, in_specs=in_specs, out_specs=...  4.02 us
    ppermute x4, starting transfers between devices, with_partner(): return lax.ppermute(value, 'core', [(0, 1), (1, 0)])  1.17 us
  transfers between devices with their start and end apart: 4, of which 1 were waited for; matrix products, arithmetic and copies ran while one was open for 0% of the time, Pallas kernels for 2%

profile of v11, /device:TPU:0, one launch (start us, length us, event | category | flops | bytes accessed | tf_op | source)
XLA Modules:
  0.0 37.0 jit_solution(11205179720146341986)
XLA Ops:
  0.6 1.2 %shard_map.76 = (bf16[16,8,640]{2,1,0:T(8,128)(2,1)S(1)}, bf16[4,128,512]{2,1,0:T(8,128)(2,1)S(1)}, bf16[4,128,512]{2,1,0:T(8,128)(2,1)S(1)}, s32[1,4]{1,0:T(1,128)S(1)}) custom-call(bf16[8,512]{1,0:T(8,128)(2,1)} %features.3, s32[1,64]{1,0:T(1,128)} %bitcast.13, bf16[4,128,512]{2,1,0:T(8,128)(2,1)} %bitcast.12, s32[1,4]{1,0:T(1,128)} %bitcast.14, ...), custom_call_target="tpu_custom_call" | custom-call | bytes 1745200 | tf_op jit(solution)/shard_map/pallas_call | solution.py:37
  1.8 0.5 %collective-permute-start = (bf16[4,128,512]{2,1,0:T(8,128)(2,1)S(1)}, bf16[4,128,512]{2,1,0:T(8,128)(2,1)S(1)}, u32[]{:S(2)}, u32[]{:S(2)}) collective-permute-start(bf16[4,128,512]{2,1,0:T(8,128)(2,1)S(1)} %get-tuple-element.18.own_blocks), channel_id=1, source_target_pairs={{0,1},{1,0},{2,3},{3,2},{4,5},{5,4},{6,7},{7,6},{8,9},{9,8},{10,11... | collective-permute-start | bytes 1572872 | tf_op jit(solution)/shard_map/ppermute | solution.py:271
  2.4 16.2 %all_to_all.10 = bf16[16,8,640]{2,1,0:T(8,128)(2,1)S(1)} all-to-all(bf16[16,8,640]{2,1,0:T(8,128)(2,1)S(1)} %get-tuple-element.17), channel_id=1, replica_groups=mesh['group'=4,'chip'=4,'core'=2] {'group','chip'}, dimensions={0} | all-to-all | bytes 327680 | tf_op jit(solution)/shard_map/all_to_all | solution.py:267
  18.5 0.0 collective-permute-start.2
  18.5 0.0 collective-permute-done.pair_blocks
  18.5 0.5 %shard_map.77 = (f32[128,128]{1,0:T(8,128)S(1)}, f32[128,128]{1,0:T(8,128)S(1)}, f32[2,128,128]{2,1,0:T(8,128)S(1)}, f32[2,128]{1,0:T(2,128)S(1)}) custom-call(bf16[128,640]{1,0:T(8,128)(2,1)S(1)} %bitcast.9, bf16[4,128,512]{2,1,0:T(8,128)(2,1)S(1)} %get-tuple-element.18.own_blocks, bf16[4,128,512]{2,1,0:T(8,128)(2,1)S(1)} %collective-permute-done.pair_blocks), custom_call_target="tpu_custom_call" | custom-call | bytes 1475584 | tf_op jit(solution)/shard_map/pallas_call | solution.py:37
  19.0 0.6 %collective-permute-start.3 = (f32[128,128]{1,0:T(8,128)S(1)}, f32[128,128]{1,0:T(8,128)S(1)}, u32[]{:S(2)}, u32[]{:S(2)}) collective-permute-start(f32[128,128]{1,0:T(8,128)S(1)} %get-tuple-element.20.pair_expo), channel_id=1, source_target_pairs={{0,1},{1,0},{2,3},{3,2},{4,5},{5,4},{6,7},{7,6},{8,9},{9,8},{10,11... | collective-permute-start | bytes 196616 | tf_op jit(solution)/shard_map/ppermute | solution.py:271
  19.6 0.1 collective-permute-start.1
  19.7 0.3 shard_map.78
  20.0 0.0 collective-permute-done.2.other_packed
  20.0 0.7 %collective-permute-done.1.other_sums = f32[2,128]{1,0:T(2,128)S(1)} collective-permute-done((f32[2,128]{1,0:T(2,128)S(1)}, f32[2,128]{1,0:T(2,128)S(1)}, u32[]{:S(2)}, u32[]{:S(2)}) %collective-permute-start.1) | collective-permute-done | bytes 1056 | tf_op jit(solution)/shard_map/ppermute | solution.py:271
  20.7 0.0 collective-permute-done.3.other_expo
  20.8 0.0 copy-start
  20.8 14.3 %all_to_all.11.received = bf16[16,8,1152]{2,1,0:T(8,128)(2,1)S(1)} all-to-all(bf16[16,8,1152]{2,1,0:T(8,128)(2,1)S(1)} %bitcast.11), channel_id=1, replica_groups=mesh['group'=4,'chip'=4,'core'=2] {'group','chip'}, dimensions={0} | all-to-all | bytes 589824 | tf_op jit(solution)/shard_map/all_to_all | solution.py:267
  35.1 0.0 copy-done
  35.1 2.0 %shard_map.80 = (f32[4,128,512]{2,1,0:T(8,128)}, f32[8,512]{1,0:T(8,128)}, f32[1,8]{1,0:T(1,128)}) custom-call(s32[1,4]{1,0:T(1,128)S(1)} %get-tuple-element.16.ids, bf16[16,8,1152]{2,1,0:T(8,128)(2,1)S(1)} %all_to_all.11.received, f32[128,128]{1,0:T(8,128)S(1)} %get-tuple-element.19.own_expo, f32[128,128]{1,0:T(8,128)S(1)} %collective-permute-done.3.other_expo, ...), custom_call_target="tpu_custom_call" | custom-call | bytes 2416688 | tf_op jit(solution)/shard_map/pallas_call | solution.py:37
  (1 shorter events, 0.0 us)
Async XLA Ops:
  1.8 16.7 %collective-permute-start = (bf16[4,128,512]{2,1,0:T(8,128)(2,1)S(1)}, bf16[4,128,512]{2,1,0:T(8,128)(2,1)S(1)}, u32[]{:S(2)}, u32[]{:S(2)}) collective-permute-start(bf16[4,128,512]{2,1,0:T(8,128)(2,1)S(1)} %get-tuple-element.18.own_blocks), channel_id=1, source_target_pairs={{0,1},{1,0},{2,3},{3,2},{4,5},{5,4},{6,7},{7,6},{8,9},{9,8},{10,11... | collective-permute-start | bytes 1572872 | tf_op jit(solution)/shard_map/ppermute | solution.py:271
  18.5 1.5 %collective-permute-start.2 = (bf16[128,640]{1,0:T(8,128)(2,1)S(1)}, bf16[128,640]{1,0:T(8,128)(2,1)S(1)}, u32[]{:S(2)}, u32[]{:S(2)}) collective-permute-start(bf16[128,640]{1,0:T(8,128)(2,1)S(1)} %bitcast.8), channel_id=1, source_target_pairs={{0,1},{1,0},{2,3},{3,2},{4,5},{5,4},{6,7},{7,6},{8,9},{9,8},{10,11... | collective-permute-start | bytes 491528 | tf_op jit(solution)/shard_map/ppermute | solution.py:271
  19.0 1.7 %collective-permute-start.3 = (f32[128,128]{1,0:T(8,128)S(1)}, f32[128,128]{1,0:T(8,128)S(1)}, u32[]{:S(2)}, u32[]{:S(2)}) collective-permute-start(f32[128,128]{1,0:T(8,128)S(1)} %get-tuple-element.20.pair_expo), channel_id=1, source_target_pairs={{0,1},{1,0},{2,3},{3,2},{4,5},{5,4},{6,7},{7,6},{8,9},{9,8},{10,11... | collective-permute-start | bytes 196616 | tf_op jit(solution)/shard_map/ppermute | solution.py:271
  19.6 1.1 %collective-permute-start.1 = (f32[2,128]{1,0:T(2,128)S(1)}, f32[2,128]{1,0:T(2,128)S(1)}, u32[]{:S(2)}, u32[]{:S(2)}) collective-permute-start(f32[2,128]{1,0:T(2,128)S(1)} %get-tuple-element.24.own_sums), channel_id=1, source_target_pairs={{0,1},{1,0},{2,3},{3,2},{4,5},{5,4},{6,7},{7,6},{8,9},{9,8},{10,11... | collective-permute-start | bytes 3080 | tf_op jit(solution)/shard_map/ppermute | solution.py:271
  20.8 14.3 %copy-start = (bf16[8,512]{1,0:T(8,128)(2,1)S(1)}, bf16[8,512]{1,0:T(8,128)(2,1)}, u32[]{:S(2)}) copy-start(bf16[8,512]{1,0:T(8,128)(2,1)} %features.3) | copy-start | bytes 24580

commit v12 on v11

--- a/solution.py
+++ b/solution.py
@@ -12,6 +12,7 @@
 logit_scale = 32.0
 cos_margin = 0.35
 norm_epsilon = 1e-06
+FIRST_GROUP = 1
 UNLISTED = 1e19
 
 VMEM = pl.BlockSpec(memory_space=pltpu.VMEM)
@@ -90,7 +91,7 @@
     unit = (rows * inverse_norm(rows)).astype(jnp.bfloat16)
     copies_out[:, :, :width] = jnp.broadcast_to(unit[None], (copies, tok_dev, width))
 
-    place = (lax.axis_index("group") * lax.axis_size("chip") + chip) * tok_dev
+    place = own_place() * tok_dev
     row = held_labels[...]
     row = jnp.concatenate([row, jnp.zeros((1, 128 - row.shape[1]), jnp.int32)], axis=1)
     row = jnp.broadcast_to(row, (tok_dev, 128))
@@ -105,8 +106,19 @@
     for move in moves[2:]:
         move.wait()
     for g in range(blocks_out.shape[0]):
-        block = centres_out[held_ids[0, g]]
-        blocks_out[g] = jnp.where(held_listed[0, g] > 0, block, jnp.full_like(block, UNLISTED))
+        group = group_at(g)
+        block = centres_out[held_ids[0, group]]
+        blocks_out[g] = jnp.where(held_listed[0, group] > 0, block, jnp.full_like(block, UNLISTED))
+
+
+def group_at(place):
+    return (place + FIRST_GROUP) % lax.axis_size("group")
+
+
+def own_place():
+    groups = lax.axis_size("group")
+    group = lax.rem(lax.axis_index("group") + groups - FIRST_GROUP, groups)
+    return group * lax.axis_size("chip") + lax.axis_index("chip")
 
 
 def select(parts, rows):
@@ -209,8 +221,38 @@
     own_rest, own_label = tile[0:1], tile[1:2]
     other_rest, other_label = tile[2:3], tile[3:4]
 
-    chip = lax.axis_index("group") * lax.axis_size("chip") + lax.axis_index("chip")
-    sample = lax.broadcasted_iota(jnp.int32, (tok_dev, 128), 0) + chip * tok_dev
+    units = jnp.concatenate([own_packed[:, :width], other_packed[:, :width]], axis=0)
+    own_scale = logit_scale / (own_rest + own_label)
+    other_scale = logit_scale / (other_rest + other_label)
+    own = own_expo[...]
+    other = other_expo[...]
+    own = jnp.where(own < 0.0, -own_rest, own) * own_scale
+    other = jnp.where(other < 0.0, -other_rest, other) * other_scale
+    weights = jnp.concatenate([own, other], axis=1)
+    named = select([ids[0, group_at(g)] for g in range(groups)], 1)
+    named = jnp.concatenate([named, named], axis=1)
+    mine = [jnp.where(named == b, weights, 0.0).astype(jnp.bfloat16) for b in range(held)]
+    slot_grad = contract(jnp.concatenate(mine, axis=0), units, 1, 0)
+    moves = []
+
+    def leave(source, target):
+        move = pltpu.make_async_copy(source, target, left.at[len(moves)])
+        move.start()
+        moves.append(move)
+
+    def block_out(b):
+        here = slot_grad[b * BLK : (b + 1) * BLK]
+        factor = norms[:, b * (128 // held) : b * (128 // held) + 1]
+        unit = centres[b].astype(jnp.float32) * factor
+        along = jnp.sum(here * unit, axis=1, keepdims=True)
+        grad[b] = factor * (here - along * unit)
+        for part in (pl.ds(0, BLK // 2), pl.ds(BLK // 2, BLK // 2)):
+            leave(grad.at[b, part], grad_out.at[b, part])
+
+    for b in range(held // 2):
+        block_out(b)
+
+    sample = lax.broadcasted_iota(jnp.int32, (tok_dev, 128), 0) + own_place() * tok_dev
     mine = lanes(tok_dev) == sample
     rest = jnp.sum(jnp.where(mine, own_rest, 0.0), axis=1, keepdims=True)
     label = jnp.sum(jnp.where(mine, own_label, 0.0), axis=1, keepdims=True)
@@ -230,41 +272,24 @@
     along = jnp.sum(unit_grad * unit, axis=1, keepdims=True)
     feature_grad[...] = inv_norm * (unit_grad - along * unit)
 
-    units = jnp.concatenate([own_packed[:, :width], other_packed[:, :width]], axis=0)
-    own_scale = logit_scale / (own_rest + own_label)
-    other_scale = logit_scale / (other_rest + other_label)
-    own = own_expo[...]
-    other = other_expo[...]
-    own = jnp.where(own < 0.0, -own_rest, own) * own_scale
-    other = jnp.where(other < 0.0, -other_rest, other) * other_scale
-    weights = jnp.concatenate([own, other], axis=1)
-    named = select([ids[0, g] for g in range(groups)], 1)
-    named = jnp.concatenate([named, named], axis=1)
-    for b in range(held):
-        mine = jnp.where(named == b, weights, 0.0).astype(jnp.bfloat16)
-        grad[b] = contract(mine, units, 1, 0)
-    moves = [
-        pltpu.make_async_copy(feature_grad, feature_out, left.at[held]),
-        pltpu.make_async_copy(loss_row, loss_out, left.at[held + 1]),
-    ]
-    for move in moves:
-        move.start()
-    per_block = 128 // held
-    for b in range(held):
-        slot_grad = grad[b]
-        factor = norms[:, b * per_block : b * per_block + 1]
-        unit = centres[b].astype(jnp.float32) * factor
-        along = jnp.sum(slot_grad * unit, axis=1, keepdims=True)
-        grad[b] = factor * (slot_grad - along * unit)
-        move = pltpu.make_async_copy(grad.at[b], grad_out.at[b], left.at[b])
-        move.start()
-        moves.append(move)
+    leave(feature_grad, feature_out)
+    leave(loss_row, loss_out)
+    for b in range(held // 2, held):
+        block_out(b)
     for move in moves:
         move.wait()
 
 
-def exchange(pieces, axes):
-    return lax.all_to_all(pieces, axes, split_axis=0, concat_axis=0, tiled=True)
+def exchange(pieces, axes, order=None):
+    return lax.all_to_all(
+        pieces, axes, split_axis=0, concat_axis=0, axis_index_groups=order, tiled=True
+    )
+
+
+def exchange_chips(pieces):
+    groups, chips = lax.axis_size("group"), lax.axis_size("chip")
+    order = [group_at(g) * chips + chip for g in range(groups) for chip in range(chips)]
+    return exchange(pieces, CHIPS, [order])
 
 
 def with_partner(value):
@@ -308,7 +333,7 @@
         ],
     )
     pair_blocks = with_partner(own_blocks)
-    own_packed = exchange(copies, CHIPS).reshape(half, width + 128)
+    own_packed = exchange_chips(copies).reshape(half, width + 128)
     other_packed = with_partner(own_packed)
     own_expo, pair_expo, inverse, sums = run(
         exponentials,
@@ -346,7 +371,7 @@
         other_packed,
         other_expo,
     )
-    received = exchange(sent.reshape(chips, tok_dev, 2 * width + 128), CHIPS)
+    received = exchange_chips(sent.reshape(chips, tok_dev, 2 * width + 128))
     outs = (shape((held, BLK, width), f32), shape((tok_dev, width), f32), shape((1, tok_dev), f32))
     centre_grad, feature_grad, loss = run(
         backward,
@@ -364,7 +389,7 @@
         out_spec=HBM,
         scratch=[
             *(pltpu.VMEM(out.shape, out.dtype) for out in outs),
-            pltpu.SemaphoreType.DMA((held + 2,)),
+            pltpu.SemaphoreType.DMA((2 * held + 2,)),
         ],
     )
     return (loss.reshape(tok_dev), feature_grad, centre_grad.reshape(held * BLK, width))

time: 37.3 us -> 35.6 us (0.954)
  blocking collectives: 30.5 us -> 28.7 us
    all_to_all x2, blocking collectives: 30.5 us -> 28.7 us  [exchange(): lax.all_to_all(pieces, axes, split_axis=0, concat_axis=0, axis_index_grou...]
where the time goes in v12:
time: 35.6 us; the launch traced here: 35.3 us
  blocking collectives  28.7 us (81%)
  Pallas kernels  4.03 us (11%)
  starting transfers between devices  1.17 us (3%)
  waiting for transfers between devices  0.71 us (2%)
  between operations  0.67 us (2%)
    all_to_all x2, blocking collectives, exchange(): lax.all_to_all(pieces, axes, split_axis=0, concat_axis=0, axis_index_grou...  28.7 us
    pallas_call x5, Pallas kernels, run(): pl.pallas_call(kernel, out_shape=out_shape, in_specs=in_specs, out_specs=...  4.03 us
    ppermute x4, starting transfers between devices, with_partner(): return lax.ppermute(value, 'core', [(0, 1), (1, 0)])  1.17 us
    ppermute x4, waiting for transfers between devices, with_partner(): return lax.ppermute(value, 'core', [(0, 1), (1, 0)])  0.71 us
  transfers between devices with their start and end apart: 4, of which 1 were waited for; matrix products, arithmetic and copies ran while one was open for 0% of the time, Pallas kernels for 2%

profile of v12, /device:TPU:0, one launch (start us, length us, event | category | flops | bytes accessed | tf_op | source)
XLA Modules:
  0.0 35.3 jit_solution(2104083223542321562)
XLA Ops:
  0.6 1.2 %shard_map.76 = (bf16[16,8,640]{2,1,0:T(8,128)(2,1)S(1)}, bf16[4,128,512]{2,1,0:T(8,128)(2,1)S(1)}, bf16[4,128,512]{2,1,0:T(8,128)(2,1)S(1)}, s32[1,4]{1,0:T(1,128)S(1)}) custom-call(bf16[8,512]{1,0:T(8,128)(2,1)} %features.3, s32[1,64]{1,0:T(1,128)} %bitcast.13, bf16[4,128,512]{2,1,0:T(8,128)(2,1)} %bitcast.12, s32[1,4]{1,0:T(1,128)} %bitcast.14, ...), custom_call_target="tpu_custom_call" | custom-call | bytes 1745200 | tf_op jit(solution)/shard_map/pallas_call | solution.py:38
  1.8 0.5 %collective-permute-start = (bf16[4,128,512]{2,1,0:T(8,128)(2,1)S(1)}, bf16[4,128,512]{2,1,0:T(8,128)(2,1)S(1)}, u32[]{:S(2)}, u32[]{:S(2)}) collective-permute-start(bf16[4,128,512]{2,1,0:T(8,128)(2,1)S(1)} %get-tuple-element.18.own_blocks), channel_id=1, source_target_pairs={{0,1},{1,0},{2,3},{3,2},{4,5},{5,4},{6,7},{7,6},{8,9},{9,8},{10,11... | collective-permute-start | bytes 1572872 | tf_op jit(solution)/shard_map/ppermute | solution.py:296
  2.4 15.3 %all_to_all.10 = bf16[16,8,640]{2,1,0:T(8,128)(2,1)S(1)} all-to-all(bf16[16,8,640]{2,1,0:T(8,128)(2,1)S(1)} %get-tuple-element.17), channel_id=1, replica_groups={{8,10,12,14,16,18,20,22,24,26,28,30,0,2,4,6},{9,11,13,15,17,19,21,23,25..., dimensions={0} | all-to-all | bytes 327680 | tf_op jit(solution)/shard_map/all_to_all | solution.py:284
  17.6 0.0 collective-permute-start.2
  17.6 0.0 collective-permute-done.pair_blocks
  17.6 0.5 %shard_map.77 = (f32[128,128]{1,0:T(8,128)S(1)}, f32[128,128]{1,0:T(8,128)S(1)}, f32[2,128,128]{2,1,0:T(8,128)S(1)}, f32[2,128]{1,0:T(2,128)S(1)}) custom-call(bf16[128,640]{1,0:T(8,128)(2,1)S(1)} %bitcast.9, bf16[4,128,512]{2,1,0:T(8,128)(2,1)S(1)} %get-tuple-element.18.own_blocks, bf16[4,128,512]{2,1,0:T(8,128)(2,1)S(1)} %collective-permute-done.pair_blocks), custom_call_target="tpu_custom_call" | custom-call | bytes 1475584 | tf_op jit(solution)/shard_map/pallas_call | solution.py:38
  18.1 0.6 %collective-permute-start.3 = (f32[128,128]{1,0:T(8,128)S(1)}, f32[128,128]{1,0:T(8,128)S(1)}, u32[]{:S(2)}, u32[]{:S(2)}) collective-permute-start(f32[128,128]{1,0:T(8,128)S(1)} %get-tuple-element.20.pair_expo), channel_id=1, source_target_pairs={{0,1},{1,0},{2,3},{3,2},{4,5},{5,4},{6,7},{7,6},{8,9},{9,8},{10,11... | collective-permute-start | bytes 196616 | tf_op jit(solution)/shard_map/ppermute | solution.py:296
  18.7 0.1 collective-permute-start.1
  18.8 0.3 shard_map.78
  19.1 0.0 collective-permute-done.2.other_packed
  19.1 0.7 %collective-permute-done.1.other_sums = f32[2,128]{1,0:T(2,128)S(1)} collective-permute-done((f32[2,128]{1,0:T(2,128)S(1)}, f32[2,128]{1,0:T(2,128)S(1)}, u32[]{:S(2)}, u32[]{:S(2)}) %collective-permute-start.1) | collective-permute-done | bytes 1056 | tf_op jit(solution)/shard_map/ppermute | solution.py:296
  19.8 0.0 collective-permute-done.3.other_expo
  19.9 0.0 copy-start
  19.9 13.4 %all_to_all.11.received = bf16[16,8,1152]{2,1,0:T(8,128)(2,1)S(1)} all-to-all(bf16[16,8,1152]{2,1,0:T(8,128)(2,1)S(1)} %bitcast.11), channel_id=1, replica_groups={{8,10,12,14,16,18,20,22,24,26,28,30,0,2,4,6},{9,11,13,15,17,19,21,23,25..., dimensions={0} | all-to-all | bytes 589824 | tf_op jit(solution)/shard_map/all_to_all | solution.py:284
  33.3 0.0 copy-done
  33.3 2.0 %shard_map.80 = (f32[4,128,512]{2,1,0:T(8,128)}, f32[8,512]{1,0:T(8,128)}, f32[1,8]{1,0:T(1,128)}) custom-call(s32[1,4]{1,0:T(1,128)S(1)} %get-tuple-element.16.ids, bf16[16,8,1152]{2,1,0:T(8,128)(2,1)S(1)} %all_to_all.11.received, f32[128,128]{1,0:T(8,128)S(1)} %get-tuple-element.19.own_expo, f32[128,128]{1,0:T(8,128)S(1)} %collective-permute-done.3.other_expo, ...), custom_call_target="tpu_custom_call" | custom-call | bytes 2416688 | tf_op jit(solution)/shard_map/pallas_call | solution.py:38
  (1 shorter events, 0.0 us)
Async XLA Ops:
  1.8 15.8 %collective-permute-start = (bf16[4,128,512]{2,1,0:T(8,128)(2,1)S(1)}, bf16[4,128,512]{2,1,0:T(8,128)(2,1)S(1)}, u32[]{:S(2)}, u32[]{:S(2)}) collective-permute-start(bf16[4,128,512]{2,1,0:T(8,128)(2,1)S(1)} %get-tuple-element.18.own_blocks), channel_id=1, source_target_pairs={{0,1},{1,0},{2,3},{3,2},{4,5},{5,4},{6,7},{7,6},{8,9},{9,8},{10,11... | collective-permute-start | bytes 1572872 | tf_op jit(solution)/shard_map/ppermute | solution.py:296
  17.6 1.5 %collective-permute-start.2 = (bf16[128,640]{1,0:T(8,128)(2,1)S(1)}, bf16[128,640]{1,0:T(8,128)(2,1)S(1)}, u32[]{:S(2)}, u32[]{:S(2)}) collective-permute-start(bf16[128,640]{1,0:T(8,128)(2,1)S(1)} %bitcast.8), channel_id=1, source_target_pairs={{0,1},{1,0},{2,3},{3,2},{4,5},{5,4},{6,7},{7,6},{8,9},{9,8},{10,11... | collective-permute-start | bytes 491528 | tf_op jit(solution)/shard_map/ppermute | solution.py:296
  18.1 1.7 %collective-permute-start.3 = (f32[128,128]{1,0:T(8,128)S(1)}, f32[128,128]{1,0:T(8,128)S(1)}, u32[]{:S(2)}, u32[]{:S(2)}) collective-permute-start(f32[128,128]{1,0:T(8,128)S(1)} %get-tuple-element.20.pair_expo), channel_id=1, source_target_pairs={{0,1},{1,0},{2,3},{3,2},{4,5},{5,4},{6,7},{7,6},{8,9},{9,8},{10,11... | collective-permute-start | bytes 196616 | tf_op jit(solution)/shard_map/ppermute | solution.py:296
  18.7 1.1 %collective-permute-start.1 = (f32[2,128]{1,0:T(2,128)S(1)}, f32[2,128]{1,0:T(2,128)S(1)}, u32[]{:S(2)}, u32[]{:S(2)}) collective-permute-start(f32[2,128]{1,0:T(2,128)S(1)} %get-tuple-element.24.own_sums), channel_id=1, source_target_pairs={{0,1},{1,0},{2,3},{3,2},{4,5},{5,4},{6,7},{7,6},{8,9},{9,8},{10,11... | collective-permute-start | bytes 3080 | tf_op jit(solution)/shard_map/ppermute | solution.py:296
  19.9 13.5 %copy-start = (bf16[8,512]{1,0:T(8,128)(2,1)S(1)}, bf16[8,512]{1,0:T(8,128)(2,1)}, u32[]{:S(2)}) copy-start(bf16[8,512]{1,0:T(8,128)(2,1)} %features.3) | copy-start | bytes 24580

commit v13 on v12

--- a/solution.py
+++ b/solution.py
@@ -16,7 +16,6 @@
 UNLISTED = 1e19
 
 VMEM = pl.BlockSpec(memory_space=pltpu.VMEM)
-SMEM = pl.BlockSpec(memory_space=pltpu.SMEM)
 HBM = pl.BlockSpec(memory_space=pltpu.HBM)
 
 
@@ -59,7 +58,7 @@
     copies_out,
     blocks_out,
     centres_out,
-    ids_out,
+    named_out,
     held_features,
     held_labels,
     held_ids,
@@ -74,8 +73,7 @@
                 (labels, held_labels),
                 (ids, held_ids),
                 (listed, held_listed),
-                (ids, ids_out),
-                (centres, centres_out),
+                *((centres.at[b], centres_out.at[b]) for b in range(centres.shape[0])),
             )
         )
     ]
@@ -105,7 +103,9 @@
     )
     for move in moves[2:]:
         move.wait()
-    for g in range(blocks_out.shape[0]):
+    groups = blocks_out.shape[0]
+    named_out[...] = select([held_ids[0, group_at(g)] for g in range(groups)], 1)
+    for g in range(groups):
         group = group_at(g)
         block = centres_out[held_ids[0, group]]
         blocks_out[g] = jnp.where(held_listed[0, group] > 0, block, jnp.full_like(block, UNLISTED))
@@ -192,7 +192,7 @@
 
 
 def backward(
-    ids,
+    named,
     received,
     own_expo,
     other_expo,
@@ -209,7 +209,6 @@
     loss_row,
     left,
 ):
-    groups = ids.shape[1]
     held = centres.shape[0]
     tok_dev, width = features.shape
 
@@ -229,8 +228,7 @@
     own = jnp.where(own < 0.0, -own_rest, own) * own_scale
     other = jnp.where(other < 0.0, -other_rest, other) * other_scale
     weights = jnp.concatenate([own, other], axis=1)
-    named = select([ids[0, group_at(g)] for g in range(groups)], 1)
-    named = jnp.concatenate([named, named], axis=1)
+    named = jnp.concatenate([named[...], named[...]], axis=1)
     mine = [jnp.where(named == b, weights, 0.0).astype(jnp.bfloat16) for b in range(held)]
     slot_grad = contract(jnp.concatenate(mine, axis=0), units, 1, 0)
     moves = []
@@ -305,13 +303,13 @@
     bf16, f32 = jnp.bfloat16, jnp.float32
     shape = jax.ShapeDtypeStruct
 
-    copies, own_blocks, blocks, ids = run(
+    copies, own_blocks, blocks, named = run(
         load,
         (
             shape((chips, tok_dev, width + 128), bf16),
             shape((groups, BLK, width), bf16),
             shape((held, BLK, width), bf16),
-            shape((1, groups), block_ids.dtype),
+            shape((1, 128), block_ids.dtype),
         ),
         [HBM] * 5,
         *(
@@ -329,7 +327,7 @@
             pltpu.VMEM((1, labels.shape[0]), labels.dtype),
             pltpu.SMEM((1, groups), block_ids.dtype),
             pltpu.SMEM((1, groups), listed.dtype),
-            pltpu.SemaphoreType.DMA((6,)),
+            pltpu.SemaphoreType.DMA((4 + held,)),
         ],
     )
     pair_blocks = with_partner(own_blocks)
@@ -376,8 +374,8 @@
     centre_grad, feature_grad, loss = run(
         backward,
         outs,
-        [SMEM] + [VMEM] * 8,
-        ids,
+        [VMEM] * 9,
+        named,
         received,
         own_expo,
         other_expo,

time: 35.6 us -> 35.1 us (0.986)
  Pallas kernels: 4.03 us -> 3.55 us
    pallas_call x5, Pallas kernels: 4.03 us -> 3.55 us  [run(): pl.pallas_call(kernel, out_shape=out_shape, in_specs=in_specs, out_specs=...]
where the time goes in v13:
time: 35.1 us; the launch traced here: 34.8 us
  blocking collectives  28.7 us (82%)
  Pallas kernels  3.55 us (10%)
  starting transfers between devices  1.17 us (3%)
  waiting for transfers between devices  0.71 us (2%)
  between operations  0.67 us (2%)
    all_to_all x2, blocking collectives, exchange(): lax.all_to_all(pieces, axes, split_axis=0, concat_axis=0, axis_index_grou...  28.7 us
    pallas_call x5, Pallas kernels, run(): pl.pallas_call(kernel, out_shape=out_shape, in_specs=in_specs, out_specs=...  3.55 us
    ppermute x4, starting transfers between devices, with_partner(): return lax.ppermute(value, 'core', [(0, 1), (1, 0)])  1.17 us
    ppermute x4, waiting for transfers between devices, with_partner(): return lax.ppermute(value, 'core', [(0, 1), (1, 0)])  0.71 us
  transfers between devices with their start and end apart: 4, of which 1 were waited for; matrix products, arithmetic and copies ran while one was open for 0% of the time, Pallas kernels for 2%

profile of v13, /device:TPU:0, one launch (start us, length us, event | category | flops | bytes accessed | tf_op | source)
XLA Modules:
  0.0 34.8 jit_solution(4182657056556109586)
XLA Ops:
  0.6 1.3 %shard_map.76 = (bf16[16,8,640]{2,1,0:T(8,128)(2,1)S(1)}, bf16[4,128,512]{2,1,0:T(8,128)(2,1)S(1)}, bf16[4,128,512]{2,1,0:T(8,128)(2,1)S(1)}, s32[1,128]{1,0:T(1,128)S(1)}) custom-call(bf16[8,512]{1,0:T(8,128)(2,1)} %features.3, s32[1,64]{1,0:T(1,128)} %bitcast.13, bf16[4,128,512]{2,1,0:T(8,128)(2,1)} %bitcast.12, s32[1,4]{1,0:T(1,128)} %bitcast.14, ...), custom_call_target="tpu_custom_call" | custom-call | bytes 1745696 | tf_op jit(solution)/shard_map/pallas_call | solution.py:37
  1.9 0.5 %collective-permute-start = (bf16[4,128,512]{2,1,0:T(8,128)(2,1)S(1)}, bf16[4,128,512]{2,1,0:T(8,128)(2,1)S(1)}, u32[]{:S(2)}, u32[]{:S(2)}) collective-permute-start(bf16[4,128,512]{2,1,0:T(8,128)(2,1)S(1)} %get-tuple-element.18.own_blocks), channel_id=1, source_target_pairs={{0,1},{1,0},{2,3},{3,2},{4,5},{5,4},{6,7},{7,6},{8,9},{9,8},{10,11... | collective-permute-start | bytes 1572872 | tf_op jit(solution)/shard_map/ppermute | solution.py:294
  2.4 15.3 %all_to_all.10 = bf16[16,8,640]{2,1,0:T(8,128)(2,1)S(1)} all-to-all(bf16[16,8,640]{2,1,0:T(8,128)(2,1)S(1)} %get-tuple-element.17), channel_id=1, replica_groups={{8,10,12,14,16,18,20,22,24,26,28,30,0,2,4,6},{9,11,13,15,17,19,21,23,25..., dimensions={0} | all-to-all | bytes 327680 | tf_op jit(solution)/shard_map/all_to_all | solution.py:282
  17.7 0.0 collective-permute-start.2
  17.7 0.0 collective-permute-done.pair_blocks
  17.7 0.5 %shard_map.77 = (f32[128,128]{1,0:T(8,128)S(1)}, f32[128,128]{1,0:T(8,128)S(1)}, f32[2,128,128]{2,1,0:T(8,128)S(1)}, f32[2,128]{1,0:T(2,128)S(1)}) custom-call(bf16[128,640]{1,0:T(8,128)(2,1)S(1)} %bitcast.9, bf16[4,128,512]{2,1,0:T(8,128)(2,1)S(1)} %get-tuple-element.18.own_blocks, bf16[4,128,512]{2,1,0:T(8,128)(2,1)S(1)} %collective-permute-done.pair_blocks), custom_call_target="tpu_custom_call" | custom-call | bytes 1475584 | tf_op jit(solution)/shard_map/pallas_call | solution.py:37
  18.2 0.6 %collective-permute-start.3 = (f32[128,128]{1,0:T(8,128)S(1)}, f32[128,128]{1,0:T(8,128)S(1)}, u32[]{:S(2)}, u32[]{:S(2)}) collective-permute-start(f32[128,128]{1,0:T(8,128)S(1)} %get-tuple-element.20.pair_expo), channel_id=1, source_target_pairs={{0,1},{1,0},{2,3},{3,2},{4,5},{5,4},{6,7},{7,6},{8,9},{9,8},{10,11... | collective-permute-start | bytes 196616 | tf_op jit(solution)/shard_map/ppermute | solution.py:294
  18.7 0.1 collective-permute-start.1
  18.8 0.3 shard_map.78
  19.2 0.0 collective-permute-done.2.other_packed
  19.2 0.7 %collective-permute-done.1.other_sums = f32[2,128]{1,0:T(2,128)S(1)} collective-permute-done((f32[2,128]{1,0:T(2,128)S(1)}, f32[2,128]{1,0:T(2,128)S(1)}, u32[]{:S(2)}, u32[]{:S(2)}) %collective-permute-start.1) | collective-permute-done | bytes 1056 | tf_op jit(solution)/shard_map/ppermute | solution.py:294
  19.9 0.0 collective-permute-done.3.other_expo
  19.9 0.0 copy-start
  19.9 13.4 %all_to_all.11.received = bf16[16,8,1152]{2,1,0:T(8,128)(2,1)S(1)} all-to-all(bf16[16,8,1152]{2,1,0:T(8,128)(2,1)S(1)} %bitcast.11), channel_id=1, replica_groups={{8,10,12,14,16,18,20,22,24,26,28,30,0,2,4,6},{9,11,13,15,17,19,21,23,25..., dimensions={0} | all-to-all | bytes 589824 | tf_op jit(solution)/shard_map/all_to_all | solution.py:282
  33.4 0.0 copy-done
  33.4 1.4 %shard_map.80 = (f32[4,128,512]{2,1,0:T(8,128)}, f32[8,512]{1,0:T(8,128)}, f32[1,8]{1,0:T(1,128)}) custom-call(s32[1,128]{1,0:T(1,128)S(1)} %get-tuple-element.16.named, bf16[16,8,1152]{2,1,0:T(8,128)(2,1)S(1)} %all_to_all.11.received, f32[128,128]{1,0:T(8,128)S(1)} %get-tuple-element.19.own_expo, f32[128,128]{1,0:T(8,128)S(1)} %collective-permute-done.3.other_expo, ...), custom_call_target="tpu_custom_call" | custom-call | bytes 2417184 | tf_op jit(solution)/shard_map/pallas_call | solution.py:37
  (1 shorter events, 0.0 us)
Async XLA Ops:
  1.9 15.8 %collective-permute-start = (bf16[4,128,512]{2,1,0:T(8,128)(2,1)S(1)}, bf16[4,128,512]{2,1,0:T(8,128)(2,1)S(1)}, u32[]{:S(2)}, u32[]{:S(2)}) collective-permute-start(bf16[4,128,512]{2,1,0:T(8,128)(2,1)S(1)} %get-tuple-element.18.own_blocks), channel_id=1, source_target_pairs={{0,1},{1,0},{2,3},{3,2},{4,5},{5,4},{6,7},{7,6},{8,9},{9,8},{10,11... | collective-permute-start | bytes 1572872 | tf_op jit(solution)/shard_map/ppermute | solution.py:294
  17.7 1.5 %collective-permute-start.2 = (bf16[128,640]{1,0:T(8,128)(2,1)S(1)}, bf16[128,640]{1,0:T(8,128)(2,1)S(1)}, u32[]{:S(2)}, u32[]{:S(2)}) collective-permute-start(bf16[128,640]{1,0:T(8,128)(2,1)S(1)} %bitcast.8), channel_id=1, source_target_pairs={{0,1},{1,0},{2,3},{3,2},{4,5},{5,4},{6,7},{7,6},{8,9},{9,8},{10,11... | collective-permute-start | bytes 491528 | tf_op jit(solution)/shard_map/ppermute | solution.py:294
  18.2 1.7 %collective-permute-start.3 = (f32[128,128]{1,0:T(8,128)S(1)}, f32[128,128]{1,0:T(8,128)S(1)}, u32[]{:S(2)}, u32[]{:S(2)}) collective-permute-start(f32[128,128]{1,0:T(8,128)S(1)} %get-tuple-element.20.pair_expo), channel_id=1, source_target_pairs={{0,1},{1,0},{2,3},{3,2},{4,5},{5,4},{6,7},{7,6},{8,9},{9,8},{10,11... | collective-permute-start | bytes 196616 | tf_op jit(solution)/shard_map/ppermute | solution.py:294
  18.7 1.1 %collective-permute-start.1 = (f32[2,128]{1,0:T(2,128)S(1)}, f32[2,128]{1,0:T(2,128)S(1)}, u32[]{:S(2)}, u32[]{:S(2)}) collective-permute-start(f32[2,128]{1,0:T(2,128)S(1)} %get-tuple-element.24.own_sums), channel_id=1, source_target_pairs={{0,1},{1,0},{2,3},{3,2},{4,5},{5,4},{6,7},{7,6},{8,9},{9,8},{10,11... | collective-permute-start | bytes 3080 | tf_op jit(solution)/shard_map/ppermute | solution.py:294
  19.9 13.5 %copy-start = (bf16[8,512]{1,0:T(8,128)(2,1)S(1)}, bf16[8,512]{1,0:T(8,128)(2,1)}, u32[]{:S(2)}) copy-start(bf16[8,512]{1,0:T(8,128)(2,1)} %features.3) | copy-start | bytes 24580

commit v14 on v13

--- a/solution.py
+++ b/solution.py
@@ -103,12 +103,17 @@
     )
     for move in moves[2:]:
         move.wait()
-    groups = blocks_out.shape[0]
-    named_out[...] = select([held_ids[0, group_at(g)] for g in range(groups)], 1)
-    for g in range(groups):
-        group = group_at(g)
-        block = centres_out[held_ids[0, group]]
-        blocks_out[g] = jnp.where(held_listed[0, group] > 0, block, jnp.full_like(block, UNLISTED))
+    groups, held = blocks_out.shape[0], centres_out.shape[0]
+    order = [group_at(g) for g in range(groups)]
+    named = [held_ids[:, group : group + 1] for group in order]
+    named_out[...] = select(named, 1)
+    for g, group in enumerate(order):
+        block = jnp.full(blocks_out.shape[1:], UNLISTED, jnp.bfloat16)
+        block_id = jnp.where(held_listed[:, group : group + 1] > 0, named[g], -1)
+        for b in range(held):
+            here = jnp.broadcast_to(block_id, (BLK, 1)) == b
+            block = jnp.where(here, centres_out[b], block)
+        blocks_out[g] = block
 
 
 def group_at(place):
@@ -129,7 +134,7 @@
     return out
 
 
-def exponentials(packed, own_blocks, pair_blocks, expo_out, pair_expo_out, inverse_out, sums_out):
+def exponentials(packed, own_blocks, pair_blocks, expo_out, inverse_out, swap_out):
     group, core = lax.axis_index("group"), lax.axis_index("core")
     groups, _, width = own_blocks.shape
     units = packed[:, :width]
@@ -139,7 +144,7 @@
     labels = digits[0:1] + (digits[1:2] << 7) + (digits[2:3] << 14)
     rest = jnp.zeros((1, 128), jnp.float32)
     at_label = jnp.zeros((1, 128), jnp.float32)
-    for k, (blocks, out) in enumerate(((own_blocks, expo_out), (pair_blocks, pair_expo_out))):
+    for k, (blocks, out) in enumerate(((own_blocks, expo_out), (pair_blocks, swap_out))):
         member = 2 * lax.axis_index("chip") + (core if k == 0 else 1 - core)
         first = (member * groups + group) * BLK
         onehot = lax.broadcasted_iota(jnp.int32, (BLK, 128), 0) == labels - first
@@ -150,18 +155,18 @@
         cosine = inverse * select([contract(blocks[g], units, 1, 1) for g in range(groups)], BLK)
         expo = jnp.exp(logit_scale * (cosine - jnp.where(onehot, cos_margin, 0.0)))
         expo = jnp.where(inverse > 0.0, expo, 0.0)
-        out[...] = jnp.where(onehot, -1.0, expo)
+        out[:BLK, :] = jnp.where(onehot, -1.0, expo)
         rest += jnp.sum(jnp.where(onehot, 0.0, expo), axis=0, keepdims=True)
         at_label += jnp.sum(jnp.where(onehot, expo, 0.0), axis=0, keepdims=True)
-    sums_out[0:1, :] = rest
-    sums_out[1:2, :] = at_label
-
-
-def shares(own_expo, pair_expo, inverse, own_blocks, pair_blocks, centres, shares_out, norms_out):
+    row = lax.broadcasted_iota(jnp.int32, (8, 128), 0)
+    swap_out[BLK:, :] = jnp.where(row == 0, rest, jnp.where(row == 1, at_label, 0.0))
+
+
+def shares(own_expo, swap, inverse, own_blocks, pair_blocks, centres, shares_out, norms_out):
     groups, _, width = own_blocks.shape
     per_group = 128 // groups
     others, label = [], []
-    for k, expo in enumerate((own_expo[...], pair_expo[...])):
+    for k, expo in enumerate((own_expo[...], swap[:BLK, :])):
         others.append((jnp.maximum(expo, 0.0) * inverse[k]).T.astype(jnp.bfloat16))
         label.append(jnp.where(expo < 0.0, 1.0, 0.0).T.astype(jnp.bfloat16))
     others = jnp.concatenate(others, axis=1)
@@ -179,11 +184,11 @@
     )
 
 
-def with_sums(shares, own_sums, other_sums, other_packed, other_expo, sent_out):
-    del other_packed, other_expo
+def with_sums(shares, swap, swapped, other_packed, sent_out):
+    del other_packed
     rows, wide = shares.shape
     sent_out[:, :wide] = shares[...]
-    total = jnp.concatenate([own_sums[...], other_sums[...]], axis=0)
+    total = jnp.concatenate([swap[BLK : BLK + 2, :], swapped[BLK : BLK + 2, :]], axis=0)
     high = total.astype(jnp.bfloat16)
     low = (total - high.astype(jnp.float32)).astype(jnp.bfloat16)
     tile = jnp.concatenate([high.astype(jnp.float32), low.astype(jnp.float32)], axis=0)
@@ -195,7 +200,7 @@
     named,
     received,
     own_expo,
-    other_expo,
+    swapped,
     own_packed,
     other_packed,
     features,
@@ -224,7 +229,7 @@
     own_scale = logit_scale / (own_rest + own_label)
     other_scale = logit_scale / (other_rest + other_label)
     own = own_expo[...]
-    other = other_expo[...]
+    other = swapped[:BLK, :]
     own = jnp.where(own < 0.0, -own_rest, own) * own_scale
     other = jnp.where(other < 0.0, -other_rest, other) * other_scale
     weights = jnp.concatenate([own, other], axis=1)
@@ -325,35 +330,29 @@
         scratch=[
             pltpu.VMEM(features.shape, features.dtype),
             pltpu.VMEM((1, labels.shape[0]), labels.dtype),
-            pltpu.SMEM((1, groups), block_ids.dtype),
-            pltpu.SMEM((1, groups), listed.dtype),
+            pltpu.VMEM((1, groups), block_ids.dtype),
+            pltpu.VMEM((1, groups), listed.dtype),
             pltpu.SemaphoreType.DMA((4 + held,)),
         ],
     )
     pair_blocks = with_partner(own_blocks)
     own_packed = exchange_chips(copies).reshape(half, width + 128)
     other_packed = with_partner(own_packed)
-    own_expo, pair_expo, inverse, sums = run(
+    own_expo, inverse, swap = run(
         exponentials,
-        (
-            shape((BLK, half), f32),
-            shape((BLK, half), f32),
-            shape((2, BLK, 128), f32),
-            shape((2, half), f32),
-        ),
+        (shape((BLK, half), f32), shape((2, BLK, 128), f32), shape((BLK + 8, half), f32)),
         [VMEM] * 3,
         own_packed,
         own_blocks,
         pair_blocks,
     )
-    other_expo = with_partner(pair_expo)
-    other_sums = with_partner(sums)
+    swapped = with_partner(swap)
     going, norms = run(
         shares,
         (shape((half, 2 * width), bf16), shape((BLK, 128), f32)),
         [VMEM] * 6,
         own_expo,
-        pair_expo,
+        swap,
         inverse,
         own_blocks,
         pair_blocks,
@@ -362,12 +361,11 @@
     sent = run(
         with_sums,
         shape((half, 2 * width + 128), bf16),
-        [VMEM] * 3 + [pl.BlockSpec(memory_space=pl.ANY)] * 2,
+        [VMEM] * 3 + [pl.BlockSpec(memory_space=pl.ANY)],
         going,
-        sums,
-        other_sums,
+        swap,
+        swapped,
         other_packed,
-        other_expo,
     )
     received = exchange_chips(sent.reshape(chips, tok_dev, 2 * width + 128))
     outs = (shape((held, BLK, width), f32), shape((tok_dev, width), f32), shape((1, tok_dev), f32))
@@ -378,7 +376,7 @@
         named,
         received,
         own_expo,
-        other_expo,
+        swapped,
         own_packed,
         other_packed,
         features,

time: 35.1 us -> 35.2 us (level)
    ppermute x4 -> x3, waiting for transfers between devices: 0.71 us -> 0.54 us  [with_partner(): return lax.ppermute(value, 'core', [(0, 1), (1, 0)])]
    ppermute x4 -> x3, starting transfers between devices: 1.17 us -> 1.09 us  [with_partner(): return lax.ppermute(value, 'core', [(0, 1), (1, 0)])]
  transfers between devices with their start and end apart: 4 -> 3, of which waited for: 1 -> 1; matrix products, arithmetic and copies ran while one was open for 0% -> 0% of each run, Pallas kernels for 2% -> 2%
where the time goes in v14:
time: 35.2 us; the launch traced here: 35 us
  blocking collectives  28.9 us (82%)
  Pallas kernels  3.8 us (11%)
  starting transfers between devices  1.09 us (3%)
  between operations  0.67 us (2%)
  waiting for transfers between devices  0.54 us (2%)
    all_to_all x2, blocking collectives, exchange(): lax.all_to_all(pieces, axes, split_axis=0, concat_axis=0, axis_index_grou...  28.9 us
    pallas_call x5, Pallas kernels, run(): pl.pallas_call(kernel, out_shape=out_shape, in_specs=in_specs, out_specs=...  3.8 us
    ppermute x3, starting transfers between devices, with_partner(): return lax.ppermute(value, 'core', [(0, 1), (1, 0)])  1.09 us
  transfers between devices with their start and end apart: 3, of which 1 were waited for; matrix products, arithmetic and copies ran while one was open for 0% of the time, Pallas kernels for 2%

profile of v14, /device:TPU:0, one launch (start us, length us, event | category | flops | bytes accessed | tf_op | source)
XLA Modules:
  0.0 35.0 jit_solution(11821049407715140860)
XLA Ops:
  0.6 1.4 %shard_map.76 = (bf16[16,8,640]{2,1,0:T(8,128)(2,1)S(1)}, bf16[4,128,512]{2,1,0:T(8,128)(2,1)S(1)}, bf16[4,128,512]{2,1,0:T(8,128)(2,1)S(1)}, s32[1,128]{1,0:T(1,128)S(1)}) custom-call(bf16[8,512]{1,0:T(8,128)(2,1)} %features.3, s32[1,64]{1,0:T(1,128)} %bitcast.13, bf16[4,128,512]{2,1,0:T(8,128)(2,1)} %bitcast.12, s32[1,4]{1,0:T(1,128)} %bitcast.14, ...), custom_call_target="tpu_custom_call" | custom-call | bytes 1745696 | tf_op jit(solution)/shard_map/pallas_call | solution.py:37
  2.1 0.5 %collective-permute-start = (bf16[4,128,512]{2,1,0:T(8,128)(2,1)S(1)}, bf16[4,128,512]{2,1,0:T(8,128)(2,1)S(1)}, u32[]{:S(2)}, u32[]{:S(2)}) collective-permute-start(bf16[4,128,512]{2,1,0:T(8,128)(2,1)S(1)} %get-tuple-element.17.own_blocks), channel_id=1, source_target_pairs={{0,1},{1,0},{2,3},{3,2},{4,5},{5,4},{6,7},{7,6},{8,9},{9,8},{10,11... | collective-permute-start | bytes 1572872 | tf_op jit(solution)/shard_map/ppermute | solution.py:299
  2.6 15.3 %all_to_all.10 = bf16[16,8,640]{2,1,0:T(8,128)(2,1)S(1)} all-to-all(bf16[16,8,640]{2,1,0:T(8,128)(2,1)S(1)} %get-tuple-element.16), channel_id=1, replica_groups={{8,10,12,14,16,18,20,22,24,26,28,30,0,2,4,6},{9,11,13,15,17,19,21,23,25..., dimensions={0} | all-to-all | bytes 327680 | tf_op jit(solution)/shard_map/all_to_all | solution.py:287
  17.9 0.0 collective-permute-start.2
  17.9 0.0 collective-permute-done.pair_blocks
  17.9 0.5 %shard_map.77 = (f32[128,128]{1,0:T(8,128)S(1)}, f32[2,128,128]{2,1,0:T(8,128)S(1)}, f32[136,128]{1,0:T(8,128)S(1)}) custom-call(bf16[128,640]{1,0:T(8,128)(2,1)S(1)} %bitcast.9, bf16[4,128,512]{2,1,0:T(8,128)(2,1)S(1)} %get-tuple-element.17.own_blocks, bf16[4,128,512]{2,1,0:T(8,128)(2,1)S(1)} %collective-permute-done.pair_blocks), custom_call_target="tpu_custom_call" | custom-call | bytes 1478656 | tf_op jit(solution)/shard_map/pallas_call | solution.py:37
  18.4 0.6 %collective-permute-start.1 = (f32[136,128]{1,0:T(8,128)S(1)}, f32[136,128]{1,0:T(8,128)S(1)}, u32[]{:S(2)}, u32[]{:S(2)}) collective-permute-start(f32[136,128]{1,0:T(8,128)S(1)} %get-tuple-element.19.swap), channel_id=1, source_target_pairs={{0,1},{1,0},{2,3},{3,2},{4,5},{5,4},{6,7},{7,6},{8,9},{9,8},{10,11... | collective-permute-start | bytes 208904 | tf_op jit(solution)/shard_map/ppermute | solution.py:299
  19.0 0.4 %shard_map.78 = (bf16[128,1024]{1,0:T(8,128)(2,1)S(1)}, f32[128,128]{1,0:T(8,128)S(1)}) custom-call(f32[128,128]{1,0:T(8,128)S(1)} %get-tuple-element.18.own_expo, f32[136,128]{1,0:T(8,128)S(1)} %get-tuple-element.19.swap, f32[2,128,128]{2,1,0:T(8,128)S(1)} %get-tuple-element.20.inverse, bf16[4,128,512]{2,1,0:T(8,128)(2,1)S(1)} %get-tuple-element.17.own_blocks, ...), custom_call_target="tpu_custom_call" | custom-call | bytes 2166784 | tf_op jit(solution)/shard_map/pallas_call | solution.py:37
  19.3 0.0 collective-permute-done.2.other_packed
  19.3 0.5 %collective-permute-done.1.swapped = f32[136,128]{1,0:T(8,128)S(1)} collective-permute-done((f32[136,128]{1,0:T(8,128)S(1)}, f32[136,128]{1,0:T(8,128)S(1)}, u32[]{:S(2)}, u32[]{:S(2)}) %collective-permute-start.1) | collective-permute-done | bytes 69664 | tf_op jit(solution)/shard_map/ppermute | solution.py:299
  19.9 0.0 copy-start
  19.9 13.6 %all_to_all.11.received = bf16[16,8,1152]{2,1,0:T(8,128)(2,1)S(1)} all-to-all(bf16[16,8,1152]{2,1,0:T(8,128)(2,1)S(1)} %bitcast.11), channel_id=1, replica_groups={{8,10,12,14,16,18,20,22,24,26,28,30,0,2,4,6},{9,11,13,15,17,19,21,23,25..., dimensions={0} | all-to-all | bytes 589824 | tf_op jit(solution)/shard_map/all_to_all | solution.py:287
  33.5 0.0 copy-done
  33.5 1.4 %shard_map.80 = (f32[4,128,512]{2,1,0:T(8,128)}, f32[8,512]{1,0:T(8,128)}, f32[1,8]{1,0:T(1,128)}) custom-call(s32[1,128]{1,0:T(1,128)S(1)} %get-tuple-element.15.named, bf16[16,8,1152]{2,1,0:T(8,128)(2,1)S(1)} %all_to_all.11.received, f32[128,128]{1,0:T(8,128)S(1)} %get-tuple-element.18.own_expo, f32[136,128]{1,0:T(8,128)S(1)} %collective-permute-done.1.swapped, ...), custom_call_target="tpu_custom_call" | custom-call | bytes 2421280 | tf_op jit(solution)/shard_map/pallas_call | solution.py:37
  (1 shorter events, 0.0 us)
Async XLA Ops:
  2.1 15.8 %collective-permute-start = (bf16[4,128,512]{2,1,0:T(8,128)(2,1)S(1)}, bf16[4,128,512]{2,1,0:T(8,128)(2,1)S(1)}, u32[]{:S(2)}, u32[]{:S(2)}) collective-permute-start(bf16[4,128,512]{2,1,0:T(8,128)(2,1)S(1)} %get-tuple-element.17.own_blocks), channel_id=1, source_target_pairs={{0,1},{1,0},{2,3},{3,2},{4,5},{5,4},{6,7},{7,6},{8,9},{9,8},{10,11... | collective-permute-start | bytes 1572872 | tf_op jit(solution)/shard_map/ppermute | solution.py:299
  17.9 1.5 %collective-permute-start.2 = (bf16[128,640]{1,0:T(8,128)(2,1)S(1)}, bf16[128,640]{1,0:T(8,128)(2,1)S(1)}, u32[]{:S(2)}, u32[]{:S(2)}) collective-permute-start(bf16[128,640]{1,0:T(8,128)(2,1)S(1)} %bitcast.8), channel_id=1, source_target_pairs={{0,1},{1,0},{2,3},{3,2},{4,5},{5,4},{6,7},{7,6},{8,9},{9,8},{10,11... | collective-permute-start | bytes 491528 | tf_op jit(solution)/shard_map/ppermute | solution.py:299
  18.4 1.5 %collective-permute-start.1 = (f32[136,128]{1,0:T(8,128)S(1)}, f32[136,128]{1,0:T(8,128)S(1)}, u32[]{:S(2)}, u32[]{:S(2)}) collective-permute-start(f32[136,128]{1,0:T(8,128)S(1)} %get-tuple-element.19.swap), channel_id=1, source_target_pairs={{0,1},{1,0},{2,3},{3,2},{4,5},{5,4},{6,7},{7,6},{8,9},{9,8},{10,11... | collective-permute-start | bytes 208904 | tf_op jit(solution)/shard_map/ppermute | solution.py:299
  19.9 13.6 %copy-start = (bf16[8,512]{1,0:T(8,128)(2,1)S(1)}, bf16[8,512]{1,0:T(8,128)(2,1)}, u32[]{:S(2)}) copy-start(bf16[8,512]{1,0:T(8,128)(2,1)} %features.3) | copy-start | bytes 24580

commit v15 on v14

--- a/solution.py
+++ b/solution.py
@@ -12,7 +12,6 @@
 logit_scale = 32.0
 cos_margin = 0.35
 norm_epsilon = 1e-06
-FIRST_GROUP = 1
 UNLISTED = 1e19
 
 VMEM = pl.BlockSpec(memory_space=pltpu.VMEM)
@@ -103,27 +102,22 @@
     )
     for move in moves[2:]:
         move.wait()
-    groups, held = blocks_out.shape[0], centres_out.shape[0]
-    order = [group_at(g) for g in range(groups)]
-    named = [held_ids[:, group : group + 1] for group in order]
-    named_out[...] = select(named, 1)
-    for g, group in enumerate(order):
-        block = jnp.full(blocks_out.shape[1:], UNLISTED, jnp.bfloat16)
-        block_id = jnp.where(held_listed[:, group : group + 1] > 0, named[g], -1)
-        for b in range(held):
-            here = jnp.broadcast_to(block_id, (BLK, 1)) == b
-            block = jnp.where(here, centres_out[b], block)
-        blocks_out[g] = block
+    groups = blocks_out.shape[0]
+    named_out[...] = select([held_ids[0, group_at(g)] for g in range(groups)], 1)
+    for g in range(groups):
+        group = group_at(g)
+        block = centres_out[held_ids[0, group]]
+        blocks_out[g] = jnp.where(held_listed[0, group] > 0, block, jnp.full_like(block, UNLISTED))
 
 
 def group_at(place):
-    return (place + FIRST_GROUP) % lax.axis_size("group")
+    return lax.axis_size("group") - 1 - place
 
 
 def own_place():
-    groups = lax.axis_size("group")
-    group = lax.rem(lax.axis_index("group") + groups - FIRST_GROUP, groups)
-    return group * lax.axis_size("chip") + lax.axis_index("chip")
+    chips = lax.axis_size("chip")
+    own = lax.axis_index("group") * chips + lax.axis_index("chip")
+    return lax.axis_size("group") * chips - 1 - own
 
 
 def select(parts, rows):
@@ -290,9 +284,7 @@
 
 
 def exchange_chips(pieces):
-    groups, chips = lax.axis_size("group"), lax.axis_size("chip")
-    order = [group_at(g) * chips + chip for g in range(groups) for chip in range(chips)]
-    return exchange(pieces, CHIPS, [order])
+    return exchange(pieces, CHIPS, [list(reversed(range(pieces.shape[0])))])
 
 
 def with_partner(value):
@@ -330,8 +322,8 @@
         scratch=[
             pltpu.VMEM(features.shape, features.dtype),
             pltpu.VMEM((1, labels.shape[0]), labels.dtype),
-            pltpu.VMEM((1, groups), block_ids.dtype),
-            pltpu.VMEM((1, groups), listed.dtype),
+            pltpu.SMEM((1, groups), block_ids.dtype),
+            pltpu.SMEM((1, groups), listed.dtype),
             pltpu.SemaphoreType.DMA((4 + held,)),
         ],
     )

time: 35.2 us -> 34.8 us (0.989)
  transfers between devices with their start and end apart: 3 -> 3, of which waited for: 1 -> 1; matrix products, arithmetic and copies ran while one was open for 0% -> 0% of each run, Pallas kernels for 2% -> 3%
where the time goes in v15:
time: 34.8 us; the launch traced here: 34.6 us
  blocking collectives  28.7 us (82%)
  Pallas kernels  3.57 us (10%)
  starting transfers between devices  1.09 us (3%)
  between operations  0.67 us (2%)
  waiting for transfers between devices  0.54 us (2%)
    all_to_all x2, blocking collectives, exchange(): lax.all_to_all(pieces, axes, split_axis=0, concat_axis=0, axis_index_grou...  28.7 us
    pallas_call x5, Pallas kernels, run(): pl.pallas_call(kernel, out_shape=out_shape, in_specs=in_specs, out_specs=...  3.57 us
    ppermute x3, starting transfers between devices, with_partner(): return lax.ppermute(value, 'core', [(0, 1), (1, 0)])  1.09 us
  transfers between devices with their start and end apart: 3, of which 1 were waited for; matrix products, arithmetic and copies ran while one was open for 0% of the time, Pallas kernels for 3%

profile of v15, /device:TPU:0, one launch (start us, length us, event | category | flops | bytes accessed | tf_op | source)
XLA Modules:
  0.0 34.6 jit_solution(3773331802165503762)
XLA Ops:
  0.6 1.3 %shard_map.76 = (bf16[16,8,640]{2,1,0:T(8,128)(2,1)S(1)}, bf16[4,128,512]{2,1,0:T(8,128)(2,1)S(1)}, bf16[4,128,512]{2,1,0:T(8,128)(2,1)S(1)}, s32[1,128]{1,0:T(1,128)S(1)}) custom-call(bf16[8,512]{1,0:T(8,128)(2,1)} %features.3, s32[1,64]{1,0:T(1,128)} %bitcast.13, bf16[4,128,512]{2,1,0:T(8,128)(2,1)} %bitcast.12, s32[1,4]{1,0:T(1,128)} %bitcast.14, ...), custom_call_target="tpu_custom_call" | custom-call | bytes 1745696 | tf_op jit(solution)/shard_map/pallas_call | solution.py:36
  1.9 0.5 %collective-permute-start = (bf16[4,128,512]{2,1,0:T(8,128)(2,1)S(1)}, bf16[4,128,512]{2,1,0:T(8,128)(2,1)S(1)}, u32[]{:S(2)}, u32[]{:S(2)}) collective-permute-start(bf16[4,128,512]{2,1,0:T(8,128)(2,1)S(1)} %get-tuple-element.17.own_blocks), channel_id=1, source_target_pairs={{0,1},{1,0},{2,3},{3,2},{4,5},{5,4},{6,7},{7,6},{8,9},{9,8},{10,11... | collective-permute-start | bytes 1572872 | tf_op jit(solution)/shard_map/ppermute | solution.py:291
  2.4 14.2 %all_to_all.10 = bf16[16,8,640]{2,1,0:T(8,128)(2,1)S(1)} all-to-all(bf16[16,8,640]{2,1,0:T(8,128)(2,1)S(1)} %get-tuple-element.16), channel_id=1, replica_groups={{30,28,26,24,22,20,18,16,14,12,10,8,6,4,2,0},{31,29,27,25,23,21,19,17,1..., dimensions={0} | all-to-all | bytes 327680 | tf_op jit(solution)/shard_map/all_to_all | solution.py:281
  16.7 0.0 collective-permute-start.2
  16.7 0.0 collective-permute-done.pair_blocks
  16.7 0.5 %shard_map.77 = (f32[128,128]{1,0:T(8,128)S(1)}, f32[2,128,128]{2,1,0:T(8,128)S(1)}, f32[136,128]{1,0:T(8,128)S(1)}) custom-call(bf16[128,640]{1,0:T(8,128)(2,1)S(1)} %bitcast.9, bf16[4,128,512]{2,1,0:T(8,128)(2,1)S(1)} %get-tuple-element.17.own_blocks, bf16[4,128,512]{2,1,0:T(8,128)(2,1)S(1)} %collective-permute-done.pair_blocks), custom_call_target="tpu_custom_call" | custom-call | bytes 1478656 | tf_op jit(solution)/shard_map/pallas_call | solution.py:36
  17.2 0.6 %collective-permute-start.1 = (f32[136,128]{1,0:T(8,128)S(1)}, f32[136,128]{1,0:T(8,128)S(1)}, u32[]{:S(2)}, u32[]{:S(2)}) collective-permute-start(f32[136,128]{1,0:T(8,128)S(1)} %get-tuple-element.19.swap), channel_id=1, source_target_pairs={{0,1},{1,0},{2,3},{3,2},{4,5},{5,4},{6,7},{7,6},{8,9},{9,8},{10,11... | collective-permute-start | bytes 208904 | tf_op jit(solution)/shard_map/ppermute | solution.py:291
  17.8 0.4 %shard_map.78 = (bf16[128,1024]{1,0:T(8,128)(2,1)S(1)}, f32[128,128]{1,0:T(8,128)S(1)}) custom-call(f32[128,128]{1,0:T(8,128)S(1)} %get-tuple-element.18.own_expo, f32[136,128]{1,0:T(8,128)S(1)} %get-tuple-element.19.swap, f32[2,128,128]{2,1,0:T(8,128)S(1)} %get-tuple-element.20.inverse, bf16[4,128,512]{2,1,0:T(8,128)(2,1)S(1)} %get-tuple-element.17.own_blocks, ...), custom_call_target="tpu_custom_call" | custom-call | bytes 2166784 | tf_op jit(solution)/shard_map/pallas_call | solution.py:36
  18.1 0.0 collective-permute-done.2.other_packed
  18.1 0.5 %collective-permute-done.1.swapped = f32[136,128]{1,0:T(8,128)S(1)} collective-permute-done((f32[136,128]{1,0:T(8,128)S(1)}, f32[136,128]{1,0:T(8,128)S(1)}, u32[]{:S(2)}, u32[]{:S(2)}) %collective-permute-start.1) | collective-permute-done | bytes 69664 | tf_op jit(solution)/shard_map/ppermute | solution.py:291
  18.7 0.0 copy-start
  18.7 14.4 %all_to_all.11.received = bf16[16,8,1152]{2,1,0:T(8,128)(2,1)S(1)} all-to-all(bf16[16,8,1152]{2,1,0:T(8,128)(2,1)S(1)} %bitcast.11), channel_id=1, replica_groups={{30,28,26,24,22,20,18,16,14,12,10,8,6,4,2,0},{31,29,27,25,23,21,19,17,1..., dimensions={0} | all-to-all | bytes 589824 | tf_op jit(solution)/shard_map/all_to_all | solution.py:281
  33.1 0.0 copy-done
  33.1 1.4 %shard_map.80 = (f32[4,128,512]{2,1,0:T(8,128)}, f32[8,512]{1,0:T(8,128)}, f32[1,8]{1,0:T(1,128)}) custom-call(s32[1,128]{1,0:T(1,128)S(1)} %get-tuple-element.15.named, bf16[16,8,1152]{2,1,0:T(8,128)(2,1)S(1)} %all_to_all.11.received, f32[128,128]{1,0:T(8,128)S(1)} %get-tuple-element.18.own_expo, f32[136,128]{1,0:T(8,128)S(1)} %collective-permute-done.1.swapped, ...), custom_call_target="tpu_custom_call" | custom-call | bytes 2421280 | tf_op jit(solution)/shard_map/pallas_call | solution.py:36
  (1 shorter events, 0.0 us)
Async XLA Ops:
  1.9 14.8 %collective-permute-start = (bf16[4,128,512]{2,1,0:T(8,128)(2,1)S(1)}, bf16[4,128,512]{2,1,0:T(8,128)(2,1)S(1)}, u32[]{:S(2)}, u32[]{:S(2)}) collective-permute-start(bf16[4,128,512]{2,1,0:T(8,128)(2,1)S(1)} %get-tuple-element.17.own_blocks), channel_id=1, source_target_pairs={{0,1},{1,0},{2,3},{3,2},{4,5},{5,4},{6,7},{7,6},{8,9},{9,8},{10,11... | collective-permute-start | bytes 1572872 | tf_op jit(solution)/shard_map/ppermute | solution.py:291
  16.7 1.5 %collective-permute-start.2 = (bf16[128,640]{1,0:T(8,128)(2,1)S(1)}, bf16[128,640]{1,0:T(8,128)(2,1)S(1)}, u32[]{:S(2)}, u32[]{:S(2)}) collective-permute-start(bf16[128,640]{1,0:T(8,128)(2,1)S(1)} %bitcast.8), channel_id=1, source_target_pairs={{0,1},{1,0},{2,3},{3,2},{4,5},{5,4},{6,7},{7,6},{8,9},{9,8},{10,11... | collective-permute-start | bytes 491528 | tf_op jit(solution)/shard_map/ppermute | solution.py:291
  17.2 1.5 %collective-permute-start.1 = (f32[136,128]{1,0:T(8,128)S(1)}, f32[136,128]{1,0:T(8,128)S(1)}, u32[]{:S(2)}, u32[]{:S(2)}) collective-permute-start(f32[136,128]{1,0:T(8,128)S(1)} %get-tuple-element.19.swap), channel_id=1, source_target_pairs={{0,1},{1,0},{2,3},{3,2},{4,5},{5,4},{6,7},{7,6},{8,9},{9,8},{10,11... | collective-permute-start | bytes 208904 | tf_op jit(solution)/shard_map/ppermute | solution.py:291
  18.7 14.4 %copy-start = (bf16[8,512]{1,0:T(8,128)(2,1)S(1)}, bf16[8,512]{1,0:T(8,128)(2,1)}, u32[]{:S(2)}) copy-start(bf16[8,512]{1,0:T(8,128)(2,1)} %features.3) | copy-start | bytes 24580

commit v16 on v13

--- a/solution.py
+++ b/solution.py
@@ -12,7 +12,6 @@
 logit_scale = 32.0
 cos_margin = 0.35
 norm_epsilon = 1e-06
-FIRST_GROUP = 1
 UNLISTED = 1e19
 
 VMEM = pl.BlockSpec(memory_space=pltpu.VMEM)
@@ -112,13 +111,14 @@
 
 
 def group_at(place):
-    return (place + FIRST_GROUP) % lax.axis_size("group")
+    groups = lax.axis_size("group")
+    return (groups - 2 - place) % groups
 
 
 def own_place():
-    groups = lax.axis_size("group")
-    group = lax.rem(lax.axis_index("group") + groups - FIRST_GROUP, groups)
-    return group * lax.axis_size("chip") + lax.axis_index("chip")
+    groups, chips = lax.axis_size("group"), lax.axis_size("chip")
+    own = lax.axis_index("group") * chips + lax.axis_index("chip")
+    return lax.rem((2 * groups - 1) * chips - 1 - own, groups * chips)
 
 
 def select(parts, rows):
@@ -129,32 +129,55 @@
     return out
 
 
-def exponentials(packed, own_blocks, pair_blocks, expo_out, pair_expo_out, inverse_out, sums_out):
-    group, core = lax.axis_index("group"), lax.axis_index("core")
-    groups, _, width = own_blocks.shape
-    units = packed[:, :width]
+def exponentials(packed, core, blocks, inverse):
+    groups, _, width = blocks.shape
     digits = jnp.sum(
         packed[:, width:].astype(jnp.float32).reshape(128 // 8, 8, 128), axis=0
     ).astype(jnp.int32)
     labels = digits[0:1] + (digits[1:2] << 7) + (digits[2:3] << 14)
-    rest = jnp.zeros((1, 128), jnp.float32)
-    at_label = jnp.zeros((1, 128), jnp.float32)
-    for k, (blocks, out) in enumerate(((own_blocks, expo_out), (pair_blocks, pair_expo_out))):
-        member = 2 * lax.axis_index("chip") + (core if k == 0 else 1 - core)
-        first = (member * groups + group) * BLK
-        onehot = lax.broadcasted_iota(jnp.int32, (BLK, 128), 0) == labels - first
-        inverse = select(
-            [inverse_norm(blocks[g].astype(jnp.float32)) for g in range(groups)], BLK
-        )
+    member = 2 * lax.axis_index("chip") + core
+    first = (member * groups + lax.axis_index("group")) * BLK
+    onehot = lax.broadcasted_iota(jnp.int32, (BLK, 128), 0) == labels - first
+    units = packed[:, :width]
+    cosine = inverse * select([contract(blocks[g], units, 1, 1) for g in range(groups)], BLK)
+    expo = jnp.exp(logit_scale * (cosine - jnp.where(onehot, cos_margin, 0.0)))
+    return jnp.where(inverse > 0.0, expo, 0.0), onehot
+
+
+def sums(parts):
+    rest = [jnp.where(onehot, 0.0, expo) for expo, onehot in parts]
+    at_label = [jnp.where(onehot, expo, 0.0) for expo, onehot in parts]
+    return [jnp.sum(sum(part), axis=0, keepdims=True) for part in (rest, at_label)]
+
+
+def forward(packed, own_blocks, pair_blocks, own_expo_out, pair_expo_out, inverse_out, sums_out):
+    core = lax.axis_index("core")
+    parts = []
+    for k, (blocks, out) in enumerate(((own_blocks, own_expo_out), (pair_blocks, pair_expo_out))):
+        norms = [inverse_norm(blocks[g].astype(jnp.float32)) for g in range(blocks.shape[0])]
+        inverse = select(norms, BLK)
         inverse_out[k] = inverse
-        cosine = inverse * select([contract(blocks[g], units, 1, 1) for g in range(groups)], BLK)
-        expo = jnp.exp(logit_scale * (cosine - jnp.where(onehot, cos_margin, 0.0)))
-        expo = jnp.where(inverse > 0.0, expo, 0.0)
+        expo, onehot = exponentials(packed, core if k == 0 else 1 - core, blocks, inverse)
         out[...] = jnp.where(onehot, -1.0, expo)
-        rest += jnp.sum(jnp.where(onehot, 0.0, expo), axis=0, keepdims=True)
-        at_label += jnp.sum(jnp.where(onehot, expo, 0.0), axis=0, keepdims=True)
-    sums_out[0:1, :] = rest
-    sums_out[1:2, :] = at_label
+        parts.append((expo, onehot))
+    sums_out[0:1, :], sums_out[1:2, :] = sums(parts)
+
+
+def forward_other(
+    packed, own_blocks, pair_blocks, inverse, own_sums, shares, expo_out, sent_out
+):
+    core = lax.axis_index("core")
+    own = exponentials(packed, core, own_blocks, inverse[0])
+    pair = exponentials(packed, 1 - core, pair_blocks, inverse[1])
+    expo_out[...] = jnp.where(own[1], -1.0, own[0])
+    rows, wide = shares.shape
+    sent_out[:, :wide] = shares[...]
+    total = jnp.concatenate([own_sums[...], *sums([own, pair])], axis=0)
+    high = total.astype(jnp.bfloat16)
+    low = (total - high.astype(jnp.float32)).astype(jnp.bfloat16)
+    tile = jnp.concatenate([high.astype(jnp.float32), low.astype(jnp.float32)], axis=0)
+    tile = jnp.broadcast_to(tile[None], (rows // 8, 8, 128))
+    sent_out[:, wide:] = tile.reshape(rows, 128).astype(jnp.bfloat16)
 
 
 def shares(own_expo, pair_expo, inverse, own_blocks, pair_blocks, centres, shares_out, norms_out):
@@ -177,18 +200,6 @@
     norms_out[...] = select(
         [inverse_norm(centres[b].astype(jnp.float32)) for b in range(held)], BLK
     )
-
-
-def with_sums(shares, own_sums, other_sums, other_packed, other_expo, sent_out):
-    del other_packed, other_expo
-    rows, wide = shares.shape
-    sent_out[:, :wide] = shares[...]
-    total = jnp.concatenate([own_sums[...], other_sums[...]], axis=0)
-    high = total.astype(jnp.bfloat16)
-    low = (total - high.astype(jnp.float32)).astype(jnp.bfloat16)
-    tile = jnp.concatenate([high.astype(jnp.float32), low.astype(jnp.float32)], axis=0)
-    tile = jnp.broadcast_to(tile[None], (rows // 8, 8, 128))
-    sent_out[:, wide:] = tile.reshape(rows, 128).astype(jnp.bfloat16)
 
 
 def backward(
@@ -285,9 +296,8 @@
 
 
 def exchange_chips(pieces):
-    groups, chips = lax.axis_size("group"), lax.axis_size("chip")
-    order = [group_at(g) * chips + chip for g in range(groups) for chip in range(chips)]
-    return exchange(pieces, CHIPS, [order])
+    size, last = pieces.shape[0], lax.axis_size("chip") + 1
+    return exchange(pieces, CHIPS, [[(size - last - i) % size for i in range(size)]])
 
 
 def with_partner(value):
@@ -333,8 +343,8 @@
     pair_blocks = with_partner(own_blocks)
     own_packed = exchange_chips(copies).reshape(half, width + 128)
     other_packed = with_partner(own_packed)
-    own_expo, pair_expo, inverse, sums = run(
-        exponentials,
+    own_expo, pair_expo, inverse, own_sums = run(
+        forward,
         (
             shape((BLK, half), f32),
             shape((BLK, half), f32),
@@ -346,8 +356,6 @@
         own_blocks,
         pair_blocks,
     )
-    other_expo = with_partner(pair_expo)
-    other_sums = with_partner(sums)
     going, norms = run(
         shares,
         (shape((half, 2 * width), bf16), shape((BLK, 128), f32)),
@@ -359,15 +367,16 @@
         pair_blocks,
         blocks,
     )
-    sent = run(
-        with_sums,
-        shape((half, 2 * width + 128), bf16),
-        [VMEM] * 3 + [pl.BlockSpec(memory_space=pl.ANY)] * 2,
+    other_expo, sent = run(
+        forward_other,
+        (shape((BLK, half), f32), shape((half, 2 * width + 128), bf16)),
+        [VMEM] * 6,
+        other_packed,
+        own_blocks,
+        pair_blocks,
+        inverse,
+        own_sums,
         going,
-        sums,
-        other_sums,
-        other_packed,
-        other_expo,
     )
     received = exchange_chips(sent.reshape(chips, tok_dev, 2 * width + 128))
     outs = (shape((held, BLK, width), f32), shape((tok_dev, width), f32), shape((1, tok_dev), f32))

time: 35.1 us -> 32.4 us (0.923)
  blocking collectives: 28.7 us -> 26.4 us
  starting transfers between devices: 1.17 us -> 0.52 us
  Pallas kernels: 3.55 us -> 4.01 us
    all_to_all x2, blocking collectives: 28.7 us -> 26.4 us  [exchange(): lax.all_to_all(pieces, axes, split_axis=0, concat_axis=0, axis_index_grou...]
    ppermute x4 -> x2, starting transfers between devices: 1.17 us -> 0.52 us  [with_partner(): return lax.ppermute(value, 'core', [(0, 1), (1, 0)])]
    pallas_call x5, Pallas kernels: 3.55 us -> 4.01 us  [run(): pl.pallas_call(kernel, out_shape=out_shape, in_specs=in_specs, out_specs=...]
    ppermute x4 -> x2, waiting for transfers between devices: 0.71 us -> 0.53 us  [with_partner(): return lax.ppermute(value, 'core', [(0, 1), (1, 0)])]
  transfers between devices with their start and end apart: 4 -> 2, of which waited for: 1 -> 1; matrix products, arithmetic and copies ran while one was open for 0% -> 0% of each run, Pallas kernels for 2% -> 3%
where the time goes in v16:
time: 32.4 us; the launch traced here: 32.2 us
  blocking collectives  26.4 us (81%)
  Pallas kernels  4.01 us (12%)
  between operations  0.66 us (2%)
  waiting for transfers between devices  0.53 us (2%)
  starting transfers between devices  0.52 us (2%)
    all_to_all x2, blocking collectives, exchange(): lax.all_to_all(pieces, axes, split_axis=0, concat_axis=0, axis_index_grou...  26.4 us
    pallas_call x5, Pallas kernels, run(): pl.pallas_call(kernel, out_shape=out_shape, in_specs=in_specs, out_specs=...  4.01 us
  transfers between devices with their start and end apart: 2, of which 1 were waited for; matrix products, arithmetic and copies ran while one was open for 0% of the time, Pallas kernels for 3%

profile of v16, /device:TPU:0, one launch (start us, length us, event | category | flops | bytes accessed | tf_op | source)
XLA Modules:
  0.0 32.2 jit_solution(11386818192044140447)
XLA Ops:
  0.6 1.3 %shard_map.76 = (bf16[16,8,640]{2,1,0:T(8,128)(2,1)S(1)}, bf16[4,128,512]{2,1,0:T(8,128)(2,1)S(1)}, bf16[4,128,512]{2,1,0:T(8,128)(2,1)S(1)}, s32[1,128]{1,0:T(1,128)S(1)}) custom-call(bf16[8,512]{1,0:T(8,128)(2,1)} %features.3, s32[1,64]{1,0:T(1,128)} %bitcast.13, bf16[4,128,512]{2,1,0:T(8,128)(2,1)} %bitcast.12, s32[1,4]{1,0:T(1,128)} %bitcast.14, ...), custom_call_target="tpu_custom_call" | custom-call | bytes 1745696 | tf_op jit(solution)/shard_map/pallas_call | solution.py:36
  1.9 0.5 %collective-permute-start.1 = (bf16[4,128,512]{2,1,0:T(8,128)(2,1)S(1)}, bf16[4,128,512]{2,1,0:T(8,128)(2,1)S(1)}, u32[]{:S(2)}, u32[]{:S(2)}) collective-permute-start(bf16[4,128,512]{2,1,0:T(8,128)(2,1)S(1)} %get-tuple-element.20.own_blocks), channel_id=1, source_target_pairs={{0,1},{1,0},{2,3},{3,2},{4,5},{5,4},{6,7},{7,6},{8,9},{9,8},{10,11... | collective-permute-start | bytes 1572872 | tf_op jit(solution)/shard_map/ppermute | solution.py:304
  2.4 13.3 %all_to_all.10 = bf16[16,8,640]{2,1,0:T(8,128)(2,1)S(1)} all-to-all(bf16[16,8,640]{2,1,0:T(8,128)(2,1)S(1)} %get-tuple-element.19), channel_id=1, replica_groups={{22,20,18,16,14,12,10,8,6,4,2,0,30,28,26,24},{23,21,19,17,15,13,11,9,7,..., dimensions={0} | all-to-all | bytes 327680 | tf_op jit(solution)/shard_map/all_to_all | solution.py:293
  15.7 0.0 collective-permute-start
  15.7 0.0 collective-permute-done.1.pair_blocks
  15.7 0.5 %shard_map.77 = (f32[128,128]{1,0:T(8,128)S(1)}, f32[128,128]{1,0:T(8,128)S(1)}, f32[2,128,128]{2,1,0:T(8,128)S(1)}, f32[2,128]{1,0:T(2,128)S(1)}) custom-call(bf16[128,640]{1,0:T(8,128)(2,1)S(1)} %bitcast.9, bf16[4,128,512]{2,1,0:T(8,128)(2,1)S(1)} %get-tuple-element.20.own_blocks, bf16[4,128,512]{2,1,0:T(8,128)(2,1)S(1)} %collective-permute-done.1.pair_blocks), custom_call_target="tpu_custom_call" | custom-call | bytes 1475584 | tf_op jit(solution)/shard_map/pallas_call | solution.py:36
  16.2 0.4 %shard_map.78 = (bf16[128,1024]{1,0:T(8,128)(2,1)S(1)}, f32[128,128]{1,0:T(8,128)S(1)}) custom-call(f32[128,128]{1,0:T(8,128)S(1)} %get-tuple-element.23.own_expo, f32[128,128]{1,0:T(8,128)S(1)} %get-tuple-element.24.pair_expo, f32[2,128,128]{2,1,0:T(8,128)S(1)} %get-tuple-element.21.inverse, bf16[4,128,512]{2,1,0:T(8,128)(2,1)S(1)} %get-tuple-element.20.own_blocks, ...), custom_call_target="tpu_custom_call" | custom-call | bytes 2162688 | tf_op jit(solution)/shard_map/pallas_call | solution.py:36
  16.6 0.5 %collective-permute-done.packed.other_packed = bf16[128,640]{1,0:T(8,128)(2,1)S(1)} collective-permute-done((bf16[128,640]{1,0:T(8,128)(2,1)S(1)}, bf16[128,640]{1,0:T(8,128)(2,1)S(1)}, u32[]{:S(2)}, u32[]{:S(2)}) %collective-permute-start) | collective-permute-done | bytes 163872 | tf_op jit(solution)/shard_map/ppermute | solution.py:304
  17.1 0.5 %shard_map.79 = (f32[128,128]{1,0:T(8,128)S(1)}, bf16[128,1152]{1,0:T(8,128)(2,1)S(1)}) custom-call(bf16[128,640]{1,0:T(8,128)(2,1)S(1)} %collective-permute-done.packed.other_packed, bf16[4,128,512]{2,1,0:T(8,128)(2,1)S(1)} %get-tuple-element.20.own_blocks, bf16[4,128,512]{2,1,0:T(8,128)(2,1)S(1)} %collective-permute-done.1.pair_blocks, ...), custom_call_target="tpu_custom_call" | custom-call | bytes 1967104 | tf_op jit(solution)/shard_map/pallas_call | solution.py:36
  17.6 0.0 copy-start
  17.6 13.1 %all_to_all.11.received = bf16[16,8,1152]{2,1,0:T(8,128)(2,1)S(1)} all-to-all(bf16[16,8,1152]{2,1,0:T(8,128)(2,1)S(1)} %bitcast.11), channel_id=1, replica_groups={{22,20,18,16,14,12,10,8,6,4,2,0,30,28,26,24},{23,21,19,17,15,13,11,9,7,..., dimensions={0} | all-to-all | bytes 589824 | tf_op jit(solution)/shard_map/all_to_all | solution.py:293
  30.7 0.0 copy-done
  30.7 1.4 %shard_map.80 = (f32[4,128,512]{2,1,0:T(8,128)}, f32[8,512]{1,0:T(8,128)}, f32[1,8]{1,0:T(1,128)}) custom-call(s32[1,128]{1,0:T(1,128)S(1)} %get-tuple-element.18.named, bf16[16,8,1152]{2,1,0:T(8,128)(2,1)S(1)} %all_to_all.11.received, f32[128,128]{1,0:T(8,128)S(1)} %get-tuple-element.23.own_expo, f32[128,128]{1,0:T(8,128)S(1)} %get-tuple-element.28.other_expo, ...), custom_call_target="tpu_custom_call" | custom-call | bytes 2417184 | tf_op jit(solution)/shard_map/pallas_call | solution.py:36
Async XLA Ops:
  1.9 13.8 %collective-permute-start.1 = (bf16[4,128,512]{2,1,0:T(8,128)(2,1)S(1)}, bf16[4,128,512]{2,1,0:T(8,128)(2,1)S(1)}, u32[]{:S(2)}, u32[]{:S(2)}) collective-permute-start(bf16[4,128,512]{2,1,0:T(8,128)(2,1)S(1)} %get-tuple-element.20.own_blocks), channel_id=1, source_target_pairs={{0,1},{1,0},{2,3},{3,2},{4,5},{5,4},{6,7},{7,6},{8,9},{9,8},{10,11... | collective-permute-start | bytes 1572872 | tf_op jit(solution)/shard_map/ppermute | solution.py:304
  15.7 1.4 %collective-permute-start = (bf16[128,640]{1,0:T(8,128)(2,1)S(1)}, bf16[128,640]{1,0:T(8,128)(2,1)S(1)}, u32[]{:S(2)}, u32[]{:S(2)}) collective-permute-start(bf16[128,640]{1,0:T(8,128)(2,1)S(1)} %bitcast.8), channel_id=1, source_target_pairs={{0,1},{1,0},{2,3},{3,2},{4,5},{5,4},{6,7},{7,6},{8,9},{9,8},{10,11... | collective-permute-start | bytes 491528 | tf_op jit(solution)/shard_map/ppermute | solution.py:304
  17.6 13.1 %copy-start = (bf16[8,512]{1,0:T(8,128)(2,1)S(1)}, bf16[8,512]{1,0:T(8,128)(2,1)}, u32[]{:S(2)}) copy-start(bf16[8,512]{1,0:T(8,128)(2,1)} %features.3) | copy-start | bytes 24580

commit v17 on v16

--- a/solution.py
+++ b/solution.py
@@ -12,6 +12,7 @@
 logit_scale = 32.0
 cos_margin = 0.35
 norm_epsilon = 1e-06
+GROUP_ORDER = (2, 0, 3, 1)
 UNLISTED = 1e19
 
 VMEM = pl.BlockSpec(memory_space=pltpu.VMEM)
@@ -102,27 +103,21 @@
     )
     for move in moves[2:]:
         move.wait()
-    groups = blocks_out.shape[0]
-    named_out[...] = select([held_ids[0, group_at(g)] for g in range(groups)], 1)
-    for g in range(groups):
-        group = group_at(g)
+    named_out[...] = select([held_ids[0, group] for group in GROUP_ORDER], 1)
+    for g, group in enumerate(GROUP_ORDER):
         block = centres_out[held_ids[0, group]]
         blocks_out[g] = jnp.where(held_listed[0, group] > 0, block, jnp.full_like(block, UNLISTED))
 
 
-def group_at(place):
-    groups = lax.axis_size("group")
-    return (groups - 2 - place) % groups
-
-
 def own_place():
     groups, chips = lax.axis_size("group"), lax.axis_size("chip")
-    own = lax.axis_index("group") * chips + lax.axis_index("chip")
-    return lax.rem((2 * groups - 1) * chips - 1 - own, groups * chips)
+    group = lax.axis_index("group")
+    place = sum(jnp.where(group == g, k, 0) for k, g in enumerate(GROUP_ORDER))
+    return (chips - 1 - lax.axis_index("chip")) * groups + place
 
 
 def select(parts, rows):
-    owner = lanes(1) // (128 // len(parts))
+    owner = lax.rem(lanes(1) // 8, len(parts))
     out = jnp.broadcast_to(parts[0], (rows, 128))
     for g in range(1, len(parts)):
         out = jnp.where(owner == g, parts[g], out)
@@ -182,20 +177,23 @@
 
 def shares(own_expo, pair_expo, inverse, own_blocks, pair_blocks, centres, shares_out, norms_out):
     groups, _, width = own_blocks.shape
-    per_group = 128 // groups
     others, label = [], []
     for k, expo in enumerate((own_expo[...], pair_expo[...])):
-        others.append((jnp.maximum(expo, 0.0) * inverse[k]).T.astype(jnp.bfloat16))
-        label.append(jnp.where(expo < 0.0, 1.0, 0.0).T.astype(jnp.bfloat16))
+        others.append((jnp.maximum(expo, 0.0) * inverse[k]).T)
+        label.append(jnp.where(expo < 0.0, 1.0, 0.0).T)
     others = jnp.concatenate(others, axis=1)
     label = jnp.concatenate(label, axis=1)
+    places = [[] for _ in range(groups)]
     for g in range(groups):
-        here = slice(g * per_group, (g + 1) * per_group)
+        rows = [part[p * 8 : p * 8 + 8] for part in (others, label) for p in range(g, 16, groups)]
         blocks = jnp.concatenate([own_blocks[g], pair_blocks[g]], axis=0)
-        both = contract(jnp.concatenate([others[here], label[here]], axis=0), blocks, 1, 0)
-        both = both.astype(jnp.bfloat16)
-        shares_out[here, :width] = both[:per_group]
-        shares_out[here, width:] = both[per_group:]
+        both = contract(jnp.concatenate(rows, axis=0).astype(jnp.bfloat16), blocks, 1, 0)
+        places[g] = [both[i * 8 : i * 8 + 8] for i in range(len(rows))]
+    for part in range(2):
+        count = 16 // groups
+        rows = [places[g][part * count + i] for i in range(count) for g in range(groups)]
+        rows = jnp.concatenate(rows, axis=0).astype(jnp.bfloat16)
+        shares_out[:, part * width : (part + 1) * width] = rows
     held = centres.shape[0]
     norms_out[...] = select(
         [inverse_norm(centres[b].astype(jnp.float32)) for b in range(held)], BLK
@@ -223,10 +221,14 @@
     held = centres.shape[0]
     tok_dev, width = features.shape
 
-    sums = received[0].astype(jnp.float32)
-    for i in range(1, received.shape[0]):
-        sums = sums + received[i].astype(jnp.float32)
-    tile = sums[:, 2 * width :]
+
+    def total_of(columns):
+        total = received[0, :, columns].astype(jnp.float32)
+        for i in range(1, received.shape[0]):
+            total = total + received[i, :, columns].astype(jnp.float32)
+        return total
+
+    tile = total_of(pl.ds(2 * width, 128))
     tile = tile[:4] + tile[4:]
     own_rest, own_label = tile[0:1], tile[1:2]
     other_rest, other_label = tile[2:3], tile[3:4]
@@ -240,8 +242,6 @@
     other = jnp.where(other < 0.0, -other_rest, other) * other_scale
     weights = jnp.concatenate([own, other], axis=1)
     named = jnp.concatenate([named[...], named[...]], axis=1)
-    mine = [jnp.where(named == b, weights, 0.0).astype(jnp.bfloat16) for b in range(held)]
-    slot_grad = contract(jnp.concatenate(mine, axis=0), units, 1, 0)
     moves = []
 
     def leave(source, target):
@@ -250,8 +250,9 @@
         moves.append(move)
 
     def block_out(b):
-        here = slot_grad[b * BLK : (b + 1) * BLK]
-        factor = norms[:, b * (128 // held) : b * (128 // held) + 1]
+        mine = jnp.where(named == b, weights, 0.0).astype(jnp.bfloat16)
+        here = contract(mine, units, 1, 0)
+        factor = norms[:, b * 8 : b * 8 + 1]
         unit = centres[b].astype(jnp.float32) * factor
         along = jnp.sum(here * unit, axis=1, keepdims=True)
         grad[b] = factor * (here - along * unit)
@@ -261,6 +262,7 @@
     for b in range(held // 2):
         block_out(b)
 
+    sums = total_of(pl.ds(0, 2 * width))
     sample = lax.broadcasted_iota(jnp.int32, (tok_dev, 128), 0) + own_place() * tok_dev
     mine = lanes(tok_dev) == sample
     rest = jnp.sum(jnp.where(mine, own_rest, 0.0), axis=1, keepdims=True)
@@ -296,8 +298,9 @@
 
 
 def exchange_chips(pieces):
-    size, last = pieces.shape[0], lax.axis_size("chip") + 1
-    return exchange(pieces, CHIPS, [[(size - last - i) % size for i in range(size)]])
+    chips = lax.axis_size("chip")
+    order = [g * chips + chip for chip in reversed(range(chips)) for g in GROUP_ORDER]
+    return exchange(pieces, CHIPS, [order])
 
 
 def with_partner(value):

time: 32.4 us -> 32.3 us (level)
  no operation moved by 1% of the time
where the time goes in v17:
time: 32.3 us; the launch traced here: 32 us
  blocking collectives  26.2 us (81%)
  Pallas kernels  4.04 us (13%)
  between operations  0.66 us (2%)
  waiting for transfers between devices  0.53 us (2%)
  starting transfers between devices  0.52 us (2%)
    all_to_all x2, blocking collectives, exchange(): lax.all_to_all(pieces, axes, split_axis=0, concat_axis=0, axis_index_grou...  26.2 us
    pallas_call x5, Pallas kernels, run(): pl.pallas_call(kernel, out_shape=out_shape, in_specs=in_specs, out_specs=...  4.04 us
  transfers between devices with their start and end apart: 2, of which 1 were waited for; matrix products, arithmetic and copies ran while one was open for 0% of the time, Pallas kernels for 3%

profile of v17, /device:TPU:0, one launch (start us, length us, event | category | flops | bytes accessed | tf_op | source)
XLA Modules:
  0.0 32.0 jit_solution(14546981059315829368)
XLA Ops:
  0.6 1.3 %shard_map.76 = (bf16[16,8,640]{2,1,0:T(8,128)(2,1)S(1)}, bf16[4,128,512]{2,1,0:T(8,128)(2,1)S(1)}, bf16[4,128,512]{2,1,0:T(8,128)(2,1)S(1)}, s32[1,128]{1,0:T(1,128)S(1)}) custom-call(bf16[8,512]{1,0:T(8,128)(2,1)} %features.3, s32[1,64]{1,0:T(1,128)} %bitcast.13, bf16[4,128,512]{2,1,0:T(8,128)(2,1)} %bitcast.12, s32[1,4]{1,0:T(1,128)} %bitcast.14, ...), custom_call_target="tpu_custom_call" | custom-call | bytes 1745696 | tf_op jit(solution)/shard_map/pallas_call | solution.py:37
  1.9 0.5 %collective-permute-start.1 = (bf16[4,128,512]{2,1,0:T(8,128)(2,1)S(1)}, bf16[4,128,512]{2,1,0:T(8,128)(2,1)S(1)}, u32[]{:S(2)}, u32[]{:S(2)}) collective-permute-start(bf16[4,128,512]{2,1,0:T(8,128)(2,1)S(1)} %get-tuple-element.20.own_blocks), channel_id=1, source_target_pairs={{0,1},{1,0},{2,3},{3,2},{4,5},{5,4},{6,7},{7,6},{8,9},{9,8},{10,11... | collective-permute-start | bytes 1572872 | tf_op jit(solution)/shard_map/ppermute | solution.py:307
  2.4 13.2 %all_to_all.10 = bf16[16,8,640]{2,1,0:T(8,128)(2,1)S(1)} all-to-all(bf16[16,8,640]{2,1,0:T(8,128)(2,1)S(1)} %get-tuple-element.19), channel_id=1, replica_groups={{22,6,30,14,20,4,28,12,18,2,26,10,16,0,24,8},{23,7,31,15,21,5,29,13,19,..., dimensions={0} | all-to-all | bytes 327680 | tf_op jit(solution)/shard_map/all_to_all | solution.py:295
  15.6 0.0 collective-permute-start
  15.6 0.0 collective-permute-done.1.pair_blocks
  15.6 0.5 %shard_map.77 = (f32[128,128]{1,0:T(8,128)S(1)}, f32[128,128]{1,0:T(8,128)S(1)}, f32[2,128,128]{2,1,0:T(8,128)S(1)}, f32[2,128]{1,0:T(2,128)S(1)}) custom-call(bf16[128,640]{1,0:T(8,128)(2,1)S(1)} %bitcast.9, bf16[4,128,512]{2,1,0:T(8,128)(2,1)S(1)} %get-tuple-element.20.own_blocks, bf16[4,128,512]{2,1,0:T(8,128)(2,1)S(1)} %collective-permute-done.1.pair_blocks), custom_call_target="tpu_custom_call" | custom-call | bytes 1475584 | tf_op jit(solution)/shard_map/pallas_call | solution.py:37
  16.1 0.4 %shard_map.78 = (bf16[128,1024]{1,0:T(8,128)(2,1)S(1)}, f32[128,128]{1,0:T(8,128)S(1)}) custom-call(f32[128,128]{1,0:T(8,128)S(1)} %get-tuple-element.23.own_expo, f32[128,128]{1,0:T(8,128)S(1)} %get-tuple-element.24.pair_expo, f32[2,128,128]{2,1,0:T(8,128)S(1)} %get-tuple-element.21.inverse, bf16[4,128,512]{2,1,0:T(8,128)(2,1)S(1)} %get-tuple-element.20.own_blocks, ...), custom_call_target="tpu_custom_call" | custom-call | bytes 2162688 | tf_op jit(solution)/shard_map/pallas_call | solution.py:37
  16.5 0.5 %collective-permute-done.packed.other_packed = bf16[128,640]{1,0:T(8,128)(2,1)S(1)} collective-permute-done((bf16[128,640]{1,0:T(8,128)(2,1)S(1)}, bf16[128,640]{1,0:T(8,128)(2,1)S(1)}, u32[]{:S(2)}, u32[]{:S(2)}) %collective-permute-start) | collective-permute-done | bytes 163872 | tf_op jit(solution)/shard_map/ppermute | solution.py:307
  17.0 0.5 %shard_map.79 = (f32[128,128]{1,0:T(8,128)S(1)}, bf16[128,1152]{1,0:T(8,128)(2,1)S(1)}) custom-call(bf16[128,640]{1,0:T(8,128)(2,1)S(1)} %collective-permute-done.packed.other_packed, bf16[4,128,512]{2,1,0:T(8,128)(2,1)S(1)} %get-tuple-element.20.own_blocks, bf16[4,128,512]{2,1,0:T(8,128)(2,1)S(1)} %collective-permute-done.1.pair_blocks, ...), custom_call_target="tpu_custom_call" | custom-call | bytes 1967104 | tf_op jit(solution)/shard_map/pallas_call | solution.py:37
  17.5 0.0 copy-start
  17.5 13.0 %all_to_all.11.received = bf16[16,8,1152]{2,1,0:T(8,128)(2,1)S(1)} all-to-all(bf16[16,8,1152]{2,1,0:T(8,128)(2,1)S(1)} %bitcast.11), channel_id=1, replica_groups={{22,6,30,14,20,4,28,12,18,2,26,10,16,0,24,8},{23,7,31,15,21,5,29,13,19,..., dimensions={0} | all-to-all | bytes 589824 | tf_op jit(solution)/shard_map/all_to_all | solution.py:295
  30.6 0.0 copy-done
  30.6 1.5 %shard_map.80 = (f32[4,128,512]{2,1,0:T(8,128)}, f32[8,512]{1,0:T(8,128)}, f32[1,8]{1,0:T(1,128)}) custom-call(s32[1,128]{1,0:T(1,128)S(1)} %get-tuple-element.18.named, bf16[16,8,1152]{2,1,0:T(8,128)(2,1)S(1)} %all_to_all.11.received, f32[128,128]{1,0:T(8,128)S(1)} %get-tuple-element.23.own_expo, f32[128,128]{1,0:T(8,128)S(1)} %get-tuple-element.28.other_expo, ...), custom_call_target="tpu_custom_call" | custom-call | bytes 2417184 | tf_op jit(solution)/shard_map/pallas_call | solution.py:37
Async XLA Ops:
  1.9 13.7 %collective-permute-start.1 = (bf16[4,128,512]{2,1,0:T(8,128)(2,1)S(1)}, bf16[4,128,512]{2,1,0:T(8,128)(2,1)S(1)}, u32[]{:S(2)}, u32[]{:S(2)}) collective-permute-start(bf16[4,128,512]{2,1,0:T(8,128)(2,1)S(1)} %get-tuple-element.20.own_blocks), channel_id=1, source_target_pairs={{0,1},{1,0},{2,3},{3,2},{4,5},{5,4},{6,7},{7,6},{8,9},{9,8},{10,11... | collective-permute-start | bytes 1572872 | tf_op jit(solution)/shard_map/ppermute | solution.py:307
  15.6 1.4 %collective-permute-start = (bf16[128,640]{1,0:T(8,128)(2,1)S(1)}, bf16[128,640]{1,0:T(8,128)(2,1)S(1)}, u32[]{:S(2)}, u32[]{:S(2)}) collective-permute-start(bf16[128,640]{1,0:T(8,128)(2,1)S(1)} %bitcast.8), channel_id=1, source_target_pairs={{0,1},{1,0},{2,3},{3,2},{4,5},{5,4},{6,7},{7,6},{8,9},{9,8},{10,11... | collective-permute-start | bytes 491528 | tf_op jit(solution)/shard_map/ppermute | solution.py:307
  17.5 13.0 %copy-start = (bf16[8,512]{1,0:T(8,128)(2,1)S(1)}, bf16[8,512]{1,0:T(8,128)(2,1)}, u32[]{:S(2)}) copy-start(bf16[8,512]{1,0:T(8,128)(2,1)} %features.3) | copy-start | bytes 24580

commit v18 on v17

--- a/solution.py
+++ b/solution.py
@@ -134,37 +134,40 @@
     first = (member * groups + lax.axis_index("group")) * BLK
     onehot = lax.broadcasted_iota(jnp.int32, (BLK, 128), 0) == labels - first
     units = packed[:, :width]
-    cosine = inverse * select([contract(blocks[g], units, 1, 1) for g in range(groups)], BLK)
+    dots = contract(blocks[...].reshape(groups * BLK, width), units, 1, 1)
+    cosine = inverse * select([dots[g * BLK : (g + 1) * BLK] for g in range(groups)], BLK)
     expo = jnp.exp(logit_scale * (cosine - jnp.where(onehot, cos_margin, 0.0)))
-    return jnp.where(inverse > 0.0, expo, 0.0), onehot
+    return jnp.where(inverse > 0.0, expo, 0.0), onehot, cosine * inverse
 
 
 def sums(parts):
-    rest = [jnp.where(onehot, 0.0, expo) for expo, onehot in parts]
-    at_label = [jnp.where(onehot, expo, 0.0) for expo, onehot in parts]
+    rest = [jnp.where(onehot, 0.0, expo) for expo, onehot, _ in parts]
+    at_label = [jnp.where(onehot, expo, 0.0) for expo, onehot, _ in parts]
     return [jnp.sum(sum(part), axis=0, keepdims=True) for part in (rest, at_label)]
 
 
-def forward(packed, own_blocks, pair_blocks, own_expo_out, pair_expo_out, inverse_out, sums_out):
+def forward(packed, own_blocks, pair_blocks, expo_out, scaled_out, inverse_out, sums_out):
     core = lax.axis_index("core")
     parts = []
-    for k, (blocks, out) in enumerate(((own_blocks, own_expo_out), (pair_blocks, pair_expo_out))):
+    for k, blocks in enumerate((own_blocks, pair_blocks)):
         norms = [inverse_norm(blocks[g].astype(jnp.float32)) for g in range(blocks.shape[0])]
         inverse = select(norms, BLK)
         inverse_out[k] = inverse
-        expo, onehot = exponentials(packed, core if k == 0 else 1 - core, blocks, inverse)
-        out[...] = jnp.where(onehot, -1.0, expo)
-        parts.append((expo, onehot))
+        part = exponentials(packed, core if k == 0 else 1 - core, blocks, inverse)
+        expo_out[k] = jnp.where(part[1], -1.0, part[0])
+        parts.append(part)
+    scaled_out[...] = parts[0][2]
     sums_out[0:1, :], sums_out[1:2, :] = sums(parts)
 
 
 def forward_other(
-    packed, own_blocks, pair_blocks, inverse, own_sums, shares, expo_out, sent_out
+    packed, own_blocks, pair_blocks, inverse, own_sums, shares, expo_out, scaled_out, sent_out
 ):
     core = lax.axis_index("core")
     own = exponentials(packed, core, own_blocks, inverse[0])
     pair = exponentials(packed, 1 - core, pair_blocks, inverse[1])
     expo_out[...] = jnp.where(own[1], -1.0, own[0])
+    scaled_out[...] = own[2]
     rows, wide = shares.shape
     sent_out[:, :wide] = shares[...]
     total = jnp.concatenate([own_sums[...], *sums([own, pair])], axis=0)
@@ -175,12 +178,12 @@
     sent_out[:, wide:] = tile.reshape(rows, 128).astype(jnp.bfloat16)
 
 
-def shares(own_expo, pair_expo, inverse, own_blocks, pair_blocks, centres, shares_out, norms_out):
+def shares(expo, inverse, own_blocks, pair_blocks, shares_out):
     groups, _, width = own_blocks.shape
     others, label = [], []
-    for k, expo in enumerate((own_expo[...], pair_expo[...])):
-        others.append((jnp.maximum(expo, 0.0) * inverse[k]).T)
-        label.append(jnp.where(expo < 0.0, 1.0, 0.0).T)
+    for k in range(2):
+        others.append((jnp.maximum(expo[k], 0.0) * inverse[k]).T)
+        label.append(jnp.where(expo[k] < 0.0, 1.0, 0.0).T)
     others = jnp.concatenate(others, axis=1)
     label = jnp.concatenate(label, axis=1)
     places = [[] for _ in range(groups)]
@@ -194,22 +197,20 @@
         rows = [places[g][part * count + i] for i in range(count) for g in range(groups)]
         rows = jnp.concatenate(rows, axis=0).astype(jnp.bfloat16)
         shares_out[:, part * width : (part + 1) * width] = rows
-    held = centres.shape[0]
-    norms_out[...] = select(
-        [inverse_norm(centres[b].astype(jnp.float32)) for b in range(held)], BLK
-    )
 
 
 def backward(
     named,
     received,
-    own_expo,
+    expo,
     other_expo,
+    scaled,
+    other_scaled,
+    inverse,
     own_packed,
     other_packed,
     features,
     centres,
-    norms,
     grad_out,
     feature_out,
     loss_out,
@@ -221,7 +222,6 @@
     held = centres.shape[0]
     tok_dev, width = features.shape
 
-
     def total_of(columns):
         total = received[0, :, columns].astype(jnp.float32)
         for i in range(1, received.shape[0]):
@@ -236,11 +236,12 @@
     units = jnp.concatenate([own_packed[:, :width], other_packed[:, :width]], axis=0)
     own_scale = logit_scale / (own_rest + own_label)
     other_scale = logit_scale / (other_rest + other_label)
-    own = own_expo[...]
+    own = expo[0]
     other = other_expo[...]
-    own = jnp.where(own < 0.0, -own_rest, own) * own_scale
-    other = jnp.where(other < 0.0, -other_rest, other) * other_scale
+    own = jnp.where(own < 0.0, -own_rest, own) * (own_scale * inverse[0])
+    other = jnp.where(other < 0.0, -other_rest, other) * (other_scale * inverse[0])
     weights = jnp.concatenate([own, other], axis=1)
+    pulls = weights * jnp.concatenate([scaled[...], other_scaled[...]], axis=1)
     named = jnp.concatenate([named[...], named[...]], axis=1)
     moves = []
 
@@ -251,11 +252,8 @@
 
     def block_out(b):
         mine = jnp.where(named == b, weights, 0.0).astype(jnp.bfloat16)
-        here = contract(mine, units, 1, 0)
-        factor = norms[:, b * 8 : b * 8 + 1]
-        unit = centres[b].astype(jnp.float32) * factor
-        along = jnp.sum(here * unit, axis=1, keepdims=True)
-        grad[b] = factor * (here - along * unit)
+        back = jnp.sum(jnp.where(named == b, pulls, 0.0), axis=1, keepdims=True)
+        grad[b] = contract(mine, units, 1, 0) - back * centres[b].astype(jnp.float32)
         for part in (pl.ds(0, BLK // 2), pl.ds(BLK // 2, BLK // 2)):
             leave(grad.at[b, part], grad_out.at[b, part])
 
@@ -346,12 +344,12 @@
     pair_blocks = with_partner(own_blocks)
     own_packed = exchange_chips(copies).reshape(half, width + 128)
     other_packed = with_partner(own_packed)
-    own_expo, pair_expo, inverse, own_sums = run(
+    expo, scaled, inverse, own_sums = run(
         forward,
         (
+            shape((2, BLK, half), f32),
             shape((BLK, half), f32),
-            shape((BLK, half), f32),
-            shape((2, BLK, 128), f32),
+            shape((2, BLK, half), f32),
             shape((2, half), f32),
         ),
         [VMEM] * 3,
@@ -359,20 +357,22 @@
         own_blocks,
         pair_blocks,
     )
-    going, norms = run(
+    going = run(
         shares,
-        (shape((half, 2 * width), bf16), shape((BLK, 128), f32)),
-        [VMEM] * 6,
-        own_expo,
-        pair_expo,
+        shape((half, 2 * width), bf16),
+        [VMEM] * 4,
+        expo,
         inverse,
         own_blocks,
         pair_blocks,
-        blocks,
-    )
-    other_expo, sent = run(
+    )
+    other_expo, other_scaled, sent = run(
         forward_other,
-        (shape((BLK, half), f32), shape((half, 2 * width + 128), bf16)),
+        (
+            shape((BLK, half), f32),
+            shape((BLK, half), f32),
+            shape((half, 2 * width + 128), bf16),
+        ),
         [VMEM] * 6,
         other_packed,
         own_blocks,
@@ -386,16 +386,18 @@
     centre_grad, feature_grad, loss = run(
         backward,
         outs,
-        [VMEM] * 9,
+        [VMEM] * 11,
         named,
         received,
-        own_expo,
+        expo,
         other_expo,
+        scaled,
+        other_scaled,
+        inverse,
         own_packed,
         other_packed,
         features,
         blocks,
-        norms,
         out_spec=HBM,
         scratch=[
             *(pltpu.VMEM(out.shape, out.dtype) for out in outs),

time: 32.3 us -> 32.9 us (1.019)
  local copies, waits for them, and re-layouts: 0.01 us -> 0.7 us
    unnamed x2, local copies, waits for them, and re-layouts: 0.01 us -> 0.7 us
where the time goes in v18:
time: 32.9 us; the launch traced here: 32.5 us
  blocking collectives  26.2 us (80%)
  Pallas kernels  3.87 us (12%)
  local copies, waits for them, and re-layouts  0.7 us (2%)
  between operations  0.65 us (2%)
  waiting for transfers between devices  0.54 us (2%)
  starting transfers between devices  0.52 us (2%)
    all_to_all x2, blocking collectives, exchange(): lax.all_to_all(pieces, axes, split_axis=0, concat_axis=0, axis_index_grou...  26.2 us
    pallas_call x5, Pallas kernels, run(): pl.pallas_call(kernel, out_shape=out_shape, in_specs=in_specs, out_specs=...  3.87 us
    unnamed x2, local copies, waits for them, and re-layouts  0.7 us
  transfers between devices with their start and end apart: 2, of which 1 were waited for; matrix products, arithmetic and copies ran while one was open for 0% of the time, Pallas kernels for 3%

profile of v18, /device:TPU:0, one launch (start us, length us, event | category | flops | bytes accessed | tf_op | source)
XLA Modules:
  0.0 32.5 jit_solution(13618754155640688232)
XLA Ops:
  0.6 1.3 %shard_map.76 = (bf16[16,8,640]{2,1,0:T(8,128)(2,1)S(1)}, bf16[4,128,512]{2,1,0:T(8,128)(2,1)S(1)}, bf16[4,128,512]{2,1,0:T(8,128)(2,1)S(1)}, s32[1,128]{1,0:T(1,128)S(1)}) custom-call(bf16[8,512]{1,0:T(8,128)(2,1)} %features.3, s32[1,64]{1,0:T(1,128)} %bitcast.13, bf16[4,128,512]{2,1,0:T(8,128)(2,1)} %bitcast.12, s32[1,4]{1,0:T(1,128)} %bitcast.14, ...), custom_call_target="tpu_custom_call" | custom-call | bytes 1745696 | tf_op jit(solution)/shard_map/pallas_call | solution.py:37
  1.9 0.5 %collective-permute-start.1 = (bf16[4,128,512]{2,1,0:T(8,128)(2,1)S(1)}, bf16[4,128,512]{2,1,0:T(8,128)(2,1)S(1)}, u32[]{:S(2)}, u32[]{:S(2)}) collective-permute-start(bf16[4,128,512]{2,1,0:T(8,128)(2,1)S(1)} %get-tuple-element.19.own_blocks), channel_id=1, source_target_pairs={{0,1},{1,0},{2,3},{3,2},{4,5},{5,4},{6,7},{7,6},{8,9},{9,8},{10,11... | collective-permute-start | bytes 1572872 | tf_op jit(solution)/shard_map/ppermute | solution.py:305
  2.4 13.2 %all_to_all.10 = bf16[16,8,640]{2,1,0:T(8,128)(2,1)S(1)} all-to-all(bf16[16,8,640]{2,1,0:T(8,128)(2,1)S(1)} %get-tuple-element.18), channel_id=1, replica_groups={{22,6,30,14,20,4,28,12,18,2,26,10,16,0,24,8},{23,7,31,15,21,5,29,13,19,..., dimensions={0} | all-to-all | bytes 327680 | tf_op jit(solution)/shard_map/all_to_all | solution.py:293
  15.6 0.0 collective-permute-start
  15.6 0.0 collective-permute-done.1.pair_blocks
  15.6 0.5 %shard_map.77 = (f32[2,128,128]{2,1,0:T(8,128)S(1)}, f32[128,128]{1,0:T(8,128)S(1)}, f32[2,128,128]{2,1,0:T(8,128)S(1)}, f32[2,128]{1,0:T(2,128)S(1)}) custom-call(bf16[128,640]{1,0:T(8,128)(2,1)S(1)} %bitcast.9, bf16[4,128,512]{2,1,0:T(8,128)(2,1)S(1)} %get-tuple-element.19.own_blocks, bf16[4,128,512]{2,1,0:T(8,128)(2,1)S(1)} %collective-permute-done.1.pair_blocks), custom_call_target="tpu_custom_call" | custom-call | bytes 1541120 | tf_op jit(solution)/shard_map/pallas_call | solution.py:37
  16.1 0.3 %shard_map.78.shares = bf16[128,1024]{1,0:T(8,128)(2,1)S(1)} custom-call(f32[2,128,128]{2,1,0:T(8,128)S(1)} %get-tuple-element.22.expo, f32[2,128,128]{2,1,0:T(8,128)S(1)} %get-tuple-element.20.inverse, bf16[4,128,512]{2,1,0:T(8,128)(2,1)S(1)} %get-tuple-element.19.own_blocks, bf16[4,128,512]{2,1,0:T(8,128)(2,1)S(1)} %collective-permute-done.1.pair_blocks), custom_call_target="tpu_custom_call" | custom-call | bytes 1572864 | tf_op jit(solution)/shard_map/pallas_call | solution.py:37
  16.5 0.5 %collective-permute-done.packed.other_packed = bf16[128,640]{1,0:T(8,128)(2,1)S(1)} collective-permute-done((bf16[128,640]{1,0:T(8,128)(2,1)S(1)}, bf16[128,640]{1,0:T(8,128)(2,1)S(1)}, u32[]{:S(2)}, u32[]{:S(2)}) %collective-permute-start) | collective-permute-done | bytes 163872 | tf_op jit(solution)/shard_map/ppermute | solution.py:305
  17.0 0.5 %shard_map.79 = (f32[128,128]{1,0:T(8,128)S(1)}, f32[128,128]{1,0:T(8,128)S(1)}, bf16[128,1152]{1,0:T(8,128)(2,1)S(1)}) custom-call(bf16[128,640]{1,0:T(8,128)(2,1)S(1)} %collective-permute-done.packed.other_packed, bf16[4,128,512]{2,1,0:T(8,128)(2,1)S(1)} %get-tuple-element.19.own_blocks, bf16[4,128,512]{2,1,0:T(8,128)(2,1)S(1)} %collective-permute-done.1.pair_blocks, ...), custom_call_target="tpu_custom_call" | custom-call | bytes 2032640 | tf_op jit(solution)/shard_map/pallas_call | solution.py:37
  17.5 13.0 %all_to_all.11.received = bf16[16,8,1152]{2,1,0:T(8,128)(2,1)S(1)} all-to-all(bf16[16,8,1152]{2,1,0:T(8,128)(2,1)S(1)} %bitcast.11), channel_id=1, replica_groups={{22,6,30,14,20,4,28,12,18,2,26,10,16,0,24,8},{23,7,31,15,21,5,29,13,19,..., dimensions={0} | all-to-all | bytes 589824 | tf_op jit(solution)/shard_map/all_to_all | solution.py:293
  30.5 0.0 copy-start
  30.5 0.7 %copy-done = bf16[8,512]{1,0:T(8,128)(2,1)S(1)} copy-done((bf16[8,512]{1,0:T(8,128)(2,1)S(1)}, bf16[8,512]{1,0:T(8,128)(2,1)}, u32[]{:S(2)}) %copy-start) | copy-done | bytes 8216
  31.2 1.3 %shard_map.80 = (f32[4,128,512]{2,1,0:T(8,128)}, f32[8,512]{1,0:T(8,128)}, f32[1,8]{1,0:T(1,128)}) custom-call(s32[1,128]{1,0:T(1,128)S(1)} %get-tuple-element.17.named, bf16[16,8,1152]{2,1,0:T(8,128)(2,1)S(1)} %all_to_all.11.received, f32[2,128,128]{2,1,0:T(8,128)S(1)} %get-tuple-element.22.expo, f32[128,128]{1,0:T(8,128)S(1)} %get-tuple-element.24.other_expo, ...), custom_call_target="tpu_custom_call" | custom-call | bytes 2679328 | tf_op jit(solution)/shard_map/pallas_call | solution.py:37
Async XLA Ops:
  1.9 13.7 %collective-permute-start.1 = (bf16[4,128,512]{2,1,0:T(8,128)(2,1)S(1)}, bf16[4,128,512]{2,1,0:T(8,128)(2,1)S(1)}, u32[]{:S(2)}, u32[]{:S(2)}) collective-permute-start(bf16[4,128,512]{2,1,0:T(8,128)(2,1)S(1)} %get-tuple-element.19.own_blocks), channel_id=1, source_target_pairs={{0,1},{1,0},{2,3},{3,2},{4,5},{5,4},{6,7},{7,6},{8,9},{9,8},{10,11... | collective-permute-start | bytes 1572872 | tf_op jit(solution)/shard_map/ppermute | solution.py:305
  15.6 1.4 %collective-permute-start = (bf16[128,640]{1,0:T(8,128)(2,1)S(1)}, bf16[128,640]{1,0:T(8,128)(2,1)S(1)}, u32[]{:S(2)}, u32[]{:S(2)}) collective-permute-start(bf16[128,640]{1,0:T(8,128)(2,1)S(1)} %bitcast.8), channel_id=1, source_target_pairs={{0,1},{1,0},{2,3},{3,2},{4,5},{5,4},{6,7},{7,6},{8,9},{9,8},{10,11... | collective-permute-start | bytes 491528 | tf_op jit(solution)/shard_map/ppermute | solution.py:305
  30.5 0.7 %copy-start = (bf16[8,512]{1,0:T(8,128)(2,1)S(1)}, bf16[8,512]{1,0:T(8,128)(2,1)}, u32[]{:S(2)}) copy-start(bf16[8,512]{1,0:T(8,128)(2,1)} %features.3) | copy-start | bytes 24580

commit v19 on v18

--- a/solution.py
+++ b/solution.py
@@ -73,7 +73,7 @@
                 (labels, held_labels),
                 (ids, held_ids),
                 (listed, held_listed),
-                *((centres.at[b], centres_out.at[b]) for b in range(centres.shape[0])),
+                (centres, centres_out),
             )
         )
     ]
@@ -314,13 +314,14 @@
     bf16, f32 = jnp.bfloat16, jnp.float32
     shape = jax.ShapeDtypeStruct
 
-    copies, own_blocks, blocks, named = run(
+    copies, own_blocks, blocks, named, own_features = run(
         load,
         (
             shape((chips, tok_dev, width + 128), bf16),
             shape((groups, BLK, width), bf16),
             shape((held, BLK, width), bf16),
             shape((1, 128), block_ids.dtype),
+            shape(features.shape, bf16),
         ),
         [HBM] * 5,
         *(
@@ -334,11 +335,10 @@
             )
         ),
         scratch=[
-            pltpu.VMEM(features.shape, features.dtype),
             pltpu.VMEM((1, labels.shape[0]), labels.dtype),
             pltpu.SMEM((1, groups), block_ids.dtype),
             pltpu.SMEM((1, groups), listed.dtype),
-            pltpu.SemaphoreType.DMA((4 + held,)),
+            pltpu.SemaphoreType.DMA((5,)),
         ],
     )
     pair_blocks = with_partner(own_blocks)
@@ -396,7 +396,7 @@
         inverse,
         own_packed,
         other_packed,
-        features,
+        own_features,
         blocks,
         out_spec=HBM,
         scratch=[

time: 32.9 us -> 32.1 us (0.976)
  local copies, waits for them, and re-layouts: 0.7 us -> 0 us
    unnamed x2 -> x0, local copies, waits for them, and re-layouts: 0.7 us -> none
where the time goes in v19:
time: 32.1 us; the launch traced here: 31.8 us
  blocking collectives  26.2 us (82%)
  Pallas kernels  3.8 us (12%)
  between operations  0.65 us (2%)
  waiting for transfers between devices  0.54 us (2%)
  starting transfers between devices  0.52 us (2%)
    all_to_all x2, blocking collectives, exchange(): lax.all_to_all(pieces, axes, split_axis=0, concat_axis=0, axis_index_grou...  26.2 us
    pallas_call x5, Pallas kernels, run(): pl.pallas_call(kernel, out_shape=out_shape, in_specs=in_specs, out_specs=...  3.8 us
  transfers between devices with their start and end apart: 2, of which 1 were waited for; matrix products, arithmetic and copies ran while one was open for 0% of the time, Pallas kernels for 3%

profile of v19, /device:TPU:0, one launch (start us, length us, event | category | flops | bytes accessed | tf_op | source)
XLA Modules:
  0.0 31.8 jit_solution(14712218338700904330)
XLA Ops:
  0.6 1.2 %shard_map.76 = (bf16[16,8,640]{2,1,0:T(8,128)(2,1)S(1)}, bf16[4,128,512]{2,1,0:T(8,128)(2,1)S(1)}, bf16[4,128,512]{2,1,0:T(8,128)(2,1)S(1)}, s32[1,128]{1,0:T(1,128)S(1)}, bf16[8,512]{1,0:T(8,128)(2,1)S(1)}) custom-call(bf16[8,512]{1,0:T(8,128)(2,1)} %features.1, s32[1,64]{1,0:T(1,128)} %bitcast.13, bf16[4,128,512]{2,1,0:T(8,128)(2,1)} %bitcast.12, ...), custom_call_target="tpu_custom_call" | custom-call | bytes 1753888 | tf_op jit(solution)/shard_map/pallas_call | solution.py:37
  1.8 0.5 %collective-permute-start.1 = (bf16[4,128,512]{2,1,0:T(8,128)(2,1)S(1)}, bf16[4,128,512]{2,1,0:T(8,128)(2,1)S(1)}, u32[]{:S(2)}, u32[]{:S(2)}) collective-permute-start(bf16[4,128,512]{2,1,0:T(8,128)(2,1)S(1)} %get-tuple-element.20.own_blocks), channel_id=1, source_target_pairs={{0,1},{1,0},{2,3},{3,2},{4,5},{5,4},{6,7},{7,6},{8,9},{9,8},{10,11... | collective-permute-start | bytes 1572872 | tf_op jit(solution)/shard_map/ppermute | solution.py:305
  2.3 13.2 %all_to_all.10 = bf16[16,8,640]{2,1,0:T(8,128)(2,1)S(1)} all-to-all(bf16[16,8,640]{2,1,0:T(8,128)(2,1)S(1)} %get-tuple-element.19), channel_id=1, replica_groups={{22,6,30,14,20,4,28,12,18,2,26,10,16,0,24,8},{23,7,31,15,21,5,29,13,19,..., dimensions={0} | all-to-all | bytes 327680 | tf_op jit(solution)/shard_map/all_to_all | solution.py:293
  15.5 0.0 collective-permute-start
  15.6 0.0 collective-permute-done.1.pair_blocks
  15.6 0.5 %shard_map.77 = (f32[2,128,128]{2,1,0:T(8,128)S(1)}, f32[128,128]{1,0:T(8,128)S(1)}, f32[2,128,128]{2,1,0:T(8,128)S(1)}, f32[2,128]{1,0:T(2,128)S(1)}) custom-call(bf16[128,640]{1,0:T(8,128)(2,1)S(1)} %bitcast.9, bf16[4,128,512]{2,1,0:T(8,128)(2,1)S(1)} %get-tuple-element.20.own_blocks, bf16[4,128,512]{2,1,0:T(8,128)(2,1)S(1)} %collective-permute-done.1.pair_blocks), custom_call_target="tpu_custom_call" | custom-call | bytes 1541120 | tf_op jit(solution)/shard_map/pallas_call | solution.py:37
  16.1 0.3 %shard_map.78.shares = bf16[128,1024]{1,0:T(8,128)(2,1)S(1)} custom-call(f32[2,128,128]{2,1,0:T(8,128)S(1)} %get-tuple-element.23.expo, f32[2,128,128]{2,1,0:T(8,128)S(1)} %get-tuple-element.21.inverse, bf16[4,128,512]{2,1,0:T(8,128)(2,1)S(1)} %get-tuple-element.20.own_blocks, bf16[4,128,512]{2,1,0:T(8,128)(2,1)S(1)} %collective-permute-done.1.pair_blocks), custom_call_target="tpu_custom_call" | custom-call | bytes 1572864 | tf_op jit(solution)/shard_map/pallas_call | solution.py:37
  16.4 0.5 %collective-permute-done.packed.other_packed = bf16[128,640]{1,0:T(8,128)(2,1)S(1)} collective-permute-done((bf16[128,640]{1,0:T(8,128)(2,1)S(1)}, bf16[128,640]{1,0:T(8,128)(2,1)S(1)}, u32[]{:S(2)}, u32[]{:S(2)}) %collective-permute-start) | collective-permute-done | bytes 163872 | tf_op jit(solution)/shard_map/ppermute | solution.py:305
  16.9 0.5 %shard_map.79 = (f32[128,128]{1,0:T(8,128)S(1)}, f32[128,128]{1,0:T(8,128)S(1)}, bf16[128,1152]{1,0:T(8,128)(2,1)S(1)}) custom-call(bf16[128,640]{1,0:T(8,128)(2,1)S(1)} %collective-permute-done.packed.other_packed, bf16[4,128,512]{2,1,0:T(8,128)(2,1)S(1)} %get-tuple-element.20.own_blocks, bf16[4,128,512]{2,1,0:T(8,128)(2,1)S(1)} %collective-permute-done.1.pair_blocks, ...), custom_call_target="tpu_custom_call" | custom-call | bytes 2032640 | tf_op jit(solution)/shard_map/pallas_call | solution.py:37
  17.4 13.0 %all_to_all.11.received = bf16[16,8,1152]{2,1,0:T(8,128)(2,1)S(1)} all-to-all(bf16[16,8,1152]{2,1,0:T(8,128)(2,1)S(1)} %bitcast.11), channel_id=1, replica_groups={{22,6,30,14,20,4,28,12,18,2,26,10,16,0,24,8},{23,7,31,15,21,5,29,13,19,..., dimensions={0} | all-to-all | bytes 589824 | tf_op jit(solution)/shard_map/all_to_all | solution.py:293
  30.5 1.3 %shard_map.80 = (f32[4,128,512]{2,1,0:T(8,128)}, f32[8,512]{1,0:T(8,128)}, f32[1,8]{1,0:T(1,128)}) custom-call(s32[1,128]{1,0:T(1,128)S(1)} %get-tuple-element.18.named, bf16[16,8,1152]{2,1,0:T(8,128)(2,1)S(1)} %all_to_all.11.received, f32[2,128,128]{2,1,0:T(8,128)S(1)} %get-tuple-element.23.expo, f32[128,128]{1,0:T(8,128)S(1)} %get-tuple-element.25.other_expo, ...), custom_call_target="tpu_custom_call" | custom-call | bytes 2679328 | tf_op jit(solution)/shard_map/pallas_call | solution.py:37
Async XLA Ops:
  1.8 13.7 %collective-permute-start.1 = (bf16[4,128,512]{2,1,0:T(8,128)(2,1)S(1)}, bf16[4,128,512]{2,1,0:T(8,128)(2,1)S(1)}, u32[]{:S(2)}, u32[]{:S(2)}) collective-permute-start(bf16[4,128,512]{2,1,0:T(8,128)(2,1)S(1)} %get-tuple-element.20.own_blocks), channel_id=1, source_target_pairs={{0,1},{1,0},{2,3},{3,2},{4,5},{5,4},{6,7},{7,6},{8,9},{9,8},{10,11... | collective-permute-start | bytes 1572872 | tf_op jit(solution)/shard_map/ppermute | solution.py:305
  15.5 1.4 %collective-permute-start = (bf16[128,640]{1,0:T(8,128)(2,1)S(1)}, bf16[128,640]{1,0:T(8,128)(2,1)S(1)}, u32[]{:S(2)}, u32[]{:S(2)}) collective-permute-start(bf16[128,640]{1,0:T(8,128)(2,1)S(1)} %bitcast.8), channel_id=1, source_target_pairs={{0,1},{1,0},{2,3},{3,2},{4,5},{5,4},{6,7},{7,6},{8,9},{9,8},{10,11... | collective-permute-start | bytes 491528 | tf_op jit(solution)/shard_map/ppermute | solution.py:305

commit v20 on v19

--- a/solution.py
+++ b/solution.py
@@ -12,7 +12,7 @@
 logit_scale = 32.0
 cos_margin = 0.35
 norm_epsilon = 1e-06
-GROUP_ORDER = (2, 0, 3, 1)
+GROUP_ORDER = (1, 3, 0, 2)
 UNLISTED = 1e19
 
 VMEM = pl.BlockSpec(memory_space=pltpu.VMEM)
@@ -160,17 +160,17 @@
     sums_out[0:1, :], sums_out[1:2, :] = sums(parts)
 
 
-def forward_other(
-    packed, own_blocks, pair_blocks, inverse, own_sums, shares, expo_out, scaled_out, sent_out
-):
-    core = lax.axis_index("core")
-    own = exponentials(packed, core, own_blocks, inverse[0])
-    pair = exponentials(packed, 1 - core, pair_blocks, inverse[1])
-    expo_out[...] = jnp.where(own[1], -1.0, own[0])
-    scaled_out[...] = own[2]
+def forward_other(packed, own_blocks, inverse, expo_out, scaled_out):
+    expo, onehot, scaled = exponentials(packed, lax.axis_index("core"), own_blocks, inverse[0])
+    expo_out[...] = jnp.where(onehot, -1.0, expo)
+    scaled_out[...] = scaled
+
+
+def with_sums(shares, own_sums, other_sums, other_expo, sent_out):
+    del other_expo
     rows, wide = shares.shape
     sent_out[:, :wide] = shares[...]
-    total = jnp.concatenate([own_sums[...], *sums([own, pair])], axis=0)
+    total = jnp.concatenate([own_sums[...], other_sums[...]], axis=0)
     high = total.astype(jnp.bfloat16)
     low = (total - high.astype(jnp.float32)).astype(jnp.bfloat16)
     tile = jnp.concatenate([high.astype(jnp.float32), low.astype(jnp.float32)], axis=0)
@@ -357,6 +357,7 @@
         own_blocks,
         pair_blocks,
     )
+    other_sums = with_partner(own_sums)
     going = run(
         shares,
         shape((half, 2 * width), bf16),
@@ -366,20 +367,22 @@
         own_blocks,
         pair_blocks,
     )
-    other_expo, other_scaled, sent = run(
+    other_expo, other_scaled = run(
         forward_other,
-        (
-            shape((BLK, half), f32),
-            shape((BLK, half), f32),
-            shape((half, 2 * width + 128), bf16),
-        ),
-        [VMEM] * 6,
+        (shape((BLK, half), f32), shape((BLK, half), f32)),
+        [VMEM] * 3,
         other_packed,
         own_blocks,
-        pair_blocks,
         inverse,
+    )
+    sent = run(
+        with_sums,
+        shape((half, 2 * width + 128), bf16),
+        [VMEM] * 3 + [pl.BlockSpec(memory_space=pl.ANY)],
+        going,
         own_sums,
-        going,
+        other_sums,
+        other_expo,
     )
     received = exchange_chips(sent.reshape(chips, tok_dev, 2 * width + 128))
     outs = (shape((held, BLK, width), f32), shape((tok_dev, width), f32), shape((1, tok_dev), f32))

time: 32.1 us -> 33.4 us (1.040)
  blocking collectives: 26.2 us -> 27.6 us
  starting transfers between devices: 0.52 us -> 1.09 us
  waiting for transfers between devices: 0.54 us -> 0.16 us
    all_to_all x2, blocking collectives: 26.2 us -> 27.6 us  [exchange(): lax.all_to_all(pieces, axes, split_axis=0, concat_axis=0, axis_index_grou...]
    ppermute x2 -> x3, starting transfers between devices: 0.52 us -> 1.09 us  [with_partner(): return lax.ppermute(value, 'core', [(0, 1), (1, 0)])]
    ppermute x2 -> x3, waiting for transfers between devices: 0.54 us -> 0.16 us  [with_partner(): return lax.ppermute(value, 'core', [(0, 1), (1, 0)])]
    pallas_call x5 -> x6, Pallas kernels: 3.8 us -> 3.63 us  [run(): pl.pallas_call(kernel, out_shape=out_shape, in_specs=in_specs, out_specs=...]
  transfers between devices with their start and end apart: 2 -> 3, of which waited for: 1 -> 1; matrix products, arithmetic and copies ran while one was open for 0% -> 0% of each run, Pallas kernels for 3% -> 3%
where the time goes in v20:
time: 33.4 us; the launch traced here: 33.1 us
  blocking collectives  27.6 us (83%)
  Pallas kernels  3.63 us (11%)
  starting transfers between devices  1.09 us (3%)
  between operations  0.66 us (2%)
    all_to_all x2, blocking collectives, exchange(): lax.all_to_all(pieces, axes, split_axis=0, concat_axis=0, axis_index_grou...  27.6 us
    pallas_call x6, Pallas kernels, run(): pl.pallas_call(kernel, out_shape=out_shape, in_specs=in_specs, out_specs=...  3.63 us
    ppermute x3, starting transfers between devices, with_partner(): return lax.ppermute(value, 'core', [(0, 1), (1, 0)])  1.09 us
  transfers between devices with their start and end apart: 3, of which 1 were waited for; matrix products, arithmetic and copies ran while one was open for 0% of the time, Pallas kernels for 3%

profile of v20, /device:TPU:0, one launch (start us, length us, event | category | flops | bytes accessed | tf_op | source)
XLA Modules:
  0.0 33.1 jit_solution(2547717589144939081)
XLA Ops:
  0.6 1.2 %shard_map.76 = (bf16[16,8,640]{2,1,0:T(8,128)(2,1)S(1)}, bf16[4,128,512]{2,1,0:T(8,128)(2,1)S(1)}, bf16[4,128,512]{2,1,0:T(8,128)(2,1)S(1)}, s32[1,128]{1,0:T(1,128)S(1)}, bf16[8,512]{1,0:T(8,128)(2,1)S(1)}) custom-call(bf16[8,512]{1,0:T(8,128)(2,1)} %features.1, s32[1,64]{1,0:T(1,128)} %bitcast.13, bf16[4,128,512]{2,1,0:T(8,128)(2,1)} %bitcast.12, ...), custom_call_target="tpu_custom_call" | custom-call | bytes 1753888 | tf_op jit(solution)/shard_map/pallas_call | solution.py:37
  1.8 0.5 %collective-permute-start = (bf16[4,128,512]{2,1,0:T(8,128)(2,1)S(1)}, bf16[4,128,512]{2,1,0:T(8,128)(2,1)S(1)}, u32[]{:S(2)}, u32[]{:S(2)}) collective-permute-start(bf16[4,128,512]{2,1,0:T(8,128)(2,1)S(1)} %get-tuple-element.19.own_blocks), channel_id=1, source_target_pairs={{0,1},{1,0},{2,3},{3,2},{4,5},{5,4},{6,7},{7,6},{8,9},{9,8},{10,11... | collective-permute-start | bytes 1572872 | tf_op jit(solution)/shard_map/ppermute | solution.py:305
  2.3 14.1 %all_to_all.10 = bf16[16,8,640]{2,1,0:T(8,128)(2,1)S(1)} all-to-all(bf16[16,8,640]{2,1,0:T(8,128)(2,1)S(1)} %get-tuple-element.18), channel_id=1, replica_groups={{14,30,6,22,12,28,4,20,10,26,2,18,8,24,0,16},{15,31,7,23,13,29,5,21,11,..., dimensions={0} | all-to-all | bytes 327680 | tf_op jit(solution)/shard_map/all_to_all | solution.py:293
  16.4 0.0 collective-permute-start.2
  16.4 0.0 collective-permute-done.pair_blocks
  16.4 0.5 %shard_map.77 = (f32[2,128,128]{2,1,0:T(8,128)S(1)}, f32[128,128]{1,0:T(8,128)S(1)}, f32[2,128,128]{2,1,0:T(8,128)S(1)}, f32[2,128]{1,0:T(2,128)S(1)}) custom-call(bf16[128,640]{1,0:T(8,128)(2,1)S(1)} %bitcast.9, bf16[4,128,512]{2,1,0:T(8,128)(2,1)S(1)} %get-tuple-element.19.own_blocks, bf16[4,128,512]{2,1,0:T(8,128)(2,1)S(1)} %collective-permute-done.pair_blocks), custom_call_target="tpu_custom_call" | custom-call | bytes 1541120 | tf_op jit(solution)/shard_map/pallas_call | solution.py:37
  16.9 0.6 %collective-permute-start.1 = (f32[2,128]{1,0:T(2,128)S(1)}, f32[2,128]{1,0:T(2,128)S(1)}, u32[]{:S(2)}, u32[]{:S(2)}) collective-permute-start(f32[2,128]{1,0:T(2,128)S(1)} %get-tuple-element.22.own_sums), channel_id=1, source_target_pairs={{0,1},{1,0},{2,3},{3,2},{4,5},{5,4},{6,7},{7,6},{8,9},{9,8},{10,11... | collective-permute-start | bytes 3080 | tf_op jit(solution)/shard_map/ppermute | solution.py:305
  17.5 0.3 %shard_map.78.shares = bf16[128,1024]{1,0:T(8,128)(2,1)S(1)} custom-call(f32[2,128,128]{2,1,0:T(8,128)S(1)} %get-tuple-element.20.expo, f32[2,128,128]{2,1,0:T(8,128)S(1)} %get-tuple-element.21.inverse, bf16[4,128,512]{2,1,0:T(8,128)(2,1)S(1)} %get-tuple-element.19.own_blocks, bf16[4,128,512]{2,1,0:T(8,128)(2,1)S(1)} %collective-permute-done.pair_blocks), custom_call_target="tpu_custom_call" | custom-call | bytes 1572864 | tf_op jit(solution)/shard_map/pallas_call | solution.py:37
  17.8 0.0 collective-permute-done.2.packed.other_packed
  17.8 0.3 shard_map.79
  18.2 0.2 collective-permute-done.1.other_sums
  18.3 13.5 %all_to_all.11.received = bf16[16,8,1152]{2,1,0:T(8,128)(2,1)S(1)} all-to-all(bf16[16,8,1152]{2,1,0:T(8,128)(2,1)S(1)} %bitcast.11), channel_id=1, replica_groups={{14,30,6,22,12,28,4,20,10,26,2,18,8,24,0,16},{15,31,7,23,13,29,5,21,11,..., dimensions={0} | all-to-all | bytes 589824 | tf_op jit(solution)/shard_map/all_to_all | solution.py:293
  31.9 1.3 %shard_map.81 = (f32[4,128,512]{2,1,0:T(8,128)}, f32[8,512]{1,0:T(8,128)}, f32[1,8]{1,0:T(1,128)}) custom-call(s32[1,128]{1,0:T(1,128)S(1)} %get-tuple-element.17.named, bf16[16,8,1152]{2,1,0:T(8,128)(2,1)S(1)} %all_to_all.11.received, f32[2,128,128]{2,1,0:T(8,128)S(1)} %get-tuple-element.20.expo, f32[128,128]{1,0:T(8,128)S(1)} %get-tuple-element.23.other_expo, ...), custom_call_target="tpu_custom_call" | custom-call | bytes 2679328 | tf_op jit(solution)/shard_map/pallas_call | solution.py:37
  (1 shorter events, 0.0 us)
Async XLA Ops:
  1.8 14.6 %collective-permute-start = (bf16[4,128,512]{2,1,0:T(8,128)(2,1)S(1)}, bf16[4,128,512]{2,1,0:T(8,128)(2,1)S(1)}, u32[]{:S(2)}, u32[]{:S(2)}) collective-permute-start(bf16[4,128,512]{2,1,0:T(8,128)(2,1)S(1)} %get-tuple-element.19.own_blocks), channel_id=1, source_target_pairs={{0,1},{1,0},{2,3},{3,2},{4,5},{5,4},{6,7},{7,6},{8,9},{9,8},{10,11... | collective-permute-start | bytes 1572872 | tf_op jit(solution)/shard_map/ppermute | solution.py:305
  16.4 1.4 %collective-permute-start.2 = (bf16[128,640]{1,0:T(8,128)(2,1)S(1)}, bf16[128,640]{1,0:T(8,128)(2,1)S(1)}, u32[]{:S(2)}, u32[]{:S(2)}) collective-permute-start(bf16[128,640]{1,0:T(8,128)(2,1)S(1)} %bitcast.8), channel_id=1, source_target_pairs={{0,1},{1,0},{2,3},{3,2},{4,5},{5,4},{6,7},{7,6},{8,9},{9,8},{10,11... | collective-permute-start | bytes 491528 | tf_op jit(solution)/shard_map/ppermute | solution.py:305
  16.9 1.4 %collective-permute-start.1 = (f32[2,128]{1,0:T(2,128)S(1)}, f32[2,128]{1,0:T(2,128)S(1)}, u32[]{:S(2)}, u32[]{:S(2)}) collective-permute-start(f32[2,128]{1,0:T(2,128)S(1)} %get-tuple-element.22.own_sums), channel_id=1, source_target_pairs={{0,1},{1,0},{2,3},{3,2},{4,5},{5,4},{6,7},{7,6},{8,9},{9,8},{10,11... | collective-permute-start | bytes 3080 | tf_op jit(solution)/shard_map/ppermute | solution.py:305

commit v21 on v19

--- a/solution.py
+++ b/solution.py
@@ -238,11 +238,12 @@
     other_scale = logit_scale / (other_rest + other_label)
     own = expo[0]
     other = other_expo[...]
-    own = jnp.where(own < 0.0, -own_rest, own) * (own_scale * inverse[0])
-    other = jnp.where(other < 0.0, -other_rest, other) * (other_scale * inverse[0])
-    weights = jnp.concatenate([own, other], axis=1)
+    own = jnp.where(own < 0.0, -own_rest, own) * own_scale
+    other = jnp.where(other < 0.0, -other_rest, other) * other_scale
+    weights = jnp.concatenate([own, other], axis=1).astype(jnp.bfloat16).astype(jnp.float32)
     pulls = weights * jnp.concatenate([scaled[...], other_scaled[...]], axis=1)
-    named = jnp.concatenate([named[...], named[...]], axis=1)
+    own_named = named[...]
+    named = jnp.concatenate([own_named, own_named], axis=1)
     moves = []
 
     def leave(source, target):
@@ -252,8 +253,10 @@
 
     def block_out(b):
         mine = jnp.where(named == b, weights, 0.0).astype(jnp.bfloat16)
-        back = jnp.sum(jnp.where(named == b, pulls, 0.0), axis=1, keepdims=True)
-        grad[b] = contract(mine, units, 1, 0) - back * centres[b].astype(jnp.float32)
+        factor = jnp.max(jnp.where(own_named == b, inverse[0], 0.0), axis=1, keepdims=True)
+        back = factor * jnp.sum(jnp.where(named == b, pulls, 0.0), axis=1, keepdims=True)
+        slot_grad = contract(mine, units, 1, 0)
+        grad[b] = factor * slot_grad - back * centres[b].astype(jnp.float32)
         for part in (pl.ds(0, BLK // 2), pl.ds(BLK // 2, BLK // 2)):
             leave(grad.at[b, part], grad_out.at[b, part])
 

time: 32.1 us -> 32.1 us (level)
  no operation moved by 1% of the time
where the time goes in v21:
time: 32.1 us; the launch traced here: 31.8 us
  blocking collectives  26.2 us (82%)
  Pallas kernels  3.84 us (12%)
  between operations  0.65 us (2%)
  waiting for transfers between devices  0.54 us (2%)
  starting transfers between devices  0.52 us (2%)
    all_to_all x2, blocking collectives, exchange(): lax.all_to_all(pieces, axes, split_axis=0, concat_axis=0, axis_index_grou...  26.2 us
    pallas_call x5, Pallas kernels, run(): pl.pallas_call(kernel, out_shape=out_shape, in_specs=in_specs, out_specs=...  3.84 us
  transfers between devices with their start and end apart: 2, of which 1 were waited for; matrix products, arithmetic and copies ran while one was open for 0% of the time, Pallas kernels for 3%

profile of v21, /device:TPU:0, one launch (start us, length us, event | category | flops | bytes accessed | tf_op | source)
XLA Modules:
  0.0 31.8 jit_solution(16484948991265021830)
XLA Ops:
  0.6 1.2 %shard_map.76 = (bf16[16,8,640]{2,1,0:T(8,128)(2,1)S(1)}, bf16[4,128,512]{2,1,0:T(8,128)(2,1)S(1)}, bf16[4,128,512]{2,1,0:T(8,128)(2,1)S(1)}, s32[1,128]{1,0:T(1,128)S(1)}, bf16[8,512]{1,0:T(8,128)(2,1)S(1)}) custom-call(bf16[8,512]{1,0:T(8,128)(2,1)} %features.1, s32[1,64]{1,0:T(1,128)} %bitcast.13, bf16[4,128,512]{2,1,0:T(8,128)(2,1)} %bitcast.12, ...), custom_call_target="tpu_custom_call" | custom-call | bytes 1753888 | tf_op jit(solution)/shard_map/pallas_call | solution.py:37
  1.8 0.5 %collective-permute-start.1 = (bf16[4,128,512]{2,1,0:T(8,128)(2,1)S(1)}, bf16[4,128,512]{2,1,0:T(8,128)(2,1)S(1)}, u32[]{:S(2)}, u32[]{:S(2)}) collective-permute-start(bf16[4,128,512]{2,1,0:T(8,128)(2,1)S(1)} %get-tuple-element.20.own_blocks), channel_id=1, source_target_pairs={{0,1},{1,0},{2,3},{3,2},{4,5},{5,4},{6,7},{7,6},{8,9},{9,8},{10,11... | collective-permute-start | bytes 1572872 | tf_op jit(solution)/shard_map/ppermute | solution.py:308
  2.3 13.2 %all_to_all.10 = bf16[16,8,640]{2,1,0:T(8,128)(2,1)S(1)} all-to-all(bf16[16,8,640]{2,1,0:T(8,128)(2,1)S(1)} %get-tuple-element.19), channel_id=1, replica_groups={{22,6,30,14,20,4,28,12,18,2,26,10,16,0,24,8},{23,7,31,15,21,5,29,13,19,..., dimensions={0} | all-to-all | bytes 327680 | tf_op jit(solution)/shard_map/all_to_all | solution.py:296
  15.5 0.0 collective-permute-start
  15.6 0.0 collective-permute-done.1.pair_blocks
  15.6 0.5 %shard_map.77 = (f32[2,128,128]{2,1,0:T(8,128)S(1)}, f32[128,128]{1,0:T(8,128)S(1)}, f32[2,128,128]{2,1,0:T(8,128)S(1)}, f32[2,128]{1,0:T(2,128)S(1)}) custom-call(bf16[128,640]{1,0:T(8,128)(2,1)S(1)} %bitcast.9, bf16[4,128,512]{2,1,0:T(8,128)(2,1)S(1)} %get-tuple-element.20.own_blocks, bf16[4,128,512]{2,1,0:T(8,128)(2,1)S(1)} %collective-permute-done.1.pair_blocks), custom_call_target="tpu_custom_call" | custom-call | bytes 1541120 | tf_op jit(solution)/shard_map/pallas_call | solution.py:37
  16.1 0.3 %shard_map.78.shares = bf16[128,1024]{1,0:T(8,128)(2,1)S(1)} custom-call(f32[2,128,128]{2,1,0:T(8,128)S(1)} %get-tuple-element.23.expo, f32[2,128,128]{2,1,0:T(8,128)S(1)} %get-tuple-element.21.inverse, bf16[4,128,512]{2,1,0:T(8,128)(2,1)S(1)} %get-tuple-element.20.own_blocks, bf16[4,128,512]{2,1,0:T(8,128)(2,1)S(1)} %collective-permute-done.1.pair_blocks), custom_call_target="tpu_custom_call" | custom-call | bytes 1572864 | tf_op jit(solution)/shard_map/pallas_call | solution.py:37
  16.4 0.5 %collective-permute-done.packed.other_packed = bf16[128,640]{1,0:T(8,128)(2,1)S(1)} collective-permute-done((bf16[128,640]{1,0:T(8,128)(2,1)S(1)}, bf16[128,640]{1,0:T(8,128)(2,1)S(1)}, u32[]{:S(2)}, u32[]{:S(2)}) %collective-permute-start) | collective-permute-done | bytes 163872 | tf_op jit(solution)/shard_map/ppermute | solution.py:308
  16.9 0.5 %shard_map.79 = (f32[128,128]{1,0:T(8,128)S(1)}, f32[128,128]{1,0:T(8,128)S(1)}, bf16[128,1152]{1,0:T(8,128)(2,1)S(1)}) custom-call(bf16[128,640]{1,0:T(8,128)(2,1)S(1)} %collective-permute-done.packed.other_packed, bf16[4,128,512]{2,1,0:T(8,128)(2,1)S(1)} %get-tuple-element.20.own_blocks, bf16[4,128,512]{2,1,0:T(8,128)(2,1)S(1)} %collective-permute-done.1.pair_blocks, ...), custom_call_target="tpu_custom_call" | custom-call | bytes 2032640 | tf_op jit(solution)/shard_map/pallas_call | solution.py:37
  17.4 13.0 %all_to_all.11.received = bf16[16,8,1152]{2,1,0:T(8,128)(2,1)S(1)} all-to-all(bf16[16,8,1152]{2,1,0:T(8,128)(2,1)S(1)} %bitcast.11), channel_id=1, replica_groups={{22,6,30,14,20,4,28,12,18,2,26,10,16,0,24,8},{23,7,31,15,21,5,29,13,19,..., dimensions={0} | all-to-all | bytes 589824 | tf_op jit(solution)/shard_map/all_to_all | solution.py:296
  30.5 1.3 %shard_map.80 = (f32[4,128,512]{2,1,0:T(8,128)}, f32[8,512]{1,0:T(8,128)}, f32[1,8]{1,0:T(1,128)}) custom-call(s32[1,128]{1,0:T(1,128)S(1)} %get-tuple-element.18.named, bf16[16,8,1152]{2,1,0:T(8,128)(2,1)S(1)} %all_to_all.11.received, f32[2,128,128]{2,1,0:T(8,128)S(1)} %get-tuple-element.23.expo, f32[128,128]{1,0:T(8,128)S(1)} %get-tuple-element.25.other_expo, ...), custom_call_target="tpu_custom_call" | custom-call | bytes 2679328 | tf_op jit(solution)/shard_map/pallas_call | solution.py:37
Async XLA Ops:
  1.8 13.7 %collective-permute-start.1 = (bf16[4,128,512]{2,1,0:T(8,128)(2,1)S(1)}, bf16[4,128,512]{2,1,0:T(8,128)(2,1)S(1)}, u32[]{:S(2)}, u32[]{:S(2)}) collective-permute-start(bf16[4,128,512]{2,1,0:T(8,128)(2,1)S(1)} %get-tuple-element.20.own_blocks), channel_id=1, source_target_pairs={{0,1},{1,0},{2,3},{3,2},{4,5},{5,4},{6,7},{7,6},{8,9},{9,8},{10,11... | collective-permute-start | bytes 1572872 | tf_op jit(solution)/shard_map/ppermute | solution.py:308
  15.5 1.4 %collective-permute-start = (bf16[128,640]{1,0:T(8,128)(2,1)S(1)}, bf16[128,640]{1,0:T(8,128)(2,1)S(1)}, u32[]{:S(2)}, u32[]{:S(2)}) collective-permute-start(bf16[128,640]{1,0:T(8,128)(2,1)S(1)} %bitcast.8), channel_id=1, source_target_pairs={{0,1},{1,0},{2,3},{3,2},{4,5},{5,4},{6,7},{7,6},{8,9},{9,8},{10,11... | collective-permute-start | bytes 491528 | tf_op jit(solution)/shard_map/ppermute | solution.py:308

commit v22 on v21

--- a/solution.py
+++ b/solution.py
@@ -73,12 +73,12 @@
                 (labels, held_labels),
                 (ids, held_ids),
                 (listed, held_listed),
-                (centres, centres_out),
+                *((centres.at[b], centres_out.at[b]) for b in range(centres.shape[0])),
             )
         )
     ]
-    for move in moves:
-        move.start()
+    for i, move in enumerate(moves):
+        move.start(priority=i % 2)
     moves[0].wait()
     moves[1].wait()
     chip = lax.axis_index("chip")
@@ -248,7 +248,7 @@
 
     def leave(source, target):
         move = pltpu.make_async_copy(source, target, left.at[len(moves)])
-        move.start()
+        move.start(priority=len(moves) % 2)
         moves.append(move)
 
     def block_out(b):
@@ -341,7 +341,7 @@
             pltpu.VMEM((1, labels.shape[0]), labels.dtype),
             pltpu.SMEM((1, groups), block_ids.dtype),
             pltpu.SMEM((1, groups), listed.dtype),
-            pltpu.SemaphoreType.DMA((5,)),
+            pltpu.SemaphoreType.DMA((4 + held,)),
         ],
     )
     pair_blocks = with_partner(own_blocks)

time: 32.1 us -> 32.2 us (level)
  no operation moved by 1% of the time
where the time goes in v22:
time: 32.2 us; the launch traced here: 31.9 us
  blocking collectives  26.2 us (81%)
  Pallas kernels  3.92 us (12%)
  between operations  0.65 us (2%)
  waiting for transfers between devices  0.54 us (2%)
  starting transfers between devices  0.52 us (2%)
    all_to_all x2, blocking collectives, exchange(): lax.all_to_all(pieces, axes, split_axis=0, concat_axis=0, axis_index_grou...  26.2 us
    pallas_call x5, Pallas kernels, run(): pl.pallas_call(kernel, out_shape=out_shape, in_specs=in_specs, out_specs=...  3.92 us
  transfers between devices with their start and end apart: 2, of which 1 were waited for; matrix products, arithmetic and copies ran while one was open for 0% of the time, Pallas kernels for 3%

profile of v22, /device:TPU:0, one launch (start us, length us, event | category | flops | bytes accessed | tf_op | source)
XLA Modules:
  0.0 31.9 jit_solution(3305204266147215923)
XLA Ops:
  0.6 1.2 %shard_map.76 = (bf16[16,8,640]{2,1,0:T(8,128)(2,1)S(1)}, bf16[4,128,512]{2,1,0:T(8,128)(2,1)S(1)}, bf16[4,128,512]{2,1,0:T(8,128)(2,1)S(1)}, s32[1,128]{1,0:T(1,128)S(1)}, bf16[8,512]{1,0:T(8,128)(2,1)S(1)}) custom-call(bf16[8,512]{1,0:T(8,128)(2,1)} %features.1, s32[1,64]{1,0:T(1,128)} %bitcast.13, bf16[4,128,512]{2,1,0:T(8,128)(2,1)} %bitcast.12, ...), custom_call_target="tpu_custom_call" | custom-call | bytes 1753888 | tf_op jit(solution)/shard_map/pallas_call | solution.py:37
  1.9 0.5 %collective-permute-start.1 = (bf16[4,128,512]{2,1,0:T(8,128)(2,1)S(1)}, bf16[4,128,512]{2,1,0:T(8,128)(2,1)S(1)}, u32[]{:S(2)}, u32[]{:S(2)}) collective-permute-start(bf16[4,128,512]{2,1,0:T(8,128)(2,1)S(1)} %get-tuple-element.20.own_blocks), channel_id=1, source_target_pairs={{0,1},{1,0},{2,3},{3,2},{4,5},{5,4},{6,7},{7,6},{8,9},{9,8},{10,11... | collective-permute-start | bytes 1572872 | tf_op jit(solution)/shard_map/ppermute | solution.py:308
  2.4 13.2 %all_to_all.10 = bf16[16,8,640]{2,1,0:T(8,128)(2,1)S(1)} all-to-all(bf16[16,8,640]{2,1,0:T(8,128)(2,1)S(1)} %get-tuple-element.19), channel_id=1, replica_groups={{22,6,30,14,20,4,28,12,18,2,26,10,16,0,24,8},{23,7,31,15,21,5,29,13,19,..., dimensions={0} | all-to-all | bytes 327680 | tf_op jit(solution)/shard_map/all_to_all | solution.py:296
  15.6 0.0 collective-permute-start
  15.6 0.0 collective-permute-done.1.pair_blocks
  15.6 0.5 %shard_map.77 = (f32[2,128,128]{2,1,0:T(8,128)S(1)}, f32[128,128]{1,0:T(8,128)S(1)}, f32[2,128,128]{2,1,0:T(8,128)S(1)}, f32[2,128]{1,0:T(2,128)S(1)}) custom-call(bf16[128,640]{1,0:T(8,128)(2,1)S(1)} %bitcast.9, bf16[4,128,512]{2,1,0:T(8,128)(2,1)S(1)} %get-tuple-element.20.own_blocks, bf16[4,128,512]{2,1,0:T(8,128)(2,1)S(1)} %collective-permute-done.1.pair_blocks), custom_call_target="tpu_custom_call" | custom-call | bytes 1541120 | tf_op jit(solution)/shard_map/pallas_call | solution.py:37
  16.1 0.3 %shard_map.78.shares = bf16[128,1024]{1,0:T(8,128)(2,1)S(1)} custom-call(f32[2,128,128]{2,1,0:T(8,128)S(1)} %get-tuple-element.23.expo, f32[2,128,128]{2,1,0:T(8,128)S(1)} %get-tuple-element.21.inverse, bf16[4,128,512]{2,1,0:T(8,128)(2,1)S(1)} %get-tuple-element.20.own_blocks, bf16[4,128,512]{2,1,0:T(8,128)(2,1)S(1)} %collective-permute-done.1.pair_blocks), custom_call_target="tpu_custom_call" | custom-call | bytes 1572864 | tf_op jit(solution)/shard_map/pallas_call | solution.py:37
  16.5 0.5 %collective-permute-done.packed.other_packed = bf16[128,640]{1,0:T(8,128)(2,1)S(1)} collective-permute-done((bf16[128,640]{1,0:T(8,128)(2,1)S(1)}, bf16[128,640]{1,0:T(8,128)(2,1)S(1)}, u32[]{:S(2)}, u32[]{:S(2)}) %collective-permute-start) | collective-permute-done | bytes 163872 | tf_op jit(solution)/shard_map/ppermute | solution.py:308
  17.0 0.5 %shard_map.79 = (f32[128,128]{1,0:T(8,128)S(1)}, f32[128,128]{1,0:T(8,128)S(1)}, bf16[128,1152]{1,0:T(8,128)(2,1)S(1)}) custom-call(bf16[128,640]{1,0:T(8,128)(2,1)S(1)} %collective-permute-done.packed.other_packed, bf16[4,128,512]{2,1,0:T(8,128)(2,1)S(1)} %get-tuple-element.20.own_blocks, bf16[4,128,512]{2,1,0:T(8,128)(2,1)S(1)} %collective-permute-done.1.pair_blocks, ...), custom_call_target="tpu_custom_call" | custom-call | bytes 2032640 | tf_op jit(solution)/shard_map/pallas_call | solution.py:37
  17.5 13.0 %all_to_all.11.received = bf16[16,8,1152]{2,1,0:T(8,128)(2,1)S(1)} all-to-all(bf16[16,8,1152]{2,1,0:T(8,128)(2,1)S(1)} %bitcast.11), channel_id=1, replica_groups={{22,6,30,14,20,4,28,12,18,2,26,10,16,0,24,8},{23,7,31,15,21,5,29,13,19,..., dimensions={0} | all-to-all | bytes 589824 | tf_op jit(solution)/shard_map/all_to_all | solution.py:296
  30.5 1.3 %shard_map.80 = (f32[4,128,512]{2,1,0:T(8,128)}, f32[8,512]{1,0:T(8,128)}, f32[1,8]{1,0:T(1,128)}) custom-call(s32[1,128]{1,0:T(1,128)S(1)} %get-tuple-element.18.named, bf16[16,8,1152]{2,1,0:T(8,128)(2,1)S(1)} %all_to_all.11.received, f32[2,128,128]{2,1,0:T(8,128)S(1)} %get-tuple-element.23.expo, f32[128,128]{1,0:T(8,128)S(1)} %get-tuple-element.25.other_expo, ...), custom_call_target="tpu_custom_call" | custom-call | bytes 2679328 | tf_op jit(solution)/shard_map/pallas_call | solution.py:37
Async XLA Ops:
  1.9 13.7 %collective-permute-start.1 = (bf16[4,128,512]{2,1,0:T(8,128)(2,1)S(1)}, bf16[4,128,512]{2,1,0:T(8,128)(2,1)S(1)}, u32[]{:S(2)}, u32[]{:S(2)}) collective-permute-start(bf16[4,128,512]{2,1,0:T(8,128)(2,1)S(1)} %get-tuple-element.20.own_blocks), channel_id=1, source_target_pairs={{0,1},{1,0},{2,3},{3,2},{4,5},{5,4},{6,7},{7,6},{8,9},{9,8},{10,11... | collective-permute-start | bytes 1572872 | tf_op jit(solution)/shard_map/ppermute | solution.py:308
  15.6 1.4 %collective-permute-start = (bf16[128,640]{1,0:T(8,128)(2,1)S(1)}, bf16[128,640]{1,0:T(8,128)(2,1)S(1)}, u32[]{:S(2)}, u32[]{:S(2)}) collective-permute-start(bf16[128,640]{1,0:T(8,128)(2,1)S(1)} %bitcast.8), channel_id=1, source_target_pairs={{0,1},{1,0},{2,3},{3,2},{4,5},{5,4},{6,7},{7,6},{8,9},{9,8},{10,11... | collective-permute-start | bytes 491528 | tf_op jit(solution)/shard_map/ppermute | solution.py:308

commit v23 on v21

--- a/solution.py
+++ b/solution.py
@@ -257,8 +257,7 @@
         back = factor * jnp.sum(jnp.where(named == b, pulls, 0.0), axis=1, keepdims=True)
         slot_grad = contract(mine, units, 1, 0)
         grad[b] = factor * slot_grad - back * centres[b].astype(jnp.float32)
-        for part in (pl.ds(0, BLK // 2), pl.ds(BLK // 2, BLK // 2)):
-            leave(grad.at[b, part], grad_out.at[b, part])
+        leave(grad.at[b], grad_out.at[b])
 
     for b in range(held // 2):
         block_out(b)
@@ -404,7 +403,7 @@
         out_spec=HBM,
         scratch=[
             *(pltpu.VMEM(out.shape, out.dtype) for out in outs),
-            pltpu.SemaphoreType.DMA((2 * held + 2,)),
+            pltpu.SemaphoreType.DMA((held + 2,)),
         ],
     )
     return (loss.reshape(tok_dev), feature_grad, centre_grad.reshape(held * BLK, width))

time: 32.1 us -> 32.1 us (level)
  no operation moved by 1% of the time
where the time goes in v23:
time: 32.1 us; the launch traced here: 31.8 us
  blocking collectives  26.2 us (82%)
  Pallas kernels  3.82 us (12%)
  between operations  0.65 us (2%)
  waiting for transfers between devices  0.54 us (2%)
  starting transfers between devices  0.52 us (2%)
    all_to_all x2, blocking collectives, exchange(): lax.all_to_all(pieces, axes, split_axis=0, concat_axis=0, axis_index_grou...  26.2 us
    pallas_call x5, Pallas kernels, run(): pl.pallas_call(kernel, out_shape=out_shape, in_specs=in_specs, out_specs=...  3.82 us
  transfers between devices with their start and end apart: 2, of which 1 were waited for; matrix products, arithmetic and copies ran while one was open for 0% of the time, Pallas kernels for 3%

profile of v23, /device:TPU:0, one launch (start us, length us, event | category | flops | bytes accessed | tf_op | source)
XLA Modules:
  0.0 31.8 jit_solution(1195674429980576979)
XLA Ops:
  0.6 1.2 %shard_map.76 = (bf16[16,8,640]{2,1,0:T(8,128)(2,1)S(1)}, bf16[4,128,512]{2,1,0:T(8,128)(2,1)S(1)}, bf16[4,128,512]{2,1,0:T(8,128)(2,1)S(1)}, s32[1,128]{1,0:T(1,128)S(1)}, bf16[8,512]{1,0:T(8,128)(2,1)S(1)}) custom-call(bf16[8,512]{1,0:T(8,128)(2,1)} %features.1, s32[1,64]{1,0:T(1,128)} %bitcast.13, bf16[4,128,512]{2,1,0:T(8,128)(2,1)} %bitcast.12, ...), custom_call_target="tpu_custom_call" | custom-call | bytes 1753888 | tf_op jit(solution)/shard_map/pallas_call | solution.py:37
  1.8 0.5 %collective-permute-start.1 = (bf16[4,128,512]{2,1,0:T(8,128)(2,1)S(1)}, bf16[4,128,512]{2,1,0:T(8,128)(2,1)S(1)}, u32[]{:S(2)}, u32[]{:S(2)}) collective-permute-start(bf16[4,128,512]{2,1,0:T(8,128)(2,1)S(1)} %get-tuple-element.20.own_blocks), channel_id=1, source_target_pairs={{0,1},{1,0},{2,3},{3,2},{4,5},{5,4},{6,7},{7,6},{8,9},{9,8},{10,11... | collective-permute-start | bytes 1572872 | tf_op jit(solution)/shard_map/ppermute | solution.py:307
  2.3 13.2 %all_to_all.10 = bf16[16,8,640]{2,1,0:T(8,128)(2,1)S(1)} all-to-all(bf16[16,8,640]{2,1,0:T(8,128)(2,1)S(1)} %get-tuple-element.19), channel_id=1, replica_groups={{22,6,30,14,20,4,28,12,18,2,26,10,16,0,24,8},{23,7,31,15,21,5,29,13,19,..., dimensions={0} | all-to-all | bytes 327680 | tf_op jit(solution)/shard_map/all_to_all | solution.py:295
  15.5 0.0 collective-permute-start
  15.6 0.0 collective-permute-done.1.pair_blocks
  15.6 0.5 %shard_map.77 = (f32[2,128,128]{2,1,0:T(8,128)S(1)}, f32[128,128]{1,0:T(8,128)S(1)}, f32[2,128,128]{2,1,0:T(8,128)S(1)}, f32[2,128]{1,0:T(2,128)S(1)}) custom-call(bf16[128,640]{1,0:T(8,128)(2,1)S(1)} %bitcast.9, bf16[4,128,512]{2,1,0:T(8,128)(2,1)S(1)} %get-tuple-element.20.own_blocks, bf16[4,128,512]{2,1,0:T(8,128)(2,1)S(1)} %collective-permute-done.1.pair_blocks), custom_call_target="tpu_custom_call" | custom-call | bytes 1541120 | tf_op jit(solution)/shard_map/pallas_call | solution.py:37
  16.1 0.3 %shard_map.78.shares = bf16[128,1024]{1,0:T(8,128)(2,1)S(1)} custom-call(f32[2,128,128]{2,1,0:T(8,128)S(1)} %get-tuple-element.23.expo, f32[2,128,128]{2,1,0:T(8,128)S(1)} %get-tuple-element.21.inverse, bf16[4,128,512]{2,1,0:T(8,128)(2,1)S(1)} %get-tuple-element.20.own_blocks, bf16[4,128,512]{2,1,0:T(8,128)(2,1)S(1)} %collective-permute-done.1.pair_blocks), custom_call_target="tpu_custom_call" | custom-call | bytes 1572864 | tf_op jit(solution)/shard_map/pallas_call | solution.py:37
  16.4 0.5 %collective-permute-done.packed.other_packed = bf16[128,640]{1,0:T(8,128)(2,1)S(1)} collective-permute-done((bf16[128,640]{1,0:T(8,128)(2,1)S(1)}, bf16[128,640]{1,0:T(8,128)(2,1)S(1)}, u32[]{:S(2)}, u32[]{:S(2)}) %collective-permute-start) | collective-permute-done | bytes 163872 | tf_op jit(solution)/shard_map/ppermute | solution.py:307
  16.9 0.5 %shard_map.79 = (f32[128,128]{1,0:T(8,128)S(1)}, f32[128,128]{1,0:T(8,128)S(1)}, bf16[128,1152]{1,0:T(8,128)(2,1)S(1)}) custom-call(bf16[128,640]{1,0:T(8,128)(2,1)S(1)} %collective-permute-done.packed.other_packed, bf16[4,128,512]{2,1,0:T(8,128)(2,1)S(1)} %get-tuple-element.20.own_blocks, bf16[4,128,512]{2,1,0:T(8,128)(2,1)S(1)} %collective-permute-done.1.pair_blocks, ...), custom_call_target="tpu_custom_call" | custom-call | bytes 2032640 | tf_op jit(solution)/shard_map/pallas_call | solution.py:37
  17.4 13.0 %all_to_all.11.received = bf16[16,8,1152]{2,1,0:T(8,128)(2,1)S(1)} all-to-all(bf16[16,8,1152]{2,1,0:T(8,128)(2,1)S(1)} %bitcast.11), channel_id=1, replica_groups={{22,6,30,14,20,4,28,12,18,2,26,10,16,0,24,8},{23,7,31,15,21,5,29,13,19,..., dimensions={0} | all-to-all | bytes 589824 | tf_op jit(solution)/shard_map/all_to_all | solution.py:295
  30.5 1.3 %shard_map.80 = (f32[4,128,512]{2,1,0:T(8,128)}, f32[8,512]{1,0:T(8,128)}, f32[1,8]{1,0:T(1,128)}) custom-call(s32[1,128]{1,0:T(1,128)S(1)} %get-tuple-element.18.named, bf16[16,8,1152]{2,1,0:T(8,128)(2,1)S(1)} %all_to_all.11.received, f32[2,128,128]{2,1,0:T(8,128)S(1)} %get-tuple-element.23.expo, f32[128,128]{1,0:T(8,128)S(1)} %get-tuple-element.25.other_expo, ...), custom_call_target="tpu_custom_call" | custom-call | bytes 2679328 | tf_op jit(solution)/shard_map/pallas_call | solution.py:37
Async XLA Ops:
  1.8 13.7 %collective-permute-start.1 = (bf16[4,128,512]{2,1,0:T(8,128)(2,1)S(1)}, bf16[4,128,512]{2,1,0:T(8,128)(2,1)S(1)}, u32[]{:S(2)}, u32[]{:S(2)}) collective-permute-start(bf16[4,128,512]{2,1,0:T(8,128)(2,1)S(1)} %get-tuple-element.20.own_blocks), channel_id=1, source_target_pairs={{0,1},{1,0},{2,3},{3,2},{4,5},{5,4},{6,7},{7,6},{8,9},{9,8},{10,11... | collective-permute-start | bytes 1572872 | tf_op jit(solution)/shard_map/ppermute | solution.py:307
  15.5 1.4 %collective-permute-start = (bf16[128,640]{1,0:T(8,128)(2,1)S(1)}, bf16[128,640]{1,0:T(8,128)(2,1)S(1)}, u32[]{:S(2)}, u32[]{:S(2)}) collective-permute-start(bf16[128,640]{1,0:T(8,128)(2,1)S(1)} %bitcast.8), channel_id=1, source_target_pairs={{0,1},{1,0},{2,3},{3,2},{4,5},{5,4},{6,7},{7,6},{8,9},{9,8},{10,11... | collective-permute-start | bytes 491528 | tf_op jit(solution)/shard_map/ppermute | solution.py:307

commit v24 on v23

--- a/solution.py
+++ b/solution.py
@@ -178,7 +178,7 @@
     sent_out[:, wide:] = tile.reshape(rows, 128).astype(jnp.bfloat16)
 
 
-def shares(expo, inverse, own_blocks, pair_blocks, shares_out):
+def shares(expo, inverse, own_blocks, pair_blocks, named, shares_out, factors_out):
     groups, _, width = own_blocks.shape
     others, label = [], []
     for k in range(2):
@@ -197,6 +197,8 @@
         rows = [places[g][part * count + i] for i in range(count) for g in range(groups)]
         rows = jnp.concatenate(rows, axis=0).astype(jnp.bfloat16)
         shares_out[:, part * width : (part + 1) * width] = rows
+    factors = [jnp.where(named[...] == b, inverse[0], 0.0) for b in range(groups)]
+    factors_out[...] = select([jnp.max(part, axis=1, keepdims=True) for part in factors], BLK)
 
 
 def backward(
@@ -206,7 +208,7 @@
     other_expo,
     scaled,
     other_scaled,
-    inverse,
+    factors,
     own_packed,
     other_packed,
     features,
@@ -242,8 +244,7 @@
     other = jnp.where(other < 0.0, -other_rest, other) * other_scale
     weights = jnp.concatenate([own, other], axis=1).astype(jnp.bfloat16).astype(jnp.float32)
     pulls = weights * jnp.concatenate([scaled[...], other_scaled[...]], axis=1)
-    own_named = named[...]
-    named = jnp.concatenate([own_named, own_named], axis=1)
+    named = jnp.concatenate([named[...], named[...]], axis=1)
     moves = []
 
     def leave(source, target):
@@ -253,7 +254,7 @@
 
     def block_out(b):
         mine = jnp.where(named == b, weights, 0.0).astype(jnp.bfloat16)
-        factor = jnp.max(jnp.where(own_named == b, inverse[0], 0.0), axis=1, keepdims=True)
+        factor = factors[:, b * 8 : b * 8 + 1]
         back = factor * jnp.sum(jnp.where(named == b, pulls, 0.0), axis=1, keepdims=True)
         slot_grad = contract(mine, units, 1, 0)
         grad[b] = factor * slot_grad - back * centres[b].astype(jnp.float32)
@@ -359,14 +360,15 @@
         own_blocks,
         pair_blocks,
     )
-    going = run(
+    going, factors = run(
         shares,
-        shape((half, 2 * width), bf16),
-        [VMEM] * 4,
+        (shape((half, 2 * width), bf16), shape((BLK, 128), f32)),
+        [VMEM] * 5,
         expo,
         inverse,
         own_blocks,
         pair_blocks,
+        named,
     )
     other_expo, other_scaled, sent = run(
         forward_other,
@@ -395,7 +397,7 @@
         other_expo,
         scaled,
         other_scaled,
-        inverse,
+        factors,
         own_packed,
         other_packed,
         own_features,
@@ -481,7 +483,7 @@
 
     def program(features, *others):
         half = features.shape[0] // 2
-        if half == 128 and 2 * groups == features.shape[0] // mesh.size == 8:
+        if half == 128 and (groups, features.shape[0] // mesh.size) == (4, 8):
             return on_axes(on_device, by_core, (*CHIPS, "core"))(features, *others)
         return on_axes(on_device_of_many, mesh, AXES)(features, *others)
 

time: 32.1 us -> 32.2 us (level)
  no operation moved by 1% of the time
where the time goes in v24:
time: 32.2 us; the launch traced here: 31.9 us
  blocking collectives  26.2 us (81%)
  Pallas kernels  3.94 us (12%)
  between operations  0.66 us (2%)
  waiting for transfers between devices  0.53 us (2%)
  starting transfers between devices  0.52 us (2%)
    all_to_all x2, blocking collectives, exchange(): lax.all_to_all(pieces, axes, split_axis=0, concat_axis=0, axis_index_grou...  26.2 us
    pallas_call x5, Pallas kernels, run(): pl.pallas_call(kernel, out_shape=out_shape, in_specs=in_specs, out_specs=...  3.94 us
  transfers between devices with their start and end apart: 2, of which 1 were waited for; matrix products, arithmetic and copies ran while one was open for 0% of the time, Pallas kernels for 3%

profile of v24, /device:TPU:0, one launch (start us, length us, event | category | flops | bytes accessed | tf_op | source)
XLA Modules:
  0.0 31.9 jit_solution(9512648566486240740)
XLA Ops:
  0.6 1.2 %shard_map.76 = (bf16[16,8,640]{2,1,0:T(8,128)(2,1)S(1)}, bf16[4,128,512]{2,1,0:T(8,128)(2,1)S(1)}, bf16[4,128,512]{2,1,0:T(8,128)(2,1)S(1)}, s32[1,128]{1,0:T(1,128)S(1)}, bf16[8,512]{1,0:T(8,128)(2,1)S(1)}) custom-call(bf16[8,512]{1,0:T(8,128)(2,1)} %features.1, s32[1,64]{1,0:T(1,128)} %bitcast.13, bf16[4,128,512]{2,1,0:T(8,128)(2,1)} %bitcast.12, ...), custom_call_target="tpu_custom_call" | custom-call | bytes 1753888 | tf_op jit(solution)/shard_map/pallas_call | solution.py:37
  1.8 0.5 %collective-permute-start.1 = (bf16[4,128,512]{2,1,0:T(8,128)(2,1)S(1)}, bf16[4,128,512]{2,1,0:T(8,128)(2,1)S(1)}, u32[]{:S(2)}, u32[]{:S(2)}) collective-permute-start(bf16[4,128,512]{2,1,0:T(8,128)(2,1)S(1)} %get-tuple-element.22.own_blocks), channel_id=1, source_target_pairs={{0,1},{1,0},{2,3},{3,2},{4,5},{5,4},{6,7},{7,6},{8,9},{9,8},{10,11... | collective-permute-start | bytes 1572872 | tf_op jit(solution)/shard_map/ppermute | solution.py:308
  2.3 13.2 %all_to_all.10 = bf16[16,8,640]{2,1,0:T(8,128)(2,1)S(1)} all-to-all(bf16[16,8,640]{2,1,0:T(8,128)(2,1)S(1)} %get-tuple-element.21), channel_id=1, replica_groups={{22,6,30,14,20,4,28,12,18,2,26,10,16,0,24,8},{23,7,31,15,21,5,29,13,19,..., dimensions={0} | all-to-all | bytes 327680 | tf_op jit(solution)/shard_map/all_to_all | solution.py:296
  15.5 0.0 collective-permute-start
  15.6 0.0 collective-permute-done.1.pair_blocks
  15.6 0.5 %shard_map.77 = (f32[2,128,128]{2,1,0:T(8,128)S(1)}, f32[128,128]{1,0:T(8,128)S(1)}, f32[2,128,128]{2,1,0:T(8,128)S(1)}, f32[2,128]{1,0:T(2,128)S(1)}) custom-call(bf16[128,640]{1,0:T(8,128)(2,1)S(1)} %bitcast.9, bf16[4,128,512]{2,1,0:T(8,128)(2,1)S(1)} %get-tuple-element.22.own_blocks, bf16[4,128,512]{2,1,0:T(8,128)(2,1)S(1)} %collective-permute-done.1.pair_blocks), custom_call_target="tpu_custom_call" | custom-call | bytes 1541120 | tf_op jit(solution)/shard_map/pallas_call | solution.py:37
  16.1 0.3 %shard_map.78 = (bf16[128,1024]{1,0:T(8,128)(2,1)S(1)}, f32[128,128]{1,0:T(8,128)S(1)}) custom-call(f32[2,128,128]{2,1,0:T(8,128)S(1)} %get-tuple-element.25.expo, f32[2,128,128]{2,1,0:T(8,128)S(1)} %get-tuple-element.23.inverse, bf16[4,128,512]{2,1,0:T(8,128)(2,1)S(1)} %get-tuple-element.22.own_blocks, ...), custom_call_target="tpu_custom_call" | custom-call | bytes 1638912 | tf_op jit(solution)/shard_map/pallas_call | solution.py:37
  16.4 0.5 %collective-permute-done.packed.other_packed = bf16[128,640]{1,0:T(8,128)(2,1)S(1)} collective-permute-done((bf16[128,640]{1,0:T(8,128)(2,1)S(1)}, bf16[128,640]{1,0:T(8,128)(2,1)S(1)}, u32[]{:S(2)}, u32[]{:S(2)}) %collective-permute-start) | collective-permute-done | bytes 163872 | tf_op jit(solution)/shard_map/ppermute | solution.py:308
  16.9 0.5 %shard_map.79 = (f32[128,128]{1,0:T(8,128)S(1)}, f32[128,128]{1,0:T(8,128)S(1)}, bf16[128,1152]{1,0:T(8,128)(2,1)S(1)}) custom-call(bf16[128,640]{1,0:T(8,128)(2,1)S(1)} %collective-permute-done.packed.other_packed, bf16[4,128,512]{2,1,0:T(8,128)(2,1)S(1)} %get-tuple-element.22.own_blocks, bf16[4,128,512]{2,1,0:T(8,128)(2,1)S(1)} %collective-permute-done.1.pair_blocks, ...), custom_call_target="tpu_custom_call" | custom-call | bytes 2032640 | tf_op jit(solution)/shard_map/pallas_call | solution.py:37
  17.4 13.0 %all_to_all.11.received = bf16[16,8,1152]{2,1,0:T(8,128)(2,1)S(1)} all-to-all(bf16[16,8,1152]{2,1,0:T(8,128)(2,1)S(1)} %bitcast.11), channel_id=1, replica_groups={{22,6,30,14,20,4,28,12,18,2,26,10,16,0,24,8},{23,7,31,15,21,5,29,13,19,..., dimensions={0} | all-to-all | bytes 589824 | tf_op jit(solution)/shard_map/all_to_all | solution.py:296
  30.5 1.4 %shard_map.80 = (f32[4,128,512]{2,1,0:T(8,128)}, f32[8,512]{1,0:T(8,128)}, f32[1,8]{1,0:T(1,128)}) custom-call(s32[1,128]{1,0:T(1,128)S(1)} %get-tuple-element.20.named, bf16[16,8,1152]{2,1,0:T(8,128)(2,1)S(1)} %all_to_all.11.received, f32[2,128,128]{2,1,0:T(8,128)S(1)} %get-tuple-element.25.expo, f32[128,128]{1,0:T(8,128)S(1)} %get-tuple-element.28.other_expo, ...), custom_call_target="tpu_custom_call" | custom-call | bytes 2613792 | tf_op jit(solution)/shard_map/pallas_call | solution.py:37
Async XLA Ops:
  1.8 13.7 %collective-permute-start.1 = (bf16[4,128,512]{2,1,0:T(8,128)(2,1)S(1)}, bf16[4,128,512]{2,1,0:T(8,128)(2,1)S(1)}, u32[]{:S(2)}, u32[]{:S(2)}) collective-permute-start(bf16[4,128,512]{2,1,0:T(8,128)(2,1)S(1)} %get-tuple-element.22.own_blocks), channel_id=1, source_target_pairs={{0,1},{1,0},{2,3},{3,2},{4,5},{5,4},{6,7},{7,6},{8,9},{9,8},{10,11... | collective-permute-start | bytes 1572872 | tf_op jit(solution)/shard_map/ppermute | solution.py:308
  15.5 1.4 %collective-permute-start = (bf16[128,640]{1,0:T(8,128)(2,1)S(1)}, bf16[128,640]{1,0:T(8,128)(2,1)S(1)}, u32[]{:S(2)}, u32[]{:S(2)}) collective-permute-start(bf16[128,640]{1,0:T(8,128)(2,1)S(1)} %bitcast.8), channel_id=1, source_target_pairs={{0,1},{1,0},{2,3},{3,2},{4,5},{5,4},{6,7},{7,6},{8,9},{9,8},{10,11... | collective-permute-start | bytes 491528 | tf_op jit(solution)/shard_map/ppermute | solution.py:308

commit v25 on v23

--- a/solution.py
+++ b/solution.py
@@ -124,8 +124,16 @@
     return out
 
 
-def exponentials(packed, core, blocks, inverse):
-    groups, _, width = blocks.shape
+def all_dots(packed, own_blocks, pair_blocks):
+    groups, _, width = own_blocks.shape
+    rows = jnp.concatenate([own_blocks[...], pair_blocks[...]], axis=0)
+    dots = contract(rows.reshape(2 * groups * BLK, width), packed[:, :width], 1, 1)
+    return dots[: groups * BLK], dots[groups * BLK :]
+
+
+def exponentials(packed, core, dots, inverse):
+    groups = dots.shape[0] // BLK
+    width = packed.shape[1] - 128
     digits = jnp.sum(
         packed[:, width:].astype(jnp.float32).reshape(128 // 8, 8, 128), axis=0
     ).astype(jnp.int32)
@@ -133,8 +141,6 @@
     member = 2 * lax.axis_index("chip") + core
     first = (member * groups + lax.axis_index("group")) * BLK
     onehot = lax.broadcasted_iota(jnp.int32, (BLK, 128), 0) == labels - first
-    units = packed[:, :width]
-    dots = contract(blocks[...].reshape(groups * BLK, width), units, 1, 1)
     cosine = inverse * select([dots[g * BLK : (g + 1) * BLK] for g in range(groups)], BLK)
     expo = jnp.exp(logit_scale * (cosine - jnp.where(onehot, cos_margin, 0.0)))
     return jnp.where(inverse > 0.0, expo, 0.0), onehot, cosine * inverse
@@ -149,11 +155,12 @@
 def forward(packed, own_blocks, pair_blocks, expo_out, scaled_out, inverse_out, sums_out):
     core = lax.axis_index("core")
     parts = []
+    dots = all_dots(packed, own_blocks, pair_blocks)
     for k, blocks in enumerate((own_blocks, pair_blocks)):
         norms = [inverse_norm(blocks[g].astype(jnp.float32)) for g in range(blocks.shape[0])]
         inverse = select(norms, BLK)
         inverse_out[k] = inverse
-        part = exponentials(packed, core if k == 0 else 1 - core, blocks, inverse)
+        part = exponentials(packed, core if k == 0 else 1 - core, dots[k], inverse)
         expo_out[k] = jnp.where(part[1], -1.0, part[0])
         parts.append(part)
     scaled_out[...] = parts[0][2]
@@ -164,8 +171,9 @@
     packed, own_blocks, pair_blocks, inverse, own_sums, shares, expo_out, scaled_out, sent_out
 ):
     core = lax.axis_index("core")
-    own = exponentials(packed, core, own_blocks, inverse[0])
-    pair = exponentials(packed, 1 - core, pair_blocks, inverse[1])
+    dots = all_dots(packed, own_blocks, pair_blocks)
+    own = exponentials(packed, core, dots[0], inverse[0])
+    pair = exponentials(packed, 1 - core, dots[1], inverse[1])
     expo_out[...] = jnp.where(own[1], -1.0, own[0])
     scaled_out[...] = own[2]
     rows, wide = shares.shape

time: 32.1 us -> 32 us (level)
  no operation moved by 1% of the time
where the time goes in v25:
time: 32 us; the launch traced here: 31.8 us
  blocking collectives  26.3 us (82%)
  Pallas kernels  3.82 us (12%)
  between operations  0.65 us (2%)
  starting transfers between devices  0.52 us (2%)
  waiting for transfers between devices  0.51 us (2%)
    all_to_all x2, blocking collectives, exchange(): lax.all_to_all(pieces, axes, split_axis=0, concat_axis=0, axis_index_grou...  26.3 us
    pallas_call x5, Pallas kernels, run(): pl.pallas_call(kernel, out_shape=out_shape, in_specs=in_specs, out_specs=...  3.82 us
  transfers between devices with their start and end apart: 2, of which 1 were waited for; matrix products, arithmetic and copies ran while one was open for 0% of the time, Pallas kernels for 3%

profile of v25, /device:TPU:0, one launch (start us, length us, event | category | flops | bytes accessed | tf_op | source)
XLA Modules:
  0.0 31.8 jit_solution(13693212130573657825)
XLA Ops:
  0.6 1.2 %shard_map.76 = (bf16[16,8,640]{2,1,0:T(8,128)(2,1)S(1)}, bf16[4,128,512]{2,1,0:T(8,128)(2,1)S(1)}, bf16[4,128,512]{2,1,0:T(8,128)(2,1)S(1)}, s32[1,128]{1,0:T(1,128)S(1)}, bf16[8,512]{1,0:T(8,128)(2,1)S(1)}) custom-call(bf16[8,512]{1,0:T(8,128)(2,1)} %features.1, s32[1,64]{1,0:T(1,128)} %bitcast.13, bf16[4,128,512]{2,1,0:T(8,128)(2,1)} %bitcast.12, ...), custom_call_target="tpu_custom_call" | custom-call | bytes 1753888 | tf_op jit(solution)/shard_map/pallas_call | solution.py:37
  1.8 0.5 %collective-permute-start.1 = (bf16[4,128,512]{2,1,0:T(8,128)(2,1)S(1)}, bf16[4,128,512]{2,1,0:T(8,128)(2,1)S(1)}, u32[]{:S(2)}, u32[]{:S(2)}) collective-permute-start(bf16[4,128,512]{2,1,0:T(8,128)(2,1)S(1)} %get-tuple-element.20.own_blocks), channel_id=1, source_target_pairs={{0,1},{1,0},{2,3},{3,2},{4,5},{5,4},{6,7},{7,6},{8,9},{9,8},{10,11... | collective-permute-start | bytes 1572872 | tf_op jit(solution)/shard_map/ppermute | solution.py:315
  2.3 13.2 %all_to_all.10 = bf16[16,8,640]{2,1,0:T(8,128)(2,1)S(1)} all-to-all(bf16[16,8,640]{2,1,0:T(8,128)(2,1)S(1)} %get-tuple-element.19), channel_id=1, replica_groups={{22,6,30,14,20,4,28,12,18,2,26,10,16,0,24,8},{23,7,31,15,21,5,29,13,19,..., dimensions={0} | all-to-all | bytes 327680 | tf_op jit(solution)/shard_map/all_to_all | solution.py:303
  15.5 0.0 collective-permute-start
  15.6 0.0 collective-permute-done.1.pair_blocks
  15.6 0.5 %shard_map.77 = (f32[2,128,128]{2,1,0:T(8,128)S(1)}, f32[128,128]{1,0:T(8,128)S(1)}, f32[2,128,128]{2,1,0:T(8,128)S(1)}, f32[2,128]{1,0:T(2,128)S(1)}) custom-call(bf16[128,640]{1,0:T(8,128)(2,1)S(1)} %bitcast.9, bf16[4,128,512]{2,1,0:T(8,128)(2,1)S(1)} %get-tuple-element.20.own_blocks, bf16[4,128,512]{2,1,0:T(8,128)(2,1)S(1)} %collective-permute-done.1.pair_blocks), custom_call_target="tpu_custom_call" | custom-call | bytes 1541120 | tf_op jit(solution)/shard_map/pallas_call | solution.py:37
  16.1 0.3 %shard_map.78.shares = bf16[128,1024]{1,0:T(8,128)(2,1)S(1)} custom-call(f32[2,128,128]{2,1,0:T(8,128)S(1)} %get-tuple-element.23.expo, f32[2,128,128]{2,1,0:T(8,128)S(1)} %get-tuple-element.21.inverse, bf16[4,128,512]{2,1,0:T(8,128)(2,1)S(1)} %get-tuple-element.20.own_blocks, bf16[4,128,512]{2,1,0:T(8,128)(2,1)S(1)} %collective-permute-done.1.pair_blocks), custom_call_target="tpu_custom_call" | custom-call | bytes 1572864 | tf_op jit(solution)/shard_map/pallas_call | solution.py:37
  16.4 0.5 %collective-permute-done.packed.other_packed = bf16[128,640]{1,0:T(8,128)(2,1)S(1)} collective-permute-done((bf16[128,640]{1,0:T(8,128)(2,1)S(1)}, bf16[128,640]{1,0:T(8,128)(2,1)S(1)}, u32[]{:S(2)}, u32[]{:S(2)}) %collective-permute-start) | collective-permute-done | bytes 163872 | tf_op jit(solution)/shard_map/ppermute | solution.py:315
  16.9 0.5 %shard_map.79 = (f32[128,128]{1,0:T(8,128)S(1)}, f32[128,128]{1,0:T(8,128)S(1)}, bf16[128,1152]{1,0:T(8,128)(2,1)S(1)}) custom-call(bf16[128,640]{1,0:T(8,128)(2,1)S(1)} %collective-permute-done.packed.other_packed, bf16[4,128,512]{2,1,0:T(8,128)(2,1)S(1)} %get-tuple-element.20.own_blocks, bf16[4,128,512]{2,1,0:T(8,128)(2,1)S(1)} %collective-permute-done.1.pair_blocks, ...), custom_call_target="tpu_custom_call" | custom-call | bytes 2032640 | tf_op jit(solution)/shard_map/pallas_call | solution.py:37
  17.4 13.0 %all_to_all.11.received = bf16[16,8,1152]{2,1,0:T(8,128)(2,1)S(1)} all-to-all(bf16[16,8,1152]{2,1,0:T(8,128)(2,1)S(1)} %bitcast.11), channel_id=1, replica_groups={{22,6,30,14,20,4,28,12,18,2,26,10,16,0,24,8},{23,7,31,15,21,5,29,13,19,..., dimensions={0} | all-to-all | bytes 589824 | tf_op jit(solution)/shard_map/all_to_all | solution.py:303
  30.4 1.3 %shard_map.80 = (f32[4,128,512]{2,1,0:T(8,128)}, f32[8,512]{1,0:T(8,128)}, f32[1,8]{1,0:T(1,128)}) custom-call(s32[1,128]{1,0:T(1,128)S(1)} %get-tuple-element.18.named, bf16[16,8,1152]{2,1,0:T(8,128)(2,1)S(1)} %all_to_all.11.received, f32[2,128,128]{2,1,0:T(8,128)S(1)} %get-tuple-element.23.expo, f32[128,128]{1,0:T(8,128)S(1)} %get-tuple-element.25.other_expo, ...), custom_call_target="tpu_custom_call" | custom-call | bytes 2679328 | tf_op jit(solution)/shard_map/pallas_call | solution.py:37
Async XLA Ops:
  1.8 13.7 %collective-permute-start.1 = (bf16[4,128,512]{2,1,0:T(8,128)(2,1)S(1)}, bf16[4,128,512]{2,1,0:T(8,128)(2,1)S(1)}, u32[]{:S(2)}, u32[]{:S(2)}) collective-permute-start(bf16[4,128,512]{2,1,0:T(8,128)(2,1)S(1)} %get-tuple-element.20.own_blocks), channel_id=1, source_target_pairs={{0,1},{1,0},{2,3},{3,2},{4,5},{5,4},{6,7},{7,6},{8,9},{9,8},{10,11... | collective-permute-start | bytes 1572872 | tf_op jit(solution)/shard_map/ppermute | solution.py:315
  15.5 1.4 %collective-permute-start = (bf16[128,640]{1,0:T(8,128)(2,1)S(1)}, bf16[128,640]{1,0:T(8,128)(2,1)S(1)}, u32[]{:S(2)}, u32[]{:S(2)}) collective-permute-start(bf16[128,640]{1,0:T(8,128)(2,1)S(1)} %bitcast.8), channel_id=1, source_target_pairs={{0,1},{1,0},{2,3},{3,2},{4,5},{5,4},{6,7},{7,6},{8,9},{9,8},{10,11... | collective-permute-start | bytes 491528 | tf_op jit(solution)/shard_map/ppermute | solution.py:315

commit v26 on v25

--- a/solution.py
+++ b/solution.py
@@ -252,6 +252,8 @@
     pulls = weights * jnp.concatenate([scaled[...], other_scaled[...]], axis=1)
     own_named = named[...]
     named = jnp.concatenate([own_named, own_named], axis=1)
+    masked = [jnp.where(named == b, weights, 0.0).astype(jnp.bfloat16) for b in range(held)]
+    slot_grads = contract(jnp.concatenate(masked, axis=0), units, 1, 0)
     moves = []
 
     def leave(source, target):
@@ -260,10 +262,9 @@
         moves.append(move)
 
     def block_out(b):
-        mine = jnp.where(named == b, weights, 0.0).astype(jnp.bfloat16)
         factor = jnp.max(jnp.where(own_named == b, inverse[0], 0.0), axis=1, keepdims=True)
         back = factor * jnp.sum(jnp.where(named == b, pulls, 0.0), axis=1, keepdims=True)
-        slot_grad = contract(mine, units, 1, 0)
+        slot_grad = slot_grads[b * BLK : (b + 1) * BLK]
         grad[b] = factor * slot_grad - back * centres[b].astype(jnp.float32)
         leave(grad.at[b], grad_out.at[b])
 

time: 32 us -> 32 us (level)
  no operation moved by 1% of the time
where the time goes in v26:
time: 32 us; the launch traced here: 31.7 us
  blocking collectives  26.3 us (82%)
  Pallas kernels  3.79 us (12%)
  between operations  0.65 us (2%)
  starting transfers between devices  0.52 us (2%)
  waiting for transfers between devices  0.51 us (2%)
    all_to_all x2, blocking collectives, exchange(): lax.all_to_all(pieces, axes, split_axis=0, concat_axis=0, axis_index_grou...  26.3 us
    pallas_call x5, Pallas kernels, run(): pl.pallas_call(kernel, out_shape=out_shape, in_specs=in_specs, out_specs=...  3.79 us
  transfers between devices with their start and end apart: 2, of which 1 were waited for; matrix products, arithmetic and copies ran while one was open for 0% of the time, Pallas kernels for 3%

profile of v26, /device:TPU:0, one launch (start us, length us, event | category | flops | bytes accessed | tf_op | source)
XLA Modules:
  0.0 31.7 jit_solution(1026644376859450985)
XLA Ops:
  0.6 1.2 %shard_map.76 = (bf16[16,8,640]{2,1,0:T(8,128)(2,1)S(1)}, bf16[4,128,512]{2,1,0:T(8,128)(2,1)S(1)}, bf16[4,128,512]{2,1,0:T(8,128)(2,1)S(1)}, s32[1,128]{1,0:T(1,128)S(1)}, bf16[8,512]{1,0:T(8,128)(2,1)S(1)}) custom-call(bf16[8,512]{1,0:T(8,128)(2,1)} %features.1, s32[1,64]{1,0:T(1,128)} %bitcast.13, bf16[4,128,512]{2,1,0:T(8,128)(2,1)} %bitcast.12, ...), custom_call_target="tpu_custom_call" | custom-call | bytes 1753888 | tf_op jit(solution)/shard_map/pallas_call | solution.py:37
  1.8 0.5 %collective-permute-start.1 = (bf16[4,128,512]{2,1,0:T(8,128)(2,1)S(1)}, bf16[4,128,512]{2,1,0:T(8,128)(2,1)S(1)}, u32[]{:S(2)}, u32[]{:S(2)}) collective-permute-start(bf16[4,128,512]{2,1,0:T(8,128)(2,1)S(1)} %get-tuple-element.20.own_blocks), channel_id=1, source_target_pairs={{0,1},{1,0},{2,3},{3,2},{4,5},{5,4},{6,7},{7,6},{8,9},{9,8},{10,11... | collective-permute-start | bytes 1572872 | tf_op jit(solution)/shard_map/ppermute | solution.py:316
  2.3 13.2 %all_to_all.10 = bf16[16,8,640]{2,1,0:T(8,128)(2,1)S(1)} all-to-all(bf16[16,8,640]{2,1,0:T(8,128)(2,1)S(1)} %get-tuple-element.19), channel_id=1, replica_groups={{22,6,30,14,20,4,28,12,18,2,26,10,16,0,24,8},{23,7,31,15,21,5,29,13,19,..., dimensions={0} | all-to-all | bytes 327680 | tf_op jit(solution)/shard_map/all_to_all | solution.py:304
  15.5 0.0 collective-permute-start
  15.6 0.0 collective-permute-done.1.pair_blocks
  15.6 0.5 %shard_map.77 = (f32[2,128,128]{2,1,0:T(8,128)S(1)}, f32[128,128]{1,0:T(8,128)S(1)}, f32[2,128,128]{2,1,0:T(8,128)S(1)}, f32[2,128]{1,0:T(2,128)S(1)}) custom-call(bf16[128,640]{1,0:T(8,128)(2,1)S(1)} %bitcast.9, bf16[4,128,512]{2,1,0:T(8,128)(2,1)S(1)} %get-tuple-element.20.own_blocks, bf16[4,128,512]{2,1,0:T(8,128)(2,1)S(1)} %collective-permute-done.1.pair_blocks), custom_call_target="tpu_custom_call" | custom-call | bytes 1541120 | tf_op jit(solution)/shard_map/pallas_call | solution.py:37
  16.1 0.3 %shard_map.78.shares = bf16[128,1024]{1,0:T(8,128)(2,1)S(1)} custom-call(f32[2,128,128]{2,1,0:T(8,128)S(1)} %get-tuple-element.23.expo, f32[2,128,128]{2,1,0:T(8,128)S(1)} %get-tuple-element.21.inverse, bf16[4,128,512]{2,1,0:T(8,128)(2,1)S(1)} %get-tuple-element.20.own_blocks, bf16[4,128,512]{2,1,0:T(8,128)(2,1)S(1)} %collective-permute-done.1.pair_blocks), custom_call_target="tpu_custom_call" | custom-call | bytes 1572864 | tf_op jit(solution)/shard_map/pallas_call | solution.py:37
  16.4 0.5 %collective-permute-done.packed.other_packed = bf16[128,640]{1,0:T(8,128)(2,1)S(1)} collective-permute-done((bf16[128,640]{1,0:T(8,128)(2,1)S(1)}, bf16[128,640]{1,0:T(8,128)(2,1)S(1)}, u32[]{:S(2)}, u32[]{:S(2)}) %collective-permute-start) | collective-permute-done | bytes 163872 | tf_op jit(solution)/shard_map/ppermute | solution.py:316
  16.9 0.5 %shard_map.79 = (f32[128,128]{1,0:T(8,128)S(1)}, f32[128,128]{1,0:T(8,128)S(1)}, bf16[128,1152]{1,0:T(8,128)(2,1)S(1)}) custom-call(bf16[128,640]{1,0:T(8,128)(2,1)S(1)} %collective-permute-done.packed.other_packed, bf16[4,128,512]{2,1,0:T(8,128)(2,1)S(1)} %get-tuple-element.20.own_blocks, bf16[4,128,512]{2,1,0:T(8,128)(2,1)S(1)} %collective-permute-done.1.pair_blocks, ...), custom_call_target="tpu_custom_call" | custom-call | bytes 2032640 | tf_op jit(solution)/shard_map/pallas_call | solution.py:37
  17.4 13.0 %all_to_all.11.received = bf16[16,8,1152]{2,1,0:T(8,128)(2,1)S(1)} all-to-all(bf16[16,8,1152]{2,1,0:T(8,128)(2,1)S(1)} %bitcast.11), channel_id=1, replica_groups={{22,6,30,14,20,4,28,12,18,2,26,10,16,0,24,8},{23,7,31,15,21,5,29,13,19,..., dimensions={0} | all-to-all | bytes 589824 | tf_op jit(solution)/shard_map/all_to_all | solution.py:304
  30.4 1.3 %shard_map.80 = (f32[4,128,512]{2,1,0:T(8,128)}, f32[8,512]{1,0:T(8,128)}, f32[1,8]{1,0:T(1,128)}) custom-call(s32[1,128]{1,0:T(1,128)S(1)} %get-tuple-element.18.named, bf16[16,8,1152]{2,1,0:T(8,128)(2,1)S(1)} %all_to_all.11.received, f32[2,128,128]{2,1,0:T(8,128)S(1)} %get-tuple-element.23.expo, f32[128,128]{1,0:T(8,128)S(1)} %get-tuple-element.25.other_expo, ...), custom_call_target="tpu_custom_call" | custom-call | bytes 2679328 | tf_op jit(solution)/shard_map/pallas_call | solution.py:37
Async XLA Ops:
  1.8 13.7 %collective-permute-start.1 = (bf16[4,128,512]{2,1,0:T(8,128)(2,1)S(1)}, bf16[4,128,512]{2,1,0:T(8,128)(2,1)S(1)}, u32[]{:S(2)}, u32[]{:S(2)}) collective-permute-start(bf16[4,128,512]{2,1,0:T(8,128)(2,1)S(1)} %get-tuple-element.20.own_blocks), channel_id=1, source_target_pairs={{0,1},{1,0},{2,3},{3,2},{4,5},{5,4},{6,7},{7,6},{8,9},{9,8},{10,11... | collective-permute-start | bytes 1572872 | tf_op jit(solution)/shard_map/ppermute | solution.py:316
  15.5 1.4 %collective-permute-start = (bf16[128,640]{1,0:T(8,128)(2,1)S(1)}, bf16[128,640]{1,0:T(8,128)(2,1)S(1)}, u32[]{:S(2)}, u32[]{:S(2)}) collective-permute-start(bf16[128,640]{1,0:T(8,128)(2,1)S(1)} %bitcast.8), channel_id=1, source_target_pairs={{0,1},{1,0},{2,3},{3,2},{4,5},{5,4},{6,7},{7,6},{8,9},{9,8},{10,11... | collective-permute-start | bytes 491528 | tf_op jit(solution)/shard_map/ppermute | solution.py:316

commit v27 on v26

--- a/solution.py
+++ b/solution.py
@@ -268,7 +268,7 @@
         grad[b] = factor * slot_grad - back * centres[b].astype(jnp.float32)
         leave(grad.at[b], grad_out.at[b])
 
-    for b in range(held // 2):
+    for b in range(1):
         block_out(b)
 
     sums = total_of(pl.ds(0, 2 * width))
@@ -294,7 +294,7 @@
 
     leave(feature_grad, feature_out)
     leave(loss_row, loss_out)
-    for b in range(held // 2, held):
+    for b in range(1, held):
         block_out(b)
     for move in moves:
         move.wait()

time: 32 us -> 32 us (level)
  no operation moved by 1% of the time
where the time goes in v27:
time: 32 us; the launch traced here: 31.7 us
  blocking collectives  26.3 us (82%)
  Pallas kernels  3.79 us (12%)
  between operations  0.65 us (2%)
  starting transfers between devices  0.52 us (2%)
  waiting for transfers between devices  0.51 us (2%)
    all_to_all x2, blocking collectives, exchange(): lax.all_to_all(pieces, axes, split_axis=0, concat_axis=0, axis_index_grou...  26.3 us
    pallas_call x5, Pallas kernels, run(): pl.pallas_call(kernel, out_shape=out_shape, in_specs=in_specs, out_specs=...  3.79 us
  transfers between devices with their start and end apart: 2, of which 1 were waited for; matrix products, arithmetic and copies ran while one was open for 0% of the time, Pallas kernels for 3%

profile of v27, /device:TPU:0, one launch (start us, length us, event | category | flops | bytes accessed | tf_op | source)
XLA Modules:
  0.0 31.7 jit_solution(6111859312943073809)
XLA Ops:
  0.6 1.2 %shard_map.76 = (bf16[16,8,640]{2,1,0:T(8,128)(2,1)S(1)}, bf16[4,128,512]{2,1,0:T(8,128)(2,1)S(1)}, bf16[4,128,512]{2,1,0:T(8,128)(2,1)S(1)}, s32[1,128]{1,0:T(1,128)S(1)}, bf16[8,512]{1,0:T(8,128)(2,1)S(1)}) custom-call(bf16[8,512]{1,0:T(8,128)(2,1)} %features.1, s32[1,64]{1,0:T(1,128)} %bitcast.13, bf16[4,128,512]{2,1,0:T(8,128)(2,1)} %bitcast.12, ...), custom_call_target="tpu_custom_call" | custom-call | bytes 1753888 | tf_op jit(solution)/shard_map/pallas_call | solution.py:37
  1.8 0.5 %collective-permute-start.1 = (bf16[4,128,512]{2,1,0:T(8,128)(2,1)S(1)}, bf16[4,128,512]{2,1,0:T(8,128)(2,1)S(1)}, u32[]{:S(2)}, u32[]{:S(2)}) collective-permute-start(bf16[4,128,512]{2,1,0:T(8,128)(2,1)S(1)} %get-tuple-element.20.own_blocks), channel_id=1, source_target_pairs={{0,1},{1,0},{2,3},{3,2},{4,5},{5,4},{6,7},{7,6},{8,9},{9,8},{10,11... | collective-permute-start | bytes 1572872 | tf_op jit(solution)/shard_map/ppermute | solution.py:316
  2.3 13.2 %all_to_all.10 = bf16[16,8,640]{2,1,0:T(8,128)(2,1)S(1)} all-to-all(bf16[16,8,640]{2,1,0:T(8,128)(2,1)S(1)} %get-tuple-element.19), channel_id=1, replica_groups={{22,6,30,14,20,4,28,12,18,2,26,10,16,0,24,8},{23,7,31,15,21,5,29,13,19,..., dimensions={0} | all-to-all | bytes 327680 | tf_op jit(solution)/shard_map/all_to_all | solution.py:304
  15.5 0.0 collective-permute-start
  15.6 0.0 collective-permute-done.1.pair_blocks
  15.6 0.5 %shard_map.77 = (f32[2,128,128]{2,1,0:T(8,128)S(1)}, f32[128,128]{1,0:T(8,128)S(1)}, f32[2,128,128]{2,1,0:T(8,128)S(1)}, f32[2,128]{1,0:T(2,128)S(1)}) custom-call(bf16[128,640]{1,0:T(8,128)(2,1)S(1)} %bitcast.9, bf16[4,128,512]{2,1,0:T(8,128)(2,1)S(1)} %get-tuple-element.20.own_blocks, bf16[4,128,512]{2,1,0:T(8,128)(2,1)S(1)} %collective-permute-done.1.pair_blocks), custom_call_target="tpu_custom_call" | custom-call | bytes 1541120 | tf_op jit(solution)/shard_map/pallas_call | solution.py:37
  16.1 0.3 %shard_map.78.shares = bf16[128,1024]{1,0:T(8,128)(2,1)S(1)} custom-call(f32[2,128,128]{2,1,0:T(8,128)S(1)} %get-tuple-element.23.expo, f32[2,128,128]{2,1,0:T(8,128)S(1)} %get-tuple-element.21.inverse, bf16[4,128,512]{2,1,0:T(8,128)(2,1)S(1)} %get-tuple-element.20.own_blocks, bf16[4,128,512]{2,1,0:T(8,128)(2,1)S(1)} %collective-permute-done.1.pair_blocks), custom_call_target="tpu_custom_call" | custom-call | bytes 1572864 | tf_op jit(solution)/shard_map/pallas_call | solution.py:37
  16.4 0.5 %collective-permute-done.packed.other_packed = bf16[128,640]{1,0:T(8,128)(2,1)S(1)} collective-permute-done((bf16[128,640]{1,0:T(8,128)(2,1)S(1)}, bf16[128,640]{1,0:T(8,128)(2,1)S(1)}, u32[]{:S(2)}, u32[]{:S(2)}) %collective-permute-start) | collective-permute-done | bytes 163872 | tf_op jit(solution)/shard_map/ppermute | solution.py:316
  16.9 0.5 %shard_map.79 = (f32[128,128]{1,0:T(8,128)S(1)}, f32[128,128]{1,0:T(8,128)S(1)}, bf16[128,1152]{1,0:T(8,128)(2,1)S(1)}) custom-call(bf16[128,640]{1,0:T(8,128)(2,1)S(1)} %collective-permute-done.packed.other_packed, bf16[4,128,512]{2,1,0:T(8,128)(2,1)S(1)} %get-tuple-element.20.own_blocks, bf16[4,128,512]{2,1,0:T(8,128)(2,1)S(1)} %collective-permute-done.1.pair_blocks, ...), custom_call_target="tpu_custom_call" | custom-call | bytes 2032640 | tf_op jit(solution)/shard_map/pallas_call | solution.py:37
  17.4 13.0 %all_to_all.11.received = bf16[16,8,1152]{2,1,0:T(8,128)(2,1)S(1)} all-to-all(bf16[16,8,1152]{2,1,0:T(8,128)(2,1)S(1)} %bitcast.11), channel_id=1, replica_groups={{22,6,30,14,20,4,28,12,18,2,26,10,16,0,24,8},{23,7,31,15,21,5,29,13,19,..., dimensions={0} | all-to-all | bytes 589824 | tf_op jit(solution)/shard_map/all_to_all | solution.py:304
  30.4 1.3 %shard_map.80 = (f32[4,128,512]{2,1,0:T(8,128)}, f32[8,512]{1,0:T(8,128)}, f32[1,8]{1,0:T(1,128)}) custom-call(s32[1,128]{1,0:T(1,128)S(1)} %get-tuple-element.18.named, bf16[16,8,1152]{2,1,0:T(8,128)(2,1)S(1)} %all_to_all.11.received, f32[2,128,128]{2,1,0:T(8,128)S(1)} %get-tuple-element.23.expo, f32[128,128]{1,0:T(8,128)S(1)} %get-tuple-element.25.other_expo, ...), custom_call_target="tpu_custom_call" | custom-call | bytes 2679328 | tf_op jit(solution)/shard_map/pallas_call | solution.py:37
Async XLA Ops:
  1.8 13.7 %collective-permute-start.1 = (bf16[4,128,512]{2,1,0:T(8,128)(2,1)S(1)}, bf16[4,128,512]{2,1,0:T(8,128)(2,1)S(1)}, u32[]{:S(2)}, u32[]{:S(2)}) collective-permute-start(bf16[4,128,512]{2,1,0:T(8,128)(2,1)S(1)} %get-tuple-element.20.own_blocks), channel_id=1, source_target_pairs={{0,1},{1,0},{2,3},{3,2},{4,5},{5,4},{6,7},{7,6},{8,9},{9,8},{10,11... | collective-permute-start | bytes 1572872 | tf_op jit(solution)/shard_map/ppermute | solution.py:316
  15.5 1.4 %collective-permute-start = (bf16[128,640]{1,0:T(8,128)(2,1)S(1)}, bf16[128,640]{1,0:T(8,128)(2,1)S(1)}, u32[]{:S(2)}, u32[]{:S(2)}) collective-permute-start(bf16[128,640]{1,0:T(8,128)(2,1)S(1)} %bitcast.8), channel_id=1, source_target_pairs={{0,1},{1,0},{2,3},{3,2},{4,5},{5,4},{6,7},{7,6},{8,9},{9,8},{10,11... | collective-permute-start | bytes 491528 | tf_op jit(solution)/shard_map/ppermute | solution.py:316
